TPU v7x, 32 devices: a whole 2x2x4 slice. The times are simulated.
32 devices in a mesh: cells: 8 (over z, y), seq: 4 (over x, core).
Axes of the slice: x: 2, y: 2, z: 4, core: 2. Of those that a mesh axis runs over, the one named last changes fastest.
Arguments:
- tokens: bfloat16 [16, 1024, 1120], P('cells', 'seq'), may hold values from -6 to 6
- first_gain: float32 [1120], replicated, may hold values from 0.1 to 1.9
- first_shift: float32 [1120], replicated, may hold values from -1.8 to 1.8
- mix_weight: bfloat16 [1120, 3360], replicated, may hold values from -0.1875 to 0.1875
- query_bias: float32 [1120], replicated, may hold values from -1.8 to 1.8
- value_bias: float32 [1120], replicated, may hold values from -1.8 to 1.8
- out_weight: bfloat16 [1120, 1120], replicated, may hold values from -1.5 to 1.5
- out_bias: float32 [1120], replicated, may hold values from -1.8 to 1.8
- second_gain: float32 [1120], replicated, may hold values from 0.1 to 1.9
- second_shift: float32 [1120], replicated, may hold values from -1.8 to 1.8
- up_weight: bfloat16 [1120, 4480], replicated, may hold values from -0.1875 to 0.1875
- up_bias: float32 [4480], replicated, may hold values from -1.8 to 1.8
- down_weight: bfloat16 [4480, 1120], replicated, may hold values from -0.09375 to 0.09375
- down_bias: float32 [1120], replicated, may hold values from -1.8 to 1.8
- cotangent: bfloat16 [16, 1024, 1120], P('cells', 'seq'), may hold values from -6 to 6
- prefix_lengths: int32 [16], P('cells'), may hold values from 1 to 8, as said below
- gene_counts: int32 [16], P('cells'), may hold values from 200 to 1023, as said below
- key_mask: int32 [16, 1024], P('cells', 'seq'), may hold values 0 or 1
Outputs:
- block_out: bfloat16 [16, 1024, 1120], P('cells', 'seq')
- tokens_gradient: bfloat16 [16, 1024, 1120], P('cells', 'seq')
- first_gain_gradient: float32 [1120], P('cells')
- first_shift_gradient: float32 [1120], P('cells')
- mix_weight_gradient: float32 [1120, 3360], P('cells', 'seq')
- query_bias_gradient: float32 [1120], P('cells')
- value_bias_gradient: float32 [1120], P('cells')
- out_weight_gradient: float32 [1120, 1120], P('cells', 'seq')
- out_bias_gradient: float32 [1120], P('cells')
- second_gain_gradient: float32 [1120], P('cells')
- second_shift_gradient: float32 [1120], P('cells')
- up_weight_gradient: float32 [1120, 4480], P('cells', 'seq')
- up_bias_gradient: float32 [4480], P('cells')
- down_weight_gradient: float32 [4480, 1120], P('cells', 'seq')
- down_bias_gradient: float32 [1120], P('cells')
Inputs may be any that keep to these rules, and one draw needn't show every extreme that they name: `prefix_lengths`: at most 8; cell 0 has 8. `gene_counts`: prefix plus genes is at most 1024; among cells k * 2 to (k+1) * 2 - 1, for every k, one cell's prefix plus genes exceeds 1024 - 1024 // 4; in the last such group that cell fills all 1024 positions.
All inputs are finite; a program needn't handle non-finite values. No bound on the sum of `key_mask` on one device may be relied on, other than what follows from the above.
Results may differ from a plain program's by a relative error of at most 0.025.
Values may be sent and summed in bfloat16 or wider, within the bound.
No kernel may reach another device: no remote copies, remote signals or barrier semaphores. Data moves between devices by JAX's collectives and lax.ppermute only.
A program may use at most 320 MiB of HBM per device.

v0:
```python
from functools import partial
import math

import jax
import jax.numpy as jnp
from jax import lax
from jax.sharding import PartitionSpec as P

HEADS = 20


def layer_norm(values, gain, shift):
    centre = jnp.mean(values, axis=-1, keepdims=True)
    centred = values - centre
    spread = jnp.mean(centred * centred, axis=-1, keepdims=True)
    return centred * lax.rsqrt(spread + 1e-05) * gain + shift


def on_device(
    tokens,
    first_gain,
    first_shift,
    mix_weight,
    query_bias,
    value_bias,
    out_weight,
    out_bias,
    second_gain,
    second_shift,
    up_weight,
    up_bias,
    down_weight,
    down_bias,
    cotangent,
    prefix_lengths,
    gene_counts,
    key_mask,
):
    cells_here, span, width = tokens.shape
    head_size = width // HEADS
    length = span * lax.axis_size("seq")
    start = lax.axis_index("seq") * span
    group = math.gcd(cells_here, max(1, 512 // span))
    blocks = cells_here // group
    scale = 1.0 / math.sqrt(head_size)
    totals = prefix_lengths + gene_counts
    row_count = cells_here * span
    own_rows = start + jnp.arange(span)
    every_row = jnp.arange(length)

    def cut(array):
        return array.reshape((blocks, group) + array.shape[1:])

    def split_heads(array):
        return array.reshape(array.shape[:2] + (HEADS, head_size))

    def flat(array):
        return array.reshape(row_count, array.shape[-1])

    def score_block(queries, keys, prefix, total, keeps, row_places, key_places):
        raw = (
            jnp.einsum("gqhe,gkhe->ghqk", queries, keys, preferred_element_type=jnp.float32) * scale
        )
        places = key_places[None, None, :]
        rows = row_places[None, :, None]
        open_key = (
            (places < total[:, None, None])
            & keeps[:, None, :]
            & ((places <= rows) | (places < prefix[:, None, None]))
        )
        seen = open_key | (places == rows)
        return jnp.where(seen[:, None], raw, -1e30)

    def scores_back(scores, log_sum, back_heads, values):
        probs = jnp.exp(scores - log_sum[..., None])
        back_probs = jnp.einsum(
            "gqhe,gkhe->ghqk", back_heads, values, preferred_element_type=jnp.float32
        )
        return (probs, back_probs)

    inputs = tokens.astype(jnp.float32)
    normed = layer_norm(inputs, first_gain, first_shift).astype(jnp.bfloat16)
    mixed = jnp.dot(normed, mix_weight, preferred_element_type=jnp.float32)
    queries = (mixed[..., :width] + query_bias).astype(jnp.bfloat16)
    keys_low = mixed[..., width : 2 * width].astype(jnp.bfloat16)
    values_low = (mixed[..., 2 * width :] + value_bias).astype(jnp.bfloat16)
    all_keys, all_values, all_mask = (
        lax.all_gather(keys_low, "seq", axis=1, tiled=True),
        lax.all_gather(values_low, "seq", axis=1, tiled=True),
        lax.all_gather(key_mask.astype(jnp.bfloat16), "seq", axis=1, tiled=True),
    )
    keeps = all_mask > 0.5
    query_heads = cut(split_heads(queries))
    key_heads = cut(split_heads(all_keys))
    value_heads = cut(split_heads(all_values))
    prefix_blocks = cut(prefix_lengths)
    total_blocks = cut(totals)
    keep_blocks = cut(keeps)

    def attend_forward(block):
        query, keys, values, prefix, total, keep = block
        scores = score_block(query, keys, prefix, total, keep, own_rows, every_row)
        top = jnp.max(scores, axis=-1, keepdims=True)
        raised = jnp.exp(scores - top)
        summed = jnp.sum(raised, axis=-1, keepdims=True)
        probs = (raised / summed).astype(jnp.bfloat16)
        result = jnp.einsum("ghqk,gkhe->gqhe", probs, values, preferred_element_type=jnp.float32)
        return (result.astype(jnp.bfloat16), (top + jnp.log(summed))[..., 0])

    attended, log_sums = lax.map(
        attend_forward,
        (query_heads, key_heads, value_heads, prefix_blocks, total_blocks, keep_blocks),
    )
    attended = attended.reshape(cells_here, span, width)
    middle = inputs + (jnp.dot(attended, out_weight, preferred_element_type=jnp.float32) + out_bias)
    second = layer_norm(middle, second_gain, second_shift).astype(jnp.bfloat16)
    upper = jnp.dot(second, up_weight, preferred_element_type=jnp.float32) + up_bias
    gelu_tanh = partial(jax.nn.gelu, approximate=True)
    active = gelu_tanh(upper).astype(jnp.bfloat16)
    result = middle + jnp.dot(active, down_weight, preferred_element_type=jnp.float32) + down_bias
    block_out = result.astype(jnp.bfloat16)
    back_out = cotangent.astype(jnp.float32)
    down_weight_back = jnp.einsum(
        "tf,td->fd", flat(active), flat(cotangent), preferred_element_type=jnp.float32
    )
    down_bias_back = jnp.sum(flat(back_out), axis=0)
    back_active = jnp.einsum(
        "ctd,fd->ctf", cotangent, down_weight, preferred_element_type=jnp.float32
    )
    gelu_value, gelu_pull = jax.vjp(gelu_tanh, upper)
    back_upper = gelu_pull(back_active)[0].astype(jnp.bfloat16)
    up_weight_back = jnp.einsum(
        "td,tf->df", flat(second), flat(back_upper), preferred_element_type=jnp.float32
    )
    up_bias_back = jnp.sum(flat(back_upper).astype(jnp.float32), axis=0)
    back_second = jnp.einsum(
        "ctf,df->ctd", back_upper, up_weight, preferred_element_type=jnp.float32
    )
    norm_value, norm_pull = jax.vjp(layer_norm, middle, second_gain, second_shift)
    middle_part, second_gain_back, second_shift_back = norm_pull(back_second)
    back_middle = back_out + middle_part
    back_branch = back_middle.astype(jnp.bfloat16)
    out_weight_back = jnp.einsum(
        "td,te->de", flat(attended), flat(back_branch), preferred_element_type=jnp.float32
    )
    out_bias_back = jnp.sum(flat(back_branch).astype(jnp.float32), axis=0)
    back_attended = jnp.einsum(
        "cte,de->ctd", back_branch, out_weight, preferred_element_type=jnp.float32
    ).astype(jnp.bfloat16)
    back_blocks = cut(split_heads(back_attended))

    def attend_backward(block):
        query, keys, values, prefix, total, keep, log_sum, back_heads = block
        scores = score_block(query, keys, prefix, total, keep, own_rows, every_row)
        probs, back_probs = scores_back(scores, log_sum, back_heads, values)
        probs_low = probs.astype(jnp.bfloat16)
        values_back = jnp.einsum(
            "ghqk,gqhe->gkhe", probs_low, back_heads, preferred_element_type=jnp.float32
        )
        centre = jnp.sum(back_probs * probs, axis=-1, keepdims=True)
        back_scores = (probs * (back_probs - centre)).astype(jnp.bfloat16)
        query_back = (
            jnp.einsum("ghqk,gkhe->gqhe", back_scores, keys, preferred_element_type=jnp.float32)
            * scale
        )
        keys_back = (
            jnp.einsum("ghqk,gqhe->gkhe", back_scores, query, preferred_element_type=jnp.float32)
            * scale
        )
        return (query_back, keys_back, values_back)

    query_back, keys_terms, values_terms = lax.map(
        attend_backward,
        (
            query_heads,
            key_heads,
            value_heads,
            prefix_blocks,
            total_blocks,
            keep_blocks,
            log_sums,
            back_blocks,
        ),
    )
    keys_back, values_back = (
        lax.psum_scatter(
            keys_terms.reshape(cells_here, length, width).astype(jnp.bfloat16),
            "seq",
            scatter_dimension=1,
            tiled=True,
        ).astype(jnp.float32),
        lax.psum_scatter(
            values_terms.reshape(cells_here, length, width).astype(jnp.bfloat16),
            "seq",
            scatter_dimension=1,
            tiled=True,
        ).astype(jnp.float32),
    )
    back_mixed = jnp.concatenate(
        [query_back.reshape(cells_here, span, width), keys_back, values_back], axis=-1
    ).astype(jnp.bfloat16)
    mix_weight_back = jnp.einsum(
        "td,te->de", flat(normed), flat(back_mixed), preferred_element_type=jnp.float32
    )
    query_bias_back = jnp.sum(flat(back_mixed[..., :width]).astype(jnp.float32), axis=0)
    value_bias_back = jnp.sum(flat(back_mixed[..., 2 * width :]).astype(jnp.float32), axis=0)
    back_normed = jnp.einsum(
        "cte,de->ctd", back_mixed, mix_weight, preferred_element_type=jnp.float32
    )
    first_value, first_pull = jax.vjp(layer_norm, inputs, first_gain, first_shift)
    inputs_part, first_gain_back, first_shift_back = first_pull(back_normed)
    tokens_back = (back_middle + inputs_part).astype(jnp.bfloat16)
    shares = (
        lax.psum_scatter(
            first_gain_back.astype(jnp.bfloat16), "cells", scatter_dimension=0, tiled=True
        ).astype(jnp.float32),
        lax.psum_scatter(
            first_shift_back.astype(jnp.bfloat16), "cells", scatter_dimension=0, tiled=True
        ).astype(jnp.float32),
        lax.psum_scatter(
            mix_weight_back.astype(jnp.bfloat16), "cells", scatter_dimension=0, tiled=True
        ).astype(jnp.float32),
        lax.psum_scatter(
            query_bias_back.astype(jnp.bfloat16), "cells", scatter_dimension=0, tiled=True
        ).astype(jnp.float32),
        lax.psum_scatter(
            value_bias_back.astype(jnp.bfloat16), "cells", scatter_dimension=0, tiled=True
        ).astype(jnp.float32),
        lax.psum_scatter(
            out_weight_back.astype(jnp.bfloat16), "cells", scatter_dimension=0, tiled=True
        ).astype(jnp.float32),
        lax.psum_scatter(
            out_bias_back.astype(jnp.bfloat16), "cells", scatter_dimension=0, tiled=True
        ).astype(jnp.float32),
        lax.psum_scatter(
            second_gain_back.astype(jnp.bfloat16), "cells", scatter_dimension=0, tiled=True
        ).astype(jnp.float32),
        lax.psum_scatter(
            second_shift_back.astype(jnp.bfloat16), "cells", scatter_dimension=0, tiled=True
        ).astype(jnp.float32),
        lax.psum_scatter(
            up_weight_back.astype(jnp.bfloat16), "cells", scatter_dimension=0, tiled=True
        ).astype(jnp.float32),
        lax.psum_scatter(
            up_bias_back.astype(jnp.bfloat16), "cells", scatter_dimension=0, tiled=True
        ).astype(jnp.float32),
        lax.psum_scatter(
            down_weight_back.astype(jnp.bfloat16), "cells", scatter_dimension=0, tiled=True
        ).astype(jnp.float32),
        lax.psum_scatter(
            down_bias_back.astype(jnp.bfloat16), "cells", scatter_dimension=0, tiled=True
        ).astype(jnp.float32),
    )
    matrices = (
        lax.psum_scatter(
            shares[2].astype(jnp.bfloat16), "seq", scatter_dimension=1, tiled=True
        ).astype(jnp.float32),
        lax.psum_scatter(
            shares[5].astype(jnp.bfloat16), "seq", scatter_dimension=1, tiled=True
        ).astype(jnp.float32),
        lax.psum_scatter(
            shares[9].astype(jnp.bfloat16), "seq", scatter_dimension=1, tiled=True
        ).astype(jnp.float32),
        lax.psum_scatter(
            shares[11].astype(jnp.bfloat16), "seq", scatter_dimension=1, tiled=True
        ).astype(jnp.float32),
    )
    vectors = lax.psum(
        (
            shares[0],
            shares[1],
            shares[3],
            shares[4],
            shares[6],
            shares[7],
            shares[8],
            shares[10],
            shares[12],
        ),
        "seq",
    )
    return (
        block_out,
        tokens_back,
        vectors[0],
        vectors[1],
        matrices[0],
        vectors[2],
        vectors[3],
        matrices[1],
        vectors[4],
        vectors[5],
        vectors[6],
        matrices[2],
        vectors[7],
        matrices[3],
        vectors[8],
    )


def solution(mesh):
    return jax.shard_map(
        on_device,
        mesh=mesh,
        in_specs=(
            P("cells", "seq", None),
            P(),
            P(),
            P(),
            P(),
            P(),
            P(),
            P(),
            P(),
            P(),
            P(),
            P(),
            P(),
            P(),
            P("cells", "seq", None),
            P("cells"),
            P("cells"),
            P("cells", "seq"),
        ),
        out_specs=(
            P("cells", "seq", None),
            P("cells", "seq", None),
            P("cells"),
            P("cells"),
            P("cells", "seq"),
            P("cells"),
            P("cells"),
            P("cells", "seq"),
            P("cells"),
            P("cells"),
            P("cells"),
            P("cells", "seq"),
            P("cells"),
            P("cells", "seq"),
            P("cells"),
        ),
        check_vma=False,
    )
```

profile of v0, /device:TPU:0, one launch (start us, length us, event | category | flops | bytes accessed | tf_op | source)
XLA Modules:
  0.0 952.6 jit_solution(16598273663415900678)
XLA Ops:
  7.2 1.6 convert_reduce_fusion
  8.9 1.6 fusion.60
  11.0 7.9 fusion.35
  19.0 2.8 copy-done.11
  21.8 1.1 slice.28
  23.1 4.1 fusion.62
  27.4 6.2 all_gather.10
  34.4 28.7 %all-gather.5.cloned.1.call-done = bf16[2,1024,1120]{1,2,0:T(8,128)(2,1)} async-done(((bf16[2,256,1120]{1,2,0:T(8,128)(2,1)}), bf16[2,1024,1120]{1,2,0:T(8,128)(2,1)}) %all-gather.5.cloned.1.call-update) | async-done | bytes 4587536 | tf_op jit(solution)/shard_map/all_gather | solution.py:88
  63.2 21.1 %fusion.11 = (f32[2,20,256]{2,1,0:T(8,128)S(1)}, f32[2,20,256,1024]{3,2,1,0:T(8,128)}) fusion(pred[2,256,1024]{2,1,0:T(8,128)(4,1)S(1)} %and_or_fusion, bf16[2,256,20,56]{1,3,2,0:T(8,128)(2,1)} %bitcast.113, bf16[2,1024,20,56]{1,3,2,0:T(8,128)(2,1)} %bitcast.110), kind=kOutput, calls=%fused_computation.16 | convolution fusion | flops 1205852160 | bytes 48242688 | tf_op jit(solution)/shard_map/while/body/eval_jaxpr/gqhe,gkhe->ghqk/dot_general | solution.py:62
  84.3 19.1 %fusion.3 = f32[2,20,256]{2,1,0:T(8,128)S(1)} fusion(f32[2,20,256]{2,1,0:T(8,128)S(1)} %get-tuple-element.177, f32[2,20,256,1024]{3,2,1,0:T(8,128)} %get-tuple-element.178, pred[2,256,1024]{2,1,0:T(8,128)(4,1)S(1)} %and_or_fusion), kind=kLoop, calls=%fused_computation.6 | loop fusion | flops 41932800 | bytes 42549248 | tf_op jit(solution)/shard_map/while/body/eval_jaxpr/reduce_sum | solution.py:105
  103.4 18.5 %fusion.64 = bf16[2,20,56,256]{3,2,1,0:T(8,128)(2,1)S(1)} fusion(bf16[2,1024,20,56]{1,3,2,0:T(8,128)(2,1)} %bitcast.115, f32[2,20,256]{2,1,0:T(8,128)S(1)} %fusion.3, f32[2,20,256]{2,1,0:T(8,128)S(1)} %get-tuple-element.177, f32[2,20,256,1024]{3,2,1,0:T(8,128)} %get-tuple-element.178, pred[2,256,1024]{2,1,0:T(8,128)(4,1)S(1)} %and_or_fusion), kind=kOutput, calls=%fused_computation.81 | convolution fusion | flops 1227407360 | bytes 48283648 | tf_op jit(solution)/shard_map/while/body/eval_jaxpr/ghqk,gkhe->gqhe/dot_general | solution.py:107
  122.0 1.8 fusion.83
  124.2 13.6 %fusion.30 = f32[2,256,4480]{2,1,0:T(8,128)} fusion(bf16[1120,4480]{1,0:T(8,128)(2,1)} %param.28, f32[4480]{0:T(1024)S(1)} %copy-done.29, f32[2,256,1120]{1,2,0:T(8,128)S(1)} %get-tuple-element.180, f32[1120]{0:T(1024)S(1)} %copy-done.23, f32[1120]{0:T(1024)S(1)} %copy-done.22, f32[2,256]{1,0:T(2,128)S(1)} %fusion.68, f32[2,256]{1,0:T(2,128)S(1)} %broadcast_multiply_fusion), kind=kOutput, calls=%fused_computation.37 | convolution fusion | flops 5143183360 | bytes 21534976 | tf_op jit(solution)/shard_map/dot_general | solution.py:117
  137.8 17.5 %fusion.84 = (bf16[4480]{0:T(1024)(128)(2,1)}, bf16[2,256,4480]{2,1,0:T(8,128)(2,1)S(1)}) fusion(f32[2,256,4480]{2,1,0:T(8,128)} %fusion.30, bf16[2,256,1120]{1,2,0:T(8,128)(2,1)S(1)} %copy-done.14, bf16[4480,1120]{0,1:T(8,128)(2,1)} %param.30), kind=kOutput, calls=%fused_computation.125 | convolution fusion | flops 5186186752 | bytes 24953600 | tf_op jit(solution)/shard_map/ctd,fd->ctf/dot_general | solution.py:127
  155.3 6.9 multiply_reduce_fusion.1
  162.2 0.6 fusion.81
  162.9 1.3 fusion.79
  164.2 1.7 convolution_convert_fusion.1
  165.9 20.1 %fusion.50 = bf16[2,20,56,1024]{3,2,1,0:T(8,128)(2,1)} fusion(bf16[2,256,20,56]{1,3,2,0:T(8,128)(2,1)S(1)} %bitcast.125, f32[2,20,256]{2,1,0:T(8,128)S(1)} %log_add_fusion, f32[2,20,256,1024]{3,2,1,0:T(8,128)} %get-tuple-element.178, pred[2,256,1024]{2,1,0:T(8,128)(4,1)S(1)} %and_or_fusion), kind=kOutput, calls=%fused_computation.58 | convolution fusion | flops 1218641920 | bytes 48242688 | tf_op jit(solution)/shard_map/while/body/eval_jaxpr/ghqk,gqhe->gkhe/dot_general | solution.py:157
  186.0 1.2 copy-done.18
  187.2 33.4 %multiply_reduce_fusion = (f32[2,20,256]{2,1,0:T(8,128)S(1)}, f32[2,20,256,1024]{3,2,1,0:T(8,128)}) fusion(f32[2,20,256]{2,1,0:T(8,128)S(1)} %log_add_fusion, f32[2,20,256,1024]{3,2,1,0:T(8,128)} %get-tuple-element.178, pred[2,256,1024]{2,1,0:T(8,128)(4,1)S(1)} %and_or_fusion, bf16[2,256,20,56]{1,3,2,0:T(8,128)(2,1)S(1)} %bitcast.126, ...), kind=kOutput, calls=%fused_computation.1 | convolution fusion | flops 1226823680 | bytes 90226688 | tf_op jit(solution)/shard_map/while/body/eval_jaxpr/gqhe,gkhe->ghqk/dot_general | solution.py:76
  220.6 34.1 %multiply_convert_fusion = bf16[2,20,256,1024]{3,2,1,0:T(8,128)(2,1)} fusion(f32[2,20,256,1024]{3,2,1,0:T(8,128)} %get-tuple-element.183, f32[2,20,256]{2,1,0:T(8,128)S(1)} %get-tuple-element.182, f32[2,20,256]{2,1,0:T(8,128)S(1)} %log_add_fusion, f32[2,20,256,1024]{3,2,1,0:T(8,128)} %get-tuple-element.178, pred[2,256,1024]{2,1,0:T(8,128)(4,1)S(1)} %and_or_fusion), kind=kLoop, calls=%fused_computation | loop fusion | flops 62914560 | bytes 105463808 | tf_op jit(solution)/shard_map/while/body/eval_jaxpr/convert_element_type | solution.py:161
  254.7 12.7 %multiply_convert_fusion.1 = bf16[2,20,56,1024]{3,2,1,0:T(8,128)(2,1)} fusion(bf16[2,256,20,56]{1,3,2,0:T(8,128)(2,1)S(1)} %bitcast.114, bf16[2,20,256,1024]{3,2,1,0:T(8,128)(2,1)} %multiply_convert_fusion), kind=kOutput, calls=%fused_computation.35 | convolution fusion | flops 1178992640 | bytes 26705920 | tf_op jit(solution)/shard_map/while/body/eval_jaxpr/ghqk,gqhe->gkhe/dot_general | solution.py:167
  267.5 1.2 copy-done.15
  268.7 13.1 %fusion.10 = bf16[4480,1120]{1,0:T(8,128)(2,1)} fusion(bf16[2,256,1120]{1,2,0:T(8,128)(2,1)S(1)} %copy-done.15, f32[2,256,4480]{2,1,0:T(8,128)} %fusion.30), kind=kOutput, calls=%fused_computation.14 | convolution fusion | flops 5163683840 | bytes 20357120 | tf_op jit(solution)/shard_map/tf,td->fd/dot_general | solution.py:123
  281.9 1.2 copy-done.13
  283.1 1.8 copy.46
  284.9 1.2 copy.45
  286.4 3.2 convolution_convert_fusion
  289.6 0.9 slice-done.4
  290.5 8.3 fusion.9
  298.7 13.6 %bitcast_reduce_fusion = (bf16[20,56]{1,0:T(8,128)(2,1)}, bf16[2,20,56,256]{3,2,1,0:T(8,128)(2,1)}) fusion(bf16[2,1024,20,56]{1,3,2,0:T(8,128)(2,1)} %bitcast.111, bf16[2,20,256,1024]{3,2,1,0:T(8,128)(2,1)} %multiply_convert_fusion), kind=kOutput, calls=%fused_computation.83 | convolution fusion | flops 1176124288 | bytes 26708160 | tf_op jit(solution)/shard_map/while/body/eval_jaxpr/ghqk,gkhe->gqhe/dot_general | solution.py:163
  312.3 2.2 reduce-scatter.20.cloned.1.call-done
  314.5 9.9 %fusion.12 = bf16[1120,3360]{1,0:T(8,128)(2,1)} fusion(bf16[2,256,1120]{1,2,0:T(8,128)(2,1)} %reduce-scatter.22.cloned.1.call-done, bf16[2,256,1120]{1,2,0:T(8,128)(2,1)} %reduce-scatter.20.cloned.1.call-done, bf16[2,256,1120]{1,2,0:T(8,128)(2,1)} %bitcast.123, bf16[2,256,1120]{1,2,0:T(8,128)(2,1)} %param.18, f32[1120]{0:T(1024)S(1)} %copy-done.47, ...), kind=kOutput, calls=%fused_computation.17 | convolution fusion | flops 3871042560 | bytes 12126976 | tf_op jit(solution)/shard_map/td,te->de/dot_general | solution.py:202
  324.4 469.4 %fusion.78 = (bf16[144,3360]{1,0:T(8,128)(2,1)}, bf16[144,1120]{1,0:T(8,128)(2,1)S(1)}, bf16[144,4480]{1,0:T(8,128)(2,1)}) fusion(bf16[1120,3360]{1,0:T(8,128)(2,1)} %fusion.12, bf16[1120,1120]{1,0:T(8,128)(2,1)} %convolution_convert_fusion, bf16[1120,4480]{1,0:T(8,128)(2,1)} %fusion.9), kind=kCustom, calls=%all-reduce-scatter.3 | all-reduce-scatter fusion | flops 10321921 | bytes 22651392
  793.8 1.5 collective-permute-start.1
  796.6 1.7 slice.18
  798.3 2.5 collective-permute-start
  800.8 0.8 concatenate.6
  801.7 1.1 copy.56
  805.4 1.0 slice.20
  806.4 4.4 collective-permute-start.2
  810.9 8.2 concatenate.5
  819.1 2.5 constant_dynamic-slice_fusion.2
  821.6 2.6 copy.54
  824.2 12.1 %fusion.47 = bf16[2,256,1120]{1,2,0:T(8,128)(2,1)} fusion(f32[2,256,1120]{1,2,0:T(8,128)S(1)} %copy-done.3, bf16[4480,1120]{0,1:T(8,128)(2,1)} %param.30, f32[1120]{0:T(1024)S(1)} %copy-done.48, f32[2,256,4480]{2,1,0:T(8,128)} %fusion.30), kind=kOutput, calls=%fused_computation.56 | convolution fusion | flops 5160386560 | bytes 22655360 | tf_op jit(solution)/shard_map/dot_general | solution.py:120
  836.5 1.6 reduce_sum.249
  838.0 7.5 concatenate.7
  845.5 1.4 constant_dynamic-slice_fusion
  846.9 3.9 copy.58
  850.9 8.6 fusion.77
  859.6 1.0 fusion.59
  860.9 34.0 %all-reduce.17 = (bf16[1120]{0:T(1024)(128)(2,1)S(1)}, bf16[1120]{0:T(1024)(128)(2,1)S(1)}, bf16[1120]{0:T(1024)(128)(2,1)S(1)}, bf16[1120]{0:T(1024)(128)(2,1)S...) all-reduce(bf16[1120]{0:T(1024)(128)(2,1)S(1)} %get-tuple-element.1, ...), channel_id=4, replica_groups=mesh['cells'=8,'seq'=4] {'cells'}, use_global_device_ids=true, to_apply=%region_14.15.clone | all-reduce | flops 13440 | bytes 53760
  895.3 10.7 %all-reduce.16 = (f32[140]{0:T(256)}, f32[140]{0:T(256)}, f32[140]{0:T(256)}, f32[140]{0:T(256)}, f32[140]{0:T(256)}, /*index=5*/f32[140]{0:T(256)}, f32[140]{0:T(256)}, f32[560]{0:T(1024)}, f32[140]{0:T(256)}) all-reduce(f32[140]{0:T(256)S(1)} %get-tuple-element.196, ...), channel_id=1, replica_groups=mesh['cells'=8,'seq'=4] {'seq'}, use_global_device_ids=true, to_apply=%region_15.16 | all-reduce | flops 1680 | bytes 13440 | tf_op jit(solution)/shard_map/psum | solution.py:268
  906.1 4.3 add_convert_fusion
  910.4 1.0 copy.57
  911.4 0.7 convert_element_type.193
  912.1 1.2 copy.55
  913.4 0.8 convert_element_type.189
  914.2 1.5 copy.59
  915.6 0.9 convert_element_type.200
  916.5 26.9 %all-reduce.21.cloned.1.call-done = bf16[560,1120]{1,0:T(8,128)(2,1)} async-done(((bf16[560,1120]{1,0:T(8,128)(2,1)}), bf16[560,1120]{1,0:T(8,128)(2,1)}) %all-reduce.21.cloned.1.call-update) | async-done | bytes 1254416
  943.5 1.3 dynamic-slice_convert_fusion
  944.7 1.2 copy.48
  (166 shorter events, 4.9 us)
Async XLA Ops:
  7.2 114.7 %copy-start = (bf16[1120,1120]{1,0:T(8,128)(2,1)S(1)}, bf16[1120,1120]{1,0:T(8,128)(2,1)}, u32[]{:S(2)}) copy-start(bf16[1120,1120]{1,0:T(8,128)(2,1)} %param.24) | copy-start | bytes 7526404
  7.2 56.0 %all-gather.5.cloned.1.call-start = ((), (), s32[]{:S(2)}) async-start(), calls=%async_computation.7 | async-start | bytes 5734400 | tf_op jit(solution)/shard_map/all_gather | solution.py:88
  8.9 10.1 %copy-start.26 = (f32[2,256]{1,0:T(2,128)}, f32[2,256]{1,0:T(2,128)S(1)}, u32[]{:S(2)}) copy-start(f32[2,256]{1,0:T(2,128)S(1)} %broadcast_multiply_fusion.1) | copy-start | bytes 6148
  11.0 7.9 copy-start.34
  19.0 2.9 copy-start.11
  21.8 1.3 copy-start.40
  23.0 4.3 copy-start.45
  23.0 4.4 copy-start.49
  23.0 4.4 copy-start.43
  23.0 80.3 %all-gather.3.cloned.1.call-start = ((), (), s32[]{:S(2)}) async-start(), calls=%async_computation.6 | async-start | bytes 5734400 | tf_op jit(solution)/shard_map/all_gather | solution.py:89
  27.2 285.1 %reduce-scatter.22.cloned.1.call-start = ((), (), s32[]{:S(2)}) async-start(), calls=%async_computation.9 | async-start | bytes 5734400 | tf_op jit(solution)/shard_map/reduce_scatter | solution.py:192
  103.4 18.5 %copy-start.7 = (bf16[2,256,1120]{1,2,0:T(8,128)(2,1)S(1)}, bf16[2,256,1120]{1,2,0:T(8,128)(2,1)}, u32[]{:S(2)}) copy-start(bf16[2,256,1120]{1,2,0:T(8,128)(2,1)} %param.18) | copy-start | bytes 3440644
  103.4 18.5 %copy-start.46 = (f32[1120]{0:T(1024)S(1)}, f32[1120]{0:T(1024)}, u32[]{:S(2)}) copy-start(f32[1120]{0:T(1024)} %param.25) | copy-start | bytes 13444
  121.9 1.9 copy-start.20
  122.0 2.2 copy-start.22
  122.0 2.2 copy-start.23
  122.0 2.2 copy-start.29
  123.8 38.4 %copy-start.2 = (f32[2,256,1120]{1,2,0:T(8,128)}, f32[2,256,1120]{1,2,0:T(8,128)S(1)}, u32[]{:S(2)}) copy-start(f32[2,256,1120]{1,2,0:T(8,128)S(1)} %get-tuple-element.180) | copy-start | bytes 6881284
  124.1 13.6 %copy-start.14 = (bf16[2,256,1120]{1,2,0:T(8,128)(2,1)S(1)}, bf16[2,256,1120]{1,2,0:T(8,128)(2,1)}, u32[]{:S(2)}) copy-start(bf16[2,256,1120]{1,2,0:T(8,128)(2,1)} %param.32) | copy-start | bytes 3440644
  124.2 31.1 %slice-start = ((s8[10035200]{0:T(1024)(128)(4,1)}), s8[4194304]{0:T(1024)(128)(4,1)S(1)}, s32[]{:S(2)}) async-start(s8[10035200]{0:T(1024)(128)(4,1)} %bitcast.117), calls=%async_computation.15 | async-start | bytes 8388608
  137.8 17.5 %slice-start.1 = ((s8[10035200]{0:T(1024)(128)(4,1)}), s8[4194304]{0:T(1024)(128)(4,1)S(1)}, s32[]{:S(2)}) async-start(s8[10035200]{0:T(1024)(128)(4,1)} %bitcast.117), calls=%async_computation.16 | async-start | bytes 8388608
  137.8 17.5 %slice-start.2 = ((s8[10035200]{0:T(1024)(128)(4,1)}), s8[1646592]{0:T(1024)(128)(4,1)S(1)}, s32[]{:S(2)}) async-start(s8[10035200]{0:T(1024)(128)(4,1)} %bitcast.117), calls=%async_computation.17 | async-start | bytes 3293184
  155.2 7.0 copy-start.51
  162.8 3.0 copy-start.5
  162.8 3.0 copy-start.30
  164.2 1.7 copy-start.12
  165.9 20.1 %copy-start.17 = (bf16[2,256,1120]{1,2,0:T(8,128)(2,1)}, bf16[2,256,1120]{1,2,0:T(8,128)(2,1)S(1)}, u32[]{:S(2)}) copy-start(bf16[2,256,1120]{1,2,0:T(8,128)(2,1)S(1)} %convolution_convert_fusion.1) | copy-start | bytes 3440644
  186.0 128.5 %reduce-scatter.20.cloned.1.call-start = ((), (), s32[]{:S(2)}) async-start(), calls=%async_computation.8 | async-start | bytes 5734400 | tf_op jit(solution)/shard_map/reduce_scatter | solution.py:186
  220.6 34.1 %copy-start.4 = (bf16[2,256,1120]{1,2,0:T(8,128)(2,1)S(1)}, bf16[2,256,1120]{1,2,0:T(8,128)(2,1)}, u32[]{:S(2)}) copy-start(bf16[2,256,1120]{1,2,0:T(8,128)(2,1)} %get-tuple-element.170) | copy-start | bytes 3440644
  267.4 638.6 %reduce-scatter.24.cloned.1.call-start = ((), (), s32[]{:S(2)}) async-start(), calls=%async_computation.10 | async-start | bytes 11612160 | tf_op jit(solution)/shard_map/reduce_scatter | solution.py:247
  281.8 3.1 copy-start.21
  281.8 628.6 %reduce-scatter.28.cloned.1.call-start = ((), (), s32[]{:S(2)}) async-start(), calls=%async_computation.12 | async-start | bytes 716800
  283.1 6.5 slice-start.3
  284.9 1.4 copy-start.19
  286.3 3.3 copy-start.3
  286.3 3.3 copy-start.24
  286.3 4.1 slice-start.4
  298.7 15.8 %copy-start.25 = (f32[1120]{0:T(1024)S(1)}, f32[1120]{0:T(1024)}, u32[]{:S(2)}) copy-start(f32[1120]{0:T(1024)} %param.19) | copy-start | bytes 13444
  298.7 15.8 %copy-start.27 = (f32[2,256]{1,0:T(2,128)S(1)}, f32[2,256]{1,0:T(2,128)}, u32[]{:S(2)}) copy-start(f32[2,256]{1,0:T(2,128)} %copy-done.26) | copy-start | bytes 6148
  298.7 15.8 %copy-start.35 = (f32[2,256]{1,0:T(2,128)S(1)}, f32[2,256]{1,0:T(2,128)}, u32[]{:S(2)}) copy-start(f32[2,256]{1,0:T(2,128)} %copy-done.34) | copy-start | bytes 6148
  298.7 15.8 %copy-start.47 = (f32[1120]{0:T(1024)S(1)}, f32[1120]{0:T(1024)}, u32[]{:S(2)}) copy-start(f32[1120]{0:T(1024)} %param.20) | copy-start | bytes 13444
  324.4 470.9 %copy-start.44 = (u32[32]{0:T(128)S(1)}, u32[32]{0:T(128)}, u32[]{:S(2)}) copy-start(u32[32]{0:T(128)} %constant.109) | copy-start | bytes 388
  793.8 9.1 copy-start.50
  793.8 7.0 collective-permute-start.1
  798.3 12.5 %collective-permute-start = (bf16[28,3360]{1,0:T(8,128)(2,1)}, bf16[28,3360]{1,0:T(8,128)(2,1)S(1)}, u32[]{:S(2)}, u32[]{:S(2)}) collective-permute-start(bf16[28,3360]{1,0:T(8,128)(2,1)} %slice.18), channel_id=1, source_target_pairs={{0,4},{4,8},{8,12},{12,16},{16,20},{20,24},{24,28},{1,5},{5,9},{9,... | collective-permute-start | bytes 564488
  802.8 109.3 %reduce-scatter.26.cloned.1.call-start = ((), (), s32[]{:S(2)}) async-start(), calls=%async_computation.11 | async-start | bytes 2150400
  806.4 31.6 %collective-permute-start.2 = (bf16[28,4480]{1,0:T(8,128)(2,1)S(1)}, bf16[28,4480]{1,0:T(8,128)(2,1)S(1)}, u32[]{:S(2)}, u32[]{:S(2)}) collective-permute-start(bf16[28,4480]{1,0:T(8,128)(2,1)S(1)} %slice.20), channel_id=1, source_target_pairs={{0,4},{4,8},{8,12},{12,16},{16,20},{20,24},{24,28},{1,5},{5,9},{9,... | collective-permute-start | bytes 752648
  821.5 2.7 copy-start.48
  824.2 12.2 %copy-start.28 = (bf16[20,56]{1,0:T(8,128)(2,1)S(1)}, bf16[20,56]{1,0:T(8,128)(2,1)}, u32[]{:S(2)}) copy-start(bf16[20,56]{1,0:T(8,128)(2,1)} %get-tuple-element.185) | copy-start | bytes 6724
  824.2 90.0 %reduce-scatter.30.cloned.1.call-start = ((), (), s32[]{:S(2)}) async-start(), calls=%async_computation.13 | async-start | bytes 2867200
  846.9 4.0 copy-start.8
  846.9 4.0 copy-start.16
  850.8 8.8 copy-start.33
  850.8 92.6 %all-reduce.21.cloned.1.call-start = ((), (), s32[]{:S(2)}) async-start(), calls=%async_computation.14 | async-start | bytes 2580480
  850.9 8.7 copy-start.9
  859.5 1.4 copy-start.10
  859.5 1.4 copy-start.36
  859.5 1.4 copy-start.37
  859.5 1.4 copy-start.38
  859.5 1.3 copy-start.41
  859.6 1.3 copy-start.42
  859.6 46.5 %copy-start.6 = (f32[2,256,1120]{1,2,0:T(8,128)S(1)}, f32[2,256,1120]{1,2,0:T(8,128)}, u32[]{:S(2)}) copy-start(f32[2,256,1120]{1,2,0:T(8,128)} %copy-done.5) | copy-start | bytes 6881284
  859.6 46.5 %copy-start.31 = (f32[2,256]{1,0:T(2,128)S(1)}, f32[2,256]{1,0:T(2,128)}, u32[]{:S(2)}) copy-start(f32[2,256]{1,0:T(2,128)} %copy-done.30) | copy-start | bytes 6148
  913.3 32.6 %copy-start.1 = (bf16[1120,1120]{1,0:T(8,128)(2,1)S(1)}, bf16[1120,1120]{1,0:T(8,128)(2,1)}, u32[]{:S(2)}) copy-start(bf16[1120,1120]{1,0:T(8,128)(2,1)} %param.24) | copy-start | bytes 7526404
  (5 other events, 5.6 us)
Sparse Core Ops, SparseCore 0:
  23.1 39.9 all-gather.4
  65.3 37.3 all-gather.2
  186.1 47.0 reduce-scatter.21
  267.6 46.8 reduce-scatter.19
  318.0 378.8 reduce-scatter.23
  802.9 22.9 reduce-scatter.27
  828.5 29.0 reduce-scatter.25
  860.4 32.6 reduce-scatter.29
  906.2 37.2 all-reduce.20
where the time goes:
time: 958 us; the launch traced here: 953 us
  blocking collectives  520 us (54%)
  matrix products  224 us (23%)
  other arithmetic  74.7 us (8%)
  waiting for transfers between devices  58 us (6%)
  local copies, waits for them, and re-layouts  49.6 us (5%)
  between operations  17.4 us (2%)
    unnamed x2, blocking collectives  503 us
    unnamed x133, local copies, waits for them, and re-layouts  45.3 us
    convert_element_type x1, other arithmetic, attend_backward(): back_scores = (probs * (back_probs - centre)).astype(jnp.bfloat16)  34.1 us
    dot_general x1, matrix products, scores_back(): jnp.einsum('gqhe,gkhe->ghqk', back_heads, values, preferred_element_type=...  33.4 us
    all_gather x1, waiting for transfers between devices, on_device(): lax.all_gather(keys_low, 'seq', axis=1, tiled=True)  28.7 us
    unnamed x16, waiting for transfers between devices  27.1 us
    dot_general x1, matrix products, score_block(): jnp.einsum('gqhe,gkhe->ghqk', queries, keys, preferred_element_type=jnp.f...  21.1 us
    dot_general x1, matrix products, attend_backward(): jnp.einsum('ghqk,gqhe->gkhe', probs_low, back_heads, preferred_element_ty...  20.1 us
  transfers between devices with their start and end apart: 12, of which 3 were waited for; matrix products, arithmetic and copies ran while one was open for 75% of the time, Pallas kernels for 0%

commit v1 on v0

--- a/solution.py
+++ b/solution.py
@@ -4,9 +4,190 @@
 import jax
 import jax.numpy as jnp
 from jax import lax
+from jax.experimental import pallas as pl
+from jax.experimental.pallas import tpu as pltpu
 from jax.sharding import PartitionSpec as P
 
 HEADS = 20
+VMEM_LIMIT = 56 * 1024 * 1024
+
+
+def bits_of(count):
+    return [1 << b for b in range(count.bit_length() - 1)]
+
+
+def swap_with(array, axis, bit):
+    count = lax.axis_size(axis)
+    return lax.ppermute(array, axis, [(i, i ^ bit) for i in range(count)])
+
+
+def spread_bits(array, seq_count, cell_count):
+    seq_bits, cell_bits = len(bits_of(seq_count)), len(bits_of(cell_count))
+    return array.reshape((2,) * (seq_bits + cell_bits) + array.shape[2:])
+
+
+def halve(part, names, axis, bit):
+    place = names.index((axis, bit))
+    keep = lax.index_in_dim(part, 0, place, keepdims=False)
+    send = lax.index_in_dim(part, 1, place, keepdims=False)
+    got = swap_with(send, axis, bit)
+    total = (keep.astype(jnp.float32) + got.astype(jnp.float32)).astype(jnp.bfloat16)
+    return total, names[:place] + names[place + 1 :]
+
+
+def bit_names(seq_count, cell_count):
+    return [("seq", b) for b in reversed(bits_of(seq_count))] + [
+        ("cells", b) for b in reversed(bits_of(cell_count))
+    ]
+
+
+def row_cover(rows, count):
+    share = rows // count
+    starts = [share * c // 8 * 8 for c in range(count)]
+    height = max(share * (c + 1) - starts[c] for c in range(count))
+    height = -(-height // 16) * 16
+    return [min(s, rows - height) for s in starts], height
+
+
+def outer_rows_kernel(starts, height, half, me_ref, left_ref, right_ref, send_ref, keep_ref, turned):
+    step = pl.program_id(0)
+
+    @pl.when(step == 0)
+    def _():
+        turned[...] = left_ref[...].T
+
+    mine = me_ref[1]
+    width = right_ref.shape[-1]
+    for first in range(0, width, 256):
+        last = min(first + 256, width)
+        block = jnp.dot(
+            turned[...], right_ref[0, :, first:last], preferred_element_type=jnp.float32
+        )
+
+        def store(target):
+            for c, start in enumerate(starts):
+                target[0, c ^ mine, :, first:last] = block[start : start + height].astype(
+                    jnp.bfloat16
+                )
+
+        pl.when(step < half)(lambda: store(send_ref))
+        pl.when(step >= half)(lambda: store(keep_ref))
+
+
+def outer_rows(left, right, cell_count, me):
+    seq_count, rows, width = right.shape
+    starts, height = row_cover(left.shape[1], cell_count)
+    half = seq_count // 2
+
+    def rel(step):
+        return jnp.where(step < half, 2 * step + 1, 2 * (step - half))
+
+    block = (1, cell_count, height, width)
+    shape = jax.ShapeDtypeStruct((half, cell_count, height, width), jnp.bfloat16)
+    return pl.pallas_call(
+        partial(outer_rows_kernel, starts, height, half),
+        out_shape=(shape, shape),
+        grid_spec=pltpu.PrefetchScalarGridSpec(
+            num_scalar_prefetch=1,
+            grid=(seq_count,),
+            in_specs=[
+                pl.BlockSpec(left.shape, lambda g, me: (0, 0)),
+                pl.BlockSpec((1, rows, width), lambda g, me: (rel(g) ^ me[0], 0, 0)),
+            ],
+            out_specs=[
+                pl.BlockSpec(block, lambda g, me: (jnp.minimum(g, half - 1), 0, 0, 0)),
+                pl.BlockSpec(block, lambda g, me: (jnp.maximum(g - half, 0), 0, 0, 0)),
+            ],
+            scratch_shapes=[pltpu.VMEM((left.shape[1], rows), jnp.bfloat16)],
+        ),
+        compiler_params=pltpu.CompilerParams(vmem_limit_bytes=VMEM_LIMIT),
+        cost_estimate=pl.CostEstimate(
+            flops=2 * rows * left.shape[1] * width * seq_count,
+            bytes_accessed=2 * (left.size + right.size + 2 * shape.size),
+            transcendentals=0,
+        ),
+        name="outer_rows",
+    )(me, left, right)
+
+
+def outer_columns_kernel(share, seq_count, me_ref, left_ref, right_ref, send_ref, keep_ref, turned):
+    @pl.when(pl.program_id(0) == 0)
+    def _():
+        turned[...] = left_ref[...].T
+
+    mine = me_ref[0]
+    block = jnp.dot(turned[...], right_ref[0], preferred_element_type=jnp.float32)
+    for s in range(seq_count):
+        rel = s ^ mine
+        piece = block[s * share : (s + 1) * share].astype(jnp.bfloat16)
+
+        def store(target):
+            target[rel >> 1, 0] = piece
+
+        pl.when((rel & 1) == 1)(lambda: store(send_ref))
+        pl.when((rel & 1) == 0)(lambda: store(keep_ref))
+
+
+def outer_columns(left, right, seq_count, me):
+    cell_count, rows, width = right.shape
+    share = left.shape[1] // seq_count
+    half = seq_count // 2
+    block = (half, 1, share, width)
+    shape = jax.ShapeDtypeStruct((half, cell_count, share, width), jnp.bfloat16)
+    return pl.pallas_call(
+        partial(outer_columns_kernel, share, seq_count),
+        out_shape=(shape, shape),
+        grid_spec=pltpu.PrefetchScalarGridSpec(
+            num_scalar_prefetch=1,
+            grid=(cell_count,),
+            in_specs=[
+                pl.BlockSpec(left.shape, lambda g, me: (0, 0)),
+                pl.BlockSpec((1, rows, width), lambda g, me: (g ^ me[1], 0, 0)),
+            ],
+            out_specs=[
+                pl.BlockSpec(block, lambda g, me: (0, g, 0, 0)),
+                pl.BlockSpec(block, lambda g, me: (0, g, 0, 0)),
+            ],
+            scratch_shapes=[pltpu.VMEM((left.shape[1], rows), jnp.bfloat16)],
+        ),
+        compiler_params=pltpu.CompilerParams(vmem_limit_bytes=VMEM_LIMIT),
+        cost_estimate=pl.CostEstimate(
+            flops=2 * rows * left.shape[1] * width * cell_count,
+            bytes_accessed=2 * (left.size + right.size + 2 * shape.size),
+            transcendentals=0,
+        ),
+        name="outer_columns",
+    )(me, left, right)
+
+
+def columns_cut(array, count):
+    rows, width = array.shape
+    return array.reshape(rows, count, width // count).transpose(1, 0, 2)
+
+
+def scattered_sum(send, keep, seq_count, cell_count, order):
+    got = swap_with(send, "seq", 1)
+    part = (keep.astype(jnp.float32) + got.astype(jnp.float32)).astype(jnp.bfloat16)
+    part = spread_bits(part, seq_count // 2, cell_count)
+    names = bit_names(seq_count, cell_count)
+    names.remove(("seq", 1))
+    for axis, bit in order(names):
+        part, names = halve(part, names, axis, bit)
+    return part
+
+
+def seq_first(names):
+    return sorted([n for n in names if n[0] == "seq"]) + sorted(n for n in names if n[0] == "cells")
+
+
+def seq_last(names):
+    cells = sorted(n for n in names if n[0] == "cells")
+    return cells + sorted(n for n in names if n[0] == "seq")
+
+
+def seq_second(names):
+    cells = sorted(n for n in names if n[0] == "cells")
+    return cells[:1] + sorted(n for n in names if n[0] == "seq") + cells[1:]
 
 
 def layer_norm(values, gain, shift):
@@ -40,6 +221,8 @@
     head_size = width // HEADS
     length = span * lax.axis_size("seq")
     start = lax.axis_index("seq") * span
+    seq_count, cell_count = lax.axis_size("seq"), lax.axis_size("cells")
+    me = jnp.stack([lax.axis_index("seq"), lax.axis_index("cells")]).astype(jnp.int32)
     group = math.gcd(cells_here, max(1, 512 // span))
     blocks = cells_here // group
     scale = 1.0 / math.sqrt(head_size)
@@ -120,18 +303,16 @@
     result = middle + jnp.dot(active, down_weight, preferred_element_type=jnp.float32) + down_bias
     block_out = result.astype(jnp.bfloat16)
     back_out = cotangent.astype(jnp.float32)
-    down_weight_back = jnp.einsum(
-        "tf,td->fd", flat(active), flat(cotangent), preferred_element_type=jnp.float32
-    )
     down_bias_back = jnp.sum(flat(back_out), axis=0)
     back_active = jnp.einsum(
         "ctd,fd->ctf", cotangent, down_weight, preferred_element_type=jnp.float32
     )
     gelu_value, gelu_pull = jax.vjp(gelu_tanh, upper)
     back_upper = gelu_pull(back_active)[0].astype(jnp.bfloat16)
-    up_weight_back = jnp.einsum(
-        "td,tf->df", flat(second), flat(back_upper), preferred_element_type=jnp.float32
-    )
+    down_shares = outer_columns(flat(cotangent), columns_cut(flat(active), cell_count), seq_count, me)
+    up_shares = outer_rows(flat(second), columns_cut(flat(back_upper), seq_count), cell_count, me)
+    down_part = scattered_sum(*down_shares, seq_count, cell_count, seq_first)
+    up_part = scattered_sum(*up_shares, seq_count, cell_count, seq_last)
     up_bias_back = jnp.sum(flat(back_upper).astype(jnp.float32), axis=0)
     back_second = jnp.einsum(
         "ctf,df->ctd", back_upper, up_weight, preferred_element_type=jnp.float32
@@ -140,9 +321,10 @@
     middle_part, second_gain_back, second_shift_back = norm_pull(back_second)
     back_middle = back_out + middle_part
     back_branch = back_middle.astype(jnp.bfloat16)
-    out_weight_back = jnp.einsum(
-        "td,te->de", flat(attended), flat(back_branch), preferred_element_type=jnp.float32
-    )
+    out_shares = outer_rows(
+        flat(attended), columns_cut(flat(back_branch), seq_count), cell_count, me
+    )
+    out_part = scattered_sum(*out_shares, seq_count, cell_count, seq_second)
     out_bias_back = jnp.sum(flat(back_branch).astype(jnp.float32), axis=0)
     back_attended = jnp.einsum(
         "cte,de->ctd", back_branch, out_weight, preferred_element_type=jnp.float32
@@ -199,9 +381,10 @@
     back_mixed = jnp.concatenate(
         [query_back.reshape(cells_here, span, width), keys_back, values_back], axis=-1
     ).astype(jnp.bfloat16)
-    mix_weight_back = jnp.einsum(
-        "td,te->de", flat(normed), flat(back_mixed), preferred_element_type=jnp.float32
-    )
+    mix_shares = outer_rows(
+        flat(normed), columns_cut(flat(back_mixed), seq_count), cell_count, me
+    )
+    mix_part = scattered_sum(*mix_shares, seq_count, cell_count, seq_second)
     query_bias_back = jnp.sum(flat(back_mixed[..., :width]).astype(jnp.float32), axis=0)
     value_bias_back = jnp.sum(flat(back_mixed[..., 2 * width :]).astype(jnp.float32), axis=0)
     back_normed = jnp.einsum(
@@ -210,74 +393,44 @@
     first_value, first_pull = jax.vjp(layer_norm, inputs, first_gain, first_shift)
     inputs_part, first_gain_back, first_shift_back = first_pull(back_normed)
     tokens_back = (back_middle + inputs_part).astype(jnp.bfloat16)
-    shares = (
-        lax.psum_scatter(
-            first_gain_back.astype(jnp.bfloat16), "cells", scatter_dimension=0, tiled=True
-        ).astype(jnp.float32),
-        lax.psum_scatter(
-            first_shift_back.astype(jnp.bfloat16), "cells", scatter_dimension=0, tiled=True
-        ).astype(jnp.float32),
-        lax.psum_scatter(
-            mix_weight_back.astype(jnp.bfloat16), "cells", scatter_dimension=0, tiled=True
-        ).astype(jnp.float32),
-        lax.psum_scatter(
-            query_bias_back.astype(jnp.bfloat16), "cells", scatter_dimension=0, tiled=True
-        ).astype(jnp.float32),
-        lax.psum_scatter(
-            value_bias_back.astype(jnp.bfloat16), "cells", scatter_dimension=0, tiled=True
-        ).astype(jnp.float32),
-        lax.psum_scatter(
-            out_weight_back.astype(jnp.bfloat16), "cells", scatter_dimension=0, tiled=True
-        ).astype(jnp.float32),
-        lax.psum_scatter(
-            out_bias_back.astype(jnp.bfloat16), "cells", scatter_dimension=0, tiled=True
-        ).astype(jnp.float32),
-        lax.psum_scatter(
-            second_gain_back.astype(jnp.bfloat16), "cells", scatter_dimension=0, tiled=True
-        ).astype(jnp.float32),
-        lax.psum_scatter(
-            second_shift_back.astype(jnp.bfloat16), "cells", scatter_dimension=0, tiled=True
-        ).astype(jnp.float32),
-        lax.psum_scatter(
-            up_weight_back.astype(jnp.bfloat16), "cells", scatter_dimension=0, tiled=True
-        ).astype(jnp.float32),
-        lax.psum_scatter(
-            up_bias_back.astype(jnp.bfloat16), "cells", scatter_dimension=0, tiled=True
-        ).astype(jnp.float32),
-        lax.psum_scatter(
-            down_weight_back.astype(jnp.bfloat16), "cells", scatter_dimension=0, tiled=True
-        ).astype(jnp.float32),
-        lax.psum_scatter(
-            down_bias_back.astype(jnp.bfloat16), "cells", scatter_dimension=0, tiled=True
-        ).astype(jnp.float32),
-    )
+
+    def own_rows_of(part, rows):
+        starts, _ = row_cover(rows, cell_count)
+        share = rows // cell_count
+        shift = jnp.array([share * c - starts[c] for c in range(cell_count)])[me[1]]
+        return lax.dynamic_slice_in_dim(part, shift, share, axis=0).astype(jnp.float32)
+
+    vectors = (
+        first_gain_back,
+        first_shift_back,
+        query_bias_back,
+        value_bias_back,
+        out_bias_back,
+        second_gain_back,
+        second_shift_back,
+        up_bias_back,
+        down_bias_back,
+    )
+    joined = jnp.concatenate([v.reshape(cell_count, -1) for v in vectors], axis=1)
+    joined = joined[jnp.arange(cell_count) ^ me[1]]
+    names = [("cells", b) for b in reversed(bits_of(cell_count))]
+    joined = joined.reshape((2,) * len(names) + joined.shape[1:])
+    for axis, bit in list(names):
+        place = names.index((axis, bit))
+        got = swap_with(lax.index_in_dim(joined, 1, place, keepdims=False), axis, bit)
+        joined = lax.index_in_dim(joined, 0, place, keepdims=False) + got
+        names.remove((axis, bit))
+    for bit in bits_of(seq_count):
+        joined = joined + swap_with(joined, "seq", bit)
+    ends = [0]
+    for v in vectors:
+        ends.append(ends[-1] + v.shape[0] // cell_count)
+    vectors = [joined[ends[i] : ends[i + 1]] for i in range(len(vectors))]
     matrices = (
-        lax.psum_scatter(
-            shares[2].astype(jnp.bfloat16), "seq", scatter_dimension=1, tiled=True
-        ).astype(jnp.float32),
-        lax.psum_scatter(
-            shares[5].astype(jnp.bfloat16), "seq", scatter_dimension=1, tiled=True
-        ).astype(jnp.float32),
-        lax.psum_scatter(
-            shares[9].astype(jnp.bfloat16), "seq", scatter_dimension=1, tiled=True
-        ).astype(jnp.float32),
-        lax.psum_scatter(
-            shares[11].astype(jnp.bfloat16), "seq", scatter_dimension=1, tiled=True
-        ).astype(jnp.float32),
-    )
-    vectors = lax.psum(
-        (
-            shares[0],
-            shares[1],
-            shares[3],
-            shares[4],
-            shares[6],
-            shares[7],
-            shares[8],
-            shares[10],
-            shares[12],
-        ),
-        "seq",
+        own_rows_of(mix_part, width),
+        own_rows_of(out_part, width),
+        own_rows_of(up_part, width),
+        down_part.T.astype(jnp.float32),
     )
     return (
         block_out,

time: 958 us -> 717 us (0.75)
  blocking collectives: 520 us -> 6.16 us
  waiting for transfers between devices: 58 us -> 183 us
  Pallas kernels: 0 us -> 62.9 us
  local copies, waits for them, and re-layouts: 49.6 us -> 111 us
  other arithmetic: 74.7 us -> 113 us
  matrix products: 224 us -> 195 us
  starting transfers between devices: 8.8 us -> 23.1 us
    unnamed x2 -> x0, blocking collectives: 503 us -> none
    ppermute x0 -> x25, waiting for transfers between devices: none -> 163 us  [swap_with(): return lax.ppermute(array, axis, [(i, i ^ bit) for i in range(count)])]
    pallas_call x0 -> x4, Pallas kernels: none -> 62.9 us  [the longest x3 48 us: outer_rows(): pl.pallas_call(partial(outer_rows_kernel, starts, height, half), out_shap...]
    convert_element_type x0 -> x5, local copies, waits for them, and re-layouts: none -> 40.7 us  [the longest x3 36.9 us: on_device(): back_mixed = jnp.concatenate([query_back.reshape(cells_here, span, width)...]
    dot_general x4 -> x0, matrix products: 34.5 us -> none  [the longest x1 13.1 us: on_device(): jnp.einsum('tf,td->fd', flat(active), flat(cotangent), preferred_element_...]
    another operation x0 -> x7, local copies, waits for them, and re-layouts: none -> 32.2 us  [the longest x6 29.8 us: columns_cut(): return array.reshape(rows, count, width // count).transpose(1, 0, 2)]
    unnamed x133 -> x117, local copies, waits for them, and re-layouts: 45.3 us -> 13.7 us
    convert_element_type x10 -> x23, other arithmetic: 8.42 us -> 38.9 us  [the longest x4 18.4 us: scattered_sum(): (keep.astype(jnp.float32) + got.astype(jnp.float32)).astype(jnp.bfloat16)]
  transfers between devices with their start and end apart: 12 -> 29, of which waited for: 3 -> 8; matrix products, arithmetic and copies ran while one was open for 75% -> 44% of each run, Pallas kernels for 0% -> 7%
where the time goes in v1:
time: 717 us; the launch traced here: 712 us
  matrix products  195 us (27%)
  waiting for transfers between devices  183 us (26%)
  other arithmetic  113 us (16%)
  local copies, waits for them, and re-layouts  111 us (15%)
  Pallas kernels  62.9 us (9%)
  starting transfers between devices  23.1 us (3%)
  between operations  17 us (2%)
    ppermute x25, waiting for transfers between devices, swap_with(): return lax.ppermute(array, axis, [(i, i ^ bit) for i in range(count)])  163 us
    pallas_call x3, Pallas kernels, outer_rows(): pl.pallas_call(partial(outer_rows_kernel, starts, height, half), out_shap...  48 us
    convert_element_type x3, local copies, waits for them, and re-layouts, on_device(): back_mixed = jnp.concatenate([query_back.reshape(cells_here, span, width)...  36.9 us
    convert_element_type x1, other arithmetic, attend_backward(): back_scores = (probs * (back_probs - centre)).astype(jnp.bfloat16)  34.3 us
    dot_general x1, matrix products, scores_back(): jnp.einsum('gqhe,gkhe->ghqk', back_heads, values, preferred_element_type=...  33.1 us
    another operation x6, local copies, waits for them, and re-layouts, columns_cut(): return array.reshape(rows, count, width // count).transpose(1, 0, 2)  29.8 us
    ppermute x25, starting transfers between devices, swap_with(): return lax.ppermute(array, axis, [(i, i ^ bit) for i in range(count)])  22.9 us
    dot_general x1, matrix products, score_block(): jnp.einsum('gqhe,gkhe->ghqk', queries, keys, preferred_element_type=jnp.f...  21.1 us
  transfers between devices with their start and end apart: 29, of which 8 were waited for; matrix products, arithmetic and copies ran while one was open for 44% of the time, Pallas kernels for 7%

profile of v1, /device:TPU:0, one launch (start us, length us, event | category | flops | bytes accessed | tf_op | source)
XLA Modules:
  0.0 712.0 jit_solution(6668279962208690019)
XLA Ops:
  7.3 1.6 convert_reduce_fusion.1
  8.9 1.6 fusion.59
  12.7 7.4 %fusion.29 = f32[2,256,3360]{1,2,0:T(8,128)S(1)} fusion(bf16[2,256,1120]{1,2,0:T(8,128)(2,1)S(1)} %fusion.57, bf16[1120,3360]{1,0:T(8,128)(2,1)} %param.24), kind=kOutput, calls=%fused_computation.39 | convolution fusion | flops 3853516800 | bytes 15554560 | tf_op jit(solution)/shard_map/dot_general | solution.py:266
  20.2 2.8 copy-done.19
  24.2 4.1 fusion.61
  28.4 2.4 copy.52
  32.8 6.2 all_gather.10
  39.6 2.4 copy.68
  44.1 20.2 %all-gather.5.cloned.1.call-done = bf16[2,1024,1120]{1,2,0:T(8,128)(2,1)} async-done(((bf16[2,256,1120]{1,2,0:T(8,128)(2,1)}), bf16[2,1024,1120]{1,2,0:T(8,128)(2,1)}) %all-gather.5.cloned.1.call-update) | async-done | bytes 4587536 | tf_op jit(solution)/shard_map/all_gather | solution.py:271
  64.3 21.1 %fusion.6 = (f32[2,20,256]{2,1,0:T(8,128)S(1)}, f32[2,20,256,1024]{3,2,1,0:T(8,128)}) fusion(pred[2,256,1024]{2,1,0:T(8,128)(4,1)S(1)} %and_or_fusion, bf16[2,256,20,56]{1,3,2,0:T(8,128)(2,1)} %bitcast.220, bf16[2,1024,20,56]{1,3,2,0:T(8,128)(2,1)} %bitcast.216), kind=kOutput, calls=%fused_computation.12 | convolution fusion | flops 1205852160 | bytes 48242688 | tf_op jit(solution)/shard_map/while/body/eval_jaxpr/gqhe,gkhe->ghqk/dot_general | solution.py:245
  85.4 19.1 %fusion = f32[2,20,256]{2,1,0:T(8,128)S(1)} fusion(f32[2,20,256]{2,1,0:T(8,128)S(1)} %get-tuple-element.151, f32[2,20,256,1024]{3,2,1,0:T(8,128)} %get-tuple-element.152, pred[2,256,1024]{2,1,0:T(8,128)(4,1)S(1)} %and_or_fusion), kind=kLoop, calls=%fused_computation.7 | loop fusion | flops 41932800 | bytes 42549248 | tf_op jit(solution)/shard_map/while/body/eval_jaxpr/reduce_sum | solution.py:288
  104.6 18.7 %fusion.65 = bf16[2,20,56,256]{3,2,1,0:T(8,128)(2,1)S(1)} fusion(bf16[2,1024,20,56]{1,3,2,0:T(8,128)(2,1)} %bitcast.223, f32[2,20,256]{2,1,0:T(8,128)S(1)} %fusion, f32[2,20,256]{2,1,0:T(8,128)S(1)} %get-tuple-element.151, f32[2,20,256,1024]{3,2,1,0:T(8,128)} %get-tuple-element.152, pred[2,256,1024]{2,1,0:T(8,128)(4,1)S(1)} %and_or_fusion), kind=kOutput, calls=%fused_computation.103 | convolution fusion | flops 1227407360 | bytes 48283648 | tf_op jit(solution)/shard_map/while/body/eval_jaxpr/ghqk,gkhe->gqhe/dot_general | solution.py:290
  123.3 1.8 fusion.97
  125.9 16.1 %multiply_convert_fusion.2 = (bf16[2,256,4480]{2,1,0:T(8,128)(2,1)}, f32[2,256,4480]{2,1,0:T(8,128)}) fusion(f32[4480]{0:T(1024)S(1)} %copy-done.49, bf16[2,256,1120]{1,2,0:T(8,128)(2,1)S(1)} %add_convert_fusion.5, bf16[1120,4480]{1,0:T(8,128)(2,1)} %param.31), kind=kOutput, calls=%fused_computation.34 | convolution fusion | flops 5160960000 | bytes 24962560 | tf_op jit(solution)/shard_map/dot_general | solution.py:300
  142.0 17.3 %convert_reduce_fusion = (f32[4480]{0:T(1024)}, bf16[2,256,4480]{2,1,0:T(8,128)(2,1)S(1)}) fusion(f32[2,256,4480]{2,1,0:T(8,128)} %get-tuple-element.156, bf16[2,256,1120]{1,2,0:T(8,128)(2,1)S(1)} %copy-done.15, bf16[4480,1120]{0,1:T(8,128)(2,1)} %param.33), kind=kOutput, calls=%fused_computation.32 | convolution fusion | flops 5188480512 | bytes 24962560 | tf_op jit(solution)/shard_map/ctd,fd->ctf/dot_general | solution.py:307
  159.3 11.2 %multiply_reduce_fusion.1 = (f32[1120]{0:T(1024)}, f32[2,256]{1,0:T(2,128)S(1)}, f32[1120]{0:T(1024)}, f32[2,256,1120]{1,2,0:T(8,128)S(1)}) fusion(f32[2,256,1120]{1,2,0:T(8,128)S(1)} %get-tuple-element.154, f32[2,256]{1,0:T(2,128)S(1)} %fusion.82, f32[2,256]{1,0:T(2,128)S(1)} %broadcast_multiply_fusion, f32[1120]{0:T(1024)S(1)} %copy-done.33, ...), kind=kOutput, calls=%fused_computation.88 | convolution fusion | flops 5142607360 | bytes 19229824 | tf_op jit(solution)/shard_map/ctf,df->ctd/dot_general | solution.py:317
  172.6 8.2 %copy.58 = bf16[2,256,1120]{1,0,2:T(2,128)(2,1)} copy(bf16[2,256,1120]{1,2,0:T(8,128)(2,1)S(1)} %get-tuple-element.118) | data formatting | bytes 2293760 | tf_op jit(solution)/shard_map/convert_element_type | solution.py:323
  180.8 2.7 convolution_convert_fusion
  185.9 2.4 copy.60.left_ref
  189.0 1.6 copy.59
  190.6 10.3 %outer_rows.4 = (bf16[2,8,144,280]{3,2,1,0:T(8,128)(2,1)}, bf16[2,8,144,280]{3,2,1,0:T(8,128)(2,1)}) custom-call(s32[2]{0:T(128)} %pad_add_fusion.me_ref, bf16[512,1120]{1,0:T(8,128)(2,1)} %copy.60.left_ref, bf16[4,512,280]{2,1,0:T(8,128)(2,1)} %bitcast.241), custom_call_target="tpu_custom_call" | custom-call | flops 1284505600 | bytes 4874240 | tf_op jit(solution)/shard_map/outer_rows/pallas_call | solution.py:87
  201.3 19.7 %fusion.48 = bf16[2,20,56,1024]{3,2,1,0:T(8,128)(2,1)} fusion(bf16[2,256,20,56]{1,3,2,0:T(8,128)(2,1)S(1)} %bitcast.238, f32[2,20,256]{2,1,0:T(8,128)S(1)} %log_add_fusion, f32[2,20,256,1024]{3,2,1,0:T(8,128)} %get-tuple-element.152, pred[2,256,1024]{2,1,0:T(8,128)(4,1)S(1)} %and_or_fusion), kind=kOutput, calls=%fused_computation.69 | convolution fusion | flops 1218641920 | bytes 48242688 | tf_op jit(solution)/shard_map/while/body/eval_jaxpr/ghqk,gqhe->gkhe/dot_general | solution.py:339
  221.1 33.1 %multiply_reduce_fusion = (f32[2,20,256]{2,1,0:T(8,128)S(1)}, f32[2,20,256,1024]{3,2,1,0:T(8,128)}) fusion(f32[2,20,256]{2,1,0:T(8,128)S(1)} %log_add_fusion, f32[2,20,256,1024]{3,2,1,0:T(8,128)} %get-tuple-element.152, pred[2,256,1024]{2,1,0:T(8,128)(4,1)S(1)} %and_or_fusion, bf16[2,256,20,56]{1,3,2,0:T(8,128)(2,1)S(1)} %bitcast.239, ...), kind=kOutput, calls=%fused_computation.2 | convolution fusion | flops 1226823680 | bytes 90226688 | tf_op jit(solution)/shard_map/while/body/eval_jaxpr/gqhe,gkhe->ghqk/dot_general | solution.py:259
  255.6 8.3 %reshape.386 = bf16[512,4,1120]{2,1,0:T(4,128)(2,1)} reshape(bf16[2,256,4480]{2,1,0:T(8,128)(2,1)} %copy-done.20) | data formatting | bytes 9175040 | tf_op jit(solution)/shard_map/reshape;reshape | solution.py:165
  263.9 10.9 %reshape.387 = bf16[512,8,560]{2,1,0:T(8,128)(2,1)} reshape(bf16[2,256,4480]{2,1,0:T(8,128)(2,1)} %get-tuple-element.155) | data formatting | bytes 9175040 | tf_op jit(solution)/shard_map/reshape;reshape | solution.py:165
  274.8 5.6 copy.105
  280.4 2.8 copy.106
  283.1 19.8 %outer_rows.5 = (bf16[2,8,144,1120]{3,2,1,0:T(8,128)(2,1)}, bf16[2,8,144,1120]{3,2,1,0:T(8,128)(2,1)}) custom-call(s32[2]{0:T(128)} %pad_add_fusion.me_ref, bf16[512,1120]{1,0:T(8,128)(2,1)} %bitcast.244, bf16[4,512,1120]{2,1,0:T(8,128)(2,1)} %bitcast.231), custom_call_target="tpu_custom_call" | custom-call | flops 5138022400 | bytes 16056320 | tf_op jit(solution)/shard_map/outer_rows/pallas_call | solution.py:87
  303.0 14.9 %outer_columns.1 = (bf16[2,8,280,560]{3,2,1,0:T(8,128)(2,1)}, bf16[2,8,280,560]{3,2,1,0:T(8,128)(2,1)}) custom-call(s32[2]{0:T(128)} %pad_add_fusion.me_ref, bf16[512,1120]{1,0:T(8,128)(2,1)} %bitcast.243, bf16[8,512,560]{2,1,0:T(8,128)(2,1)} %bitcast.230), custom_call_target="tpu_custom_call" | custom-call | flops 5138022400 | bytes 15769600 | tf_op jit(solution)/shard_map/outer_columns/pallas_call | solution.py:137
  318.3 2.0 add_convert_fusion.3
  324.0 34.3 %multiply_convert_fusion = bf16[2,20,256,1024]{3,2,1,0:T(8,128)(2,1)} fusion(f32[2,20,256,1024]{3,2,1,0:T(8,128)} %get-tuple-element.159, f32[2,20,256]{2,1,0:T(8,128)S(1)} %get-tuple-element.158, f32[2,20,256]{2,1,0:T(8,128)S(1)} %log_add_fusion, f32[2,20,256,1024]{3,2,1,0:T(8,128)} %get-tuple-element.152, pred[2,256,1024]{2,1,0:T(8,128)(4,1)S(1)} %and_or_fusion), kind=kLoop, calls=%fused_computation.1 | loop fusion | flops 62914560 | bytes 105463808 | tf_op jit(solution)/shard_map/while/body/eval_jaxpr/convert_element_type | solution.py:343
  360.7 12.7 %multiply_convert_fusion.1 = bf16[2,20,56,1024]{3,2,1,0:T(8,128)(2,1)} fusion(bf16[2,256,20,56]{1,3,2,0:T(8,128)(2,1)S(1)} %bitcast.221, bf16[2,20,256,1024]{3,2,1,0:T(8,128)(2,1)} %multiply_convert_fusion), kind=kOutput, calls=%fused_computation.33 | convolution fusion | flops 1178992640 | bytes 26705920 | tf_op jit(solution)/shard_map/while/body/eval_jaxpr/ghqk,gqhe->gkhe/dot_general | solution.py:349
  375.1 15.0 %convolution_multiply_fusion = bf16[2,20,56,256]{3,2,1,0:T(8,128)(2,1)} fusion(bf16[2,1024,20,56]{1,3,2,0:T(8,128)(2,1)} %bitcast.217, bf16[2,20,256,1024]{3,2,1,0:T(8,128)(2,1)} %multiply_convert_fusion), kind=kOutput, calls=%fused_computation.109 | convolution fusion | flops 1175552000 | bytes 26705920 | tf_op jit(solution)/shard_map/while/body/eval_jaxpr/ghqk,gkhe->gqhe/dot_general | solution.py:345
  390.2 6.5 add_convert_fusion
  396.6 2.1 fusion.91
  398.7 1.9 copy.71
  401.8 5.5 add_convert_fusion.1
  407.3 1.9 fusion.92
  409.3 1.8 copy.107
  411.2 2.5 collective-permute-start.14
  413.7 9.2 %fusion.44 = bf16[2,256,1120]{1,2,0:T(8,128)(2,1)} fusion(f32[2,256,1120]{1,2,0:T(8,128)S(1)} %copy-done.9, bf16[2,256,4480]{2,1,0:T(8,128)(2,1)S(1)} %bitcast.233, bf16[4480,1120]{0,1:T(8,128)(2,1)} %param.33, f32[1120]{0:T(1024)S(1)} %copy-done.51), kind=kOutput, calls=%fused_computation.63 | convolution fusion | flops 5139742720 | bytes 18067840 | tf_op jit(solution)/shard_map/dot_general | solution.py:303
  424.0 56.4 %collective-permute-done.21 = bf16[2,2,2,280,560]{4,3,0,1,2:T(8,128)(2,1)} collective-permute-done((bf16[2,2,2,280,560]{4,3,0,1,2:T(8,128)(2,1)}, bf16[2,2,2,280,560]{4,3,0,1,2:T(8,128)(2,1)}, u32[]{:S(2)}, u32[]{:S(2)}) %collective-permute-start.21) | collective-permute-done | bytes 2508832 | tf_op jit(solution)/shard_map/ppermute | solution.py:21
  480.4 3.4 fusion.31
  487.2 2.4 fusion.32
  493.0 1.7 maximum_convert_fusion
  494.8 1.7 copy-done.5
  496.5 22.4 %copy.53 = bf16[2,256,3360]{1,0,2:T(2,128)(2,1)} copy(bf16[2,256,3360]{1,2,0:T(8,128)(2,1)S(1)} %maximum_convert_fusion) | data formatting | bytes 6881280 | tf_op jit(solution)/shard_map/convert_element_type | solution.py:383
  518.9 8.7 %convert_element_type.380 = bf16[512,4,840]{0,2,1:T(8,128)(2,1)} reshape(bf16[2,256,3360]{1,0,2:T(2,128)(2,1)} %copy.53) | data formatting | bytes 6881280 | tf_op jit(solution)/shard_map/convert_element_type | solution.py:383
  527.5 5.8 copy.54
  533.4 17.9 %outer_rows.3 = (bf16[2,8,144,840]{3,2,1,0:T(8,128)(2,1)}, bf16[2,8,144,840]{3,2,1,0:T(8,128)(2,1)}) custom-call(s32[2]{0:T(128)} %pad_add_fusion.me_ref, bf16[512,1120]{1,0:T(8,128)(2,1)} %bitcast.242, bf16[4,512,840]{2,1,0:T(8,128)(2,1)} %bitcast.237), custom_call_target="tpu_custom_call" | custom-call | flops 3853516800 | bytes 12328960 | tf_op jit(solution)/shard_map/outer_rows/pallas_call | solution.py:87
  551.5 9.2 %fusion.88 = (f32[1120]{0:T(1024)S(1)}, f32[2,256]{1,0:T(2,128)S(1)}, f32[2,256,1120]{1,2,0:T(8,128)}) fusion(f32[1120]{0:T(1024)S(1)} %copy-done.30, f32[2,256]{1,0:T(2,128)S(1)} %copy-done.32, bf16[2,256,1120]{1,2,0:T(8,128)(2,1)S(1)} %copy-done.4, bf16[1120,3360]{1,0:T(8,128)(2,1)} %param.24, bf16[2,256,1120]{1,2,0:T(8,128)(2,1)S(1)} %copy-done.28, ...), kind=kOutput, calls=%fused_computation.184 | convolution fusion | flops 3867277824 | bytes 14420736 | tf_op jit(solution)/shard_map/cte,de->ctd/dot_general | solution.py:390
  560.8 2.7 fusion.58
  563.6 4.4 convert_reduce_fusion.2
  568.1 2.0 convert_reduce_fusion.4
  571.2 2.5 collective-permute-start
  573.7 3.2 fusion.47
  577.6 4.4 add_convert_fusion.2
  586.4 43.1 %collective-permute-done.2 = f32[1680]{0:T(1024)S(1)} collective-permute-done((f32[1680]{0:T(1024)S(1)}, f32[1680]{0:T(1024)S(1)}, u32[]{:S(2)}, u32[]{:S(2)}) %collective-permute-start.2) | collective-permute-done | bytes 6752 | tf_op jit(solution)/shard_map/ppermute | solution.py:21
  629.5 1.6 fusion.51
  632.5 2.4 collective-permute-done.4
  638.7 33.8 %collective-permute-done.18 = bf16[2,144,1120]{2,1,0:T(8,128)(2,1)S(1)} collective-permute-done((bf16[2,144,1120]{2,1,0:T(8,128)(2,1)S(1)}, bf16[2,144,1120]{2,1,0:T(8,128)(2,1)S(1)}, u32[]{:S(2)}, u32[]{:S(2)}) %collective-permute-start.18) | collective-permute-done | bytes 645152 | tf_op jit(solution)/shard_map/ppermute | solution.py:21
  674.6 4.9 collective-permute-done.24
  680.5 10.0 %collective-permute-done.8 = bf16[2,144,840]{2,1,0:T(8,128)(2,1)S(1)} collective-permute-done((bf16[2,144,840]{2,1,0:T(8,128)(2,1)S(1)}, bf16[2,144,840]{2,1,0:T(8,128)(2,1)S(1)}, u32[]{:S(2)}, u32[]{:S(2)}) %collective-permute-start.8) | collective-permute-done | bytes 483872 | tf_op jit(solution)/shard_map/ppermute | solution.py:21
  691.8 12.5 %collective-permute-done.9 = bf16[144,840]{1,0:T(8,128)(2,1)S(1)} collective-permute-done((bf16[144,840]{1,0:T(8,128)(2,1)S(1)}, bf16[144,840]{1,0:T(8,128)(2,1)S(1)}, u32[]{:S(2)}, u32[]{:S(2)}) %collective-permute-start.9) | collective-permute-done | bytes 241952 | tf_op jit(solution)/shard_map/ppermute | solution.py:21
  (244 shorter events, 48.3 us)
Async XLA Ops:
  7.2 116.1 %copy-start = (bf16[1120,1120]{1,0:T(8,128)(2,1)S(1)}, bf16[1120,1120]{1,0:T(8,128)(2,1)}, u32[]{:S(2)}) copy-start(bf16[1120,1120]{1,0:T(8,128)(2,1)} %param.27) | copy-start | bytes 7526404
  7.2 57.1 %all-gather.5.cloned.1.call-start = ((), (), s32[]{:S(2)}) async-start(), calls=%async_computation.3 | async-start | bytes 5734400 | tf_op jit(solution)/shard_map/all_gather | solution.py:271
  12.7 7.4 %copy-start.21 = (bf16[2,256,1120]{1,2,0:T(8,128)(2,1)}, bf16[2,256,1120]{1,2,0:T(8,128)(2,1)S(1)}, u32[]{:S(2)}) copy-start(bf16[2,256,1120]{1,2,0:T(8,128)(2,1)S(1)} %fusion.57) | copy-start | bytes 3440644
  24.1 80.4 %all-gather.3.cloned.1.call-start = ((), (), s32[]{:S(2)}) async-start(), calls=%async_computation.2 | async-start | bytes 5734400 | tf_op jit(solution)/shard_map/all_gather | solution.py:272
  28.3 4.5 copy-start.52
  28.3 4.5 copy-start.47
  28.3 464.7 %reduce-scatter.5.cloned.1.call-start = ((), (), s32[]{:S(2)}) async-start(), calls=%async_computation.5 | async-start | bytes 5734400 | tf_op jit(solution)/shard_map/reduce_scatter | solution.py:374
  104.5 18.7 %copy-start.3 = (bf16[2,256,1120]{1,2,0:T(8,128)(2,1)S(1)}, bf16[2,256,1120]{1,2,0:T(8,128)(2,1)}, u32[]{:S(2)}) copy-start(bf16[2,256,1120]{1,2,0:T(8,128)(2,1)} %param.21) | copy-start | bytes 3440644
  104.6 18.7 %copy-start.50 = (f32[1120]{0:T(1024)S(1)}, f32[1120]{0:T(1024)}, u32[]{:S(2)}) copy-start(f32[1120]{0:T(1024)} %param.28) | copy-start | bytes 13444
  125.1 45.5 %copy-start.8 = (f32[2,256,1120]{1,2,0:T(8,128)}, f32[2,256,1120]{1,2,0:T(8,128)S(1)}, u32[]{:S(2)}) copy-start(f32[2,256,1120]{1,2,0:T(8,128)S(1)} %get-tuple-element.154) | copy-start | bytes 6881284
  125.9 16.1 %copy-start.23 = (bf16[2,256,1120]{1,2,0:T(8,128)(2,1)}, bf16[2,256,1120]{1,2,0:T(8,128)(2,1)S(1)}, u32[]{:S(2)}) copy-start(bf16[2,256,1120]{1,2,0:T(8,128)(2,1)S(1)} %add_convert_fusion.5) | copy-start | bytes 3440644
  125.9 16.1 %copy-start.15 = (bf16[2,256,1120]{1,2,0:T(8,128)(2,1)S(1)}, bf16[2,256,1120]{1,2,0:T(8,128)(2,1)}, u32[]{:S(2)}) copy-start(bf16[2,256,1120]{1,2,0:T(8,128)(2,1)} %param.35) | copy-start | bytes 3440644
  159.3 11.2 %copy-start.20 = (bf16[2,256,4480]{2,1,0:T(8,128)(2,1)}, bf16[2,256,4480]{2,1,0:T(8,128)(2,1)S(1)}, u32[]{:S(2)}) copy-start(bf16[2,256,4480]{2,1,0:T(8,128)(2,1)S(1)} %get-tuple-element.162) | copy-start | bytes 13762564
  171.2 9.5 %copy-start.7 = (f32[2,256,1120]{1,2,0:T(8,128)}, f32[2,256,1120]{1,2,0:T(8,128)S(1)}, u32[]{:S(2)}) copy-start(f32[2,256,1120]{1,2,0:T(8,128)S(1)} %get-tuple-element.120) | copy-start | bytes 6881284
  171.2 9.5 %copy-start.40 = (f32[2,256]{1,0:T(2,128)}, f32[2,256]{1,0:T(2,128)S(1)}, u32[]{:S(2)}) copy-start(f32[2,256]{1,0:T(2,128)S(1)} %negate_multiply_fusion.1) | copy-start | bytes 6148
  190.6 10.7 %copy-start.26 = (bf16[2,256,1120]{1,2,0:T(8,128)(2,1)S(1)}, bf16[2,256,1120]{1,2,0:T(8,128)(2,1)}, u32[]{:S(2)}) copy-start(bf16[2,256,1120]{1,2,0:T(8,128)(2,1)} %convolution_convert_fusion) | copy-start | bytes 3440644
  200.9 117.5 %collective-permute-start.10 = (bf16[2,8,144,280]{3,2,1,0:T(8,128)(2,1)}, bf16[2,8,144,280]{3,2,1,0:T(8,128)(2,1)}, u32[]{:S(2)}, u32[]{:S(2)}) collective-permute-start(bf16[2,8,144,280]{3,2,1,0:T(8,128)(2,1)} %get-tuple-element.101), channel_id=1, source_target_pairs={{0,1},{1,0},{2,3},{3,2},{4,5},{5,4},{6,7},{7,6},{8,9},{9,8},{10,11... | collective-permute-start | bytes 3870728 | tf_op jit(solution)/shard_map/ppermute | solution.py:21
  221.0 33.2 %copy-start.24 = (bf16[2,256,1120]{1,2,0:T(8,128)(2,1)S(1)}, bf16[2,256,1120]{1,2,0:T(8,128)(2,1)}, u32[]{:S(2)}) copy-start(bf16[2,256,1120]{1,2,0:T(8,128)(2,1)} %copy-done.23) | copy-start | bytes 3440644
  221.1 272.0 %reduce-scatter.3.cloned.1.call-start = ((), (), s32[]{:S(2)}) async-start(), calls=%async_computation.4 | async-start | bytes 5734400 | tf_op jit(solution)/shard_map/reduce_scatter | solution.py:368
  274.8 5.6 copy-start.10
  302.9 98.9 %collective-permute-start.15 = (bf16[2,8,144,1120]{3,2,1,0:T(8,128)(2,1)}, bf16[2,8,144,1120]{3,2,1,0:T(8,128)(2,1)}, u32[]{:S(2)}, u32[]{:S(2)}) collective-permute-start(bf16[2,8,144,1120]{3,2,1,0:T(8,128)(2,1)} %get-tuple-element.103), channel_id=1, source_target_pairs={{0,1},{1,0},{2,3},{3,2},{4,5},{5,4},{6,7},{7,6},{8,9},{9,8},{10,11... | collective-permute-start | bytes 15482888 | tf_op jit(solution)/shard_map/ppermute | solution.py:21
  303.0 15.3 %copy-start.27 = (bf16[2,8,144,280]{3,2,1,0:T(8,128)(2,1)S(1)}, bf16[2,8,144,280]{3,2,1,0:T(8,128)(2,1)}, u32[]{:S(2)}) copy-start(bf16[2,8,144,280]{3,2,1,0:T(8,128)(2,1)} %get-tuple-element.100) | copy-start | bytes 3870724
  317.9 72.2 %collective-permute-start.20 = (bf16[2,8,280,560]{3,2,1,0:T(8,128)(2,1)}, bf16[2,8,280,560]{3,2,1,0:T(8,128)(2,1)}, u32[]{:S(2)}, u32[]{:S(2)}) collective-permute-start(bf16[2,8,280,560]{3,2,1,0:T(8,128)(2,1)} %get-tuple-element.105), channel_id=1, source_target_pairs={{0,1},{1,0},{2,3},{3,2},{4,5},{5,4},{6,7},{7,6},{8,9},{9,8},{10,11... | collective-permute-start | bytes 15052808 | tf_op jit(solution)/shard_map/ppermute | solution.py:21
  322.5 35.9 %collective-permute-start.11 = (bf16[2,2,2,144,280]{4,3,1,2,0:T(8,128)(2,1)}, bf16[2,2,2,144,280]{4,3,1,2,0:T(8,128)(2,1)}, u32[]{:S(2)}, u32[]{:S(2)}) collective-permute-start(bf16[2,2,2,144,280]{4,3,1,2,0:T(8,128)(2,1)} %bitcast.215), channel_id=1, source_target_pairs={{0,4},{4,0},{8,12},{12,8},{16,20},{20,16},{24,28},{28,24},{1,5},{5... | collective-permute-start | bytes 1935368 | tf_op jit(solution)/shard_map/ppermute | solution.py:21
  324.0 34.3 %copy-start.25 = (bf16[2,2,2,1,144,280]{5,4,3,2,1,0:T(8,128)(2,1)S(1)}, bf16[2,2,2,1,144,280]{5,4,3,2,1,0:T(8,128)(2,1)}, u32[]{:S(2)}) copy-start(bf16[2,2,2,1,144,280]{5,4,3,2,1,0:T(8,128)(2,1)} %get-tuple-element.129) | copy-start | bytes 1935364
  359.9 13.5 %collective-permute-start.12 = (bf16[2,2,144,280]{3,2,0,1:T(8,128)(2,1)S(1)}, bf16[2,2,144,280]{3,2,0,1:T(8,128)(2,1)S(1)}, u32[]{:S(2)}, u32[]{:S(2)}) collective-permute-start(bf16[2,2,144,280]{3,2,0,1:T(8,128)(2,1)S(1)} %slice_bitcast_fusion.12), channel_id=1, source_target_pairs={{0,2},{1,3},{2,0},{3,1},{4,6},{5,7},{6,4},{7,5},{8,10},{9,11},{10,... | collective-permute-start | bytes 967688 | tf_op jit(solution)/shard_map/ppermute | solution.py:21
  373.5 16.6 %collective-permute-start.13 = (bf16[2,144,280]{2,1,0:T(8,128)(2,1)S(1)}, bf16[2,144,280]{2,1,0:T(8,128)(2,1)S(1)}, u32[]{:S(2)}, u32[]{:S(2)}) collective-permute-start(bf16[2,144,280]{2,1,0:T(8,128)(2,1)S(1)} %slice_bitcast_fusion.20), channel_id=1, source_target_pairs={{0,8},{4,12},{8,0},{12,4},{16,24},{20,28},{24,16},{28,20},{1,9},{5... | collective-permute-start | bytes 483848 | tf_op jit(solution)/shard_map/ppermute | solution.py:21
  400.6 79.8 %collective-permute-start.21 = (bf16[2,2,2,280,560]{4,3,0,1,2:T(8,128)(2,1)}, bf16[2,2,2,280,560]{4,3,0,1,2:T(8,128)(2,1)}, u32[]{:S(2)}, u32[]{:S(2)}) collective-permute-start(bf16[2,2,2,280,560]{4,3,0,1,2:T(8,128)(2,1)} %copy.71), channel_id=1, source_target_pairs={{0,2},{1,3},{2,0},{3,1},{4,6},{5,7},{6,4},{7,5},{8,10},{9,11},{10,... | collective-permute-start | bytes 7526408 | tf_op jit(solution)/shard_map/ppermute | solution.py:21
  401.8 11.8 %slice-start = ((s8[4587520]{0:T(1024)(128)(4,1)}), s8[4194304]{0:T(1024)(128)(4,1)S(1)}, s32[]{:S(2)}) async-start(s8[4587520]{0:T(1024)(128)(4,1)} %bitcast.232), calls=%async_computation.6 | async-start | bytes 8388608
  407.3 6.4 slice-start.1
  409.3 4.4 copy-start.9
  409.3 4.4 copy-start.51
  411.1 75.5 %collective-permute-start.16 = (bf16[2,2,2,144,1120]{4,3,0,1,2:T(8,128)(2,1)}, bf16[2,2,2,144,1120]{4,3,0,1,2:T(8,128)(2,1)}, u32[]{:S(2)}, u32[]{:S(2)}) collective-permute-start(bf16[2,2,2,144,1120]{4,3,0,1,2:T(8,128)(2,1)} %bitcast.213), channel_id=1, source_target_pairs={{0,4},{4,0},{8,12},{12,8},{16,20},{20,16},{24,28},{28,24},{1,5},{5... | collective-permute-start | bytes 7741448 | tf_op jit(solution)/shard_map/ppermute | solution.py:21
  411.2 11.7 %copy-start.37 = (f32[4480]{0:T(1024)S(1)}, f32[4480]{0:T(1024)}, u32[]{:S(2)}) copy-start(f32[4480]{0:T(1024)} %get-tuple-element.161) | copy-start | bytes 53764
  411.2 11.8 %copy-start.46 = (f32[1120]{0:T(1024)S(1)}, f32[1120]{0:T(1024)}, u32[]{:S(2)}) copy-start(f32[1120]{0:T(1024)} %get-tuple-element.106) | copy-start | bytes 13444
  411.2 11.9 %copy-start.45 = (f32[1120]{0:T(1024)S(1)}, f32[1120]{0:T(1024)}, u32[]{:S(2)}) copy-start(f32[1120]{0:T(1024)} %get-tuple-element.112) | copy-start | bytes 13444
  411.2 12.0 %copy-start.34 = (f32[1120]{0:T(1024)S(1)}, f32[1120]{0:T(1024)}, u32[]{:S(2)}) copy-start(f32[1120]{0:T(1024)} %get-tuple-element.117) | copy-start | bytes 13444
  411.2 12.0 %collective-permute-start.14 = (bf16[144,280]{1,0:T(8,128)(2,1)S(1)}, bf16[144,280]{1,0:T(8,128)(2,1)S(1)}, u32[]{:S(2)}, u32[]{:S(2)}) collective-permute-start(bf16[144,280]{1,0:T(8,128)(2,1)S(1)} %get-tuple-element.137), channel_id=1, source_target_pairs={{0,16},{4,20},{8,24},{12,28},{16,0},{20,4},{24,8},{28,12},{1,17},{... | collective-permute-start | bytes 241928 | tf_op jit(solution)/shard_map/ppermute | solution.py:21
  483.9 5.7 copy-start.11
  485.1 88.5 %collective-permute-start.22 = (bf16[2,2,280,560]{3,2,0,1:T(8,128)(2,1)}, bf16[2,2,280,560]{3,2,0,1:T(8,128)(2,1)}, u32[]{:S(2)}, u32[]{:S(2)}) collective-permute-start(bf16[2,2,280,560]{3,2,0,1:T(8,128)(2,1)} %slice_bitcast_fusion), channel_id=1, source_target_pairs={{0,4},{4,0},{8,12},{12,8},{16,20},{20,16},{24,28},{28,24},{1,5},{5... | collective-permute-start | bytes 3763208 | tf_op jit(solution)/shard_map/ppermute | solution.py:21
  491.5 138.0 %collective-permute-start.17 = (bf16[2,2,144,1120]{3,2,0,1:T(8,128)(2,1)}, bf16[2,2,144,1120]{3,2,0,1:T(8,128)(2,1)}, u32[]{:S(2)}, u32[]{:S(2)}) collective-permute-start(bf16[2,2,144,1120]{3,2,0,1:T(8,128)(2,1)} %slice_bitcast_fusion.2), channel_id=1, source_target_pairs={{0,8},{4,12},{8,0},{12,4},{16,24},{20,28},{24,16},{28,20},{1,9},{5... | collective-permute-start | bytes 3870728 | tf_op jit(solution)/shard_map/ppermute | solution.py:21
  533.4 18.0 %copy-start.4 = (bf16[2,256,1120]{1,2,0:T(8,128)(2,1)S(1)}, bf16[2,256,1120]{1,2,0:T(8,128)(2,1)}, u32[]{:S(2)}) copy-start(bf16[2,256,1120]{1,2,0:T(8,128)(2,1)} %param.21) | copy-start | bytes 3440644
  533.4 18.0 %copy-start.28 = (bf16[2,256,1120]{1,2,0:T(8,128)(2,1)S(1)}, bf16[2,256,1120]{1,2,0:T(8,128)(2,1)}, u32[]{:S(2)}) copy-start(bf16[2,256,1120]{1,2,0:T(8,128)(2,1)} %reduce-scatter.5.cloned.1.call-done) | copy-start | bytes 3440644
  533.4 18.1 %copy-start.29 = (bf16[2,256,1120]{1,2,0:T(8,128)(2,1)S(1)}, bf16[2,256,1120]{1,2,0:T(8,128)(2,1)}, u32[]{:S(2)}) copy-start(bf16[2,256,1120]{1,2,0:T(8,128)(2,1)} %reduce-scatter.3.cloned.1.call-done) | copy-start | bytes 3440644
  533.4 18.1 %copy-start.30 = (f32[1120]{0:T(1024)S(1)}, f32[1120]{0:T(1024)}, u32[]{:S(2)}) copy-start(f32[1120]{0:T(1024)} %param.22) | copy-start | bytes 13444
  533.4 18.1 %copy-start.32 = (f32[2,256]{1,0:T(2,128)S(1)}, f32[2,256]{1,0:T(2,128)}, u32[]{:S(2)}) copy-start(f32[2,256]{1,0:T(2,128)} %copy-done.31) | copy-start | bytes 6148
  551.3 9.5 %copy-start.39 = (f32[2,256]{1,0:T(2,128)S(1)}, f32[2,256]{1,0:T(2,128)}, u32[]{:S(2)}) copy-start(f32[2,256]{1,0:T(2,128)} %copy-done.38) | copy-start | bytes 6148
  551.3 9.5 %copy-start.36 = (f32[2,256]{1,0:T(2,128)S(1)}, f32[2,256]{1,0:T(2,128)}, u32[]{:S(2)}) copy-start(f32[2,256]{1,0:T(2,128)} %copy-done.35) | copy-start | bytes 6148
  551.3 26.2 %collective-permute-start.5 = (bf16[2,8,144,840]{3,2,1,0:T(8,128)(2,1)}, bf16[2,8,144,840]{3,2,1,0:T(8,128)(2,1)}, u32[]{:S(2)}, u32[]{:S(2)}) collective-permute-start(bf16[2,8,144,840]{3,2,1,0:T(8,128)(2,1)} %get-tuple-element.85), channel_id=1, source_target_pairs={{0,1},{1,0},{2,3},{3,2},{4,5},{5,4},{6,7},{7,6},{8,9},{9,8},{10,11... | collective-permute-start | bytes 11612168 | tf_op jit(solution)/shard_map/ppermute | solution.py:21
  571.2 5.7 collective-permute-start
  577.0 7.1 collective-permute-start.1
  582.3 47.2 %copy-start.13 = (bf16[2,2,2,144,1120]{4,3,0,1,2:T(8,128)(2,1)S(1)}, bf16[2,2,2,144,1120]{4,3,0,1,2:T(8,128)(2,1)}, u32[]{:S(2)}) copy-start(bf16[2,2,2,144,1120]{4,3,0,1,2:T(8,128)(2,1)} %copy-done.12) | copy-start | bytes 7741444
  582.5 53.7 %collective-permute-start.6 = (bf16[2,2,2,144,840]{4,3,1,2,0:T(8,128)(2,1)S(1)}, bf16[2,2,2,144,840]{4,3,1,2,0:T(8,128)(2,1)S(1)}, u32[]{:S(2)}, u32[]{:S(2)}) collective-permute-start(bf16[2,2,2,144,840]{4,3,1,2,0:T(8,128)(2,1)S(1)} %bitcast.240), channel_id=1, source_target_pairs={{0,4},{4,0},{8,12},{12,8},{16,20},{20,16},{24,28},{28,24},{1,5},{5... | collective-permute-start | bytes 5806088 | tf_op jit(solution)/shard_map/ppermute | solution.py:21
  584.1 45.4 %collective-permute-start.2 = (f32[1680]{0:T(1024)S(1)}, f32[1680]{0:T(1024)S(1)}, u32[]{:S(2)}, u32[]{:S(2)}) collective-permute-start(f32[1680]{0:T(1024)S(1)} %get-tuple-element.115), channel_id=1, source_target_pairs={{0,4},{4,0},{8,12},{12,8},{16,20},{20,16},{24,28},{28,24},{1,5},{5... | collective-permute-start | bytes 20168 | tf_op jit(solution)/shard_map/ppermute | solution.py:21
  584.8 52.7 %collective-permute-start.23 = (bf16[2,280,560]{2,1,0:T(8,128)(2,1)S(1)}, bf16[2,280,560]{2,1,0:T(8,128)(2,1)S(1)}, u32[]{:S(2)}, u32[]{:S(2)}) collective-permute-start(bf16[2,280,560]{2,1,0:T(8,128)(2,1)S(1)} %slice_bitcast_fusion.6), channel_id=1, source_target_pairs={{0,8},{4,12},{8,0},{12,4},{16,24},{20,28},{24,16},{28,20},{1,9},{5... | collective-permute-start | bytes 1881608 | tf_op jit(solution)/shard_map/ppermute | solution.py:21
  629.5 1.7 collective-permute-start.3
  631.2 3.7 collective-permute-start.4
  631.9 40.6 %collective-permute-start.18 = (bf16[2,144,1120]{2,1,0:T(8,128)(2,1)S(1)}, bf16[2,144,1120]{2,1,0:T(8,128)(2,1)S(1)}, u32[]{:S(2)}, u32[]{:S(2)}) collective-permute-start(bf16[2,144,1120]{2,1,0:T(8,128)(2,1)S(1)} %slice_bitcast_fusion.8), channel_id=1, source_target_pairs={{0,16},{4,20},{8,24},{12,28},{16,0},{20,4},{24,8},{28,12},{1,17},{... | collective-permute-start | bytes 1935368 | tf_op jit(solution)/shard_map/ppermute | solution.py:21
  636.9 35.8 %collective-permute-start.7 = (bf16[2,2,144,840]{3,2,0,1:T(8,128)(2,1)S(1)}, bf16[2,2,144,840]{3,2,0,1:T(8,128)(2,1)S(1)}, u32[]{:S(2)}, u32[]{:S(2)}) collective-permute-start(bf16[2,2,144,840]{3,2,0,1:T(8,128)(2,1)S(1)} %slice_bitcast_fusion.4), channel_id=1, source_target_pairs={{0,2},{1,3},{2,0},{3,1},{4,6},{5,7},{6,4},{7,5},{8,10},{9,11},{10,... | collective-permute-start | bytes 2903048 | tf_op jit(solution)/shard_map/ppermute | solution.py:21
  637.8 41.8 %collective-permute-start.24 = (bf16[280,560]{1,0:T(8,128)(2,1)S(1)}, bf16[280,560]{1,0:T(8,128)(2,1)S(1)}, u32[]{:S(2)}, u32[]{:S(2)}) collective-permute-start(bf16[280,560]{1,0:T(8,128)(2,1)S(1)} %slice_bitcast_fusion.14), channel_id=1, source_target_pairs={{0,16},{4,20},{8,24},{12,28},{16,0},{20,4},{24,8},{28,12},{1,17},{... | collective-permute-start | bytes 940808 | tf_op jit(solution)/shard_map/ppermute | solution.py:21
  673.0 17.5 %collective-permute-start.8 = (bf16[2,144,840]{2,1,0:T(8,128)(2,1)S(1)}, bf16[2,144,840]{2,1,0:T(8,128)(2,1)S(1)}, u32[]{:S(2)}, u32[]{:S(2)}) collective-permute-start(bf16[2,144,840]{2,1,0:T(8,128)(2,1)S(1)} %slice_bitcast_fusion.10), channel_id=1, source_target_pairs={{0,8},{4,12},{8,0},{12,4},{16,24},{20,28},{24,16},{28,20},{1,9},{5... | collective-permute-start | bytes 1451528 | tf_op jit(solution)/shard_map/ppermute | solution.py:21
  673.1 17.7 %collective-permute-start.19 = (bf16[144,1120]{1,0:T(8,128)(2,1)S(1)}, bf16[144,1120]{1,0:T(8,128)(2,1)S(1)}, u32[]{:S(2)}, u32[]{:S(2)}) collective-permute-start(bf16[144,1120]{1,0:T(8,128)(2,1)S(1)} %get-tuple-element.133), channel_id=1, source_target_pairs={{0,2},{1,3},{2,0},{3,1},{4,6},{5,7},{6,4},{7,5},{8,10},{9,11},{10,... | collective-permute-start | bytes 967688 | tf_op jit(solution)/shard_map/ppermute | solution.py:21
  679.5 25.7 %copy-start.1 = (bf16[1120,1120]{1,0:T(8,128)(2,1)S(1)}, bf16[1120,1120]{1,0:T(8,128)(2,1)}, u32[]{:S(2)}) copy-start(bf16[1120,1120]{1,0:T(8,128)(2,1)} %param.27) | copy-start | bytes 7526404
  690.7 13.6 %collective-permute-start.9 = (bf16[144,840]{1,0:T(8,128)(2,1)S(1)}, bf16[144,840]{1,0:T(8,128)(2,1)S(1)}, u32[]{:S(2)}, u32[]{:S(2)}) collective-permute-start(bf16[144,840]{1,0:T(8,128)(2,1)S(1)} %get-tuple-element.135), channel_id=1, source_target_pairs={{0,16},{4,20},{8,24},{12,28},{16,0},{20,4},{24,8},{28,12},{1,17},{... | collective-permute-start | bytes 725768 | tf_op jit(solution)/shard_map/ppermute | solution.py:21
  (21 other events, 49.4 us)
Sparse Core Ops, SparseCore 0:
  24.2 40.0 all-gather.4
  66.4 37.3 all-gather.2
  221.2 46.9 reduce-scatter.4
  373.5 62.9 reduce-scatter.2

commit v2 on v0

v2 whole, which is shorter than its diff:
```python
from functools import partial
import math

import jax
import jax.numpy as jnp
from jax import lax
from jax.experimental import pallas as pl
from jax.experimental.pallas import tpu as pltpu
from jax.sharding import PartitionSpec as P

HEADS = 20
LANES = 128
TILE = 256
HEAD_PAD = 64
MASKED = -1e30
ONE_ROW = 56
SPLIT_ROW = 57
VMEM_LIMIT = 56 * 1024 * 1024
SHORT = pl.CostEstimate(flops=1, bytes_accessed=1, transcendentals=0)


def bits_of(count):
    return [1 << b for b in range(count.bit_length() - 1)]


def swap_with(array, axis, bit):
    count = lax.axis_size(axis)
    return lax.ppermute(array, axis, [(i, i ^ bit) for i in range(count)])


def without_bit(index, bit):
    return (index // (2 * bit)) * bit + index % bit


def add_halves_kernel(count, *refs):
    for n in range(count):
        mine_away, got_away, mine_here, got_here = refs[4 * n : 4 * n + 4]
        first = sum(refs[4 * p].shape[1] for p in range(n))
        rows = slice(first, first + mine_away.shape[1])
        for mine, got, result in (
            (mine_away, got_away, refs[4 * count]),
            (mine_here, got_here, refs[4 * count + 1]),
        ):
            total = mine[...].astype(jnp.float32) + got[...].astype(jnp.float32)
            result[:, rows, :] = total.astype(jnp.bfloat16)


def add_halves(pairs, bit):
    count, _, width = pairs[0][0].shape
    rows = sum(mine.shape[1] for mine, _ in pairs)
    shape = jax.ShapeDtypeStruct((count // 2, rows, width), jnp.bfloat16)
    in_specs, inputs = [], []
    for mine, got in pairs:
        for value in (bit, 0):
            spec = pl.BlockSpec(
                (1,) + mine.shape[1:],
                lambda g, value=value: ((g // bit) * (2 * bit) + value + g % bit, 0, 0),
            )
            in_specs += [spec, spec]
            inputs += [mine, got]
    out = pl.BlockSpec((1, rows, width), lambda g: (g, 0, 0))
    return pl.pallas_call(
        partial(add_halves_kernel, len(pairs)),
        out_shape=(shape, shape),
        grid=(count // 2,),
        in_specs=in_specs,
        out_specs=(out, out),
        compiler_params=pltpu.CompilerParams(vmem_limit_bytes=VMEM_LIMIT),
        cost_estimate=SHORT,
        name="add_halves",
    )(*inputs)


class Reduction:
    def __init__(self, label, names, order, send, keep, kind=None):
        self.labels = [label]
        self.kind = kind
        self.names, self.order = list(names), list(order)
        self.keep = keep
        self.heights = [keep.shape[1]]
        self.leave(send)

    def leave(self, send):
        axis, bit = self.order.pop(0)
        self.names.remove((axis, bit))
        self.got = swap_with(send, axis, bit)

    def step(self, last, *others):
        place = self.names.index(self.order[0])
        bit = 1 << (len(self.names) - 1 - place)
        pairs = [order_after((p.keep, p.got), last) for p in (self,) + others]
        for other in others:
            assert (other.names, other.order) == (self.names, self.order)
            self.heights += other.heights
            self.labels += other.labels
            other.labels, other.order = [], []
        send, self.keep = add_halves(pairs, bit)
        self.leave(send)
        return self.keep

    def finish(self, last):
        while self.order:
            last = self.step(last)
        total = order_after(self.keep, last).astype(jnp.float32) + self.got.astype(jnp.float32)
        ends = [sum(self.heights[:n]) for n in range(len(self.heights) + 1)]
        return {label: total[0, a:b] for label, a, b in zip(self.labels, ends, ends[1:])}


def row_cover(rows, count, unit=16):
    share = rows // count
    starts = [share * c // 8 * 8 for c in range(count)]
    height = max(share * (c + 1) - starts[c] for c in range(count))
    height = -(-height // unit) * unit
    return [min(s, rows - height) for s in starts], height


def head_groups(heads):
    first = -(-heads * 3 // 5)
    return [(0, first, 0), (first, heads - first, 3 * first)]


def no_grid_call(body, out_shape, name, flops, inputs, scratch, scalars=1):
    in_specs = [pl.BlockSpec(memory_space=pltpu.SMEM)] * scalars
    in_specs += [pl.BlockSpec(memory_space=pltpu.VMEM)] * (len(inputs) - scalars)
    moved = sum(x.size * x.dtype.itemsize for x in inputs)
    moved += sum(math.prod(x.shape) * x.dtype.itemsize for x in jax.tree.leaves(out_shape))
    return pl.pallas_call(
        body,
        out_shape=out_shape,
        in_specs=in_specs,
        out_specs=jax.tree.map(lambda _: pl.BlockSpec(memory_space=pltpu.VMEM), out_shape),
        scratch_shapes=scratch,
        compiler_params=pltpu.CompilerParams(vmem_limit_bytes=VMEM_LIMIT),
        cost_estimate=SHORT,
        name=name,
    )(*inputs)


def make_diagonal(diag_ref, keys, tile, prefix):
    first = tile * TILE
    shape = (TILE, TILE)
    key_at = lax.broadcasted_iota(jnp.int32, shape, 0)
    row_at = lax.broadcasted_iota(jnp.int32, shape, 1)
    opened = keys[first : first + TILE, ONE_ROW : ONE_ROW + 1].astype(jnp.float32) > -1.0
    near = (key_at <= row_at) | (key_at + first < prefix)
    seen = (near & opened) | (key_at == row_at)
    diag_ref[tile] = jnp.where(seen, 0.0, MASKED)


def without_mask(keys):
    lane = lax.broadcasted_iota(jnp.int32, keys.shape, 1)
    return jnp.where(lane == ONE_ROW, 0.0, keys.astype(jnp.float32)).astype(jnp.bfloat16)


def turned_rows(columns):
    return columns.astype(jnp.float32).T.astype(jnp.bfloat16)


def split_rows(columns, value):
    row = lax.broadcasted_iota(jnp.int32, columns.shape, 0)
    result = columns.astype(jnp.float32)
    for place in range(3):
        part = value.astype(jnp.bfloat16).astype(jnp.float32)
        value = value - part
        result = jnp.where(row == SPLIT_ROW + place, part, result)
    return result.astype(jnp.bfloat16)


def forward_kernel(seq_count, span, heads, head_size, rate, scalars, *refs):
    blocks, (weight, bias) = refs[:seq_count], refs[seq_count : seq_count + 2]
    groups = head_groups(heads)
    *qkv_groups, out = refs[seq_count + 2 : seq_count + 3 + len(groups)]
    *parts, rows, diag, scores = refs[seq_count + 3 + len(groups) :]
    me, prefix = scalars[0], scalars[2]
    length = span * seq_count
    tiles = length // TILE
    for r in range(seq_count):
        mixed = jnp.dot(weight[...], blocks[r][...], preferred_element_type=jnp.float32)
        mixed = (mixed + bias[...]).astype(jnp.bfloat16)
        place = pl.ds(pl.multiple_of((me ^ r) * span, LANES), span)
        mixed = mixed.reshape(3 * heads, HEAD_PAD, span)
        for (_, count, base), qkv in zip(groups, qkv_groups):
            qkv[:, :, place] = mixed[base : base + 3 * count]

    def turn(first, count, qkv, h, carry):
        rows[first + h] = turned_rows(qkv[count + h])
        return carry

    for (first, count, _), qkv in zip(groups, qkv_groups):
        lax.fori_loop(0, count, partial(turn, first, count, qkv), 0)
    for tile in range(tiles):
        make_diagonal(diag, rows.at[0], tile, prefix)

    def one_head(start, count, qkv, h, carry):
        for tile in range(tiles):
            across = slice(tile * TILE, (tile + 1) * TILE)
            query = qkv[h, :, across]
            tops = None
            for j in range(tile + 1):
                down = slice(j * TILE, (j + 1) * TILE)
                keys = rows[start + h, down, :]
                if j == tile:
                    keys = without_mask(keys)
                block = jnp.dot(keys, query, preferred_element_type=jnp.float32)
                if j == tile:
                    block = block + diag[tile]
                scores[down, :] = block
                top = jnp.max(block.reshape(TILE // 8, 8, TILE), axis=0)
                tops = top if tops is None else jnp.maximum(tops, top)
            top = jnp.max(tops, axis=0, keepdims=True)
            total = jnp.zeros((HEAD_PAD, TILE), jnp.float32)
            for j in range(tile + 1):
                down = slice(j * TILE, (j + 1) * TILE)
                probs = jnp.exp2((scores[down, :] - top) * rate).astype(jnp.bfloat16)
                total += jnp.dot(
                    qkv[2 * count + h, :, down], probs, preferred_element_type=jnp.float32
                )
            summed = total[ONE_ROW : ONE_ROW + 1]
            row = lax.broadcasted_iota(jnp.int32, total.shape, 0)
            log_sum = top * rate + jnp.log2(summed)
            out[start + h, :, across] = jnp.where(row == ONE_ROW, log_sum, total / summed)
        return carry

    for (first, count, _), qkv in zip(groups, qkv_groups):
        lax.fori_loop(0, count, partial(one_head, first, count, qkv), 0)
    for r in range(seq_count):
        place = pl.ds(pl.multiple_of((me ^ r) * span, LANES), span)
        piece = out[:, :head_size, place].reshape(heads * head_size, span)
        parts[r][...] = piece.astype(jnp.bfloat16)


def backward_kernel(
    seq_count, places, cell, span, first_head, heads, head_size, rate, earlier, scalars, *refs
):
    qkv, out, *rest = refs[:-9] if earlier is not None else refs[:-7]
    arrays = rest[: 1 + max(n for n, _ in places)]
    if earlier is not None:
        weights, backs = rest[len(arrays) : -earlier], rest[-earlier:]
        result, away, here_sums = refs[-9:-6]
    else:
        result = refs[-7]
    back, query_rows, key_rows, value_rows, gathered, diag = refs[-6:]
    me, prefix = scalars[0], scalars[2]
    length = span * seq_count
    tiles = length // TILE
    scale = 1.0 / math.sqrt(head_size)
    for r in range(seq_count):
        place = pl.ds(pl.multiple_of((me ^ r) * span, LANES), span)
        gathered[:, :, place] = arrays[places[r][0]][
            places[r][1], cell, first_head : first_head + heads
        ]
    key_rows[...] = turned_rows(qkv[heads])
    for tile in range(tiles):
        make_diagonal(diag, key_rows, tile, prefix)

    def one_head(h, carry):
        key_rows[...] = turned_rows(qkv[heads + h])
        value_rows[...] = turned_rows(qkv[2 * heads + h])
        held = gathered[h]
        centre = jnp.sum(
            held[:head_size].astype(jnp.float32) * out[first_head + h, :head_size],
            axis=0,
            keepdims=True,
        )
        gathered[h] = split_rows(held, -centre)
        log_sum = out[first_head + h, ONE_ROW : ONE_ROW + 1, :]
        qkv_q = split_rows(qkv[h], -log_sum / rate)
        query_rows[...] = jnp.zeros_like(query_rows)
        for j in range(tiles):
            down = slice(j * TILE, (j + 1) * TILE)
            keys, values = key_rows[down, :], value_rows[down, :]
            keys_column = qkv[heads + h, :, down]
            keys_back = jnp.zeros((TILE, HEAD_PAD), jnp.float32)
            values_back = jnp.zeros((TILE, HEAD_PAD), jnp.float32)
            for i in range(j, tiles):
                across = slice(i * TILE, (i + 1) * TILE)
                query = qkv_q[:, across]
                back_out = gathered[h, :, across]
                if i == j:
                    block = jnp.dot(without_mask(keys), query, preferred_element_type=jnp.float32)
                    block = block + diag[i]
                else:
                    block = jnp.dot(keys, query, preferred_element_type=jnp.float32)
                probs = jnp.exp2(block * rate)
                back_probs = jnp.dot(values, back_out, preferred_element_type=jnp.float32)
                back_scores = (probs * back_probs).astype(jnp.bfloat16)
                probs = probs.astype(jnp.bfloat16)
                turned = (((1,), (1,)), ((), ()))
                values_back += lax.dot_general(
                    probs, back_out, turned, preferred_element_type=jnp.float32
                )
                keys_back += lax.dot_general(
                    back_scores, query, turned, preferred_element_type=jnp.float32
                )
                query_rows[:, across] += jnp.dot(
                    keys_column, back_scores, preferred_element_type=jnp.float32
                )
            back[heads + h, down, :] = (keys_back * scale).astype(jnp.bfloat16)
            back[2 * heads + h, down, :] = values_back.astype(jnp.bfloat16)
        back[h] = (query_rows[...] * scale).T.astype(jnp.bfloat16)
        return carry

    lax.fori_loop(0, heads, one_head, 0)
    for block in range(seq_count):
        here = slice(block * span, (block + 1) * span)
        there = pl.ds(pl.multiple_of((me ^ block) * span, LANES), span)
        for first in range(0, 3 * heads, 2):
            pieces = [back[p, here, :] for p in range(first, min(first + 2, 3 * heads))]
            joined = pieces[0] if len(pieces) == 1 else jnp.concatenate(pieces, axis=1)
            left = first * HEAD_PAD
            result[there, left : left + joined.shape[1]] = joined
    if earlier is None:
        return
    for r in range(seq_count):
        target = away if r & 1 else here_sums
        turned = (((1,), (1,)), ((), ()))
        total = 0.0
        for weight, dense in zip(weights, [*backs, result]):
            total += lax.dot_general(
                weight[...],
                dense[r * span : (r + 1) * span, :],
                turned,
                preferred_element_type=jnp.float32,
            )
        target[r >> 1] = total.astype(jnp.bfloat16)


def attend_forward(scalars, blocks, weight, bias, heads, head_size):
    seq_count, span = len(blocks), blocks[0].shape[1]
    length = seq_count * span
    rate = math.log2(math.e) / math.sqrt(head_size)
    flops = 2 * weight.size * length + 4 * heads * HEAD_PAD * length * length
    return no_grid_call(
        partial(forward_kernel, seq_count, span, heads, head_size, rate),
        tuple(
            jax.ShapeDtypeStruct((3 * count, HEAD_PAD, length), jnp.bfloat16)
            for _, count, _ in head_groups(heads)
        )
        + (jax.ShapeDtypeStruct((heads, HEAD_PAD, length), jnp.float32),)
        + (jax.ShapeDtypeStruct((heads * head_size, span), jnp.bfloat16),) * seq_count,
        "attend_forward",
        flops,
        [scalars, *blocks, weight, bias],
        [
            pltpu.VMEM((heads, length, HEAD_PAD), jnp.bfloat16),
            pltpu.VMEM((length // TILE, TILE, TILE), jnp.float32),
            pltpu.VMEM((length, TILE), jnp.float32),
        ],
    )


def attend_backward(
    scalars, cell, qkv, out, arrays, places, first_head, head_size, weights=None, backs=()
):
    seq_count, span = len(places), arrays[0].shape[-1]
    heads = qkv.shape[0] // 3
    length = seq_count * span
    rate = math.log2(math.e) / math.sqrt(head_size)
    earlier = len(backs) if weights else None
    inputs = [scalars, qkv, out, *arrays]
    results = (jax.ShapeDtypeStruct((length, 3 * heads * HEAD_PAD), jnp.bfloat16),)
    if weights:
        inputs += [*weights, *backs]
        shape = (seq_count // 2, weights[0].shape[0], span)
        results += (jax.ShapeDtypeStruct(shape, jnp.bfloat16),) * 2
    return no_grid_call(
        partial(
            backward_kernel,
            seq_count,
            places,
            cell,
            span,
            first_head,
            heads,
            head_size,
            rate,
            earlier,
        ),
        results,
        "attend_backward",
        1,
        inputs,
        [
            pltpu.VMEM((3 * heads, length, HEAD_PAD), jnp.bfloat16),
            pltpu.VMEM((HEAD_PAD, length), jnp.float32),
            pltpu.VMEM((length, HEAD_PAD), jnp.bfloat16),
            pltpu.VMEM((length, HEAD_PAD), jnp.bfloat16),
            pltpu.VMEM((heads, HEAD_PAD, length), jnp.bfloat16),
            pltpu.VMEM((length // TILE, TILE, TILE), jnp.float32),
        ],
    )


def mix_outer_kernel(cell_count, share, cuts, count, scalars, *refs):
    blocks, backs = refs[: -count - 7], refs[-count - 7 : -7]
    *results, sums, turned, whole_sum = refs[-7:]
    span = blocks[0].shape[1]
    features = turned.shape[0]
    for n, block in enumerate(blocks):
        turned[:, n * span : (n + 1) * span] = block[:features, :]
    width = backs[0].shape[1]
    length = backs[0].shape[0]
    sums[...] = sum(
        jnp.sum(back[...].astype(jnp.float32), axis=0, keepdims=True) for back in backs
    )
    for first in range(0, width, TILE):
        last = min(first + TILE, width)
        total = None
        for n, back in enumerate(backs):
            part = jnp.dot(
                turned[:, n * length : (n + 1) * length],
                back[:, first:last],
                preferred_element_type=jnp.float32,
            )
            total = part if total is None else total + part
        whole_sum[:, first:last] = total
    for k in range(cell_count):
        c = k ^ scalars[1]
        start = jnp.minimum(lax.div(c * share, 8) * 8, features - cuts[-1])
        block = whole_sum[pl.ds(pl.multiple_of(start, 8), cuts[-1]), :].astype(jnp.bfloat16)
        for n, bit in enumerate((1, 2)):
            target = results[2 * n + (0 if k & bit else 1)]
            target[without_bit(k, bit)] = block[cuts[n] : cuts[n + 1]]


def mix_outer(scalars, blocks, backs, features, cell_count):
    _, height = row_cover(features, cell_count)
    cuts = (0, -(-height // 2 // 16) * 16, height)
    width = backs[0].shape[1]
    positions = sum(b.shape[0] for b in backs)
    halves = [(cell_count // 2, cuts[n + 1] - cuts[n], width) for n in (0, 0, 1, 1)]
    return no_grid_call(
        partial(mix_outer_kernel, cell_count, features // cell_count, cuts, len(backs)),
        tuple(jax.ShapeDtypeStruct(shape, jnp.bfloat16) for shape in halves)
        + (jax.ShapeDtypeStruct((1, width), jnp.float32),),
        "mix_outer",
        2 * positions * features * width,
        [scalars, *blocks, *backs],
        [
            pltpu.VMEM((features, positions), jnp.bfloat16),
            pltpu.VMEM((features, width), jnp.float32),
        ],
    )


def gathered_blocks(block, seq_count):
    held = {0: block}
    for bit in list(reversed(bits_of(seq_count))):
        held.update({r | bit: swap_with(x, "seq", bit) for r, x in list(held.items())})
    return [held[r] for r in range(seq_count)]


def route_upper(upper):
    return swap_with(upper, "seq", upper.shape[0])


def route_rest(lower, got):
    seq_count = 2 * len(lower)
    arrays = [x[None] for x in lower] + [got]
    held = {r: (r, 0) for r in range(len(lower))}
    held.update({len(lower) + r: (len(lower), r) for r in range(len(lower))})
    for bit in list(reversed(bits_of(seq_count)))[1:]:
        away = [r for r in held if r & bit]
        arrays.append(swap_with(jnp.stack([arrays[held[r][0]][held[r][1]] for r in away]), "seq", bit))
        held.update({r: (len(arrays) - 1, n) for n, r in enumerate(away)})
    return arrays, [held[r] for r in range(seq_count)]


def exchanged_blocks(blocks):
    return [blocks[0]] + [swap_with(blocks[r], "seq", r) for r in range(1, len(blocks))]


def chunks(width):
    return [(first, min(first + TILE, width)) for first in range(0, width, TILE)]


def dot(left, right):
    return jnp.dot(left, right, preferred_element_type=jnp.float32)


def dot_turned(left, right):
    return lax.dot_general(
        left, right, (((1,), (1,)), ((), ())), preferred_element_type=jnp.float32
    )


def centred_columns(values):
    centred = values - jnp.mean(values, axis=0, keepdims=True)
    spread = jnp.mean(centred * centred, axis=0, keepdims=True)
    rise = lax.rsqrt(spread + 1e-05)
    return centred * rise, rise


def norm_pull(normal, rise, back, gain):
    scaled = back * gain
    inner = scaled - jnp.mean(scaled, axis=0, keepdims=True)
    inner = inner - normal * jnp.mean(scaled * normal, axis=0, keepdims=True)
    return rise * inner


def columns_of(lines):
    turned = lines[...].T
    return [turned[:, n : n + 1] for n in range(8)]


def lines_of(columns):
    rows = columns[0].shape[0]
    room = [jnp.zeros((rows, 8 - len(columns)), jnp.float32)] if len(columns) < 8 else []
    return jnp.concatenate(list(columns) + room, axis=1).T


def first_norm_kernel(tokens, lines, hidden, *results):
    width = tokens.shape[1]
    gain, shift = columns_of(lines)[:2]
    for c, result in enumerate(results):
        normal, _ = centred_columns(tokens[c].astype(jnp.float32))
        result[:width, :] = (normal * gain + shift).astype(jnp.bfloat16)
        shape = (result.shape[0] - width, result.shape[1])
        mark = lax.broadcasted_iota(jnp.int32, shape, 0) == 0
        result[width:, :] = jnp.where(mark, hidden[c : c + 1, :], 0.0).astype(jnp.bfloat16)


def first_norm(tokens, lines, hidden, features):
    cells, _, span = tokens.shape
    return no_grid_call(
        first_norm_kernel,
        (jax.ShapeDtypeStruct((features, span), jnp.bfloat16),) * cells,
        "first_norm",
        10 * tokens.size,
        [tokens, lines, hidden],
        [],
        scalars=0,
    )


def second_norm_kernel(seq_count, scalars, weight, tokens, lines, *refs):
    parts = refs[:seq_count]
    middle, second, second_turned, attended, gather = refs[seq_count:]
    share = parts[0].shape[0]
    _, _, gain, shift, bias, *_ = columns_of(lines)
    for r in range(seq_count):
        place = pl.ds(pl.multiple_of((scalars[0] ^ r) * share, 8), share)
        gather[place, :] = parts[r][...].astype(jnp.float32)
    attended[...] = gather[: attended.shape[0], :].astype(jnp.bfloat16)
    total = dot(weight[...].T, attended[...])
    total = tokens[...].astype(jnp.float32) + (total + bias)
    middle[...] = total
    normal, _ = centred_columns(total)
    normed = (normal * gain + shift).astype(jnp.bfloat16)
    second_turned[...] = normed
    second[...] = normed.T


def second_norm(scalars, weight, tokens, lines, parts):
    width, span = tokens.shape
    seq_count = len(parts)
    return no_grid_call(
        partial(second_norm_kernel, seq_count),
        (
            jax.ShapeDtypeStruct((width, span), jnp.float32),
            jax.ShapeDtypeStruct((span, width), jnp.bfloat16),
            jax.ShapeDtypeStruct((width, span), jnp.bfloat16),
            jax.ShapeDtypeStruct((width, span), jnp.bfloat16),
        ),
        "second_norm",
        2 * span * width * width,
        [scalars, weight, tokens, lines, *parts],
        [pltpu.VMEM((seq_count * parts[0].shape[0], span), jnp.float32)],
    )


def weights_kernel(seq_count, heads, head_size, scalars, mix, weight, *turned):
    width = mix.shape[0]
    here = heads * head_size
    groups = head_groups(heads)
    weight[...] = jnp.zeros_like(weight)
    for s in range(seq_count):

        @pl.when(scalars[0] == s)
        def _():
            for p in range(3):
                first = s * here
                last = min(first + here, width)
                if last <= first:
                    continue
                start = (p * width + first) // LANES * LANES
                stop = min(-(-(p * width + last) // LANES) * LANES, mix.shape[1])
                block = mix[:, start:stop].astype(jnp.float32)
                block = block[:, p * width + first - start : p * width + last - start].T
                for group_first, count, base in groups:
                    for n in range(count):
                        h = group_first + n
                        if (h + 1) * head_size > last - first:
                            continue
                        place = (base + p * count + n) * HEAD_PAD
                        piece = block[h * head_size : (h + 1) * head_size]
                        room = jnp.zeros((HEAD_PAD - head_size, width), jnp.float32)
                        piece = jnp.concatenate([piece, room])
                        weight[place : place + HEAD_PAD, :width] = piece.astype(jnp.bfloat16)

    room = weight.shape[1] - width
    for (_, count, base), columns in zip(groups, turned):
        rows = slice(base * HEAD_PAD, (base + 3 * count) * HEAD_PAD)
        columns[...] = weight[rows, :width].T
        rows = slice((base + count) * HEAD_PAD, (base + 2 * count) * HEAD_PAD)
        row = lax.broadcasted_iota(jnp.int32, (count * HEAD_PAD, room), 0)
        lane = lax.broadcasted_iota(jnp.int32, (count * HEAD_PAD, room), 1)
        mark = (lane == 0) & (lax.rem(row, HEAD_PAD) == ONE_ROW)
        weight[rows, width:] = jnp.where(mark, 1.0, 0.0).astype(jnp.bfloat16)


def own_weights(scalars, mix, features, seq_count, heads, head_size):
    width = mix.shape[0]
    return no_grid_call(
        partial(weights_kernel, seq_count, heads, head_size),
        (jax.ShapeDtypeStruct((3 * heads * HEAD_PAD, features), jnp.bfloat16),)
        + tuple(
            jax.ShapeDtypeStruct((width, 3 * count * HEAD_PAD), jnp.bfloat16)
            for _, count, _ in head_groups(heads)
        ),
        "own_weights",
        1,
        [scalars, mix],
        [],
    )


def active_back_kernel(cotangent, down, result):
    for first, last in chunks(down.shape[1]):
        result[:, first:last] = dot(cotangent[...], down[:, first:last])


def active_back(scalars, cotangent, down):
    rows, width = cotangent.shape
    tile = hidden_tile(down.shape[1])
    shape = jax.ShapeDtypeStruct((rows, down.shape[1]), jnp.float32)
    return grid_call(
        lambda me, *refs: active_back_kernel(*refs),
        (down.shape[1] // tile,),
        [whole(cotangent), pl.BlockSpec((width, tile), lambda g, me: (0, g))],
        pl.BlockSpec((rows, tile), lambda g, me: (0, g)),
        shape,
        [],
        "active_back",
        1,
        (scalars, cotangent, down),
        1,
    )


def hidden_kernel(back_active, up, up_bias, *refs):
    *parts, active, back_upper, bias_back, second = refs

    @pl.when(pl.program_id(0) == 0)
    def _():
        for c, part in enumerate(parts):
            second[c * part.shape[0] : (c + 1) * part.shape[0], :] = part[...]

    inner = math.sqrt(2.0 / math.pi)
    for first, last in chunks(up.shape[1]):
        upper = dot(second[...], up[:, first:last]) + up_bias[:, first:last]
        back = back_active[:, first:last]
        square = upper * upper
        bend = jnp.tanh(inner * upper * (1.0 + 0.044715 * square))
        half = 0.5 + 0.5 * bend
        slope = half + (0.5 * inner) * upper * (1.0 - bend * bend) * (1.0 + 0.134145 * square)
        active[:, first:last] = (upper * half).astype(jnp.bfloat16)
        back = (back * slope).astype(jnp.bfloat16)
        back_upper[:, first:last] = back
        bias_back[:, first:last] = jnp.sum(back.astype(jnp.float32), axis=0, keepdims=True)


def grid_call(
    body, grid, in_specs, out_specs, out_shape, scratch, name, flops, inputs, moved, aliases=None
):
    return pl.pallas_call(
        body,
        out_shape=out_shape,
        grid_spec=pltpu.PrefetchScalarGridSpec(
            num_scalar_prefetch=1,
            grid=grid,
            in_specs=in_specs,
            out_specs=out_specs,
            scratch_shapes=scratch,
        ),
        compiler_params=pltpu.CompilerParams(vmem_limit_bytes=VMEM_LIMIT),
        cost_estimate=SHORT,
        input_output_aliases=aliases or {},
        name=name,
    )(*inputs)


def whole(array):
    zeros = (0,) * array.ndim
    return pl.BlockSpec(array.shape, lambda g, me: zeros)


def hidden_tile(hidden):
    return max(t for t in range(LANES, 1024, LANES) if hidden % t == 0)


def hidden_layer(scalars, second, back_active, up, up_bias):
    rows = sum(part.shape[0] for part in second)
    width = up.shape[0]
    hidden = up.shape[1]
    tile = hidden_tile(hidden)
    weight = pl.BlockSpec((width, tile), lambda g, me: (0, g))
    out = pl.BlockSpec((rows, tile), lambda g, me: (0, g))
    line = pl.BlockSpec((1, tile), lambda g, me: (0, g))
    return grid_call(
        lambda me, *refs: hidden_kernel(*refs),
        (hidden // tile,),
        [out, weight, line] + [whole(part) for part in second],
        [out, out, line],
        (
            jax.ShapeDtypeStruct((rows, hidden), jnp.bfloat16),
            jax.ShapeDtypeStruct((rows, hidden), jnp.bfloat16),
            jax.ShapeDtypeStruct((1, hidden), jnp.float32),
        ),
        [pltpu.VMEM((rows, width), jnp.bfloat16)],
        "hidden_layer",
        4 * rows * up.size,
        (scalars, back_active, up, up_bias, *second),
        4 * up.size + 4 * rows * hidden,
    )


def middle_back_kernel(
    seq_count,
    cells,
    scalars,
    back_upper,
    up,
    lines,
    cotangent,
    weight,
    *refs,
):
    middle, (back_middle, back_branch, sums) = refs[:cells], refs[cells : cells + 3]
    *parts, total, back_heads = refs[cells + 3 :]
    half = seq_count // 2
    step = pl.program_id(0)

    @pl.when(step == 0)
    def _():
        total[...] = jnp.zeros_like(total)

    for first, last in chunks(total.shape[1]):
        total[:, first:last] += dot_turned(up[...], back_upper[first:last, :])

    @pl.when(step == pl.num_programs(0) - 1)
    def _():
        span = cotangent.shape[2]
        heads = parts[0].shape[1]
        head_size = back_heads.shape[0] // (seq_count * heads)
        gain = columns_of(lines)[2]
        totals = [0.0] * 4
        for c in range(cells):
            here = slice(c * span, (c + 1) * span)
            normal, rise = centred_columns(middle[c][...])
            back = total[:, here]
            back_out = cotangent[c].astype(jnp.float32)
            back_mid = back_out + norm_pull(normal, rise, back, gain)
            back_middle[:, here] = back_mid
            branch = back_mid.astype(jnp.bfloat16)
            back_branch[:, here] = branch
            for n, term in enumerate((back * normal, back, branch.astype(jnp.float32), back_out)):
                totals[n] = totals[n] + jnp.sum(term, axis=1, keepdims=True)
            back_heads[: weight.shape[0], :] = dot(weight[...], branch)
            if back_heads.shape[0] > weight.shape[0]:
                rest = back_heads.shape[0] - weight.shape[0]
                back_heads[weight.shape[0] :, :] = jnp.zeros((rest, span), jnp.float32)
            for r in range(seq_count):
                first = (scalars[0] ^ r) * heads * head_size
                part = back_heads[pl.ds(pl.multiple_of(first, 8), heads * head_size), :]
                room = jnp.zeros((heads, HEAD_PAD - head_size, span), jnp.float32)
                part = jnp.concatenate([part.reshape(heads, head_size, span), room], axis=1)
                target = parts[r].at[c] if r < half else parts[half].at[r - half, c]
                target[...] = part.astype(jnp.bfloat16)
        sums[...] = lines_of(totals)


def middle_back(scalars, back_upper, up, middle, lines, cotangent, weight, seq_count, heads):
    rows, hidden = back_upper.shape
    cells, width, span = cotangent.shape
    head_size = width // HEADS
    tile = hidden_tile(hidden)
    outs = [
        jax.ShapeDtypeStruct((width, rows), jnp.float32),
        jax.ShapeDtypeStruct((width, rows), jnp.bfloat16),
        jax.ShapeDtypeStruct((8, width), jnp.float32),
    ]
    block = (cells, heads, HEAD_PAD, span)
    outs += [jax.ShapeDtypeStruct(block, jnp.bfloat16)] * (seq_count // 2)
    outs += [jax.ShapeDtypeStruct((seq_count // 2,) + block, jnp.bfloat16)]
    return grid_call(
        partial(middle_back_kernel, seq_count, cells),
        (hidden // tile,),
        [
            pl.BlockSpec((rows, tile), lambda g, me: (0, g)),
            pl.BlockSpec((width, tile), lambda g, me: (0, g)),
            whole(lines),
            whole(cotangent),
            whole(weight),
        ]
        + [whole(m) for m in middle],
        [whole(o) for o in outs],
        outs,
        [
            pltpu.VMEM((width, rows), jnp.float32),
            pltpu.VMEM((seq_count * heads * head_size, span), jnp.float32),
        ],
        "middle_back",
        2 * rows * up.size + 2 * rows * width * width,
        (scalars, back_upper, up, lines, cotangent, weight, *middle),
        1,
    )


def block_out_kernel(active, down, lines, *refs):
    *middle, result, total = refs
    step = pl.program_id(0)

    @pl.when(step == 0)
    def _():
        bias = columns_of(lines)[5]
        for c, part in enumerate(middle):
            span = part.shape[1]
            total[:, c * span : (c + 1) * span] = part[...] + bias

    for first, last in chunks(total.shape[1]):
        total[:, first:last] += dot_turned(down[...], active[first:last, :])

    @pl.when(step == pl.num_programs(0) - 1)
    def _():
        cells, _, span = result.shape
        for c in range(cells):
            result[c] = total[:, c * span : (c + 1) * span].astype(jnp.bfloat16)


def block_output(scalars, active, down, middle, lines):
    rows, hidden = active.shape
    cells, width = len(middle), middle[0].shape[0]
    tile = hidden_tile(hidden)
    out = jax.ShapeDtypeStruct((cells, width, rows // cells), jnp.bfloat16)
    return grid_call(
        lambda me, *refs: block_out_kernel(*refs),
        (hidden // tile,),
        [
            pl.BlockSpec((rows, tile), lambda g, me: (0, g)),
            pl.BlockSpec((width, tile), lambda g, me: (0, g)),
            whole(lines),
        ]
        + [whole(m) for m in middle],
        whole(out),
        out,
        [pltpu.VMEM((width, rows), jnp.float32)],
        "block_output",
        2 * rows * down.size,
        (scalars, active, down, lines, *middle),
        1,
    )


def take_columns(piece, right, count, which):
    width = piece.shape[1]
    for s in range(count):

        @pl.when(which == s)
        def _():
            first = s * width // LANES * LANES
            last = min(-(-(s + 1) * width // LANES) * LANES, right.shape[1])
            block = right[:, first:last]
            piece[...] = block[:, s * width - first : (s + 1) * width - first]


def up_outer_kernel(seq_count, cells, share, cut, zbit, split, scalars, right, *refs):
    left, rest = refs[:cells], refs[cells:]
    got = rest[0] if split else None
    *results, total, piece, joined = rest[3 if split else 0 :]
    rows = left[0].shape[0]
    core = 0 if split else 1

    @pl.when(pl.program_id(0) == 0)
    def _():
        for c, part in enumerate(left):
            joined[:, c * part.shape[1] : (c + 1) * part.shape[1]] = part[...]

    take_columns(piece, right, seq_count, (2 * pl.program_id(0) + core) ^ scalars[0])
    for first, last in chunks(piece.shape[1]):
        total[:, first:last] = dot(joined[...], piece[:, first:last])
    cell_count = results[0].shape[1] * (2 if split else 1)
    height = results[0].shape[2] if not split else got.shape[2]
    for k in range(cell_count):
        c = k ^ scalars[1]
        start = jnp.minimum(lax.div(c * share, 8) * 8, rows - height)
        block = total[pl.ds(pl.multiple_of(start, 8), height), :]
        if split:
            block = block + got[0, k].astype(jnp.float32)
            for n, (bit, part) in enumerate(((1, block[:cut]), (zbit, block[cut:]))):
                target = results[2 * n + (0 if k & bit else 1)]
                target[0, without_bit(k, bit)] = part.astype(jnp.bfloat16)
        else:
            results[0][0, k] = block.astype(jnp.bfloat16)


def up_outer(scalars, left, right, seq_count, cell_count, got=None, lower=None):
    tokens, width = right.shape[0], right.shape[1] // seq_count
    rows = left[0].shape[0]
    _, height = row_cover(rows, cell_count)
    half = seq_count // 2
    split = got is not None
    cut = two_thirds(height)
    in_specs = [whole(right)] + [whole(part) for part in left]
    inputs = [scalars, right, *left]
    aliases = {}
    if split:
        in_specs.append(pl.BlockSpec((1,) + got.shape[1:], lambda g, me: (g, 0, 0, 0)))
        in_specs += [pl.BlockSpec(memory_space=pl.ANY)] * 2
        inputs += [got, *lower]
        aliases = {len(inputs) - 2: 2, len(inputs) - 1: 3}
        outs = [(half, cell_count // 2, cut, width)] * 2 + [lower[0].shape] * 2
        low = height - cut
        blocks = [pl.BlockSpec((1,) + outs[0][1:], lambda g, me: (g, 0, 0, 0))] * 2
        blocks += [
            pl.BlockSpec((1, cell_count // 2, low, width), lambda g, me: (g, 0, 1, 0))
        ] * 2
    else:
        outs = [(half, cell_count, height, width)]
        blocks = [pl.BlockSpec((1,) + outs[0][1:], lambda g, me: (g, 0, 0, 0))]
    return grid_call(
        partial(
            up_outer_kernel,
            seq_count,
            len(left),
            rows // cell_count,
            cut,
            cell_count // seq_count,
            split,
        ),
        (half,),
        in_specs,
        blocks,
        [jax.ShapeDtypeStruct(out, jnp.bfloat16) for out in outs],
        [
            pltpu.VMEM((rows, width), jnp.float32),
            pltpu.VMEM((tokens, width), jnp.bfloat16),
            pltpu.VMEM((rows, tokens), jnp.bfloat16),
        ],
        "up_outer",
        1,
        inputs,
        1,
        aliases,
    )


def two_thirds(height):
    return -(-height * 2 // 3 // 16) * 16


def down_outer_kernel(seq_count, inner, cut, split, scalars, left, right, *refs):
    got = refs[0] if split else None
    *results, total, piece, wide, own = refs[1 if split else 0 :]
    half = seq_count // 2
    share = own.shape[0] // half
    span = left.shape[2]
    width = piece.shape[1] // inner
    low = scalars[1] & (inner - 1)
    step = pl.program_id(0)
    core = 0 if split else 1
    starts, height = row_cover(share, inner)

    @pl.when(step == 0)
    def _():
        for c in range(left.shape[0]):
            wide[:, c * span : (c + 1) * span] = left[c].astype(jnp.float32)
        for x in range(half):
            for s in range(seq_count):

                @pl.when(((2 * x + core) ^ scalars[0]) == s)
                def _():
                    own[x * share : (x + 1) * share, :] = wide[s * share : (s + 1) * share, :]

    take_columns(piece, right, seq_count, step ^ lax.div(scalars[1], inner))
    for first, last in chunks(piece.shape[1]):
        total[:, first:last] = dot(own[...].astype(jnp.bfloat16), piece[:, first:last])
    for q in range(inner):
        for x in range(half):
            block = total[x * share : (x + 1) * share, q * width : (q + 1) * width]
            block = jnp.concatenate([block[s : s + height] for s in starts], axis=1)
            if split:
                block = block + got[x, q ^ low].astype(jnp.float32)
                away = 2 * x >= half
                target = results[0 if away else 1]
                target[x % (half // 2), q ^ low] = block[:cut].astype(jnp.bfloat16)
                rest = block[cut:].astype(jnp.bfloat16)

                @pl.when(step & 1 == 1)
                def _():
                    results[2][x, q ^ low] = rest

                @pl.when(step & 1 == 0)
                def _():
                    results[3][x, q ^ low] = rest

            else:
                results[0][x, q ^ low] = block.astype(jnp.bfloat16)


def down_outer(scalars, left, right, seq_count, cell_count, got=None):
    tokens, width = right.shape[0], right.shape[1] // seq_count
    half = seq_count // 2
    inner = cell_count // seq_count
    share = left.shape[1] // seq_count
    split = got is not None
    _, height = row_cover(share, inner)
    cut = two_thirds(height)
    in_specs = [whole(left), whole(right)]
    inputs = [scalars, left, right]
    if split:
        in_specs.append(pl.BlockSpec((half, inner) + got.shape[2:], lambda g, me: (0, g, 0, 0)))
        inputs.append(got)
        low = height - cut
        outs = [(half // 2, cell_count, cut, width)] * 2
        outs += [(half, cell_count // 2, 2 * low, width)] * 2
        blocks = [pl.BlockSpec((half // 2, inner, cut, width), lambda g, me: (0, g, 0, 0))] * 2
        blocks += [pl.BlockSpec((half, inner, low, width), lambda g, me: (0, g // 2, 0, 0))] * 2
    else:
        outs = [(half, cell_count, height, width)]
        blocks = [pl.BlockSpec((half, inner, height, width), lambda g, me: (0, g, 0, 0))]
    return grid_call(
        partial(down_outer_kernel, seq_count, inner, cut, split),
        (seq_count,),
        in_specs,
        blocks,
        [jax.ShapeDtypeStruct(out, jnp.bfloat16) for out in outs],
        [
            pltpu.VMEM((half * share, width), jnp.float32),
            pltpu.VMEM((tokens, width), jnp.bfloat16),
            pltpu.VMEM((left.shape[1], tokens), jnp.float32),
            pltpu.VMEM((half * share, tokens), jnp.float32),
        ],
        "down_outer",
        1,
        inputs,
        1,
    )


def out_outer_kernel(seq_count, cells, share, scalars, right, *refs):
    left, (result, total, joined) = refs[:cells], refs[cells:]
    for c, part in enumerate(left):
        joined[:, c * part.shape[1] : (c + 1) * part.shape[1]] = part[...]
    rows = total.shape[0]
    for first, last in chunks(total.shape[1]):
        total[:, first:last] = dot_turned(joined[...], right[first:last, :])
    width = total.shape[1] // seq_count
    part = result.shape[2]
    for k in range(result.shape[1]):
        c = k ^ scalars[1]
        start = jnp.minimum(lax.div(c * share, 8) * 8, rows - seq_count * part)
        block = total[pl.ds(pl.multiple_of(start, 8), seq_count * part), :]
        for s in range(seq_count):
            piece = block[:, s * width : (s + 1) * width]
            groups = [piece[i * part : (i + 1) * part] for i in range(seq_count)]
            place = s ^ scalars[0]
            place = (place & 1) * (seq_count // 2) + (place >> 1)
            result[place, k] = jnp.concatenate(groups, axis=1).astype(jnp.bfloat16)


def out_outer(scalars, left, right, seq_count, cell_count):
    rows, tokens = right.shape
    _, height = row_cover(rows, cell_count, 16 * seq_count)
    shape = (seq_count, cell_count, height // seq_count, rows)
    return no_grid_call(
        partial(out_outer_kernel, seq_count, len(left), rows // cell_count),
        jax.ShapeDtypeStruct(shape, jnp.bfloat16),
        "out_outer",
        1,
        [scalars, right, *left],
        [pltpu.VMEM((rows, rows), jnp.float32), pltpu.VMEM((rows, tokens), jnp.bfloat16)],
    )


def mix_columns_kernel(heads, head_size, scalars, *refs):
    *blocks, result = refs
    places = {}
    for first, count, base in head_groups(heads):
        places.update({(p, first + n): base + p * count + n for p in range(3) for n in range(count)})
    seq_count = len(blocks)
    share = result.shape[1]
    width = HEADS * head_size
    for mine in range(seq_count):

        @pl.when(scalars[0] == mine)
        def _():
            for p in range(3):
                for head in range(HEADS):
                    first = p * width + head * head_size - mine * share
                    cut_left, cut_right = max(0, -first), min(head_size, share - first)
                    if cut_left >= cut_right:
                        continue
                    block = blocks[(head // heads) ^ mine]
                    source = places[p, head % heads] * HEAD_PAD
                    base = source // LANES * LANES
                    piece = block[:, base : min(base + LANES, block.shape[1])].astype(jnp.float32)
                    source -= base
                    result[:, first + cut_left : first + cut_right] = piece[
                        :, source + cut_left : source + cut_right
                    ]


def mix_columns(scalars, blocks, heads, head_size):
    rows = blocks[0].shape[0]
    return no_grid_call(
        partial(mix_columns_kernel, heads, head_size),
        jax.ShapeDtypeStruct((rows, 3 * HEADS * head_size // len(blocks)), jnp.float32),
        "mix_columns",
        1,
        [scalars, *blocks],
        [],
    )


def tokens_back_kernel(tokens, lines, back_middle, *refs):
    cells, _, span = tokens.shape
    terms, (result, sums) = refs[: 2 * cells], refs[2 * cells :]
    gain = columns_of(lines)[0]
    totals = [0.0] * 2
    for c in range(cells):
        normal, rise = centred_columns(tokens[c].astype(jnp.float32))
        back = terms[2 * c][...].astype(jnp.float32) + terms[2 * c + 1][...].astype(jnp.float32)
        back_in = back_middle[:, c * span : (c + 1) * span]
        back_in = back_in + norm_pull(normal, rise, back, gain)
        result[c] = back_in.astype(jnp.bfloat16)
        for n, term in enumerate((back * normal, back)):
            totals[n] = totals[n] + jnp.sum(term, axis=1, keepdims=True)
    sums[...] = lines_of(totals)


def tokens_back(tokens, lines, back_middle, terms):
    return no_grid_call(
        tokens_back_kernel,
        (
            jax.ShapeDtypeStruct(tokens.shape, jnp.bfloat16),
            jax.ShapeDtypeStruct((8, tokens.shape[1]), jnp.float32),
        ),
        "tokens_back",
        20 * tokens.size,
        [tokens, lines, back_middle, *terms],
        [],
        scalars=0,
    )


def order_after(values, *earlier):
    values, _ = lax.optimization_barrier((values, earlier))
    return values


def advance(parts, last):
    groups = {}
    running = [part for part in parts if part.order]
    arrived = [part.got for part in running]
    for part in running:
        part.got = order_after(part.got, arrived)
        key = (part.kind, tuple(part.names), tuple(part.order), part.keep.shape[2])
        groups.setdefault(key, []).append(part)
    for first, *others in groups.values():
        last = first.step(last, *others)
    return last


def on_device(
    tokens,
    first_gain,
    first_shift,
    mix_weight,
    query_bias,
    value_bias,
    out_weight,
    out_bias,
    second_gain,
    second_shift,
    up_weight,
    up_bias,
    down_weight,
    down_bias,
    cotangent,
    prefix_lengths,
    gene_counts,
    key_mask,
):
    cells_here, span, width = tokens.shape
    head_size = width // HEADS
    length = span * lax.axis_size("seq")
    start = lax.axis_index("seq") * span
    seq_count, cell_count = lax.axis_size("seq"), lax.axis_size("cells")
    me = jnp.stack([lax.axis_index("seq"), lax.axis_index("cells")]).astype(jnp.int32)
    totals = prefix_lengths + gene_counts
    row_count = cells_here * span
    own_rows = start + jnp.arange(span)
    heads_here = -(-HEADS // seq_count)
    head_total = heads_here * seq_count
    features = -(-(width + 1) // LANES) * LANES
    scalars = [jnp.concatenate([me, prefix_lengths[c : c + 1]]) for c in range(cells_here)]

    def flat(array):
        return array.reshape(row_count, array.shape[-1])

    def own_heads(array, at):
        lead = array.shape[:at]
        pad = [(0, 0)] * array.ndim
        pad[at] = (0, (head_total - HEADS) * head_size)
        array = jnp.pad(array, pad)
        here = heads_here * head_size
        array = lax.dynamic_slice_in_dim(array, me[0] * here, here, axis=at)
        return array.reshape(lead + (heads_here, head_size))

    def padded_heads(array, fills=()):
        room = HEAD_PAD - head_size
        tail = jnp.array(list(fills) + [0.0] * (room - len(fills)), array.dtype)
        tail = jnp.broadcast_to(tail, array.shape[:-1] + (room,))
        return jnp.concatenate([array, tail], axis=-1)

    bias_parts = (
        padded_heads(own_heads(query_bias, 0), (1.0,)),
        padded_heads(jnp.zeros((heads_here, head_size), jnp.float32), (0.0, 1.0, 1.0, 1.0)),
        padded_heads(own_heads(value_bias, 0), (1.0, 1.0, 1.0, 1.0)),
    )
    groups = head_groups(heads_here)
    bias = jnp.concatenate([p[h : h + n] for h, n, _ in groups for p in bias_parts]).reshape(-1, 1)

    open_here = (key_mask == 1) & (own_rows[None, :] < totals[:, None])
    hidden = jnp.where(open_here, 0.0, MASKED).astype(jnp.float32)
    nothing = jnp.zeros_like(first_gain)
    lines = jnp.stack(
        [first_gain, first_shift, second_gain, second_shift, out_bias, down_bias]
        + [nothing, nothing]
    )
    tokens_turned = tokens.transpose(0, 2, 1)
    cotangent_turned = cotangent.transpose(0, 2, 1)
    down_turned = down_weight.T
    normed = first_norm(tokens_turned, lines, hidden, features)
    weight, *weights_turned = own_weights(
        order_after(scalars[0], normed), mix_weight, features, seq_count, heads_here, head_size
    )
    own_cotangent = order_after(flat(cotangent), normed)
    x_bits = [b for b in reversed(bits_of(seq_count)) if b > 1]
    near = swap_with(jnp.stack(normed), "seq", 1)
    held = [{0: normed[c]} for c in range(cells_here)]
    earlier = ()
    for c in range(cells_here):
        for bit in x_bits:
            for r, block in list(held[c].items()):
                held[c][r | bit] = swap_with(order_after(block, *earlier), "seq", bit)
        earlier = (held[c][x_bits[0]], weight)
    back_active = active_back(
        scalars[0], order_after(own_cotangent, weight, held[0]), down_turned
    )
    normed_blocks = []
    for c in range(cells_here):
        after = (weight,) if c == 0 else (back_active,)
        for r, block in list(held[c].items()):
            held[c][r | 1] = near[c] if r == 0 else swap_with(order_after(block, *after), "seq", 1)
        normed_blocks.append([held[c][r] for r in range(seq_count)])

    attended, kept = [], []
    last = (back_active, bias)
    for c in range(cells_here):
        results = attend_forward(
            scalars[c], order_after(normed_blocks[c], *last), weight, bias, heads_here, head_size
        )
        qkv, out, parts = results[: len(groups)], results[len(groups)], results[len(groups) + 1 :]
        last = (out,)
        kept.append((qkv, out))
        attended.append(exchanged_blocks(parts))
    middle, second, second_turned, attended_turned = [], [], [], []
    for c in range(cells_here):
        results = second_norm(
            scalars[0],
            out_weight,
            tokens_turned[c],
            lines,
            order_after(attended[c], *last),
        )
        last = (results[0],)
        for held, result in zip((middle, second, second_turned, attended_turned), results):
            held.append(result)
    active, back_upper, up_bias_back = hidden_layer(
        scalars[0], second, back_active, up_weight, up_bias.reshape(1, -1)
    )
    (down_send,) = down_outer(scalars[0], cotangent_turned, active, seq_count, cell_count)
    down_got = swap_with(down_send, "seq", 1)
    (up_send,) = up_outer(
        scalars[0], second_turned, order_after(back_upper, down_send), seq_count, cell_count
    )
    up_got = swap_with(up_send, "seq", 1)
    *down_halves, lower_send, lower_keep = down_outer(
        scalars[0], cotangent_turned, order_after(active, up_send), seq_count, cell_count, down_got
    )
    *up_halves, lower_send, lower_keep = up_outer(
        scalars[0],
        second_turned,
        order_after(back_upper, down_halves),
        seq_count,
        cell_count,
        up_got,
        (lower_send, lower_keep),
    )

    def flat_blocks(array):
        return array.reshape((-1,) + array.shape[-2:])

    x_bits = [("seq", b) for b in reversed(bits_of(seq_count)) if b > 1]
    cell_bits = [("cells", b) for b in reversed(bits_of(cell_count))]
    names = x_bits + cell_bits
    y_bit, z_bit = ("cells", 1), ("cells", cell_count // seq_count)
    rest = [n for n in reversed(cell_bits) if n not in (y_bit, z_bit)]
    running = [
        Reduction("down", names, x_bits + [y_bit, z_bit] + rest, *map(flat_blocks, down_halves)),
        Reduction("up", names, [y_bit, z_bit] + x_bits + rest, *map(flat_blocks, up_halves)),
        Reduction(
            "both",
            names,
            [z_bit] + x_bits + [y_bit] + rest,
            flat_blocks(lower_send),
            flat_blocks(lower_keep),
        ),
    ]
    back_middle, back_branch, middle_sums, *back_heads = middle_back(
        scalars[0],
        order_after(back_upper, up_halves),
        up_weight,
        middle,
        lines,
        cotangent_turned,
        out_weight,
        seq_count,
        heads_here,
    )
    back_upper_half = route_upper(back_heads[-1])
    down_part, up_part, both_part = running
    last = down_part.step(back_heads)
    out_shares = out_outer(
        scalars[0],
        attended_turned,
        order_after(back_branch, last),
        seq_count,
        cell_count,
    )
    out_part = Reduction(
        "out",
        [("seq", 1)] + names,
        [("seq", 1), y_bit] + x_bits + [z_bit] + rest,
        flat_blocks(out_shares[seq_count // 2 :]),
        flat_blocks(out_shares[: seq_count // 2]),
    )
    last = advance([up_part, both_part], out_shares)
    back_arrays, back_places = route_rest(back_heads[:-1], order_after(back_upper_half, last))
    last = out_part.step(last)
    running.append(out_part)
    block_out = block_output(
        scalars[0], order_after(active, last), down_turned, middle, lines
    )
    last = block_out
    seq_bits = [("seq", 1)] + x_bits
    mixed_back, mix_parts = [[], []], []
    back_normed, bias_backs = [], []

    def mix_reductions(group, last):
        *halves, sums = mix_outer(
            scalars[0],
            [x for c in normed_blocks for x in c],
            order_after(mixed_back[group], last),
            width,
            cell_count,
        )
        bias_backs.append(sums)
        label = ["first", "second"][group]
        return [
            Reduction(label + " upper", cell_bits, [y_bit, z_bit] + rest, *halves[:2]),
            Reduction(label + " lower", cell_bits, [z_bit, y_bit] + rest, *halves[2:]),
        ], halves[0]

    for c in range(cells_here):
        qkv, out = kept[c]
        final = c == cells_here - 1
        for group, (first_head, _, _) in enumerate(groups):
            weights = weights_turned if group == len(groups) - 1 else None
            back, *sums = attend_backward(
                scalars[c],
                c,
                qkv[group],
                out,
                order_after(back_arrays, last),
                back_places,
                first_head,
                head_size,
                weights,
                [mixed_back[0][c]] if weights else (),
            )
            last = back
            mixed_back[group].append(back)
            if weights:
                back_normed.append(Reduction("normed", seq_bits, seq_bits, *sums, kind=c))
            else:
                running = [part for part in running if part.labels]
                last = advance(running, last)
                if c > 0:
                    last = back_normed[c - 1].step(last)
            if final:
                parts, last = mix_reductions(group, last)
                mix_parts.append(parts)
    ahead = [part for part in running if part.order]
    last = advance(mix_parts[0], (last, [part.got for part in back_normed[:-1]]))
    last = back_normed[-1].step(last)
    done = [part.got for part in running if not part.order]
    last = advance(mix_parts[1] + ahead, (last, done))
    last = advance(mix_parts[0], last)
    while any(part.order for part in back_normed):
        for part in back_normed:
            last = part.step(last) if part.order else last
    terms = [x for part in back_normed for x in (part.keep[0], part.got[0])]
    tokens_gradient, first_sums = tokens_back(
        tokens_turned, lines, back_middle, order_after(terms, last)
    )
    last = tokens_gradient
    running += mix_parts[0] + mix_parts[1]
    running = [part for part in running if part.labels]
    while any(part.order for part in running):
        last = advance(running, last)
    blocks = {}
    for part in running:
        blocks.update(part.finish(last))
    low = blocks["both"].shape[0] // 2

    def ungrouped(block, starts, share):
        pieces = jnp.split(block, len(starts), axis=1)
        cuts = [share * n - start for n, start in enumerate(starts)]
        return jnp.concatenate([p[c : c + share] for p, c in zip(pieces, cuts)])

    down_part = jnp.concatenate([blocks["down"], blocks["both"][:low]])
    down_share = width // seq_count
    down_starts, _ = row_cover(down_share, cell_count // seq_count)
    down_part = ungrouped(down_part, down_starts, down_share // len(down_starts))
    up_part = jnp.concatenate([blocks["up"], blocks["both"][low:]])
    mix_part = jnp.concatenate(
        [
            jnp.concatenate([blocks[g + " upper"], blocks[g + " lower"]])
            for g in ("first", "second")
        ],
        axis=1,
    )
    mix_part = mix_columns(
        scalars[0],
        gathered_blocks(mix_part.astype(jnp.bfloat16), seq_count),
        heads_here,
        head_size,
    )
    group = blocks["out"].shape[0]
    out_part = ungrouped(blocks["out"], [group * n for n in range(seq_count)], group)
    bias_backs = [
        sums.reshape(3, count, HEAD_PAD)[..., :head_size]
        for sums, (_, count, _) in zip(bias_backs, groups)
    ]
    bias_back = jnp.concatenate(bias_backs, axis=1)

    def all_heads(array):
        wide = jnp.zeros((head_total * head_size,), jnp.float32)
        wide = lax.dynamic_update_slice(
            wide, array.reshape(-1), (me[0] * heads_here * head_size,)
        )
        return wide[:width]

    query_bias_back, value_bias_back = all_heads(bias_back[0]), all_heads(bias_back[2])
    def own_rows_of(part, unit=16):
        starts, _ = row_cover(width, cell_count, unit)
        share = width // cell_count
        shift = jnp.array([share * c - starts[c] for c in range(cell_count)])[me[1]]
        return lax.dynamic_slice_in_dim(part, shift, share, axis=0)

    vectors = (
        first_sums[0],
        first_sums[1],
        query_bias_back,
        value_bias_back,
        middle_sums[2],
        middle_sums[0],
        middle_sums[1],
        up_bias_back.reshape(-1),
        middle_sums[3],
    )
    joined = jnp.concatenate([v.reshape(cell_count, -1) for v in vectors], axis=1)
    joined = joined[jnp.arange(cell_count) ^ me[1]]
    names = [("cells", b) for b in reversed(bits_of(cell_count))]
    joined = joined.reshape((2,) * len(names) + joined.shape[1:])
    for axis, bit in list(names):
        place = names.index((axis, bit))
        got = swap_with(lax.index_in_dim(joined, 1, place, keepdims=False), axis, bit)
        joined = lax.index_in_dim(joined, 0, place, keepdims=False) + got
        names.remove((axis, bit))
    for bit in bits_of(seq_count):
        joined = joined + swap_with(joined, "seq", bit)
    ends = [0]
    for v in vectors:
        ends.append(ends[-1] + v.shape[0] // cell_count)
    vectors = [joined[ends[i] : ends[i + 1]] for i in range(len(vectors))]
    matrices = (
        own_rows_of(mix_part),
        own_rows_of(out_part, 16 * seq_count),
        own_rows_of(up_part),
        down_part.T,
    )
    return (
        block_out.transpose(0, 2, 1),
        tokens_gradient.transpose(0, 2, 1),
        vectors[0],
        vectors[1],
        matrices[0],
        vectors[2],
        vectors[3],
        matrices[1],
        vectors[4],
        vectors[5],
        vectors[6],
        matrices[2],
        vectors[7],
        matrices[3],
        vectors[8],
    )


def solution(mesh):
    return jax.shard_map(
        on_device,
        mesh=mesh,
        in_specs=(
            P("cells", "seq", None),
            P(),
            P(),
            P(),
            P(),
            P(),
            P(),
            P(),
            P(),
            P(),
            P(),
            P(),
            P(),
            P(),
            P("cells", "seq", None),
            P("cells"),
            P("cells"),
            P("cells", "seq"),
        ),
        out_specs=(
            P("cells", "seq", None),
            P("cells", "seq", None),
            P("cells"),
            P("cells"),
            P("cells", "seq"),
            P("cells"),
            P("cells"),
            P("cells", "seq"),
            P("cells"),
            P("cells"),
            P("cells"),
            P("cells", "seq"),
            P("cells"),
            P("cells", "seq"),
            P("cells"),
        ),
        check_vma=False,
    )
```

time: 958 us -> 462 us (0.48)
  blocking collectives: 520 us -> 0 us
  Pallas kernels: 0 us -> 293 us
  matrix products: 224 us -> 0 us
  other arithmetic: 74.7 us -> 10.3 us
  starting transfers between devices: 8.8 us -> 48.5 us
  between operations: 17.4 us -> 5.64 us
    unnamed x2 -> x0, blocking collectives: 503 us -> none
    pallas_call x0 -> x42, Pallas kernels: none -> 293 us  [the longest x15 134 us: no_grid_call(): pl.pallas_call(body, out_shape=out_shape, in_specs=in_specs, out_specs=ja...]
    dot_general x18 -> x0, matrix products: 224 us -> none  [the longest x1 33.4 us: scores_back(): jnp.einsum('gqhe,gkhe->ghqk', back_heads, values, preferred_element_type=...]
    ppermute x0 -> x52, waiting for transfers between devices: none -> 54.4 us  [swap_with(): return lax.ppermute(array, axis, [(i, i ^ bit) for i in range(count)])]
    ppermute x0 -> x52, starting transfers between devices: none -> 48.5 us  [swap_with(): return lax.ppermute(array, axis, [(i, i ^ bit) for i in range(count)])]
    convert_element_type x13 -> x0, other arithmetic: 46.7 us -> none  [the longest x1 34.1 us: attend_backward(): back_scores = (probs * (back_probs - centre)).astype(jnp.bfloat16)]
    all_gather x2 -> x0, waiting for transfers between devices: 28.8 us -> none  [the longest x1 28.7 us: on_device(): lax.all_gather(keys_low, 'seq', axis=1, tiled=True)]
    unnamed x133 -> x147, local copies, waits for them, and re-layouts: 45.3 us -> 18.1 us
  transfers between devices with their start and end apart: 12 -> 52, of which waited for: 3 -> 13; matrix products, arithmetic and copies ran while one was open for 75% -> 6% of each run, Pallas kernels for 0% -> 45%
where the time goes in v2:
time: 462 us; the launch traced here: 454 us
  Pallas kernels  293 us (63%)
  waiting for transfers between devices  54.4 us (12%)
  starting transfers between devices  48.5 us (10%)
  local copies, waits for them, and re-layouts  42.3 us (9%)
  other arithmetic  10.3 us (2%)
  between operations  5.64 us (1%)
    pallas_call x15, Pallas kernels, no_grid_call(): pl.pallas_call(body, out_shape=out_shape, in_specs=in_specs, out_specs=ja...  134 us
    pallas_call x8, Pallas kernels, grid_call(): pl.pallas_call(body, out_shape=out_shape, grid_spec=pltpu.PrefetchScalarG...  106 us
    ppermute x52, waiting for transfers between devices, swap_with(): return lax.ppermute(array, axis, [(i, i ^ bit) for i in range(count)])  54.4 us
    pallas_call x19, Pallas kernels, add_halves(): pl.pallas_call(partial(add_halves_kernel, len(pairs)), out_shape=(shape,...  53.2 us
    ppermute x52, starting transfers between devices, swap_with(): return lax.ppermute(array, axis, [(i, i ^ bit) for i in range(count)])  48.5 us
    unnamed x147, local copies, waits for them, and re-layouts  18.1 us
  transfers between devices with their start and end apart: 52, of which 13 were waited for; matrix products, arithmetic and copies ran while one was open for 6% of the time, Pallas kernels for 45%

profile of v2, /device:TPU:0, one launch (start us, length us, event | category | flops | bytes accessed | tf_op | source)
XLA Modules:
  0.0 454.4 jit_solution(473393677100498516)
XLA Ops:
  7.5 3.3 first_norm.1
  10.8 2.9 collective-permute-start
  13.8 2.4 pad_maximum_fusion
  18.0 7.5 %own_weights.1 = (bf16[960,1152]{1,0:T(8,128)(2,1)}, bf16[1120,576]{1,0:T(8,128)(2,1)}, bf16[1120,384]{1,0:T(8,128)(2,1)}) custom-call(s32[3]{0:T(128)} %pad_add_fusion.scalars.me, bf16[1120,3360]{1,0:T(8,128)(2,1)} %mix.1), custom_call_target="tpu_custom_call" | custom-call | flops 1 | bytes 1 | tf_op jit(solution)/shard_map/own_weights/pallas_call | solution.py:127
  25.5 1.8 collective-permute-done.refs_2_
  27.3 1.7 collective-permute-start.6
  33.6 12.8 %active_back.1.refs_0_ = f32[512,4480]{1,0:T(8,128)} custom-call(s32[3]{0:T(128)} %pad_add_fusion.scalars.me, bf16[512,1120]{1,0:T(8,128)(2,1)} %bitcast.91, bf16[1120,4480]{1,0:T(8,128)(2,1)} %bitcast.64), custom_call_target="tpu_custom_call" | custom-call | flops 1 | bytes 1 | tf_op jit(solution)/shard_map/active_back/pallas_call | solution.py:676
  46.9 2.4 slice_bitcast_fusion
  50.1 15.5 %attend_forward.2 = (bf16[9,64,1024]{2,1,0:T(8,128)(2,1)}, bf16[6,64,1024]{2,1,0:T(8,128)(2,1)}, f32[5,64,1024]{2,1,0:T(8,128)}, bf16[280,256]{1,0:T(8,128)(2,1)...) custom-call(s32[3]{0:T(128)} %pad_add_fusion.scalars.me, ...), custom_call_target="tpu_custom_call" | custom-call | flops 1 | bytes 1 | tf_op jit(solution)/shard_map/attend_forward/pallas_call | solution.py:127
  69.6 16.2 %attend_forward.3 = (bf16[9,64,1024]{2,1,0:T(8,128)(2,1)}, bf16[6,64,1024]{2,1,0:T(8,128)(2,1)}, f32[5,64,1024]{2,1,0:T(8,128)}, bf16[280,256]{1,0:T(8,128)(2,1)...) custom-call(s32[3]{0:T(128)} %pad_add_fusion.2.scalars, ...), custom_call_target="tpu_custom_call" | custom-call | flops 1 | bytes 1 | tf_op jit(solution)/shard_map/attend_forward/pallas_call | solution.py:127
  90.4 5.2 %second_norm.2 = (f32[1120,256]{1,0:T(8,128)}, bf16[256,1120]{1,0:T(8,128)(2,1)}, bf16[1120,256]{1,0:T(8,128)(2,1)}, bf16[1120,256]{1,0:T(8,128)(2,1)}) custom-call(s32[3]{0:T(128)} %pad_add_fusion.scalars.me, bf16[1120,1120]{1,0:T(8,128)(2,1)} %weight.5, bf16[1120,256]{1,0:T(8,128)(2,1)} %get-tuple-element.476.tokens, f32[8,1120]{1,0:T(8,128)} %stack.52.lines.refs_2_, ...), custom_call_target="tpu_custom_call" | custom-call | flops 1 | bytes 1 | tf_op jit(solution)/shard_map/second_norm/pallas_call | solution.py:127
  96.4 5.2 %second_norm.3 = (f32[1120,256]{1,0:T(8,128)}, bf16[256,1120]{1,0:T(8,128)(2,1)}, bf16[1120,256]{1,0:T(8,128)(2,1)}, bf16[1120,256]{1,0:T(8,128)(2,1)}) custom-call(s32[3]{0:T(128)} %pad_add_fusion.scalars.me, bf16[1120,1120]{1,0:T(8,128)(2,1)} %weight.5, bf16[1120,256]{1,0:T(8,128)(2,1)} %get-tuple-element.475.tokens, f32[8,1120]{1,0:T(8,128)} %stack.52.lines.refs_2_, ...), custom_call_target="tpu_custom_call" | custom-call | flops 1 | bytes 1 | tf_op jit(solution)/shard_map/second_norm/pallas_call | solution.py:127
  101.6 18.1 %hidden_layer.1 = (bf16[512,4480]{1,0:T(8,128)(2,1)}, bf16[512,4480]{1,0:T(8,128)(2,1)}, f32[1,4480]{1,0:T(1,128)}) custom-call(s32[3]{0:T(128)} %pad_add_fusion.scalars.me, f32[512,4480]{1,0:T(8,128)} %active_back.1.refs_0_, bf16[1120,4480]{1,0:T(8,128)(2,1)} %up.1, f32[1,4480]{1,0:T(1,128)} %reshape.110.refs_2_, ...), custom_call_target="tpu_custom_call" | custom-call | flops 1 | bytes 1 | tf_op jit(solution)/shard_map/hidden_layer/pallas_call | solution.py:676
  119.7 10.2 %down_outer.2 = bf16[2,8,144,1120]{3,2,1,0:T(8,128)(2,1)} custom-call(s32[3]{0:T(128)} %pad_add_fusion.scalars.me, bf16[2,1120,256]{2,1,0:T(8,128)(2,1)} %bitcast.66, bf16[512,4480]{1,0:T(8,128)(2,1)} %get-tuple-element.313.right.refs_0_), custom_call_target="tpu_custom_call" | custom-call | flops 1 | bytes 1 | tf_op jit(solution)/shard_map/down_outer/pallas_call | solution.py:676
  130.1 9.8 %up_outer.2 = bf16[2,8,144,1120]{3,2,1,0:T(8,128)(2,1)} custom-call(s32[3]{0:T(128)} %pad_add_fusion.scalars.me, bf16[512,4480]{1,0:T(8,128)(2,1)} %get-tuple-element.288.right.back_upper, bf16[1120,256]{1,0:T(8,128)(2,1)} %get-tuple-element.278.refs_0_, bf16[1120,256]{1,0:T(8,128)(2,1)} %get-tuple-element.279.refs_1_), custom_call_target="tpu_custom_call" | custom-call | flops 1 | bytes 1 | tf_op jit(solution)/shard_map/up_outer/pallas_call | solution.py:676
  139.9 2.3 copy-done.14
  142.2 12.8 %down_outer.3 = (bf16[1,8,96,1120]{3,2,1,0:T(8,128)(2,1)}, bf16[1,8,96,1120]{3,2,1,0:T(8,128)(2,1)}, bf16[2,4,96,1120]{3,2,1,0:T(8,128)(2,1)}, bf16[2,4,96,1120]{3,2,1,0:T(8,128)(2,1)}) custom-call(s32[3]{0:T(128)} %pad_add_fusion.scalars.me, bf16[2,1120,256]{2,1,0:T(8,128)(2,1)} %bitcast.67, bf16[512,4480]{1,0:T(8,128)(2,1)} %get-tuple-element.313.right.refs_0_, ...), custom_call_target="tpu_custom_call" | custom-call | flops 1 | bytes 1 | tf_op jit(solution)/shard_map/down_outer/pallas_call | solution.py:676
  155.4 11.0 %up_outer.3 = (bf16[2,4,96,1120]{3,2,1,0:T(8,128)(2,1)}, bf16[2,4,96,1120]{3,2,1,0:T(8,128)(2,1)}, bf16[2,4,96,1120]{3,2,1,0:T(8,128)(2,1)}, bf16[2,4,96,1120]{3,2,1,0:T(8,128)(2,1)}) custom-call(s32[3]{0:T(128)} %pad_add_fusion.scalars.me, bf16[512,4480]{1,0:T(8,128)(2,1)} %get-tuple-element.288.right.back_upper, ...), custom_call_target="tpu_custom_call", output_to_operand_aliasing={{2}: (5, {}), {3}: (6, {})} | custom-call | flops 1 | bytes 1 | tf_op jit(solution)/shard_map/up_outer/pallas_call | solution.py:676
  169.5 18.3 %middle_back.1 = (f32[1120,512]{1,0:T(8,128)}, bf16[1120,512]{1,0:T(8,128)(2,1)}, f32[8,1120]{1,0:T(8,128)}, bf16[2,5,64,256]{3,2,1,0:T(8,128)(2,1)}, bf16[2,5,6...) custom-call(s32[3]{0:T(128)} %pad_add_fusion.scalars.me, ...), custom_call_target="tpu_custom_call" | custom-call | flops 1 | bytes 1 | tf_op jit(solution)/shard_map/middle_back/pallas_call | solution.py:676
  187.8 8.3 %collective-permute-done.13.refs_1_.refs_3_ = bf16[8,96,1120]{2,1,0:T(8,128)(2,1)S(1)} collective-permute-done((bf16[8,96,1120]{2,1,0:T(8,128)(2,1)}, bf16[8,96,1120]{2,1,0:T(8,128)(2,1)S(1)}, u32[]{:S(2)}, u32[]{:S(2)}) %collective-permute-start.13) | collective-permute-done | bytes 1720352 | tf_op jit(solution)/shard_map/ppermute | solution.py:28
  197.4 4.1 add_halves.19
  201.5 6.2 %out_outer.1 = bf16[4,8,48,1120]{3,2,1,0:T(8,128)(2,1)} custom-call(s32[3]{0:T(128)} %pad_add_fusion.scalars.me, bf16[1120,512]{1,0:T(8,128)(2,1)} %get-tuple-element.297.right, bf16[1120,256]{1,0:T(8,128)(2,1)} %get-tuple-element.298.refs_0_, bf16[1120,256]{1,0:T(8,128)(2,1)} %get-tuple-element.299.refs_1_), custom_call_target="tpu_custom_call" | custom-call | flops 1 | bytes 1 | tf_op jit(solution)/shard_map/out_outer/pallas_call | solution.py:127
  207.7 3.6 fusion.8
  212.9 4.2 add_halves.20
  217.1 4.2 add_halves.21
  221.2 1.7 collective-permute-start.22
  227.3 6.1 %add_halves.22 = (bf16[8,48,1120]{2,1,0:T(8,128)(2,1)}, bf16[8,48,1120]{2,1,0:T(8,128)(2,1)}) custom-call(bf16[16,48,1120]{2,1,0:T(8,128)(2,1)} %bitcast.69, bf16[16,48,1120]{2,1,0:T(8,128)(2,1)} %copy-done.8, bf16[16,48,1120]{2,1,0:T(8,128)(2,1)} %bitcast.70, bf16[16,48,1120]{2,1,0:T(8,128)(2,1)} %copy-done.8), custom_call_target="tpu_custom_call" | custom-call | flops 1 | bytes 1 | tf_op jit(solution)/shard_map/add_halves/pallas_call | solution.py:62
  234.0 12.7 %block_output.1 = bf16[2,1120,256]{2,1,0:T(8,128)(2,1)} custom-call(s32[3]{0:T(128)} %pad_add_fusion.scalars.me, bf16[512,4480]{1,0:T(8,128)(2,1)} %get-tuple-element.313.right.refs_0_, bf16[1120,4480]{1,0:T(8,128)(2,1)} %bitcast.65, f32[8,1120]{1,0:T(8,128)} %stack.52.lines.refs_2_, f32[1120,256]{1,0:T(8,128)} %get-tuple-element.269.refs_0_.refs_3_, ...), custom_call_target="tpu_custom_call" | custom-call | flops 1 | bytes 1 | tf_op jit(solution)/shard_map/block_output/pallas_call | solution.py:676
  247.6 12.6 %attend_backward.4.refs_8_ = bf16[1024,576]{1,0:T(8,128)(2,1)} custom-call(s32[3]{0:T(128)} %pad_add_fusion.scalars.me, bf16[9,64,1024]{2,1,0:T(8,128)(2,1)} %get-tuple-element.325.refs_0_, f32[5,64,1024]{2,1,0:T(8,128)} %get-tuple-element.254.refs_1_, bf16[1,2,5,64,256]{4,3,2,1,0:T(8,128)(2,1)} %bitcast.87, bf16[1,2,5,64,256]{4,3,2,1,0:T(8,128)(2,1)} %bitcast.78, ...), custom_call_target="tpu_custom_call" | custom-call | flops 1 | bytes 1 | tf_op jit(solution)/shard_map/attend_backward/pallas_call | solution.py:127
  260.2 4.7 %collective-permute-done.19.refs_1_.refs_3_ = bf16[8,48,1120]{2,1,0:T(8,128)(2,1)S(1)} collective-permute-done((bf16[8,48,1120]{2,1,0:T(8,128)(2,1)}, bf16[8,48,1120]{2,1,0:T(8,128)(2,1)S(1)}, u32[]{:S(2)}, u32[]{:S(2)}) %collective-permute-start.19) | collective-permute-done | bytes 860192 | tf_op jit(solution)/shard_map/ppermute | solution.py:28
  264.9 2.7 add_halves.23
  267.6 2.4 add_halves.24
  270.0 2.4 add_halves.25
  272.4 3.6 add_halves.26
  276.0 14.1 %attend_backward.5 = (bf16[1024,384]{1,0:T(8,128)(2,1)}, bf16[2,1120,256]{2,1,0:T(8,128)(2,1)}, bf16[2,1120,256]{2,1,0:T(8,128)(2,1)}) custom-call(s32[3]{0:T(128)} %pad_add_fusion.scalars.me, bf16[6,64,1024]{2,1,0:T(8,128)(2,1)} %get-tuple-element.315.refs_0_, f32[5,64,1024]{2,1,0:T(8,128)} %get-tuple-element.254.refs_1_, ...), custom_call_target="tpu_custom_call" | custom-call | flops 1 | bytes 1 | tf_op jit(solution)/shard_map/attend_backward/pallas_call | solution.py:127
  294.2 12.2 %attend_backward.6.refs_9_.refs_8_ = bf16[1024,576]{1,0:T(8,128)(2,1)} custom-call(s32[3]{0:T(128)} %pad_add_fusion.2.scalars, bf16[9,64,1024]{2,1,0:T(8,128)(2,1)} %get-tuple-element.356.refs_0_, f32[5,64,1024]{2,1,0:T(8,128)} %get-tuple-element.259.refs_1_, bf16[1,2,5,64,256]{4,3,2,1,0:T(8,128)(2,1)} %bitcast.89, bf16[1,2,5,64,256]{4,3,2,1,0:T(8,128)(2,1)} %bitcast.80, ...), custom_call_target="tpu_custom_call" | custom-call | flops 1 | bytes 1 | tf_op jit(solution)/shard_map/attend_backward/pallas_call | solution.py:127
  306.4 5.8 %collective-permute-done.26.refs_5_.refs_7_ = bf16[2,96,1120]{2,1,0:T(8,128)(2,1)S(1)} collective-permute-done((bf16[2,96,1120]{2,1,0:T(8,128)(2,1)S(1)}, bf16[2,96,1120]{2,1,0:T(8,128)(2,1)S(1)}, u32[]{:S(2)}, u32[]{:S(2)}) %collective-permute-start.26) | collective-permute-done | bytes 430112 | tf_op jit(solution)/shard_map/ppermute | solution.py:28
  313.6 3.1 add_halves.27
  316.8 2.1 add_halves.28
  319.9 2.7 add_halves.29
  322.6 8.1 %mix_outer.2 = (bf16[4,80,576]{2,1,0:T(8,128)(2,1)}, bf16[4,80,576]{2,1,0:T(8,128)(2,1)}, bf16[4,64,576]{2,1,0:T(8,128)(2,1)}, bf16[4,64,576]{2,1,0:T(8,128)(2,1)}, f32[1,576]{1,0:T(1,128)}) custom-call(s32[3]{0:T(128)} %pad_add_fusion.scalars.me, bf16[1152,256]{1,0:T(8,128)(2,1)} %get-tuple-element.244.refs_0_, ...), custom_call_target="tpu_custom_call" | custom-call | flops 1 | bytes 1 | tf_op jit(solution)/shard_map/mix_outer/pallas_call | solution.py:127
  330.7 14.0 %attend_backward.7 = (bf16[1024,384]{1,0:T(8,128)(2,1)}, bf16[2,1120,256]{2,1,0:T(8,128)(2,1)}, bf16[2,1120,256]{2,1,0:T(8,128)(2,1)}) custom-call(s32[3]{0:T(128)} %pad_add_fusion.2.scalars, bf16[6,64,1024]{2,1,0:T(8,128)(2,1)} %get-tuple-element.378.refs_0_, f32[5,64,1024]{2,1,0:T(8,128)} %get-tuple-element.259.refs_1_, ...), custom_call_target="tpu_custom_call" | custom-call | flops 1 | bytes 1 | tf_op jit(solution)/shard_map/attend_backward/pallas_call | solution.py:127
  346.9 2.6 collective-permute-start.38
  350.1 6.3 %mix_outer.3 = (bf16[4,80,384]{2,1,0:T(8,128)(2,1)}, bf16[4,80,384]{2,1,0:T(8,128)(2,1)}, bf16[4,64,384]{2,1,0:T(8,128)(2,1)}, bf16[4,64,384]{2,1,0:T(8,128)(2,1)}, f32[1,384]{1,0:T(1,128)}) custom-call(s32[3]{0:T(128)} %pad_add_fusion.scalars.me, bf16[1152,256]{1,0:T(8,128)(2,1)} %get-tuple-element.244.refs_0_, ...), custom_call_target="tpu_custom_call" | custom-call | flops 1 | bytes 1 | tf_op jit(solution)/shard_map/mix_outer/pallas_call | solution.py:127
  356.5 14.3 %collective-permute-done.30.refs_1_.refs_3_ = bf16[4,64,576]{2,1,0:T(8,128)(2,1)S(1)} collective-permute-done((bf16[4,64,576]{2,1,0:T(8,128)(2,1)S(1)}, bf16[4,64,576]{2,1,0:T(8,128)(2,1)S(1)}, u32[]{:S(2)}, u32[]{:S(2)}) %collective-permute-start.30) | collective-permute-done | bytes 294944 | tf_op jit(solution)/shard_map/ppermute | solution.py:28
  371.5 1.9 add_halves.30
  373.5 1.9 add_halves.31
  376.4 2.9 add_halves.32
  386.4 2.5 collective-permute-start.35
  389.2 5.9 %collective-permute-done.35.refs_1_.refs_3_ = bf16[2,48,1120]{2,1,0:T(8,128)(2,1)S(1)} collective-permute-done((bf16[2,48,1120]{2,1,0:T(8,128)(2,1)S(1)}, bf16[2,48,1120]{2,1,0:T(8,128)(2,1)S(1)}, u32[]{:S(2)}, u32[]{:S(2)}) %collective-permute-start.35) | collective-permute-done | bytes 215072 | tf_op jit(solution)/shard_map/ppermute | solution.py:28
  395.1 2.1 collective-permute-done.37.refs_1_.refs_3_
  398.9 1.7 collective-permute-start.33
  400.6 1.7 add_halves.33
  406.4 1.9 add_halves.35
  409.2 2.0 add_halves.36
  411.2 2.1 collective-permute-start.46
  414.2 5.9 %tokens_back.1 = (bf16[2,1120,256]{2,1,0:T(8,128)(2,1)}, f32[8,1120]{1,0:T(8,128)}) custom-call(bf16[2,1120,256]{2,1,0:T(8,128)(2,1)} %bitcast.74, f32[8,1120]{1,0:T(8,128)} %stack.52.lines.refs_2_, f32[1120,512]{1,0:T(8,128)} %get-tuple-element.314.back_middle, bf16[1120,256]{1,0:T(8,128)(2,1)} %bitcast.95, bf16[1120,256]{1,0:T(8,128)(2,1)} %bitcast.96, ...), custom_call_target="tpu_custom_call" | custom-call | flops 1 | bytes 1 | tf_op jit(solution)/shard_map/tokens_back/pallas_call | solution.py:127
  420.1 1.8 add_halves.37
  426.1 2.8 collective-permute-done.39
  428.9 2.0 collective-permute-start.40
  432.7 4.7 %collective-permute-done.47 = bf16[1,144,384]{2,1,0:T(8,128)(2,1)S(1)} collective-permute-done((bf16[1,144,384]{2,1,0:T(8,128)(2,1)S(1)}, bf16[1,144,384]{2,1,0:T(8,128)(2,1)S(1)}, u32[]{:S(2)}, u32[]{:S(2)}) %collective-permute-start.47) | collective-permute-done | bytes 110624 | tf_op jit(solution)/shard_map/ppermute | solution.py:28
  440.3 2.2 collective-permute-done.41
  450.1 2.2 mix_columns.1
  452.4 1.9 constant_dynamic-slice_fusion
  (325 shorter events, 74.7 us)
Async XLA Ops:
  10.8 16.5 %collective-permute-start = (bf16[1152,256]{1,0:T(8,128)(2,1)}, bf16[1152,256]{1,0:T(8,128)(2,1)S(1)}, u32[]{:S(2)}, u32[]{:S(2)}) collective-permute-start(bf16[1152,256]{1,0:T(8,128)(2,1)} %get-tuple-element.244.refs_0_), channel_id=1, source_target_pairs={{0,2},{1,3},{2,0},{3,1},{4,6},{5,7},{6,4},{7,5},{8,10},{9,11},{10,... | collective-permute-start | bytes 1769480 | tf_op jit(solution)/shard_map/ppermute | solution.py:28
  16.2 30.8 %collective-permute-start.1 = (bf16[2,1152,256]{2,1,0:T(8,128)(2,1)}, bf16[2,1152,256]{2,1,0:T(8,128)(2,1)}, u32[]{:S(2)}, u32[]{:S(2)}) collective-permute-start(bf16[2,1152,256]{2,1,0:T(8,128)(2,1)} %pad_maximum_fusion), channel_id=1, source_target_pairs={{0,1},{1,0},{2,3},{3,2},{4,5},{5,4},{6,7},{7,6},{8,9},{9,8},{10,11... | collective-permute-start | bytes 3538952 | tf_op jit(solution)/shard_map/ppermute | solution.py:28
  27.3 19.1 %collective-permute-start.6 = (bf16[1152,256]{1,0:T(8,128)(2,1)S(1)}, bf16[1152,256]{1,0:T(8,128)(2,1)S(1)}, u32[]{:S(2)}, u32[]{:S(2)}) collective-permute-start(bf16[1152,256]{1,0:T(8,128)(2,1)S(1)} %copy-done.4), channel_id=1, source_target_pairs={{0,2},{1,3},{2,0},{3,1},{4,6},{5,7},{6,4},{7,5},{8,10},{9,11},{10,... | collective-permute-start | bytes 1769480 | tf_op jit(solution)/shard_map/ppermute | solution.py:28
  30.9 18.4 %collective-permute-start.2 = (bf16[1152,256]{1,0:T(8,128)(2,1)S(1)}, bf16[1152,256]{1,0:T(8,128)(2,1)S(1)}, u32[]{:S(2)}, u32[]{:S(2)}) collective-permute-start(bf16[1152,256]{1,0:T(8,128)(2,1)S(1)} %collective-permute-done.refs_2_), channel_id=1, source_target_pairs={{0,1},{1,0},{2,3},{3,2},{4,5},{5,4},{6,7},{7,6},{8,9},{9,8},{10,11... | collective-permute-start | bytes 1769480 | tf_op jit(solution)/shard_map/ppermute | solution.py:28
  46.4 19.2 %copy-start.11 = (bf16[1152,256]{1,0:T(8,128)(2,1)}, bf16[1152,256]{1,0:T(8,128)(2,1)S(1)}, u32[]{:S(2)}) copy-start(bf16[1152,256]{1,0:T(8,128)(2,1)S(1)} %collective-permute-done.6.refs_2_.refs_6_) | copy-start | bytes 1769476
  46.4 22.3 %collective-permute-start.7 = (bf16[1152,256]{1,0:T(8,128)(2,1)S(1)}, bf16[1152,256]{1,0:T(8,128)(2,1)S(1)}, u32[]{:S(2)}, u32[]{:S(2)}) collective-permute-start(bf16[1152,256]{1,0:T(8,128)(2,1)S(1)} %collective-permute-done.6.refs_2_.refs_6_), channel_id=1, source_target_pairs={{0,1},{1,0},{2,3},{3,2},{4,5},{5,4},{6,7},{7,6},{8,9},{9,8},{10,11... | collective-permute-start | bytes 1769480 | tf_op jit(solution)/shard_map/ppermute | solution.py:28
  65.6 20.8 %collective-permute-start.3 = (bf16[280,256]{1,0:T(8,128)(2,1)}, bf16[280,256]{1,0:T(8,128)(2,1)S(1)}, u32[]{:S(2)}, u32[]{:S(2)}) collective-permute-start(bf16[280,256]{1,0:T(8,128)(2,1)} %get-tuple-element.249), channel_id=1, source_target_pairs={{0,1},{1,0},{2,3},{3,2},{4,5},{5,4},{6,7},{7,6},{8,9},{9,8},{10,11... | collective-permute-start | bytes 430088 | tf_op jit(solution)/shard_map/ppermute | solution.py:28
  67.1 22.6 %collective-permute-start.4 = (bf16[280,256]{1,0:T(8,128)(2,1)}, bf16[280,256]{1,0:T(8,128)(2,1)S(1)}, u32[]{:S(2)}, u32[]{:S(2)}) collective-permute-start(bf16[280,256]{1,0:T(8,128)(2,1)} %get-tuple-element.250), channel_id=1, source_target_pairs={{0,2},{1,3},{2,0},{3,1},{4,6},{5,7},{6,4},{7,5},{8,10},{9,11},{10,... | collective-permute-start | bytes 430088 | tf_op jit(solution)/shard_map/ppermute | solution.py:28
  67.4 22.4 %collective-permute-start.5 = (bf16[280,256]{1,0:T(8,128)(2,1)}, bf16[280,256]{1,0:T(8,128)(2,1)S(1)}, u32[]{:S(2)}, u32[]{:S(2)}) collective-permute-start(bf16[280,256]{1,0:T(8,128)(2,1)} %get-tuple-element.251), channel_id=1, source_target_pairs={{0,3},{1,2},{2,1},{3,0},{4,7},{5,6},{6,5},{7,4},{8,11},{9,10},{10,... | collective-permute-start | bytes 430088 | tf_op jit(solution)/shard_map/ppermute | solution.py:28
  69.6 18.5 %copy-start.3 = (bf16[2,256,1120]{1,2,0:T(8,128)(2,1)S(1)}, bf16[2,256,1120]{1,2,0:T(8,128)(2,1)}, u32[]{:S(2)}) copy-start(bf16[2,256,1120]{1,2,0:T(8,128)(2,1)} %param.24) | copy-start | bytes 3440644
  85.8 9.9 %collective-permute-start.10 = (bf16[280,256]{1,0:T(8,128)(2,1)}, bf16[280,256]{1,0:T(8,128)(2,1)S(1)}, u32[]{:S(2)}, u32[]{:S(2)}) collective-permute-start(bf16[280,256]{1,0:T(8,128)(2,1)} %get-tuple-element.268), channel_id=1, source_target_pairs={{0,3},{1,2},{2,1},{3,0},{4,7},{5,6},{6,5},{7,4},{8,11},{9,10},{10,... | collective-permute-start | bytes 430088 | tf_op jit(solution)/shard_map/ppermute | solution.py:28
  86.2 9.5 %collective-permute-start.8 = (bf16[280,256]{1,0:T(8,128)(2,1)}, bf16[280,256]{1,0:T(8,128)(2,1)S(1)}, u32[]{:S(2)}, u32[]{:S(2)}) collective-permute-start(bf16[280,256]{1,0:T(8,128)(2,1)} %get-tuple-element.266), channel_id=1, source_target_pairs={{0,1},{1,0},{2,3},{3,2},{4,5},{5,4},{6,7},{7,6},{8,9},{9,8},{10,11... | collective-permute-start | bytes 430088 | tf_op jit(solution)/shard_map/ppermute | solution.py:28
  86.4 9.2 %collective-permute-start.9 = (bf16[280,256]{1,0:T(8,128)(2,1)}, bf16[280,256]{1,0:T(8,128)(2,1)S(1)}, u32[]{:S(2)}, u32[]{:S(2)}) collective-permute-start(bf16[280,256]{1,0:T(8,128)(2,1)} %get-tuple-element.267), channel_id=1, source_target_pairs={{0,2},{1,3},{2,0},{3,1},{4,6},{5,7},{6,4},{7,5},{8,10},{9,11},{10,... | collective-permute-start | bytes 430088 | tf_op jit(solution)/shard_map/ppermute | solution.py:28
  129.9 10.0 %collective-permute-start.11 = (bf16[2,8,144,1120]{3,2,1,0:T(8,128)(2,1)}, bf16[2,8,144,1120]{3,2,1,0:T(8,128)(2,1)S(1)}, u32[]{:S(2)}, u32[]{:S(2)}) collective-permute-start(bf16[2,8,144,1120]{3,2,1,0:T(8,128)(2,1)} %down_outer.2), channel_id=1, source_target_pairs={{0,1},{1,0},{2,3},{3,2},{4,5},{5,4},{6,7},{7,6},{8,9},{9,8},{10,11... | collective-permute-start | bytes 15482888 | tf_op jit(solution)/shard_map/ppermute | solution.py:28
  139.9 15.5 %collective-permute-start.12 = (bf16[2,8,144,1120]{3,2,1,0:T(8,128)(2,1)}, bf16[2,8,144,1120]{3,2,1,0:T(8,128)(2,1)}, u32[]{:S(2)}, u32[]{:S(2)}) collective-permute-start(bf16[2,8,144,1120]{3,2,1,0:T(8,128)(2,1)} %up_outer.2), channel_id=1, source_target_pairs={{0,1},{1,0},{2,3},{3,2},{4,5},{5,4},{6,7},{7,6},{8,9},{9,8},{10,11... | collective-permute-start | bytes 15482888 | tf_op jit(solution)/shard_map/ppermute | solution.py:28
  154.9 41.2 %collective-permute-start.13 = (bf16[8,96,1120]{2,1,0:T(8,128)(2,1)}, bf16[8,96,1120]{2,1,0:T(8,128)(2,1)S(1)}, u32[]{:S(2)}, u32[]{:S(2)}) collective-permute-start(bf16[8,96,1120]{2,1,0:T(8,128)(2,1)} %bitcast.102), channel_id=1, source_target_pairs={{0,2},{1,3},{2,0},{3,1},{4,6},{5,7},{6,4},{7,5},{8,10},{9,11},{10,... | collective-permute-start | bytes 5160968 | tf_op jit(solution)/shard_map/ppermute | solution.py:28
  166.3 45.3 %collective-permute-start.15 = (bf16[8,96,1120]{2,1,0:T(8,128)(2,1)}, bf16[8,96,1120]{2,1,0:T(8,128)(2,1)S(1)}, u32[]{:S(2)}, u32[]{:S(2)}) collective-permute-start(bf16[8,96,1120]{2,1,0:T(8,128)(2,1)} %bitcast.93), channel_id=1, source_target_pairs={{0,8},{4,12},{8,0},{12,4},{16,24},{20,28},{24,16},{28,20},{1,9},{5... | collective-permute-start | bytes 5160968 | tf_op jit(solution)/shard_map/ppermute | solution.py:28
  168.0 43.6 %collective-permute-start.16 = (bf16[8,96,1120]{2,1,0:T(8,128)(2,1)}, bf16[8,96,1120]{2,1,0:T(8,128)(2,1)S(1)}, u32[]{:S(2)}, u32[]{:S(2)}) collective-permute-start(bf16[8,96,1120]{2,1,0:T(8,128)(2,1)} %bitcast.101), channel_id=1, source_target_pairs={{0,4},{4,0},{8,12},{12,8},{16,20},{20,16},{24,28},{28,24},{1,5},{5... | collective-permute-start | bytes 5160968 | tf_op jit(solution)/shard_map/ppermute | solution.py:28
  211.3 14.8 %collective-permute-start.14 = (bf16[16,48,1120]{2,1,0:T(8,128)(2,1)S(1)}, bf16[16,48,1120]{2,1,0:T(8,128)(2,1)S(1)}, u32[]{:S(2)}, u32[]{:S(2)}) collective-permute-start(bf16[16,48,1120]{2,1,0:T(8,128)(2,1)S(1)} %bitcast.92), channel_id=1, source_target_pairs={{0,1},{1,0},{2,3},{3,2},{4,5},{5,4},{6,7},{7,6},{8,9},{9,8},{10,11... | collective-permute-start | bytes 5160968 | tf_op jit(solution)/shard_map/ppermute | solution.py:28
  211.3 22.5 %collective-permute-start.17 = (bf16[2,2,5,64,256]{4,3,2,1,0:T(8,128)(2,1)}, bf16[2,2,5,64,256]{4,3,2,1,0:T(8,128)(2,1)S(1)}, u32[]{:S(2)}, u32[]{:S(2)}) collective-permute-start(bf16[2,2,5,64,256]{4,3,2,1,0:T(8,128)(2,1)} %get-tuple-element.293), channel_id=1, source_target_pairs={{0,2},{1,3},{2,0},{3,1},{4,6},{5,7},{6,4},{7,5},{8,10},{9,11},{10,... | collective-permute-start | bytes 1966088 | tf_op jit(solution)/shard_map/ppermute | solution.py:28
  221.2 38.9 %collective-permute-start.22 = (bf16[4,96,1120]{2,1,0:T(8,128)(2,1)}, bf16[4,96,1120]{2,1,0:T(8,128)(2,1)S(1)}, u32[]{:S(2)}, u32[]{:S(2)}) collective-permute-start(bf16[4,96,1120]{2,1,0:T(8,128)(2,1)} %get-tuple-element.320), channel_id=1, source_target_pairs={{0,2},{1,3},{2,0},{3,1},{4,6},{5,7},{6,4},{7,5},{8,10},{9,11},{10,... | collective-permute-start | bytes 2580488 | tf_op jit(solution)/shard_map/ppermute | solution.py:28
  223.0 37.2 %collective-permute-start.21 = (bf16[4,96,1120]{2,1,0:T(8,128)(2,1)}, bf16[4,96,1120]{2,1,0:T(8,128)(2,1)S(1)}, u32[]{:S(2)}, u32[]{:S(2)}) collective-permute-start(bf16[4,96,1120]{2,1,0:T(8,128)(2,1)} %get-tuple-element.319), channel_id=1, source_target_pairs={{0,8},{4,12},{8,0},{12,4},{16,24},{20,28},{24,16},{28,20},{1,9},{5... | collective-permute-start | bytes 2580488 | tf_op jit(solution)/shard_map/ppermute | solution.py:28
  224.5 35.7 %collective-permute-start.20 = (bf16[4,96,1120]{2,1,0:T(8,128)(2,1)}, bf16[4,96,1120]{2,1,0:T(8,128)(2,1)S(1)}, u32[]{:S(2)}, u32[]{:S(2)}) collective-permute-start(bf16[4,96,1120]{2,1,0:T(8,128)(2,1)} %get-tuple-element.318), channel_id=1, source_target_pairs={{0,4},{4,0},{8,12},{12,8},{16,20},{20,16},{24,28},{28,24},{1,5},{5... | collective-permute-start | bytes 2580488 | tf_op jit(solution)/shard_map/ppermute | solution.py:28
  233.3 31.6 %collective-permute-start.19 = (bf16[8,48,1120]{2,1,0:T(8,128)(2,1)}, bf16[8,48,1120]{2,1,0:T(8,128)(2,1)S(1)}, u32[]{:S(2)}, u32[]{:S(2)}) collective-permute-start(bf16[8,48,1120]{2,1,0:T(8,128)(2,1)} %get-tuple-element.317), channel_id=1, source_target_pairs={{0,4},{4,0},{8,12},{12,8},{16,20},{20,16},{24,28},{28,24},{1,5},{5... | collective-permute-start | bytes 2580488 | tf_op jit(solution)/shard_map/ppermute | solution.py:28
  233.9 12.8 %collective-permute-start.18 = (bf16[2,2,5,64,256]{4,3,2,1,0:T(8,128)(2,1)S(1)}, bf16[2,2,5,64,256]{4,3,2,1,0:T(8,128)(2,1)S(1)}, u32[]{:S(2)}, u32[]{:S(2)}) collective-permute-start(bf16[2,2,5,64,256]{4,3,2,1,0:T(8,128)(2,1)S(1)} %pad_maximum_fusion.2), channel_id=1, source_target_pairs={{0,1},{1,0},{2,3},{3,2},{4,5},{5,4},{6,7},{7,6},{8,9},{9,8},{10,11... | collective-permute-start | bytes 1966088 | tf_op jit(solution)/shard_map/ppermute | solution.py:28
  276.0 14.1 %copy-start.62 = (bf16[4,48,1120]{2,1,0:T(8,128)(2,1)S(1)}, bf16[4,48,1120]{2,1,0:T(8,128)(2,1)}, u32[]{:S(2)}) copy-start(bf16[4,48,1120]{2,1,0:T(8,128)(2,1)} %get-tuple-element.350) | copy-start | bytes 1290244
  276.0 14.7 %copy-start.61 = (bf16[2,96,1120]{2,1,0:T(8,128)(2,1)S(1)}, bf16[2,96,1120]{2,1,0:T(8,128)(2,1)}, u32[]{:S(2)}) copy-start(bf16[2,96,1120]{2,1,0:T(8,128)(2,1)} %get-tuple-element.353) | copy-start | bytes 1290244
  276.0 16.2 %copy-start.60 = (bf16[2,96,1120]{2,1,0:T(8,128)(2,1)S(1)}, bf16[2,96,1120]{2,1,0:T(8,128)(2,1)}, u32[]{:S(2)}) copy-start(bf16[2,96,1120]{2,1,0:T(8,128)(2,1)} %get-tuple-element.352) | copy-start | bytes 1290244
  276.0 17.7 %copy-start.59 = (bf16[2,96,1120]{2,1,0:T(8,128)(2,1)S(1)}, bf16[2,96,1120]{2,1,0:T(8,128)(2,1)}, u32[]{:S(2)}) copy-start(bf16[2,96,1120]{2,1,0:T(8,128)(2,1)} %get-tuple-element.351) | copy-start | bytes 1290244
  290.1 28.8 %collective-permute-start.23 = (bf16[2,1120,256]{2,1,0:T(8,128)(2,1)}, bf16[2,1120,256]{2,1,0:T(8,128)(2,1)S(1)}, u32[]{:S(2)}, u32[]{:S(2)}) collective-permute-start(bf16[2,1120,256]{2,1,0:T(8,128)(2,1)} %get-tuple-element.349), channel_id=1, source_target_pairs={{0,1},{1,0},{2,3},{3,2},{4,5},{5,4},{6,7},{7,6},{8,9},{9,8},{10,11... | collective-permute-start | bytes 3440648 | tf_op jit(solution)/shard_map/ppermute | solution.py:28
  290.1 16.3 %collective-permute-start.24 = (bf16[4,48,1120]{2,1,0:T(8,128)(2,1)S(1)}, bf16[4,48,1120]{2,1,0:T(8,128)(2,1)S(1)}, u32[]{:S(2)}, u32[]{:S(2)}) collective-permute-start(bf16[4,48,1120]{2,1,0:T(8,128)(2,1)S(1)} %copy-done.62), channel_id=1, source_target_pairs={{0,2},{1,3},{2,0},{3,1},{4,6},{5,7},{6,4},{7,5},{8,10},{9,11},{10,... | collective-permute-start | bytes 1290248 | tf_op jit(solution)/shard_map/ppermute | solution.py:28
  290.6 15.7 %collective-permute-start.27 = (bf16[2,96,1120]{2,1,0:T(8,128)(2,1)S(1)}, bf16[2,96,1120]{2,1,0:T(8,128)(2,1)S(1)}, u32[]{:S(2)}, u32[]{:S(2)}) collective-permute-start(bf16[2,96,1120]{2,1,0:T(8,128)(2,1)S(1)} %copy-done.61), channel_id=1, source_target_pairs={{0,4},{4,0},{8,12},{12,8},{16,20},{20,16},{24,28},{28,24},{1,5},{5... | collective-permute-start | bytes 1290248 | tf_op jit(solution)/shard_map/ppermute | solution.py:28
  292.2 19.9 %collective-permute-start.26 = (bf16[2,96,1120]{2,1,0:T(8,128)(2,1)S(1)}, bf16[2,96,1120]{2,1,0:T(8,128)(2,1)S(1)}, u32[]{:S(2)}, u32[]{:S(2)}) collective-permute-start(bf16[2,96,1120]{2,1,0:T(8,128)(2,1)S(1)} %copy-done.60), channel_id=1, source_target_pairs={{0,2},{1,3},{2,0},{3,1},{4,6},{5,7},{6,4},{7,5},{8,10},{9,11},{10,... | collective-permute-start | bytes 1290248 | tf_op jit(solution)/shard_map/ppermute | solution.py:28
  293.7 18.4 %collective-permute-start.25 = (bf16[2,96,1120]{2,1,0:T(8,128)(2,1)S(1)}, bf16[2,96,1120]{2,1,0:T(8,128)(2,1)S(1)}, u32[]{:S(2)}, u32[]{:S(2)}) collective-permute-start(bf16[2,96,1120]{2,1,0:T(8,128)(2,1)S(1)} %copy-done.59), channel_id=1, source_target_pairs={{0,8},{4,12},{8,0},{12,4},{16,24},{20,28},{24,16},{28,20},{1,9},{5... | collective-permute-start | bytes 1290248 | tf_op jit(solution)/shard_map/ppermute | solution.py:28
  330.7 14.6 %copy-start.63 = (bf16[4,80,576]{2,1,0:T(8,128)(2,1)S(1)}, bf16[4,80,576]{2,1,0:T(8,128)(2,1)}, u32[]{:S(2)}) copy-start(bf16[4,80,576]{2,1,0:T(8,128)(2,1)} %get-tuple-element.381) | copy-start | bytes 1105924
  330.7 16.1 %copy-start.57 = (bf16[1,288,1120]{2,1,0:T(8,128)(2,1)S(1)}, bf16[1,288,1120]{2,1,0:T(8,128)(2,1)}, u32[]{:S(2)}) copy-start(bf16[1,288,1120]{2,1,0:T(8,128)(2,1)} %get-tuple-element.417) | copy-start | bytes 1935364
  330.7 18.7 %copy-start.64 = (bf16[4,64,576]{2,1,0:T(8,128)(2,1)S(1)}, bf16[4,64,576]{2,1,0:T(8,128)(2,1)}, u32[]{:S(2)}) copy-start(bf16[4,64,576]{2,1,0:T(8,128)(2,1)} %get-tuple-element.389) | copy-start | bytes 884740
  344.8 30.6 %collective-permute-start.29 = (bf16[2,1120,256]{2,1,0:T(8,128)(2,1)}, bf16[2,1120,256]{2,1,0:T(8,128)(2,1)S(1)}, u32[]{:S(2)}, u32[]{:S(2)}) collective-permute-start(bf16[2,1120,256]{2,1,0:T(8,128)(2,1)} %get-tuple-element.387), channel_id=1, source_target_pairs={{0,1},{1,0},{2,3},{3,2},{4,5},{5,4},{6,7},{7,6},{8,9},{9,8},{10,11... | collective-permute-start | bytes 3440648 | tf_op jit(solution)/shard_map/ppermute | solution.py:28
  344.8 26.0 %collective-permute-start.28 = (bf16[1,1120,256]{2,1,0:T(8,128)(2,1)S(1)}, bf16[1,1120,256]{2,1,0:T(8,128)(2,1)S(1)}, u32[]{:S(2)}, u32[]{:S(2)}) collective-permute-start(bf16[1,1120,256]{2,1,0:T(8,128)(2,1)S(1)} %copy-done.58), channel_id=1, source_target_pairs={{0,2},{1,3},{2,0},{3,1},{4,6},{5,7},{6,4},{7,5},{8,10},{9,11},{10,... | collective-permute-start | bytes 1720328 | tf_op jit(solution)/shard_map/ppermute | solution.py:28
  345.3 25.4 %collective-permute-start.31 = (bf16[4,80,576]{2,1,0:T(8,128)(2,1)S(1)}, bf16[4,80,576]{2,1,0:T(8,128)(2,1)S(1)}, u32[]{:S(2)}, u32[]{:S(2)}) collective-permute-start(bf16[4,80,576]{2,1,0:T(8,128)(2,1)S(1)} %copy-done.63), channel_id=1, source_target_pairs={{0,4},{4,0},{8,12},{12,8},{16,20},{20,16},{24,28},{28,24},{1,5},{5... | collective-permute-start | bytes 1105928 | tf_op jit(solution)/shard_map/ppermute | solution.py:28
  346.9 53.8 %collective-permute-start.38 = (bf16[1,288,1120]{2,1,0:T(8,128)(2,1)S(1)}, bf16[1,288,1120]{2,1,0:T(8,128)(2,1)S(1)}, u32[]{:S(2)}, u32[]{:S(2)}) collective-permute-start(bf16[1,288,1120]{2,1,0:T(8,128)(2,1)S(1)} %copy-done.57), channel_id=1, source_target_pairs={{0,16},{4,20},{8,24},{12,28},{16,0},{20,4},{24,8},{28,12},{1,17},{... | collective-permute-start | bytes 1935368 | tf_op jit(solution)/shard_map/ppermute | solution.py:28
  349.4 21.3 %collective-permute-start.30 = (bf16[4,64,576]{2,1,0:T(8,128)(2,1)S(1)}, bf16[4,64,576]{2,1,0:T(8,128)(2,1)S(1)}, u32[]{:S(2)}, u32[]{:S(2)}) collective-permute-start(bf16[4,64,576]{2,1,0:T(8,128)(2,1)S(1)} %copy-done.64), channel_id=1, source_target_pairs={{0,8},{4,12},{8,0},{12,4},{16,24},{20,28},{24,16},{28,20},{1,9},{5... | collective-permute-start | bytes 884744 | tf_op jit(solution)/shard_map/ppermute | solution.py:28
  376.4 26.2 %copy-start.52 = (f32[8,1120]{1,0:T(8,128)S(1)}, f32[8,1120]{1,0:T(8,128)}, u32[]{:S(2)}) copy-start(f32[8,1120]{1,0:T(8,128)} %get-tuple-element.441) | copy-start | bytes 107524
  376.4 26.6 %copy-start.55 = (f32[1,384]{1,0:T(1,128)S(1)}, f32[1,384]{1,0:T(1,128)}, u32[]{:S(2)}) copy-start(f32[1,384]{1,0:T(1,128)} %get-tuple-element.440) | copy-start | bytes 4612
  376.4 26.7 %copy-start.53 = (f32[1,576]{1,0:T(1,128)S(1)}, f32[1,576]{1,0:T(1,128)}, u32[]{:S(2)}) copy-start(f32[1,576]{1,0:T(1,128)} %get-tuple-element.439) | copy-start | bytes 6916
  379.3 34.0 %collective-permute-start.32 = (bf16[1,1120,256]{2,1,0:T(8,128)(2,1)}, bf16[1,1120,256]{2,1,0:T(8,128)(2,1)S(1)}, u32[]{:S(2)}, u32[]{:S(2)}) collective-permute-start(bf16[1,1120,256]{2,1,0:T(8,128)(2,1)} %get-tuple-element.406), channel_id=1, source_target_pairs={{0,2},{1,3},{2,0},{3,1},{4,6},{5,7},{6,4},{7,5},{8,10},{9,11},{10,... | collective-permute-start | bytes 1720328 | tf_op jit(solution)/shard_map/ppermute | solution.py:28
  380.8 16.4 %collective-permute-start.36 = (bf16[4,80,384]{2,1,0:T(8,128)(2,1)S(1)}, bf16[4,80,384]{2,1,0:T(8,128)(2,1)S(1)}, u32[]{:S(2)}, u32[]{:S(2)}) collective-permute-start(bf16[4,80,384]{2,1,0:T(8,128)(2,1)S(1)} %copy-done.65), channel_id=1, source_target_pairs={{0,4},{4,0},{8,12},{12,8},{16,20},{20,16},{24,28},{28,24},{1,5},{5... | collective-permute-start | bytes 737288 | tf_op jit(solution)/shard_map/ppermute | solution.py:28
  386.4 8.7 %collective-permute-start.35 = (bf16[2,48,1120]{2,1,0:T(8,128)(2,1)S(1)}, bf16[2,48,1120]{2,1,0:T(8,128)(2,1)S(1)}, u32[]{:S(2)}, u32[]{:S(2)}) collective-permute-start(bf16[2,48,1120]{2,1,0:T(8,128)(2,1)S(1)} %copy-done.66), channel_id=1, source_target_pairs={{0,8},{4,12},{8,0},{12,4},{16,24},{20,28},{24,16},{28,20},{1,9},{5... | collective-permute-start | bytes 645128 | tf_op jit(solution)/shard_map/ppermute | solution.py:28
  388.9 8.3 %collective-permute-start.37 = (bf16[4,64,384]{2,1,0:T(8,128)(2,1)S(1)}, bf16[4,64,384]{2,1,0:T(8,128)(2,1)S(1)}, u32[]{:S(2)}, u32[]{:S(2)}) collective-permute-start(bf16[4,64,384]{2,1,0:T(8,128)(2,1)S(1)} %copy-done.67), channel_id=1, source_target_pairs={{0,8},{4,12},{8,0},{12,4},{16,24},{20,28},{24,16},{28,20},{1,9},{5... | collective-permute-start | bytes 589832 | tf_op jit(solution)/shard_map/ppermute | solution.py:28
  397.2 9.2 %collective-permute-start.34 = (bf16[2,64,576]{2,1,0:T(8,128)(2,1)}, bf16[2,64,576]{2,1,0:T(8,128)(2,1)S(1)}, u32[]{:S(2)}, u32[]{:S(2)}) collective-permute-start(bf16[2,64,576]{2,1,0:T(8,128)(2,1)} %get-tuple-element.408), channel_id=1, source_target_pairs={{0,4},{4,0},{8,12},{12,8},{16,20},{20,16},{24,28},{28,24},{1,5},{5... | collective-permute-start | bytes 442376 | tf_op jit(solution)/shard_map/ppermute | solution.py:28
  398.9 7.5 %collective-permute-start.33 = (bf16[2,80,576]{2,1,0:T(8,128)(2,1)}, bf16[2,80,576]{2,1,0:T(8,128)(2,1)S(1)}, u32[]{:S(2)}, u32[]{:S(2)}) collective-permute-start(bf16[2,80,576]{2,1,0:T(8,128)(2,1)} %get-tuple-element.407), channel_id=1, source_target_pairs={{0,8},{4,12},{8,0},{12,4},{16,24},{20,28},{24,16},{28,20},{1,9},{5... | collective-permute-start | bytes 552968 | tf_op jit(solution)/shard_map/ppermute | solution.py:28
  402.3 10.9 %collective-permute-start.44 = (bf16[2,80,384]{2,1,0:T(8,128)(2,1)}, bf16[2,80,384]{2,1,0:T(8,128)(2,1)S(1)}, u32[]{:S(2)}, u32[]{:S(2)}) collective-permute-start(bf16[2,80,384]{2,1,0:T(8,128)(2,1)} %get-tuple-element.443), channel_id=1, source_target_pairs={{0,8},{4,12},{8,0},{12,4},{16,24},{20,28},{24,16},{28,20},{1,9},{5... | collective-permute-start | bytes 368648 | tf_op jit(solution)/shard_map/ppermute | solution.py:28
  404.9 8.4 %collective-permute-start.45 = (bf16[2,64,384]{2,1,0:T(8,128)(2,1)}, bf16[2,64,384]{2,1,0:T(8,128)(2,1)S(1)}, u32[]{:S(2)}, u32[]{:S(2)}) collective-permute-start(bf16[2,64,384]{2,1,0:T(8,128)(2,1)} %get-tuple-element.444), channel_id=1, source_target_pairs={{0,4},{4,0},{8,12},{12,8},{16,20},{20,16},{24,28},{28,24},{1,5},{5... | collective-permute-start | bytes 294920 | tf_op jit(solution)/shard_map/ppermute | solution.py:28
  408.3 17.5 %collective-permute-start.51 = (bf16[1,48,1120]{2,1,0:T(8,128)(2,1)}, bf16[1,48,1120]{2,1,0:T(8,128)(2,1)S(1)}, u32[]{:S(2)}, u32[]{:S(2)}) collective-permute-start(bf16[1,48,1120]{2,1,0:T(8,128)(2,1)} %get-tuple-element.457), channel_id=1, source_target_pairs={{0,16},{4,20},{8,24},{12,28},{16,0},{20,4},{24,8},{28,12},{1,17},{... | collective-permute-start | bytes 322568 | tf_op jit(solution)/shard_map/ppermute | solution.py:28
  411.2 14.8 %collective-permute-start.46 = (bf16[1,144,576]{2,1,0:T(8,128)(2,1)}, bf16[1,144,576]{2,1,0:T(8,128)(2,1)S(1)}, u32[]{:S(2)}, u32[]{:S(2)}) collective-permute-start(bf16[1,144,576]{2,1,0:T(8,128)(2,1)} %get-tuple-element.453), channel_id=1, source_target_pairs={{0,16},{4,20},{8,24},{12,28},{16,0},{20,4},{24,8},{28,12},{1,17},{... | collective-permute-start | bytes 497672 | tf_op jit(solution)/shard_map/ppermute | solution.py:28
  423.9 5.0 %collective-permute-start.39 = (f32[2,2,1680]{2,1,0:T(2,128)S(1)}, f32[2,2,1680]{2,1,0:T(2,128)S(1)}, u32[]{:S(2)}, u32[]{:S(2)}) collective-permute-start(f32[2,2,1680]{2,1,0:T(2,128)S(1)} %squeeze.86), channel_id=1, source_target_pairs={{0,16},{4,20},{8,24},{12,28},{16,0},{20,4},{24,8},{28,12},{1,17},{... | collective-permute-start | bytes 80648 | tf_op jit(solution)/shard_map/ppermute | solution.py:28
  428.9 3.8 collective-permute-start.40
  431.0 6.4 %collective-permute-start.47 = (bf16[1,144,384]{2,1,0:T(8,128)(2,1)S(1)}, bf16[1,144,384]{2,1,0:T(8,128)(2,1)S(1)}, u32[]{:S(2)}, u32[]{:S(2)}) collective-permute-start(bf16[1,144,384]{2,1,0:T(8,128)(2,1)S(1)} %copy-done.68), channel_id=1, source_target_pairs={{0,16},{4,20},{8,24},{12,28},{16,0},{20,4},{24,8},{28,12},{1,17},{... | collective-permute-start | bytes 331784 | tf_op jit(solution)/shard_map/ppermute | solution.py:28
  437.6 7.1 %collective-permute-start.49 = (bf16[144,960]{1,0:T(8,128)(2,1)S(1)}, bf16[144,960]{1,0:T(8,128)(2,1)S(1)}, u32[]{:S(2)}, u32[]{:S(2)}) collective-permute-start(bf16[144,960]{1,0:T(8,128)(2,1)S(1)} %maximum_maximum_fusion.refs_0_), channel_id=1, source_target_pairs={{0,2},{1,3},{2,0},{3,1},{4,6},{5,7},{6,4},{7,5},{8,10},{9,11},{10,... | collective-permute-start | bytes 829448 | tf_op jit(solution)/shard_map/ppermute | solution.py:28
  438.8 3.7 collective-permute-start.41
  442.5 1.2 collective-permute-start.42
  443.7 3.7 collective-permute-start.43
  444.6 4.0 collective-permute-start.48
  444.7 4.0 collective-permute-start.50
  (61 other events, 303.1 us)

commit v3 on v2

--- a/solution.py
+++ b/solution.py
@@ -15,8 +15,15 @@
 MASKED = -1e30
 ONE_ROW = 56
 SPLIT_ROW = 57
-VMEM_LIMIT = 56 * 1024 * 1024
+VMEM_LIMIT = 20 * 1024 * 1024
 SHORT = pl.CostEstimate(flops=1, bytes_accessed=1, transcendentals=0)
+
+
+COSTS = {'widen': 3, 'attend_forward': 14, 'own_weights': 4}
+
+
+def cost(name):
+    return pl.CostEstimate(flops=COSTS.get(name, 0) * 10**9 + 1, bytes_accessed=1, transcendentals=0)
 
 
 def bits_of(count):
@@ -131,7 +138,7 @@
         out_specs=jax.tree.map(lambda _: pl.BlockSpec(memory_space=pltpu.VMEM), out_shape),
         scratch_shapes=scratch,
         compiler_params=pltpu.CompilerParams(vmem_limit_bytes=VMEM_LIMIT),
-        cost_estimate=SHORT,
+        cost_estimate=cost(name),
         name=name,
     )(*inputs)
 
@@ -166,16 +173,22 @@
     return result.astype(jnp.bfloat16)
 
 
-def forward_kernel(seq_count, span, heads, head_size, rate, scalars, *refs):
-    blocks, (weight, bias) = refs[:seq_count], refs[seq_count : seq_count + 2]
+def forward_kernel(seq_count, cell, span, heads, head_size, rate, scalars, *refs):
+    blocks, (weight, bias, gain, shift) = refs[:seq_count], refs[seq_count : seq_count + 4]
     groups = head_groups(heads)
-    *qkv_groups, out = refs[seq_count + 2 : seq_count + 3 + len(groups)]
-    *parts, rows, diag, scores = refs[seq_count + 3 + len(groups) :]
-    me, prefix = scalars[0], scalars[2]
+    *qkv_groups, out, normed = refs[seq_count + 4 : seq_count + 6 + len(groups)]
+    *parts, rows, diag, scores = refs[seq_count + 6 + len(groups) :]
+    width = gain.shape[0]
+    gain, shift = columns_of(gain, shift)
+    me, prefix = scalars[0], scalars[2 + cell]
     length = span * seq_count
     tiles = length // TILE
     for r in range(seq_count):
-        mixed = jnp.dot(weight[...], blocks[r][...], preferred_element_type=jnp.float32)
+        here = slice(r * span, (r + 1) * span)
+        normal, _ = centred_columns(blocks[r][:width, :].astype(jnp.float32))
+        normed[:width, here] = (normal * gain + shift).astype(jnp.bfloat16)
+        normed[width:, here] = blocks[r][width:, :]
+        mixed = jnp.dot(weight[...], normed[:, here], preferred_element_type=jnp.float32)
         mixed = (mixed + bias[...]).astype(jnp.bfloat16)
         place = pl.ds(pl.multiple_of((me ^ r) * span, LANES), span)
         mixed = mixed.reshape(3 * heads, HEAD_PAD, span)
@@ -229,18 +242,10 @@
         parts[r][...] = piece.astype(jnp.bfloat16)
 
 
-def backward_kernel(
-    seq_count, places, cell, span, first_head, heads, head_size, rate, earlier, scalars, *refs
-):
-    qkv, out, *rest = refs[:-9] if earlier is not None else refs[:-7]
-    arrays = rest[: 1 + max(n for n, _ in places)]
-    if earlier is not None:
-        weights, backs = rest[len(arrays) : -earlier], rest[-earlier:]
-        result, away, here_sums = refs[-9:-6]
-    else:
-        result = refs[-7]
+def backward_kernel(seq_count, places, cell, span, first_head, heads, head_size, rate, scalars, *refs):
+    qkv, out, *arrays, result = refs[:-6]
     back, query_rows, key_rows, value_rows, gathered, diag = refs[-6:]
-    me, prefix = scalars[0], scalars[2]
+    me, prefix = scalars[0], scalars[2 + cell]
     length = span * seq_count
     tiles = length // TILE
     scale = 1.0 / math.sqrt(head_size)
@@ -309,38 +314,26 @@
             joined = pieces[0] if len(pieces) == 1 else jnp.concatenate(pieces, axis=1)
             left = first * HEAD_PAD
             result[there, left : left + joined.shape[1]] = joined
-    if earlier is None:
-        return
-    for r in range(seq_count):
-        target = away if r & 1 else here_sums
-        turned = (((1,), (1,)), ((), ()))
-        total = 0.0
-        for weight, dense in zip(weights, [*backs, result]):
-            total += lax.dot_general(
-                weight[...],
-                dense[r * span : (r + 1) * span, :],
-                turned,
-                preferred_element_type=jnp.float32,
-            )
-        target[r >> 1] = total.astype(jnp.bfloat16)
-
-
-def attend_forward(scalars, blocks, weight, bias, heads, head_size):
+
+def attend_forward(scalars, cell, blocks, weight, bias, gain, shift, heads, head_size):
     seq_count, span = len(blocks), blocks[0].shape[1]
     length = seq_count * span
     rate = math.log2(math.e) / math.sqrt(head_size)
     flops = 2 * weight.size * length + 4 * heads * HEAD_PAD * length * length
     return no_grid_call(
-        partial(forward_kernel, seq_count, span, heads, head_size, rate),
+        partial(forward_kernel, seq_count, cell, span, heads, head_size, rate),
         tuple(
             jax.ShapeDtypeStruct((3 * count, HEAD_PAD, length), jnp.bfloat16)
             for _, count, _ in head_groups(heads)
         )
-        + (jax.ShapeDtypeStruct((heads, HEAD_PAD, length), jnp.float32),)
+        + (
+            jax.ShapeDtypeStruct((heads, HEAD_PAD, length), jnp.float32),
+            jax.ShapeDtypeStruct((blocks[0].shape[0], length), jnp.bfloat16),
+        )
         + (jax.ShapeDtypeStruct((heads * head_size, span), jnp.bfloat16),) * seq_count,
         "attend_forward",
         flops,
-        [scalars, *blocks, weight, bias],
+        [scalars, *blocks, weight, bias, gain, shift],
         [
             pltpu.VMEM((heads, length, HEAD_PAD), jnp.bfloat16),
             pltpu.VMEM((length // TILE, TILE, TILE), jnp.float32),
@@ -349,37 +342,19 @@
     )
 
 
-def attend_backward(
-    scalars, cell, qkv, out, arrays, places, first_head, head_size, weights=None, backs=()
-):
+def attend_backward(scalars, cell, qkv, out, arrays, places, first_head, head_size):
     seq_count, span = len(places), arrays[0].shape[-1]
     heads = qkv.shape[0] // 3
     length = seq_count * span
     rate = math.log2(math.e) / math.sqrt(head_size)
-    earlier = len(backs) if weights else None
-    inputs = [scalars, qkv, out, *arrays]
-    results = (jax.ShapeDtypeStruct((length, 3 * heads * HEAD_PAD), jnp.bfloat16),)
-    if weights:
-        inputs += [*weights, *backs]
-        shape = (seq_count // 2, weights[0].shape[0], span)
-        results += (jax.ShapeDtypeStruct(shape, jnp.bfloat16),) * 2
     return no_grid_call(
         partial(
-            backward_kernel,
-            seq_count,
-            places,
-            cell,
-            span,
-            first_head,
-            heads,
-            head_size,
-            rate,
-            earlier,
+            backward_kernel, seq_count, places, cell, span, first_head, heads, head_size, rate
         ),
-        results,
+        jax.ShapeDtypeStruct((length, 3 * heads * HEAD_PAD), jnp.bfloat16),
         "attend_backward",
         1,
-        inputs,
+        [scalars, qkv, out, *arrays],
         [
             pltpu.VMEM((3 * heads, length, HEAD_PAD), jnp.bfloat16),
             pltpu.VMEM((HEAD_PAD, length), jnp.float32),
@@ -391,29 +366,48 @@
     )
 
 
+def normed_back_kernel(seq_count, count, *refs):
+    weights, backs = refs[:count], refs[count : 2 * count]
+    tokens, results = refs[2 * count : 2 * count + seq_count], refs[2 * count + seq_count : -1]
+    sums = refs[-1]
+    width, span = results[0].shape
+    totals = [0.0] * 2
+    for r in range(seq_count):
+        rows = slice(r * span, (r + 1) * span)
+        back = sum(dot_turned(w[...], part[rows, :]) for w, part in zip(weights, backs))
+        results[r][...] = back.astype(jnp.bfloat16)
+        normal, _ = centred_columns(tokens[r][:width, :].astype(jnp.float32))
+        for n, term in enumerate((back * normal, back)):
+            totals[n] = totals[n] + jnp.sum(term, axis=1, keepdims=True)
+    sums[...] = lines_of(totals)
+
+
+def normed_back(weights, backs, tokens):
+    seq_count = len(tokens)
+    span = backs[0].shape[0] // seq_count
+    width = weights[0].shape[0]
+    shape = jax.ShapeDtypeStruct((width, span), jnp.bfloat16)
+    return no_grid_call(
+        partial(normed_back_kernel, seq_count, len(backs)),
+        (shape,) * seq_count + (jax.ShapeDtypeStruct((8, width), jnp.float32),),
+        "normed_back",
+        1,
+        [*weights, *backs, *tokens],
+        [],
+        scalars=0,
+    )
+
+
 def mix_outer_kernel(cell_count, share, cuts, count, scalars, *refs):
-    blocks, backs = refs[: -count - 7], refs[-count - 7 : -7]
-    *results, sums, turned, whole_sum = refs[-7:]
-    span = blocks[0].shape[1]
-    features = turned.shape[0]
-    for n, block in enumerate(blocks):
-        turned[:, n * span : (n + 1) * span] = block[:features, :]
-    width = backs[0].shape[1]
-    length = backs[0].shape[0]
+    normed, backs, (*results, sums, whole_sum) = refs[:count], refs[count : 2 * count], refs[2 * count :]
+    features, width = whole_sum.shape
     sums[...] = sum(
         jnp.sum(back[...].astype(jnp.float32), axis=0, keepdims=True) for back in backs
     )
-    for first in range(0, width, TILE):
-        last = min(first + TILE, width)
-        total = None
-        for n, back in enumerate(backs):
-            part = jnp.dot(
-                turned[:, n * length : (n + 1) * length],
-                back[:, first:last],
-                preferred_element_type=jnp.float32,
-            )
-            total = part if total is None else total + part
-        whole_sum[:, first:last] = total
+    for first, last in chunks(width):
+        whole_sum[:, first:last] = sum(
+            dot(left[:features, :], back[:, first:last]) for left, back in zip(normed, backs)
+        )
     for k in range(cell_count):
         c = k ^ scalars[1]
         start = jnp.minimum(lax.div(c * share, 8) * 8, features - cuts[-1])
@@ -423,23 +417,19 @@
             target[without_bit(k, bit)] = block[cuts[n] : cuts[n + 1]]
 
 
-def mix_outer(scalars, blocks, backs, features, cell_count):
+def mix_outer(scalars, normed, backs, features, cell_count):
     _, height = row_cover(features, cell_count)
     cuts = (0, -(-height // 2 // 16) * 16, height)
     width = backs[0].shape[1]
-    positions = sum(b.shape[0] for b in backs)
     halves = [(cell_count // 2, cuts[n + 1] - cuts[n], width) for n in (0, 0, 1, 1)]
     return no_grid_call(
         partial(mix_outer_kernel, cell_count, features // cell_count, cuts, len(backs)),
         tuple(jax.ShapeDtypeStruct(shape, jnp.bfloat16) for shape in halves)
         + (jax.ShapeDtypeStruct((1, width), jnp.float32),),
         "mix_outer",
-        2 * positions * features * width,
-        [scalars, *blocks, *backs],
-        [
-            pltpu.VMEM((features, positions), jnp.bfloat16),
-            pltpu.VMEM((features, width), jnp.float32),
-        ],
+        1,
+        [scalars, *normed, *backs],
+        [pltpu.VMEM((features, width), jnp.float32)],
     )
 
 
@@ -448,6 +438,50 @@
     for bit in list(reversed(bits_of(seq_count))):
         held.update({r | bit: swap_with(x, "seq", bit) for r, x in list(held.items())})
     return [held[r] for r in range(seq_count)]
+
+
+class PositionSum:
+    def __init__(self, blocks):
+        self.held = dict(enumerate(blocks))
+        self.bits = bits_of(len(blocks))
+        self.leave()
+
+    def leave(self):
+        bit = self.bits.pop(0)
+        self.got = {r: swap_with(self.held[r | bit], "seq", bit) for r in self.held if not r & bit}
+
+    def step(self, last):
+        held, got = order_after((self.held, self.got), last)
+        self.held = {r: add_low(held[r], x) for r, x in got.items()}
+        self.leave()
+        return self.held[0]
+
+    def terms(self):
+        return [self.held[0], self.got[0]]
+
+
+class VectorSum:
+    def __init__(self, blocks, seq_count):
+        cells = [("cells", bit) for bit in reversed(bits_of(blocks.shape[0]))]
+        self.order = cells + [("seq", bit) for bit in bits_of(seq_count)]
+        self.leave(blocks)
+
+    def leave(self, blocks):
+        axis, bit = self.order.pop(0)
+        half = blocks.shape[0] // 2 if axis == "cells" else 0
+        self.keep = blocks[:half] if half else blocks
+        self.got = swap_with(blocks[half:], axis, bit)
+
+    def step(self, last):
+        keep, got = order_after((self.keep, self.got), last)
+        self.keep = keep + got
+        if self.order:
+            self.leave(self.keep)
+        return self.keep
+
+
+def add_low(left, right):
+    return (left.astype(jnp.float32) + right.astype(jnp.float32)).astype(jnp.bfloat16)
 
 
 def route_upper(upper):
@@ -498,9 +532,11 @@
     return rise * inner
 
 
-def columns_of(lines):
-    turned = lines[...].T
-    return [turned[:, n : n + 1] for n in range(8)]
+def columns_of(*vectors):
+    rows = [vector[...].reshape(1, -1) for vector in vectors]
+    rows += [jnp.zeros_like(rows[0])] * (8 - len(rows))
+    turned = jnp.concatenate(rows, axis=0).T
+    return [turned[:, n : n + 1] for n in range(len(vectors))]
 
 
 def lines_of(columns):
@@ -509,35 +545,38 @@
     return jnp.concatenate(list(columns) + room, axis=1).T
 
 
-def first_norm_kernel(tokens, lines, hidden, *results):
-    width = tokens.shape[1]
-    gain, shift = columns_of(lines)[:2]
-    for c, result in enumerate(results):
-        normal, _ = centred_columns(tokens[c].astype(jnp.float32))
-        result[:width, :] = (normal * gain + shift).astype(jnp.bfloat16)
-        shape = (result.shape[0] - width, result.shape[1])
-        mark = lax.broadcasted_iota(jnp.int32, shape, 0) == 0
-        result[width:, :] = jnp.where(mark, hidden[c : c + 1, :], 0.0).astype(jnp.bfloat16)
-
-
-def first_norm(tokens, lines, hidden, features):
-    cells, _, span = tokens.shape
-    return no_grid_call(
-        first_norm_kernel,
-        (jax.ShapeDtypeStruct((features, span), jnp.bfloat16),) * cells,
-        "first_norm",
-        10 * tokens.size,
-        [tokens, lines, hidden],
+def widen_kernel(cell, cells, scalars, tokens, key_mask, result):
+    width, span = tokens.shape[1:]
+    place = lax.broadcasted_iota(jnp.int32, (1, span), 1) + scalars[0] * span
+    result[:width, :] = tokens[0]
+    seen = (key_mask[cell : cell + 1, :] == 1) & (place < scalars[2 + cells + cell])
+    shape = (result.shape[0] - width, span)
+    mark = lax.broadcasted_iota(jnp.int32, shape, 0) == 0
+    hidden = jnp.where(seen, 0.0, MASKED)
+    result[width:, :] = jnp.where(mark, hidden, 0.0).astype(jnp.bfloat16)
+
+
+def widen(scalars, cell, tokens, key_mask, features):
+    cells, width, span = tokens.shape
+    return grid_call(
+        partial(widen_kernel, cell, cells),
+        (1,),
+        [pl.BlockSpec((1, width, span), lambda g, me: (cell, 0, 0)), whole(key_mask)],
+        pl.BlockSpec((features, span), lambda g, me: (0, 0)),
+        jax.ShapeDtypeStruct((features, span), jnp.bfloat16),
         [],
-        scalars=0,
-    )
-
-
-def second_norm_kernel(seq_count, scalars, weight, tokens, lines, *refs):
+        "widen",
+        1,
+        (scalars, tokens, key_mask),
+        1,
+    )
+
+
+def second_norm_kernel(seq_count, scalars, weight, tokens, gain, shift, bias, *refs):
     parts = refs[:seq_count]
     middle, second, second_turned, attended, gather = refs[seq_count:]
     share = parts[0].shape[0]
-    _, _, gain, shift, bias, *_ = columns_of(lines)
+    gain, shift, bias = columns_of(gain, shift, bias)
     for r in range(seq_count):
         place = pl.ds(pl.multiple_of((scalars[0] ^ r) * share, 8), share)
         gather[place, :] = parts[r][...].astype(jnp.float32)
@@ -551,7 +590,7 @@
     second[...] = normed.T
 
 
-def second_norm(scalars, weight, tokens, lines, parts):
+def second_norm(scalars, weight, tokens, vectors, parts):
     width, span = tokens.shape
     seq_count = len(parts)
     return no_grid_call(
@@ -564,16 +603,24 @@
         ),
         "second_norm",
         2 * span * width * width,
-        [scalars, weight, tokens, lines, *parts],
+        [scalars, weight, tokens, *vectors, *parts],
         [pltpu.VMEM((seq_count * parts[0].shape[0], span), jnp.float32)],
     )
 
 
-def weights_kernel(seq_count, heads, head_size, scalars, mix, weight, *turned):
+def weights_kernel(seq_count, heads, head_size, scalars, mix, query, value, weight, bias, *turned):
     width = mix.shape[0]
     here = heads * head_size
     groups = head_groups(heads)
     weight[...] = jnp.zeros_like(weight)
+    vectors = columns_of(query, value)
+    row = lax.broadcasted_iota(jnp.int32, (HEAD_PAD, 1), 0)
+    for _, count, base in groups:
+        for p, least in ((0, (ONE_ROW, ONE_ROW + 1)), (1, (SPLIT_ROW, HEAD_PAD)), (2, (ONE_ROW, HEAD_PAD))):
+            fill = jnp.where((row >= least[0]) & (row < least[1]), 1.0, 0.0)
+            for n in range(count):
+                place = (base + p * count + n) * HEAD_PAD
+                bias[place : place + HEAD_PAD, :] = fill
     for s in range(seq_count):
 
         @pl.when(scalars[0] == s)
@@ -597,6 +644,9 @@
                         room = jnp.zeros((HEAD_PAD - head_size, width), jnp.float32)
                         piece = jnp.concatenate([piece, room])
                         weight[place : place + HEAD_PAD, :width] = piece.astype(jnp.bfloat16)
+                        if p != 1:
+                            own = vectors[p // 2][first + h * head_size : first + (h + 1) * head_size]
+                            bias[place : place + head_size, :] = own
 
     room = weight.shape[1] - width
     for (_, count, base), columns in zip(groups, turned):
@@ -609,18 +659,21 @@
         weight[rows, width:] = jnp.where(mark, 1.0, 0.0).astype(jnp.bfloat16)
 
 
-def own_weights(scalars, mix, features, seq_count, heads, head_size):
+def own_weights(scalars, mix, query, value, features, seq_count, heads, head_size):
     width = mix.shape[0]
     return no_grid_call(
         partial(weights_kernel, seq_count, heads, head_size),
-        (jax.ShapeDtypeStruct((3 * heads * HEAD_PAD, features), jnp.bfloat16),)
+        (
+            jax.ShapeDtypeStruct((3 * heads * HEAD_PAD, features), jnp.bfloat16),
+            jax.ShapeDtypeStruct((3 * heads * HEAD_PAD, 1), jnp.float32),
+        )
         + tuple(
             jax.ShapeDtypeStruct((width, 3 * count * HEAD_PAD), jnp.bfloat16)
             for _, count, _ in head_groups(heads)
         ),
         "own_weights",
         1,
-        [scalars, mix],
+        [scalars, mix, query, value],
         [],
     )
 
@@ -684,7 +737,7 @@
             scratch_shapes=scratch,
         ),
         compiler_params=pltpu.CompilerParams(vmem_limit_bytes=VMEM_LIMIT),
-        cost_estimate=SHORT,
+        cost_estimate=cost(name),
         input_output_aliases=aliases or {},
         name=name,
     )(*inputs)
@@ -731,7 +784,7 @@
     scalars,
     back_upper,
     up,
-    lines,
+    gain,
     cotangent,
     weight,
     *refs,
@@ -753,14 +806,14 @@
         span = cotangent.shape[2]
         heads = parts[0].shape[1]
         head_size = back_heads.shape[0] // (seq_count * heads)
-        gain = columns_of(lines)[2]
+        (gain_column,) = columns_of(gain)
         totals = [0.0] * 4
         for c in range(cells):
             here = slice(c * span, (c + 1) * span)
             normal, rise = centred_columns(middle[c][...])
             back = total[:, here]
             back_out = cotangent[c].astype(jnp.float32)
-            back_mid = back_out + norm_pull(normal, rise, back, gain)
+            back_mid = back_out + norm_pull(normal, rise, back, gain_column)
             back_middle[:, here] = back_mid
             branch = back_mid.astype(jnp.bfloat16)
             back_branch[:, here] = branch
@@ -780,7 +833,7 @@
         sums[...] = lines_of(totals)
 
 
-def middle_back(scalars, back_upper, up, middle, lines, cotangent, weight, seq_count, heads):
+def middle_back(scalars, back_upper, up, middle, gain, cotangent, weight, seq_count, heads):
     rows, hidden = back_upper.shape
     cells, width, span = cotangent.shape
     head_size = width // HEADS
@@ -799,7 +852,7 @@
         [
             pl.BlockSpec((rows, tile), lambda g, me: (0, g)),
             pl.BlockSpec((width, tile), lambda g, me: (0, g)),
-            whole(lines),
+            whole(gain),
             whole(cotangent),
             whole(weight),
         ]
@@ -812,21 +865,21 @@
         ],
         "middle_back",
         2 * rows * up.size + 2 * rows * width * width,
-        (scalars, back_upper, up, lines, cotangent, weight, *middle),
-        1,
-    )
-
-
-def block_out_kernel(active, down, lines, *refs):
+        (scalars, back_upper, up, gain, cotangent, weight, *middle),
+        1,
+    )
+
+
+def block_out_kernel(active, down, bias, *refs):
     *middle, result, total = refs
     step = pl.program_id(0)
 
     @pl.when(step == 0)
     def _():
-        bias = columns_of(lines)[5]
+        (bias_column,) = columns_of(bias)
         for c, part in enumerate(middle):
             span = part.shape[1]
-            total[:, c * span : (c + 1) * span] = part[...] + bias
+            total[:, c * span : (c + 1) * span] = part[...] + bias_column
 
     for first, last in chunks(total.shape[1]):
         total[:, first:last] += dot_turned(down[...], active[first:last, :])
@@ -838,7 +891,7 @@
             result[c] = total[:, c * span : (c + 1) * span].astype(jnp.bfloat16)
 
 
-def block_output(scalars, active, down, middle, lines):
+def block_output(scalars, active, down, middle, bias):
     rows, hidden = active.shape
     cells, width = len(middle), middle[0].shape[0]
     tile = hidden_tile(hidden)
@@ -849,7 +902,7 @@
         [
             pl.BlockSpec((rows, tile), lambda g, me: (0, g)),
             pl.BlockSpec((width, tile), lambda g, me: (0, g)),
-            whole(lines),
+            whole(bias),
         ]
         + [whole(m) for m in middle],
         whole(out),
@@ -857,7 +910,7 @@
         [pltpu.VMEM((width, rows), jnp.float32)],
         "block_output",
         2 * rows * down.size,
-        (scalars, active, down, lines, *middle),
+        (scalars, active, down, bias, *middle),
         1,
     )
 
@@ -1056,23 +1109,26 @@
     for first, last in chunks(total.shape[1]):
         total[:, first:last] = dot_turned(joined[...], right[first:last, :])
     width = total.shape[1] // seq_count
-    part = result.shape[2]
-    for k in range(result.shape[1]):
+    _, cell_count, part, room = result.shape
+    groups = room // width
+    for k in range(cell_count):
         c = k ^ scalars[1]
-        start = jnp.minimum(lax.div(c * share, 8) * 8, rows - seq_count * part)
-        block = total[pl.ds(pl.multiple_of(start, 8), seq_count * part), :]
+        start = jnp.minimum(lax.div(c * share, 8) * 8, rows - groups * part)
+        block = total[pl.ds(pl.multiple_of(start, 8), groups * part), :]
         for s in range(seq_count):
             piece = block[:, s * width : (s + 1) * width]
-            groups = [piece[i * part : (i + 1) * part] for i in range(seq_count)]
+            pieces = [piece[i * part : (i + 1) * part] for i in range(groups)]
+            pieces.append(jnp.zeros((part, room - groups * width), jnp.float32))
             place = s ^ scalars[0]
             place = (place & 1) * (seq_count // 2) + (place >> 1)
-            result[place, k] = jnp.concatenate(groups, axis=1).astype(jnp.bfloat16)
-
-
-def out_outer(scalars, left, right, seq_count, cell_count):
+            result[place, k] = jnp.concatenate(pieces, axis=1).astype(jnp.bfloat16)
+
+
+def out_outer(scalars, left, right, room, seq_count, cell_count):
     rows, tokens = right.shape
-    _, height = row_cover(rows, cell_count, 16 * seq_count)
-    shape = (seq_count, cell_count, height // seq_count, rows)
+    groups = room * seq_count // rows
+    _, height = row_cover(rows, cell_count, 16 * groups)
+    shape = (seq_count, cell_count, height // groups, room)
     return no_grid_call(
         partial(out_outer_kernel, seq_count, len(left), rows // cell_count),
         jax.ShapeDtypeStruct(shape, jnp.bfloat16),
@@ -1080,6 +1136,53 @@
         1,
         [scalars, right, *left],
         [pltpu.VMEM((rows, rows), jnp.float32), pltpu.VMEM((rows, tokens), jnp.bfloat16)],
+    )
+
+
+def vector_kernel(cells, heads, head_size, seq_count, scalars, middle, hidden, *refs):
+    first, sums, (result, own) = refs[:cells], refs[cells:-2], refs[-2:]
+    own[...] = jnp.zeros_like(own)
+    width = middle.shape[1]
+    for s in range(seq_count):
+
+        @pl.when(scalars[0] == s)
+        def _():
+            for (start, count, _), part in zip(head_groups(heads), sums):
+                for n in range(count):
+                    at = ((s * heads) + start + n) * head_size
+                    if at >= width:
+                        continue
+                    for row, p in enumerate((0, 2)):
+                        source = (p * count + n) * HEAD_PAD
+                        own[row : row + 1, at : at + head_size] = part[
+                            :, source : source + head_size
+                        ]
+
+    total = sum(part[0:2, :] for part in first)
+    lines = [total[0:1], total[1:2], own[0:1, :], own[1:2, :]]
+    lines += [middle[n : n + 1, :] for n in (2, 0, 1, 3)]
+    count, rows, share = result.shape
+    for c in range(count):
+        place = c ^ scalars[1]
+        for n, line in enumerate(lines):
+            result[place, n : n + 1, :] = line[:, c * share : (c + 1) * share]
+        for n in range(rows - 8):
+            at = (c * (rows - 8) + n) * share
+            result[place, 8 + n : 9 + n, :] = hidden[:, at : at + share]
+
+
+def vector_blocks(
+    scalars, first, sums, middle, hidden, heads, head_size, seq_count, cell_count
+):
+    share = middle.shape[1] // cell_count
+    rows = 8 + hidden.shape[1] // middle.shape[1]
+    return no_grid_call(
+        partial(vector_kernel, len(first), heads, head_size, seq_count),
+        jax.ShapeDtypeStruct((cell_count, rows, share), jnp.float32),
+        "vector_blocks",
+        1,
+        [scalars, middle, hidden, *first, *sums],
+        [pltpu.VMEM((8, middle.shape[1]), jnp.float32)],
     )
 
 
@@ -1123,32 +1226,25 @@
     )
 
 
-def tokens_back_kernel(tokens, lines, back_middle, *refs):
+def tokens_back_kernel(tokens, gain, back_middle, *refs):
+    *terms, result = refs
     cells, _, span = tokens.shape
-    terms, (result, sums) = refs[: 2 * cells], refs[2 * cells :]
-    gain = columns_of(lines)[0]
-    totals = [0.0] * 2
+    (gain,) = columns_of(gain)
     for c in range(cells):
         normal, rise = centred_columns(tokens[c].astype(jnp.float32))
         back = terms[2 * c][...].astype(jnp.float32) + terms[2 * c + 1][...].astype(jnp.float32)
         back_in = back_middle[:, c * span : (c + 1) * span]
         back_in = back_in + norm_pull(normal, rise, back, gain)
         result[c] = back_in.astype(jnp.bfloat16)
-        for n, term in enumerate((back * normal, back)):
-            totals[n] = totals[n] + jnp.sum(term, axis=1, keepdims=True)
-    sums[...] = lines_of(totals)
-
-
-def tokens_back(tokens, lines, back_middle, terms):
+
+
+def tokens_back(tokens, gain, back_middle, terms):
     return no_grid_call(
         tokens_back_kernel,
-        (
-            jax.ShapeDtypeStruct(tokens.shape, jnp.bfloat16),
-            jax.ShapeDtypeStruct((8, tokens.shape[1]), jnp.float32),
-        ),
+        jax.ShapeDtypeStruct(tokens.shape, jnp.bfloat16),
         "tokens_back",
-        20 * tokens.size,
-        [tokens, lines, back_middle, *terms],
+        1,
+        [tokens, gain, back_middle, *terms],
         [],
         scalars=0,
     )
@@ -1204,104 +1300,88 @@
     heads_here = -(-HEADS // seq_count)
     head_total = heads_here * seq_count
     features = -(-(width + 1) // LANES) * LANES
-    scalars = [jnp.concatenate([me, prefix_lengths[c : c + 1]]) for c in range(cells_here)]
+    scalars = jnp.concatenate([me, prefix_lengths, totals])
 
     def flat(array):
         return array.reshape(row_count, array.shape[-1])
 
-    def own_heads(array, at):
-        lead = array.shape[:at]
-        pad = [(0, 0)] * array.ndim
-        pad[at] = (0, (head_total - HEADS) * head_size)
-        array = jnp.pad(array, pad)
-        here = heads_here * head_size
-        array = lax.dynamic_slice_in_dim(array, me[0] * here, here, axis=at)
-        return array.reshape(lead + (heads_here, head_size))
-
-    def padded_heads(array, fills=()):
-        room = HEAD_PAD - head_size
-        tail = jnp.array(list(fills) + [0.0] * (room - len(fills)), array.dtype)
-        tail = jnp.broadcast_to(tail, array.shape[:-1] + (room,))
-        return jnp.concatenate([array, tail], axis=-1)
-
-    bias_parts = (
-        padded_heads(own_heads(query_bias, 0), (1.0,)),
-        padded_heads(jnp.zeros((heads_here, head_size), jnp.float32), (0.0, 1.0, 1.0, 1.0)),
-        padded_heads(own_heads(value_bias, 0), (1.0, 1.0, 1.0, 1.0)),
-    )
     groups = head_groups(heads_here)
-    bias = jnp.concatenate([p[h : h + n] for h, n, _ in groups for p in bias_parts]).reshape(-1, 1)
-
-    open_here = (key_mask == 1) & (own_rows[None, :] < totals[:, None])
-    hidden = jnp.where(open_here, 0.0, MASKED).astype(jnp.float32)
-    nothing = jnp.zeros_like(first_gain)
-    lines = jnp.stack(
-        [first_gain, first_shift, second_gain, second_shift, out_bias, down_bias]
-        + [nothing, nothing]
-    )
     tokens_turned = tokens.transpose(0, 2, 1)
     cotangent_turned = cotangent.transpose(0, 2, 1)
     down_turned = down_weight.T
-    normed = first_norm(tokens_turned, lines, hidden, features)
-    weight, *weights_turned = own_weights(
-        order_after(scalars[0], normed), mix_weight, features, seq_count, heads_here, head_size
-    )
-    own_cotangent = order_after(flat(cotangent), normed)
+    wide = []
+    for c in range(cells_here):
+        wide.append(widen(order_after(scalars, wide), c, tokens_turned, key_mask, features))
+    weight, bias, *weights_turned = own_weights(
+        order_after(scalars, wide),
+        mix_weight,
+        query_bias,
+        value_bias,
+        features,
+        seq_count,
+        heads_here,
+        head_size,
+    )
     x_bits = [b for b in reversed(bits_of(seq_count)) if b > 1]
-    near = swap_with(jnp.stack(normed), "seq", 1)
-    held = [{0: normed[c]} for c in range(cells_here)]
-    earlier = ()
+    near = [swap_with(block, "seq", 1) for block in wide]
+    back_active = active_back(scalars, order_after(flat(cotangent), weight), down_turned)
+    held = [{0: wide[c]} for c in range(cells_here)]
     for c in range(cells_here):
         for bit in x_bits:
             for r, block in list(held[c].items()):
-                held[c][r | bit] = swap_with(order_after(block, *earlier), "seq", bit)
-        earlier = (held[c][x_bits[0]], weight)
-    back_active = active_back(
-        scalars[0], order_after(own_cotangent, weight, held[0]), down_turned
-    )
-    normed_blocks = []
+                after = (held[c - 1][x_bits[0]], back_active) if c > 0 else ()
+                held[c][r | bit] = swap_with(order_after(block, *after), "seq", bit)
+
+    attended, kept = [], []
+    last = (back_active,)
+    blocks, normed = [], []
     for c in range(cells_here):
-        after = (weight,) if c == 0 else (back_active,)
+        after = last
         for r, block in list(held[c].items()):
             held[c][r | 1] = near[c] if r == 0 else swap_with(order_after(block, *after), "seq", 1)
-        normed_blocks.append([held[c][r] for r in range(seq_count)])
-
-    attended, kept = [], []
-    last = (back_active, bias)
-    for c in range(cells_here):
+        blocks.append([held[c][r] for r in range(seq_count)])
         results = attend_forward(
-            scalars[c], order_after(normed_blocks[c], *last), weight, bias, heads_here, head_size
+            scalars,
+            c,
+            order_after(blocks[c], *last),
+            weight,
+            bias,
+            first_gain,
+            first_shift,
+            heads_here,
+            head_size,
         )
-        qkv, out, parts = results[: len(groups)], results[len(groups)], results[len(groups) + 1 :]
+        qkv, (out, normed_cell, *parts) = results[: len(groups)], results[len(groups) :]
         last = (out,)
         kept.append((qkv, out))
+        normed.append(normed_cell)
         attended.append(exchanged_blocks(parts))
     middle, second, second_turned, attended_turned = [], [], [], []
     for c in range(cells_here):
         results = second_norm(
-            scalars[0],
+            scalars,
             out_weight,
             tokens_turned[c],
-            lines,
+            (second_gain, second_shift, out_bias),
             order_after(attended[c], *last),
         )
         last = (results[0],)
         for held, result in zip((middle, second, second_turned, attended_turned), results):
             held.append(result)
     active, back_upper, up_bias_back = hidden_layer(
-        scalars[0], second, back_active, up_weight, up_bias.reshape(1, -1)
-    )
-    (down_send,) = down_outer(scalars[0], cotangent_turned, active, seq_count, cell_count)
+        scalars, second, back_active, up_weight, up_bias.reshape(1, -1)
+    )
+    (down_send,) = down_outer(scalars, cotangent_turned, active, seq_count, cell_count)
     down_got = swap_with(down_send, "seq", 1)
     (up_send,) = up_outer(
-        scalars[0], second_turned, order_after(back_upper, down_send), seq_count, cell_count
+        scalars, second_turned, order_after(back_upper, down_send), seq_count, cell_count
     )
     up_got = swap_with(up_send, "seq", 1)
     *down_halves, lower_send, lower_keep = down_outer(
-        scalars[0], cotangent_turned, order_after(active, up_send), seq_count, cell_count, down_got
+        scalars, cotangent_turned, order_after(active, up_send), seq_count, cell_count, down_got
     )
     *up_halves, lower_send, lower_keep = up_outer(
-        scalars[0],
+        scalars,
         second_turned,
         order_after(back_upper, down_halves),
         seq_count,
@@ -1330,11 +1410,11 @@
         ),
     ]
     back_middle, back_branch, middle_sums, *back_heads = middle_back(
-        scalars[0],
+        scalars,
         order_after(back_upper, up_halves),
         up_weight,
         middle,
-        lines,
+        second_gain,
         cotangent_turned,
         out_weight,
         seq_count,
@@ -1342,37 +1422,36 @@
     )
     back_upper_half = route_upper(back_heads[-1])
     down_part, up_part, both_part = running
-    last = down_part.step(back_heads)
     out_shares = out_outer(
-        scalars[0],
+        scalars,
         attended_turned,
-        order_after(back_branch, last),
+        order_after(back_branch, back_heads),
+        3 * groups[0][1] * HEAD_PAD,
         seq_count,
         cell_count,
     )
     out_part = Reduction(
         "out",
         [("seq", 1)] + names,
-        [("seq", 1), y_bit] + x_bits + [z_bit] + rest,
+        [("seq", 1)] + x_bits + [y_bit, z_bit] + rest,
         flat_blocks(out_shares[seq_count // 2 :]),
         flat_blocks(out_shares[: seq_count // 2]),
     )
-    last = advance([up_part, both_part], out_shares)
-    back_arrays, back_places = route_rest(back_heads[:-1], order_after(back_upper_half, last))
-    last = out_part.step(last)
-    running.append(out_part)
     block_out = block_output(
-        scalars[0], order_after(active, last), down_turned, middle, lines
-    )
-    last = block_out
-    seq_bits = [("seq", 1)] + x_bits
+        scalars, order_after(active, out_shares), down_turned, middle, down_bias
+    )
+    last = down_part.step(block_out)
+    back_arrays, back_places = route_rest(
+        back_heads[:-1], order_after(back_upper_half, last)
+    )
+    last = advance([up_part, both_part], last)
     mixed_back, mix_parts = [[], []], []
-    back_normed, bias_backs = [], []
+    back_normed, bias_backs, first_sums = [], [], []
 
     def mix_reductions(group, last):
         *halves, sums = mix_outer(
-            scalars[0],
-            [x for c in normed_blocks for x in c],
+            scalars,
+            normed,
             order_after(mixed_back[group], last),
             width,
             cell_count,
@@ -1384,53 +1463,88 @@
             Reduction(label + " lower", cell_bits, [z_bit, y_bit] + rest, *halves[2:]),
         ], halves[0]
 
+    def attend_group(c, group, last):
+        qkv, out = kept[c]
+        back = attend_backward(
+            scalars,
+            c,
+            qkv[group],
+            out,
+            order_after(back_arrays, last),
+            back_places,
+            groups[group][0],
+            head_size,
+        )
+        mixed_back[group].append(back)
+        return back
+
+    def normed_reduction(c, last):
+        *parts, sums = normed_back(
+            weights_turned, [order_after(mixed_back[g][c], last) for g in range(2)], blocks[c]
+        )
+        first_sums.append(sums)
+        back_normed.append(PositionSum(parts))
+        return sums
+
     for c in range(cells_here):
-        qkv, out = kept[c]
         final = c == cells_here - 1
-        for group, (first_head, _, _) in enumerate(groups):
-            weights = weights_turned if group == len(groups) - 1 else None
-            back, *sums = attend_backward(
-                scalars[c],
-                c,
-                qkv[group],
-                out,
-                order_after(back_arrays, last),
-                back_places,
-                first_head,
-                head_size,
-                weights,
-                [mixed_back[0][c]] if weights else (),
-            )
-            last = back
-            mixed_back[group].append(back)
-            if weights:
-                back_normed.append(Reduction("normed", seq_bits, seq_bits, *sums, kind=c))
-            else:
-                running = [part for part in running if part.labels]
-                last = advance(running, last)
-                if c > 0:
-                    last = back_normed[c - 1].step(last)
-            if final:
-                parts, last = mix_reductions(group, last)
-                mix_parts.append(parts)
-    ahead = [part for part in running if part.order]
-    last = advance(mix_parts[0], (last, [part.got for part in back_normed[:-1]]))
-    last = back_normed[-1].step(last)
-    done = [part.got for part in running if not part.order]
-    last = advance(mix_parts[1] + ahead, (last, done))
+        last = attend_group(c, 0, last)
+        if final:
+            for earlier in range(c):
+                last = normed_reduction(earlier, last)
+            last = advance(running, last)
+            last = out_part.step(last)
+            parts, last = mix_reductions(0, last)
+            mix_parts.append(parts)
+            for part in back_normed:
+                last = part.step(last)
+        last = attend_group(c, 1, last)
+        if c == 0:
+            last = advance(running, last)
+    while len(out_part.order) >= len(cell_bits):
+        last = out_part.step(last)
+    parts, last = mix_reductions(1, last)
+    mix_parts.append(parts + [out_part])
     last = advance(mix_parts[0], last)
-    while any(part.order for part in back_normed):
+    last = normed_reduction(cells_here - 1, last)
+    done = [part.got for part in running if part.labels and not part.order]
+    vectors = VectorSum(
+        vector_blocks(
+            scalars,
+            order_after(first_sums, last),
+            bias_backs,
+            middle_sums,
+            up_bias_back,
+            heads_here,
+            head_size,
+            seq_count,
+            cell_count,
+        ),
+        seq_count,
+    )
+    last = advance(mix_parts[1], (last, [part.got for part in back_normed[:-1]]))
+    last = vectors.step(last)
+    last = advance(mix_parts[0], last)
+    last = back_normed[-1].step((last, done))
+    last = vectors.step(last)
+    last = advance(mix_parts[1], last)
+    last = vectors.step(last)
+    while any(part.bits for part in back_normed):
         for part in back_normed:
-            last = part.step(last) if part.order else last
-    terms = [x for part in back_normed for x in (part.keep[0], part.got[0])]
-    tokens_gradient, first_sums = tokens_back(
-        tokens_turned, lines, back_middle, order_after(terms, last)
-    )
-    last = tokens_gradient
+            last = part.step(last) if part.bits else last
     running += mix_parts[0] + mix_parts[1]
     running = [part for part in running if part.labels]
     while any(part.order for part in running):
         last = advance(running, last)
+    while vectors.order:
+        last = vectors.step(last)
+    terms = [x for part in back_normed for x in part.terms()]
+    tokens_gradient = tokens_back(
+        tokens_turned, first_gain, back_middle, order_after(terms, last)
+    )
+    last = tokens_gradient
+    joined = vectors.step(last)[0]
+    vectors = [*(joined[n] for n in range(7)), joined[8:].reshape(-1), joined[7]]
     blocks = {}
     for part in running:
         blocks.update(part.finish(last))
@@ -1454,62 +1568,25 @@
         axis=1,
     )
     mix_part = mix_columns(
-        scalars[0],
+        scalars,
         gathered_blocks(mix_part.astype(jnp.bfloat16), seq_count),
         heads_here,
         head_size,
     )
     group = blocks["out"].shape[0]
-    out_part = ungrouped(blocks["out"], [group * n for n in range(seq_count)], group)
-    bias_backs = [
-        sums.reshape(3, count, HEAD_PAD)[..., :head_size]
-        for sums, (_, count, _) in zip(bias_backs, groups)
-    ]
-    bias_back = jnp.concatenate(bias_backs, axis=1)
-
-    def all_heads(array):
-        wide = jnp.zeros((head_total * head_size,), jnp.float32)
-        wide = lax.dynamic_update_slice(
-            wide, array.reshape(-1), (me[0] * heads_here * head_size,)
-        )
-        return wide[:width]
-
-    query_bias_back, value_bias_back = all_heads(bias_back[0]), all_heads(bias_back[2])
+    out_groups = blocks["out"].shape[1] * seq_count // width
+    out_part = blocks["out"][:, : out_groups * (width // seq_count)]
+    out_part = ungrouped(out_part, [group * n for n in range(out_groups)], group)
+
     def own_rows_of(part, unit=16):
         starts, _ = row_cover(width, cell_count, unit)
         share = width // cell_count
         shift = jnp.array([share * c - starts[c] for c in range(cell_count)])[me[1]]
         return lax.dynamic_slice_in_dim(part, shift, share, axis=0)
 
-    vectors = (
-        first_sums[0],
-        first_sums[1],
-        query_bias_back,
-        value_bias_back,
-        middle_sums[2],
-        middle_sums[0],
-        middle_sums[1],
-        up_bias_back.reshape(-1),
-        middle_sums[3],
-    )
-    joined = jnp.concatenate([v.reshape(cell_count, -1) for v in vectors], axis=1)
-    joined = joined[jnp.arange(cell_count) ^ me[1]]
-    names = [("cells", b) for b in reversed(bits_of(cell_count))]
-    joined = joined.reshape((2,) * len(names) + joined.shape[1:])
-    for axis, bit in list(names):
-        place = names.index((axis, bit))
-        got = swap_with(lax.index_in_dim(joined, 1, place, keepdims=False), axis, bit)
-        joined = lax.index_in_dim(joined, 0, place, keepdims=False) + got
-        names.remove((axis, bit))
-    for bit in bits_of(seq_count):
-        joined = joined + swap_with(joined, "seq", bit)
-    ends = [0]
-    for v in vectors:
-        ends.append(ends[-1] + v.shape[0] // cell_count)
-    vectors = [joined[ends[i] : ends[i + 1]] for i in range(len(vectors))]
     matrices = (
         own_rows_of(mix_part),
-        own_rows_of(out_part, 16 * seq_count),
+        own_rows_of(out_part, 16 * out_groups),
         own_rows_of(up_part),
         down_part.T,
     )

time: 462 us -> 361 us (0.78)
  Pallas kernels: 293 us -> 191 us
  local copies, waits for them, and re-layouts: 42.3 us -> 49.4 us
    pallas_call x19 -> x17, Pallas kernels: 53.2 us -> 11.3 us  [add_halves(): pl.pallas_call(partial(add_halves_kernel, len(pairs)), out_shape=(shape,...]
    pallas_call x15 -> x17, Pallas kernels: 134 us -> 97.9 us  [no_grid_call(): pl.pallas_call(body, out_shape=out_shape, in_specs=in_specs, out_specs=ja...]
    unnamed x147 -> x177, local copies, waits for them, and re-layouts: 18.1 us -> 45.5 us
    pallas_call x8 -> x10, Pallas kernels: 106 us -> 81.9 us  [grid_call(): pl.pallas_call(body, out_shape=out_shape, grid_spec=pltpu.PrefetchScalarG...]
    another operation x19 -> x0, local copies, waits for them, and re-layouts: 5.59 us -> none  [the longest x8 4.87 us: on_device(): jnp.stack([first_gain, first_shift, second_gain, second_shift, out_bias,...]
    ppermute x52 -> x55, waiting for transfers between devices: 54.4 us -> 52.4 us  [swap_with(): return lax.ppermute(array, axis, [(i, i ^ bit) for i in range(count)])]
    ppermute x52 -> x55, starting transfers between devices: 48.5 us -> 47.5 us  [swap_with(): return lax.ppermute(array, axis, [(i, i ^ bit) for i in range(count)])]
  transfers between devices with their start and end apart: 52 -> 55, of which waited for: 13 -> 16; matrix products, arithmetic and copies ran while one was open for 6% -> 3% of each run, Pallas kernels for 45% -> 45%
where the time goes in v3:
time: 361 us; the launch traced here: 354 us
  Pallas kernels  191 us (53%)
  waiting for transfers between devices  52.4 us (15%)
  local copies, waits for them, and re-layouts  49.4 us (14%)
  starting transfers between devices  47.5 us (13%)
  other arithmetic  7.67 us (2%)
  between operations  6.25 us (2%)
    pallas_call x17, Pallas kernels, no_grid_call(): pl.pallas_call(body, out_shape=out_shape, in_specs=in_specs, out_specs=ja...  97.9 us
    pallas_call x10, Pallas kernels, grid_call(): pl.pallas_call(body, out_shape=out_shape, grid_spec=pltpu.PrefetchScalarG...  81.9 us
    ppermute x55, waiting for transfers between devices, swap_with(): return lax.ppermute(array, axis, [(i, i ^ bit) for i in range(count)])  52.4 us
    ppermute x55, starting transfers between devices, swap_with(): return lax.ppermute(array, axis, [(i, i ^ bit) for i in range(count)])  47.5 us
    unnamed x177, local copies, waits for them, and re-layouts  45.5 us
    pallas_call x17, Pallas kernels, add_halves(): pl.pallas_call(partial(add_halves_kernel, len(pairs)), out_shape=(shape,...  11.3 us
  transfers between devices with their start and end apart: 55, of which 16 were waited for; matrix products, arithmetic and copies ran while one was open for 3% of the time, Pallas kernels for 45%

profile of v3, /device:TPU:0, one launch (start us, length us, event | category | flops | bytes accessed | tf_op | source)
XLA Modules:
  0.0 354.3 jit_solution(11913775268481365037)
XLA Ops:
  2.1 1.3 copy-done.19
  5.1 2.6 collective-permute-start.1
  7.7 1.4 widen.3.refs_0_.refs_4_
  9.9 3.2 copy-done.75
  13.0 3.0 own_weights.1
  17.2 4.2 %copy-done.2 = bf16[4480,1120]{0,1:T(8,128)(2,1)S(1)} copy-done((bf16[4480,1120]{0,1:T(8,128)(2,1)S(1)}, bf16[4480,1120]{0,1:T(8,128)(2,1)}, u32[]{:S(2)}) %copy-start.2) | copy-done | bytes 10035224
  21.3 9.9 %active_back.1.refs_0_ = f32[512,4480]{1,0:T(8,128)S(1)} custom-call(s32[6]{0:T(128)S(1)} %pad_add_fusion.scalars.me, bf16[512,1120]{1,0:T(8,128)(2,1)S(1)} %bitcast.74, bf16[1120,4480]{1,0:T(8,128)(2,1)S(1)} %bitcast.52), custom_call_target="tpu_custom_call" | custom-call | flops 1 | bytes 1 | tf_op jit(solution)/shard_map/active_back/pallas_call | solution.py:729
  33.6 1.3 copy-done.52
  34.9 14.0 %attend_forward.2 = (bf16[9,64,1024]{2,1,0:T(8,128)(2,1)S(1)}, bf16[6,64,1024]{2,1,0:T(8,128)(2,1)S(1)}, f32[5,64,1024]{2,1,0:T(8,128)S(1)}, bf16[1152,1024]{1,0...) custom-call(s32[6]{0:T(128)S(1)} %pad_add_fusion.scalars.me, ...), custom_call_target="tpu_custom_call" | custom-call | flops 14000000000 | bytes 1 | tf_op jit(solution)/shard_map/attend_forward/pallas_call | solution.py:134
  54.2 14.6 %attend_forward.3 = (bf16[9,64,1024]{2,1,0:T(8,128)(2,1)S(1)}, bf16[6,64,1024]{2,1,0:T(8,128)(2,1)S(1)}, f32[5,64,1024]{2,1,0:T(8,128)S(1)}, bf16[1152,1024]{1,0...) custom-call(s32[6]{0:T(128)S(1)} %pad_add_fusion.scalars.me, ...), custom_call_target="tpu_custom_call" | custom-call | flops 14000000000 | bytes 1 | tf_op jit(solution)/shard_map/attend_forward/pallas_call | solution.py:134
  73.3 2.8 second_norm.2
  77.7 2.0 collective-permute-done.11.refs_3_
  79.8 2.8 second_norm.3
  82.6 4.6 %copy-done = bf16[1120,4480]{1,0:T(8,128)(2,1)S(1)} copy-done((bf16[1120,4480]{1,0:T(8,128)(2,1)S(1)}, bf16[1120,4480]{1,0:T(8,128)(2,1)}, u32[]{:S(2)}) %copy-start) | copy-done | bytes 10035224
  87.2 15.3 %hidden_layer.1 = (bf16[512,4480]{1,0:T(8,128)(2,1)S(1)}, bf16[512,4480]{1,0:T(8,128)(2,1)S(1)}, f32[1,4480]{1,0:T(1,128)S(1)}) custom-call(s32[6]{0:T(128)S(1)} %pad_add_fusion.scalars.me, f32[512,4480]{1,0:T(8,128)S(1)} %active_back.1.refs_0_, bf16[1120,4480]{1,0:T(8,128)(2,1)S(1)} %copy-done, f32[1,4480]{1,0:T(1,128)S(1)} %reshape.84.refs_2_, ...), custom_call_target="tpu_custom_call" | custom-call | flops 1 | bytes 1 | tf_op jit(solution)/shard_map/hidden_layer/pallas_call | solution.py:729
  102.5 7.7 %down_outer.2 = bf16[2,8,144,1120]{3,2,1,0:T(8,128)(2,1)} custom-call(s32[6]{0:T(128)S(1)} %pad_add_fusion.scalars.me, bf16[2,1120,256]{2,1,0:T(8,128)(2,1)S(1)} %bitcast.54, bf16[512,4480]{1,0:T(8,128)(2,1)S(1)} %get-tuple-element.314.right.refs_0_), custom_call_target="tpu_custom_call" | custom-call | flops 1 | bytes 1 | tf_op jit(solution)/shard_map/down_outer/pallas_call | solution.py:729
  110.5 6.9 %up_outer.2 = bf16[2,8,144,1120]{3,2,1,0:T(8,128)(2,1)} custom-call(s32[6]{0:T(128)S(1)} %pad_add_fusion.scalars.me, bf16[512,4480]{1,0:T(8,128)(2,1)S(1)} %get-tuple-element.305.right.back_upper, bf16[1120,256]{1,0:T(8,128)(2,1)S(1)} %get-tuple-element.295.refs_0_, bf16[1120,256]{1,0:T(8,128)(2,1)S(1)} %get-tuple-element.296.refs_1_), custom_call_target="tpu_custom_call" | custom-call | flops 1 | bytes 1 | tf_op jit(solution)/shard_map/up_outer/pallas_call | solution.py:729
  117.4 1.8 collective-permute-done.12.refs_0_
  119.2 2.4 copy-done.10
  121.5 2.5 copy-done.11
  124.0 9.6 %down_outer.3 = (bf16[1,8,96,1120]{3,2,1,0:T(8,128)(2,1)}, bf16[1,8,96,1120]{3,2,1,0:T(8,128)(2,1)S(1)}, bf16[2,4,96,1120]{3,2,1,0:T(8,128)(2,1)}, bf16[2,4,96,1120]{3,2,1,0:T(8,128)(2,1)S(1)}) custom-call(s32[6]{0:T(128)S(1)} %pad_add_fusion.scalars.me, bf16[2,1120,256]{2,1,0:T(8,128)(2,1)S(1)} %bitcast.55, ...), custom_call_target="tpu_custom_call" | custom-call | flops 1 | bytes 1 | tf_op jit(solution)/shard_map/down_outer/pallas_call | solution.py:729
  133.7 1.3 collective-permute-start.15
  135.0 7.3 %up_outer.3 = (bf16[2,4,96,1120]{3,2,1,0:T(8,128)(2,1)}, bf16[2,4,96,1120]{3,2,1,0:T(8,128)(2,1)S(1)}, bf16[2,4,96,1120]{3,2,1,0:T(8,128)(2,1)}, bf16[2,4,96,1120]{3,2,1,0:T(8,128)(2,1)S(1)}) custom-call(s32[6]{0:T(128)S(1)} %pad_add_fusion.scalars.me, ...), custom_call_target="tpu_custom_call", output_to_operand_aliasing={{2}: (5, {}), {3}: (6, {})} | custom-call | flops 1 | bytes 1 | tf_op jit(solution)/shard_map/up_outer/pallas_call | solution.py:729
  142.3 1.6 collective-permute-start.17
  143.8 1.6 collective-permute-start.18
  145.4 3.8 %copy-done.1 = bf16[1120,4480]{1,0:T(8,128)(2,1)S(1)} copy-done((bf16[1120,4480]{1,0:T(8,128)(2,1)S(1)}, bf16[1120,4480]{1,0:T(8,128)(2,1)}, u32[]{:S(2)}) %copy-start.1) | copy-done | bytes 10035224
  149.3 13.0 %middle_back.1 = (f32[1120,512]{1,0:T(8,128)S(1)}, bf16[1120,512]{1,0:T(8,128)(2,1)S(1)}, f32[8,1120]{1,0:T(8,128)S(1)}, bf16[2,5,64,256]{3,2,1,0:T(8,128)(2,1)S...) custom-call(s32[6]{0:T(128)S(1)} %pad_add_fusion.scalars.me, ...), custom_call_target="tpu_custom_call" | custom-call | flops 1 | bytes 1 | tf_op jit(solution)/shard_map/middle_back/pallas_call | solution.py:729
  162.2 1.4 copy-done.28
  164.4 3.1 out_outer.1
  167.5 3.8 %copy-done.3 = bf16[4480,1120]{0,1:T(8,128)(2,1)S(1)} copy-done((bf16[4480,1120]{0,1:T(8,128)(2,1)S(1)}, bf16[4480,1120]{0,1:T(8,128)(2,1)}, u32[]{:S(2)}) %copy-start.3) | copy-done | bytes 10035224
  171.4 10.3 %block_output.1 = bf16[2,1120,256]{2,1,0:T(8,128)(2,1)} custom-call(s32[6]{0:T(128)S(1)} %pad_add_fusion.scalars.me, bf16[512,4480]{1,0:T(8,128)(2,1)S(1)} %get-tuple-element.314.right.refs_0_, bf16[1120,4480]{1,0:T(8,128)(2,1)S(1)} %bitcast.53, f32[1120]{0:T(1024)S(1)} %copy-done.73, f32[1120,256]{1,0:T(8,128)S(1)} %get-tuple-element.286.refs_0_.refs_3_, ...), custom_call_target="tpu_custom_call" | custom-call | flops 1 | bytes 1 | tf_op jit(solution)/shard_map/block_output/pallas_call | solution.py:729
  181.7 2.6 add_halves.17
  184.6 2.6 add_halves.18
  187.2 2.7 add_halves.19
  189.8 1.1 collective-permute-start.19
  191.4 1.4 collective-permute-start.20
  193.9 3.8 %collective-permute-done.16.refs_5_ = bf16[2,2,5,64,256]{4,3,2,1,0:T(8,128)(2,1)S(1)} collective-permute-done((bf16[2,2,5,64,256]{4,3,2,1,0:T(8,128)(2,1)S(1)}, bf16[2,2,5,64,256]{4,3,2,1,0:T(8,128)(2,1)S(1)}, u32[]{:S(2)}, u32[]{:S(2)}) %collective-permute-start.16) | collective-permute-done | bytes 655392 | tf_op jit(solution)/shard_map/ppermute | solution.py:35
  197.6 9.6 %attend_backward.4.refs_2_ = bf16[1024,576]{1,0:T(8,128)(2,1)S(1)} custom-call(s32[6]{0:T(128)S(1)} %pad_add_fusion.scalars.me, bf16[9,64,1024]{2,1,0:T(8,128)(2,1)S(1)} %copy-done.35, f32[5,64,1024]{2,1,0:T(8,128)S(1)} %copy-done.15, bf16[1,2,5,64,256]{4,3,2,1,0:T(8,128)(2,1)S(1)} %bitcast.70, bf16[1,2,5,64,256]{4,3,2,1,0:T(8,128)(2,1)S(1)} %bitcast.62, ...), custom_call_target="tpu_custom_call" | custom-call | flops 1 | bytes 1 | tf_op jit(solution)/shard_map/attend_backward/pallas_call | solution.py:134
  207.3 6.7 %attend_backward.5.refs_3_.refs_2_ = bf16[1024,384]{1,0:T(8,128)(2,1)S(1)} custom-call(s32[6]{0:T(128)S(1)} %pad_add_fusion.scalars.me, bf16[6,64,1024]{2,1,0:T(8,128)(2,1)S(1)} %copy-done.39, f32[5,64,1024]{2,1,0:T(8,128)S(1)} %copy-done.15, bf16[1,2,5,64,256]{4,3,2,1,0:T(8,128)(2,1)S(1)} %bitcast.71, bf16[1,2,5,64,256]{4,3,2,1,0:T(8,128)(2,1)S(1)} %bitcast.63, ...), custom_call_target="tpu_custom_call" | custom-call | flops 1 | bytes 1 | tf_op jit(solution)/shard_map/attend_backward/pallas_call | solution.py:134
  216.5 1.6 collective-permute-start.25
  218.2 9.6 %attend_backward.6.refs_3_.refs_2_ = bf16[1024,576]{1,0:T(8,128)(2,1)S(1)} custom-call(s32[6]{0:T(128)S(1)} %pad_add_fusion.scalars.me, bf16[9,64,1024]{2,1,0:T(8,128)(2,1)S(1)} %copy-done.33, f32[5,64,1024]{2,1,0:T(8,128)S(1)} %copy-done.13, bf16[1,2,5,64,256]{4,3,2,1,0:T(8,128)(2,1)S(1)} %bitcast.72, bf16[1,2,5,64,256]{4,3,2,1,0:T(8,128)(2,1)S(1)} %bitcast.64, ...), custom_call_target="tpu_custom_call" | custom-call | flops 1 | bytes 1 | tf_op jit(solution)/shard_map/attend_backward/pallas_call | solution.py:134
  227.8 5.7 %normed_back.2 = (bf16[1120,256]{1,0:T(8,128)(2,1)S(1)}, bf16[1120,256]{1,0:T(8,128)(2,1)S(1)}, bf16[1120,256]{1,0:T(8,128)(2,1)S(1)}, bf16[1120,256]{1,0:T(8,128)(2,1)S(1)}, f32[8,1120]{1,0:T(8,128)S(1)}) custom-call(bf16[1120,576]{1,0:T(8,128)(2,1)S(1)} %copy-done.9, bf16[1120,384]{1,0:T(8,128)(2,1)S(1)} %copy-done.23, ...), custom_call_target="tpu_custom_call" | custom-call | flops 1 | bytes 1 | tf_op jit(solution)/shard_map/normed_back/pallas_call | solution.py:134
  236.4 4.6 %mix_outer.2 = (bf16[4,80,576]{2,1,0:T(8,128)(2,1)S(1)}, bf16[4,80,576]{2,1,0:T(8,128)(2,1)S(1)}, bf16[4,64,576]{2,1,0:T(8,128)(2,1)S(1)}, bf16[4,64,576]{2,1,0:T(8,128)(2,1)S(1)}, f32[1,576]{1,0:T(1,128)S(1)}) custom-call(s32[6]{0:T(128)S(1)} %pad_add_fusion.scalars.me, bf16[1152,1024]{1,0:T(8,128)(2,1)S(1)} %get-tuple-element.368.refs_0_, ...), custom_call_target="tpu_custom_call" | custom-call | flops 1 | bytes 1 | tf_op jit(solution)/shard_map/mix_outer/pallas_call | solution.py:134
  240.9 1.6 collective-permute-start.30
  244.0 6.6 %attend_backward.7.refs_3_ = bf16[1024,384]{1,0:T(8,128)(2,1)S(1)} custom-call(s32[6]{0:T(128)S(1)} %pad_add_fusion.scalars.me, bf16[6,64,1024]{2,1,0:T(8,128)(2,1)S(1)} %copy-done.37, f32[5,64,1024]{2,1,0:T(8,128)S(1)} %copy-done.13, bf16[1,2,5,64,256]{4,3,2,1,0:T(8,128)(2,1)S(1)} %bitcast.73, bf16[1,2,5,64,256]{4,3,2,1,0:T(8,128)(2,1)S(1)} %bitcast.65, ...), custom_call_target="tpu_custom_call" | custom-call | flops 1 | bytes 1 | tf_op jit(solution)/shard_map/attend_backward/pallas_call | solution.py:134
  250.6 1.4 collective-permute-done.29.refs_1_.refs_3_
  252.5 3.0 collective-permute-done.31.refs_1_.refs_3_
  256.0 3.2 mix_outer.3
  259.2 1.6 collective-permute-start.38
  263.5 1.6 collective-permute-start.39
  265.1 4.8 %collective-permute-done.35.refs_5_.refs_7_ = bf16[2,64,576]{2,1,0:T(8,128)(2,1)S(1)} collective-permute-done((bf16[2,64,576]{2,1,0:T(8,128)(2,1)S(1)}, bf16[2,64,576]{2,1,0:T(8,128)(2,1)S(1)}, u32[]{:S(2)}, u32[]{:S(2)}) %collective-permute-start.35) | collective-permute-done | bytes 147488 | tf_op jit(solution)/shard_map/ppermute | solution.py:35
  269.9 2.5 collective-permute-start.40
  272.4 1.5 collective-permute-start.37
  273.9 5.7 %normed_back.3 = (bf16[1120,256]{1,0:T(8,128)(2,1)S(1)}, bf16[1120,256]{1,0:T(8,128)(2,1)S(1)}, bf16[1120,256]{1,0:T(8,128)(2,1)S(1)}, bf16[1120,256]{1,0:T(8,128)(2,1)S(1)}, f32[8,1120]{1,0:T(8,128)S(1)}) custom-call(bf16[1120,576]{1,0:T(8,128)(2,1)S(1)} %copy-done.9, bf16[1120,384]{1,0:T(8,128)(2,1)S(1)} %copy-done.23, ...), custom_call_target="tpu_custom_call" | custom-call | flops 1 | bytes 1 | tf_op jit(solution)/shard_map/normed_back/pallas_call | solution.py:134
  283.9 19.1 %collective-permute-done.36 = f32[4,12,140]{2,1,0:T(8,128)S(1)} collective-permute-done((f32[4,12,140]{2,1,0:T(8,128)S(1)}, f32[4,12,140]{2,1,0:T(8,128)S(1)}, u32[]{:S(2)}, u32[]{:S(2)}) %collective-permute-start.36) | collective-permute-done | bytes 26912 | tf_op jit(solution)/shard_map/ppermute | solution.py:35
  303.1 1.5 collective-permute-start.46
  305.4 2.0 collective-permute-start.42
  319.5 1.8 collective-permute-start.49
  321.3 1.2 collective-permute-start.54
  322.5 1.7 collective-permute-start.50
  328.5 4.5 %tokens_back.1 = bf16[2,1120,256]{2,1,0:T(8,128)(2,1)} custom-call(bf16[2,1120,256]{2,1,0:T(8,128)(2,1)S(1)} %bitcast.78, f32[1120]{0:T(1024)S(1)} %copy-done.74, f32[1120,512]{1,0:T(8,128)S(1)} %copy-done.29, bf16[1120,256]{1,0:T(8,128)(2,1)S(1)} %copy-done.30, bf16[1120,256]{1,0:T(8,128)(2,1)S(1)} %copy-done.59, bf16[1120,256]{1,0:T(8,128)(2,1)S(1)} %copy-done.31, ...), custom_call_target="tpu_custom_call" | custom-call | flops 1 | bytes 1 | tf_op jit(solution)/shard_map/tokens_back/pallas_call | solution.py:134
  333.3 3.2 collective-permute-done.49
  336.6 4.2 %collective-permute-done.50 = bf16[1,144,384]{2,1,0:T(8,128)(2,1)S(1)} collective-permute-done((bf16[1,144,384]{2,1,0:T(8,128)(2,1)}, bf16[1,144,384]{2,1,0:T(8,128)(2,1)S(1)}, u32[]{:S(2)}, u32[]{:S(2)}) %collective-permute-start.50) | collective-permute-done | bytes 110624 | tf_op jit(solution)/shard_map/ppermute | solution.py:35
  343.8 6.0 %collective-permute-done.52.refs_2_ = bf16[144,960]{1,0:T(8,128)(2,1)S(1)} collective-permute-done((bf16[144,960]{1,0:T(8,128)(2,1)S(1)}, bf16[144,960]{1,0:T(8,128)(2,1)S(1)}, u32[]{:S(2)}, u32[]{:S(2)}) %collective-permute-start.52) | collective-permute-done | bytes 276512 | tf_op jit(solution)/shard_map/ppermute | solution.py:35
  (308 shorter events, 56.5 us)
Async XLA Ops:
  4.6 27.5 %collective-permute-start = (bf16[1152,256]{1,0:T(8,128)(2,1)S(1)}, bf16[1152,256]{1,0:T(8,128)(2,1)S(1)}, u32[]{:S(2)}, u32[]{:S(2)}) collective-permute-start(bf16[1152,256]{1,0:T(8,128)(2,1)S(1)} %widen.2.refs_0_.refs_4_), channel_id=1, source_target_pairs={{0,1},{1,0},{2,3},{3,2},{4,5},{5,4},{6,7},{7,6},{8,9},{9,8},{10,11... | collective-permute-start | bytes 1769480 | tf_op jit(solution)/shard_map/ppermute | solution.py:35
  5.1 26.1 %collective-permute-start.1 = (bf16[1152,256]{1,0:T(8,128)(2,1)S(1)}, bf16[1152,256]{1,0:T(8,128)(2,1)}, u32[]{:S(2)}, u32[]{:S(2)}) collective-permute-start(bf16[1152,256]{1,0:T(8,128)(2,1)S(1)} %widen.2.refs_0_.refs_4_), channel_id=1, source_target_pairs={{0,2},{1,3},{2,0},{3,1},{4,6},{5,7},{6,4},{7,5},{8,10},{9,11},{10,... | collective-permute-start | bytes 1769480 | tf_op jit(solution)/shard_map/ppermute | solution.py:35
  31.2 2.4 collective-permute-start.2
  31.7 22.4 %collective-permute-start.6 = (bf16[1152,256]{1,0:T(8,128)(2,1)}, bf16[1152,256]{1,0:T(8,128)(2,1)S(1)}, u32[]{:S(2)}, u32[]{:S(2)}) collective-permute-start(bf16[1152,256]{1,0:T(8,128)(2,1)} %widen.3.refs_0_.refs_4_), channel_id=1, source_target_pairs={{0,1},{1,0},{2,3},{3,2},{4,5},{5,4},{6,7},{7,6},{8,9},{9,8},{10,11... | collective-permute-start | bytes 1769480 | tf_op jit(solution)/shard_map/ppermute | solution.py:35
  31.8 20.1 %collective-permute-start.7 = (bf16[1152,256]{1,0:T(8,128)(2,1)}, bf16[1152,256]{1,0:T(8,128)(2,1)S(1)}, u32[]{:S(2)}, u32[]{:S(2)}) collective-permute-start(bf16[1152,256]{1,0:T(8,128)(2,1)} %widen.3.refs_0_.refs_4_), channel_id=1, source_target_pairs={{0,2},{1,3},{2,0},{3,1},{4,6},{5,7},{6,4},{7,5},{8,10},{9,11},{10,... | collective-permute-start | bytes 1769480 | tf_op jit(solution)/shard_map/ppermute | solution.py:35
  51.9 16.9 %copy-start.44 = (bf16[1152,256]{1,0:T(8,128)(2,1)}, bf16[1152,256]{1,0:T(8,128)(2,1)S(1)}, u32[]{:S(2)}) copy-start(bf16[1152,256]{1,0:T(8,128)(2,1)S(1)} %collective-permute-done.7.refs_2_.refs_6_) | copy-start | bytes 1769476
  52.0 2.2 collective-permute-start.8
  52.3 20.5 %collective-permute-start.3 = (bf16[280,256]{1,0:T(8,128)(2,1)S(1)}, bf16[280,256]{1,0:T(8,128)(2,1)S(1)}, u32[]{:S(2)}, u32[]{:S(2)}) collective-permute-start(bf16[280,256]{1,0:T(8,128)(2,1)S(1)} %get-tuple-element.266), channel_id=1, source_target_pairs={{0,1},{1,0},{2,3},{3,2},{4,5},{5,4},{6,7},{7,6},{8,9},{9,8},{10,11... | collective-permute-start | bytes 430088 | tf_op jit(solution)/shard_map/ppermute | solution.py:35
  52.5 20.8 %collective-permute-start.4 = (bf16[280,256]{1,0:T(8,128)(2,1)S(1)}, bf16[280,256]{1,0:T(8,128)(2,1)S(1)}, u32[]{:S(2)}, u32[]{:S(2)}) collective-permute-start(bf16[280,256]{1,0:T(8,128)(2,1)S(1)} %get-tuple-element.267), channel_id=1, source_target_pairs={{0,2},{1,3},{2,0},{3,1},{4,6},{5,7},{6,4},{7,5},{8,10},{9,11},{10,... | collective-permute-start | bytes 430088 | tf_op jit(solution)/shard_map/ppermute | solution.py:35
  53.6 19.6 %copy-start.20 = (bf16[2,256,1120]{1,2,0:T(8,128)(2,1)S(1)}, bf16[2,256,1120]{1,2,0:T(8,128)(2,1)}, u32[]{:S(2)}) copy-start(bf16[2,256,1120]{1,2,0:T(8,128)(2,1)} %param.21) | copy-start | bytes 3440644
  53.6 19.7 %collective-permute-start.5 = (bf16[280,256]{1,0:T(8,128)(2,1)S(1)}, bf16[280,256]{1,0:T(8,128)(2,1)S(1)}, u32[]{:S(2)}, u32[]{:S(2)}) collective-permute-start(bf16[280,256]{1,0:T(8,128)(2,1)S(1)} %get-tuple-element.268), channel_id=1, source_target_pairs={{0,3},{1,2},{2,1},{3,0},{4,7},{5,6},{6,5},{7,4},{8,11},{9,10},{10,... | collective-permute-start | bytes 430088 | tf_op jit(solution)/shard_map/ppermute | solution.py:35
  54.2 19.1 %copy-start.4 = (bf16[1120,1120]{1,0:T(8,128)(2,1)S(1)}, bf16[1120,1120]{1,0:T(8,128)(2,1)}, u32[]{:S(2)}) copy-start(bf16[1120,1120]{1,0:T(8,128)(2,1)} %weight.5) | copy-start | bytes 7526404
  71.0 6.8 %collective-permute-start.10 = (bf16[280,256]{1,0:T(8,128)(2,1)S(1)}, bf16[280,256]{1,0:T(8,128)(2,1)S(1)}, u32[]{:S(2)}, u32[]{:S(2)}) collective-permute-start(bf16[280,256]{1,0:T(8,128)(2,1)S(1)} %get-tuple-element.284), channel_id=1, source_target_pairs={{0,2},{1,3},{2,0},{3,1},{4,6},{5,7},{6,4},{7,5},{8,10},{9,11},{10,... | collective-permute-start | bytes 430088 | tf_op jit(solution)/shard_map/ppermute | solution.py:35
  71.9 7.8 %collective-permute-start.11 = (bf16[280,256]{1,0:T(8,128)(2,1)S(1)}, bf16[280,256]{1,0:T(8,128)(2,1)S(1)}, u32[]{:S(2)}, u32[]{:S(2)}) collective-permute-start(bf16[280,256]{1,0:T(8,128)(2,1)S(1)} %get-tuple-element.285), channel_id=1, source_target_pairs={{0,3},{1,2},{2,1},{3,0},{4,7},{5,6},{6,5},{7,4},{8,11},{9,10},{10,... | collective-permute-start | bytes 430088 | tf_op jit(solution)/shard_map/ppermute | solution.py:35
  72.8 6.9 %collective-permute-start.9 = (bf16[280,256]{1,0:T(8,128)(2,1)S(1)}, bf16[280,256]{1,0:T(8,128)(2,1)S(1)}, u32[]{:S(2)}, u32[]{:S(2)}) collective-permute-start(bf16[280,256]{1,0:T(8,128)(2,1)S(1)} %get-tuple-element.283), channel_id=1, source_target_pairs={{0,1},{1,0},{2,3},{3,2},{4,5},{5,4},{6,7},{7,6},{8,9},{9,8},{10,11... | collective-permute-start | bytes 430088 | tf_op jit(solution)/shard_map/ppermute | solution.py:35
  77.7 32.7 %copy-start.24 = (bf16[1120,256]{1,0:T(8,128)(2,1)}, bf16[1120,256]{1,0:T(8,128)(2,1)S(1)}, u32[]{:S(2)}) copy-start(bf16[1120,256]{1,0:T(8,128)(2,1)S(1)} %get-tuple-element.295.refs_0_) | copy-start | bytes 1720324
  82.5 20.0 %copy-start.16 = (f32[1120,256]{1,0:T(8,128)}, f32[1120,256]{1,0:T(8,128)S(1)}, u32[]{:S(2)}) copy-start(f32[1120,256]{1,0:T(8,128)S(1)} %get-tuple-element.306.refs_1_.refs_4_) | copy-start | bytes 3440644
  82.5 20.0 %copy-start.62 = (bf16[1120,256]{1,0:T(8,128)(2,1)}, bf16[1120,256]{1,0:T(8,128)(2,1)S(1)}, u32[]{:S(2)}) copy-start(bf16[1120,256]{1,0:T(8,128)(2,1)S(1)} %get-tuple-element.313.refs_1_) | copy-start | bytes 1720324
  82.5 27.9 %copy-start.26 = (bf16[1120,256]{1,0:T(8,128)(2,1)}, bf16[1120,256]{1,0:T(8,128)(2,1)S(1)}, u32[]{:S(2)}) copy-start(bf16[1120,256]{1,0:T(8,128)(2,1)S(1)} %get-tuple-element.296.refs_1_) | copy-start | bytes 1720324
  110.2 9.0 %collective-permute-start.12 = (bf16[2,8,144,1120]{3,2,1,0:T(8,128)(2,1)}, bf16[2,8,144,1120]{3,2,1,0:T(8,128)(2,1)S(1)}, u32[]{:S(2)}, u32[]{:S(2)}) collective-permute-start(bf16[2,8,144,1120]{3,2,1,0:T(8,128)(2,1)} %down_outer.2), channel_id=1, source_target_pairs={{0,1},{1,0},{2,3},{3,2},{4,5},{5,4},{6,7},{7,6},{8,9},{9,8},{10,11... | collective-permute-start | bytes 15482888 | tf_op jit(solution)/shard_map/ppermute | solution.py:35
  117.4 17.6 %collective-permute-start.13 = (bf16[2,8,144,1120]{3,2,1,0:T(8,128)(2,1)}, bf16[2,8,144,1120]{3,2,1,0:T(8,128)(2,1)S(1)}, u32[]{:S(2)}, u32[]{:S(2)}) collective-permute-start(bf16[2,8,144,1120]{3,2,1,0:T(8,128)(2,1)} %up_outer.2), channel_id=1, source_target_pairs={{0,1},{1,0},{2,3},{3,2},{4,5},{5,4},{6,7},{7,6},{8,9},{9,8},{10,11... | collective-permute-start | bytes 15482888 | tf_op jit(solution)/shard_map/ppermute | solution.py:35
  133.7 48.0 %collective-permute-start.15 = (bf16[8,96,1120]{2,1,0:T(8,128)(2,1)}, bf16[8,96,1120]{2,1,0:T(8,128)(2,1)}, u32[]{:S(2)}, u32[]{:S(2)}) collective-permute-start(bf16[8,96,1120]{2,1,0:T(8,128)(2,1)} %bitcast.12), channel_id=1, source_target_pairs={{0,2},{1,3},{2,0},{3,1},{4,6},{5,7},{6,4},{7,5},{8,10},{9,11},{10,... | collective-permute-start | bytes 5160968 | tf_op jit(solution)/shard_map/ppermute | solution.py:35
  142.3 42.1 %collective-permute-start.17 = (bf16[8,96,1120]{2,1,0:T(8,128)(2,1)}, bf16[8,96,1120]{2,1,0:T(8,128)(2,1)}, u32[]{:S(2)}, u32[]{:S(2)}) collective-permute-start(bf16[8,96,1120]{2,1,0:T(8,128)(2,1)} %bitcast.14), channel_id=1, source_target_pairs={{0,8},{4,12},{8,0},{12,4},{16,24},{20,28},{24,16},{28,20},{1,9},{5... | collective-permute-start | bytes 5160968 | tf_op jit(solution)/shard_map/ppermute | solution.py:35
  143.8 40.7 %collective-permute-start.18 = (bf16[8,96,1120]{2,1,0:T(8,128)(2,1)}, bf16[8,96,1120]{2,1,0:T(8,128)(2,1)}, u32[]{:S(2)}, u32[]{:S(2)}) collective-permute-start(bf16[8,96,1120]{2,1,0:T(8,128)(2,1)} %bitcast.15), channel_id=1, source_target_pairs={{0,4},{4,0},{8,12},{12,8},{16,20},{20,16},{24,28},{28,24},{1,5},{5... | collective-permute-start | bytes 5160968 | tf_op jit(solution)/shard_map/ppermute | solution.py:35
  163.6 29.6 %collective-permute-start.14 = (bf16[2,2,5,64,256]{4,3,2,1,0:T(8,128)(2,1)S(1)}, bf16[2,2,5,64,256]{4,3,2,1,0:T(8,128)(2,1)S(1)}, u32[]{:S(2)}, u32[]{:S(2)}) collective-permute-start(bf16[2,2,5,64,256]{4,3,2,1,0:T(8,128)(2,1)S(1)} %get-tuple-element.310), channel_id=1, source_target_pairs={{0,2},{1,3},{2,0},{3,1},{4,6},{5,7},{6,4},{7,5},{8,10},{9,11},{10,... | collective-permute-start | bytes 1966088 | tf_op jit(solution)/shard_map/ppermute | solution.py:35
  189.8 24.1 %collective-permute-start.19 = (bf16[4,96,1120]{2,1,0:T(8,128)(2,1)S(1)}, bf16[4,96,1120]{2,1,0:T(8,128)(2,1)S(1)}, u32[]{:S(2)}, u32[]{:S(2)}) collective-permute-start(bf16[4,96,1120]{2,1,0:T(8,128)(2,1)S(1)} %get-tuple-element.338), channel_id=1, source_target_pairs={{0,2},{1,3},{2,0},{3,1},{4,6},{5,7},{6,4},{7,5},{8,10},{9,11},{10,... | collective-permute-start | bytes 2580488 | tf_op jit(solution)/shard_map/ppermute | solution.py:35
  191.0 23.0 %collective-permute-start.21 = (bf16[4,96,1120]{2,1,0:T(8,128)(2,1)S(1)}, bf16[4,96,1120]{2,1,0:T(8,128)(2,1)S(1)}, u32[]{:S(2)}, u32[]{:S(2)}) collective-permute-start(bf16[4,96,1120]{2,1,0:T(8,128)(2,1)S(1)} %get-tuple-element.340), channel_id=1, source_target_pairs={{0,8},{4,12},{8,0},{12,4},{16,24},{20,28},{24,16},{28,20},{1,9},{5... | collective-permute-start | bytes 2580488 | tf_op jit(solution)/shard_map/ppermute | solution.py:35
  191.4 22.5 %collective-permute-start.20 = (bf16[4,96,1120]{2,1,0:T(8,128)(2,1)S(1)}, bf16[4,96,1120]{2,1,0:T(8,128)(2,1)S(1)}, u32[]{:S(2)}, u32[]{:S(2)}) collective-permute-start(bf16[4,96,1120]{2,1,0:T(8,128)(2,1)S(1)} %get-tuple-element.339), channel_id=1, source_target_pairs={{0,4},{4,0},{8,12},{12,8},{16,20},{20,16},{24,28},{28,24},{1,5},{5... | collective-permute-start | bytes 2580488 | tf_op jit(solution)/shard_map/ppermute | solution.py:35
  193.1 41.3 %collective-permute-start.24 = (bf16[16,80,576]{2,1,0:T(8,128)(2,1)S(1)}, bf16[16,80,576]{2,1,0:T(8,128)(2,1)S(1)}, u32[]{:S(2)}, u32[]{:S(2)}) collective-permute-start(bf16[16,80,576]{2,1,0:T(8,128)(2,1)S(1)} %bitcast.79), channel_id=1, source_target_pairs={{0,1},{1,0},{2,3},{3,2},{4,5},{5,4},{6,7},{7,6},{8,9},{9,8},{10,11... | collective-permute-start | bytes 4423688 | tf_op jit(solution)/shard_map/ppermute | solution.py:35
  193.3 4.3 %collective-permute-start.16 = (bf16[2,2,5,64,256]{4,3,2,1,0:T(8,128)(2,1)S(1)}, bf16[2,2,5,64,256]{4,3,2,1,0:T(8,128)(2,1)S(1)}, u32[]{:S(2)}, u32[]{:S(2)}) collective-permute-start(bf16[2,2,5,64,256]{4,3,2,1,0:T(8,128)(2,1)S(1)} %pad_maximum_fusion.1), channel_id=1, source_target_pairs={{0,1},{1,0},{2,3},{3,2},{4,5},{5,4},{6,7},{7,6},{8,9},{9,8},{10,11... | collective-permute-start | bytes 1966088 | tf_op jit(solution)/shard_map/ppermute | solution.py:35
  214.9 18.7 %collective-permute-start.27 = (bf16[2,96,1120]{2,1,0:T(8,128)(2,1)S(1)}, bf16[2,96,1120]{2,1,0:T(8,128)(2,1)S(1)}, u32[]{:S(2)}, u32[]{:S(2)}) collective-permute-start(bf16[2,96,1120]{2,1,0:T(8,128)(2,1)S(1)} %get-tuple-element.372), channel_id=1, source_target_pairs={{0,4},{4,0},{8,12},{12,8},{16,20},{20,16},{24,28},{28,24},{1,5},{5... | collective-permute-start | bytes 1290248 | tf_op jit(solution)/shard_map/ppermute | solution.py:35
  215.6 18.5 %collective-permute-start.26 = (bf16[2,96,1120]{2,1,0:T(8,128)(2,1)S(1)}, bf16[2,96,1120]{2,1,0:T(8,128)(2,1)S(1)}, u32[]{:S(2)}, u32[]{:S(2)}) collective-permute-start(bf16[2,96,1120]{2,1,0:T(8,128)(2,1)S(1)} %get-tuple-element.371), channel_id=1, source_target_pairs={{0,2},{1,3},{2,0},{3,1},{4,6},{5,7},{6,4},{7,5},{8,10},{9,11},{10,... | collective-permute-start | bytes 1290248 | tf_op jit(solution)/shard_map/ppermute | solution.py:35
  216.5 17.6 %collective-permute-start.25 = (bf16[2,96,1120]{2,1,0:T(8,128)(2,1)S(1)}, bf16[2,96,1120]{2,1,0:T(8,128)(2,1)S(1)}, u32[]{:S(2)}, u32[]{:S(2)}) collective-permute-start(bf16[2,96,1120]{2,1,0:T(8,128)(2,1)S(1)} %get-tuple-element.370), channel_id=1, source_target_pairs={{0,8},{4,12},{8,0},{12,4},{16,24},{20,28},{24,16},{28,20},{1,9},{5... | collective-permute-start | bytes 1290248 | tf_op jit(solution)/shard_map/ppermute | solution.py:35
  233.5 9.5 %collective-permute-start.22 = (bf16[1120,256]{1,0:T(8,128)(2,1)S(1)}, bf16[1120,256]{1,0:T(8,128)(2,1)S(1)}, u32[]{:S(2)}, u32[]{:S(2)}) collective-permute-start(bf16[1120,256]{1,0:T(8,128)(2,1)S(1)} %get-tuple-element.365), channel_id=1, source_target_pairs={{0,1},{1,0},{2,3},{3,2},{4,5},{5,4},{6,7},{7,6},{8,9},{9,8},{10,11... | collective-permute-start | bytes 1720328 | tf_op jit(solution)/shard_map/ppermute | solution.py:35
  233.6 9.4 %collective-permute-start.23 = (bf16[1120,256]{1,0:T(8,128)(2,1)S(1)}, bf16[1120,256]{1,0:T(8,128)(2,1)S(1)}, u32[]{:S(2)}, u32[]{:S(2)}) collective-permute-start(bf16[1120,256]{1,0:T(8,128)(2,1)S(1)} %get-tuple-element.367), channel_id=1, source_target_pairs={{0,1},{1,0},{2,3},{3,2},{4,5},{5,4},{6,7},{7,6},{8,9},{9,8},{10,11... | collective-permute-start | bytes 1720328 | tf_op jit(solution)/shard_map/ppermute | solution.py:35
  235.3 20.2 %collective-permute-start.31 = (bf16[8,80,576]{2,1,0:T(8,128)(2,1)S(1)}, bf16[8,80,576]{2,1,0:T(8,128)(2,1)S(1)}, u32[]{:S(2)}, u32[]{:S(2)}) collective-permute-start(bf16[8,80,576]{2,1,0:T(8,128)(2,1)S(1)} %get-tuple-element.404), channel_id=1, source_target_pairs={{0,2},{1,3},{2,0},{3,1},{4,6},{5,7},{6,4},{7,5},{8,10},{9,11},{10,... | collective-permute-start | bytes 2211848 | tf_op jit(solution)/shard_map/ppermute | solution.py:35
  240.9 11.5 %collective-permute-start.30 = (bf16[4,80,576]{2,1,0:T(8,128)(2,1)S(1)}, bf16[4,80,576]{2,1,0:T(8,128)(2,1)S(1)}, u32[]{:S(2)}, u32[]{:S(2)}) collective-permute-start(bf16[4,80,576]{2,1,0:T(8,128)(2,1)S(1)} %get-tuple-element.389), channel_id=1, source_target_pairs={{0,4},{4,0},{8,12},{12,8},{16,20},{20,16},{24,28},{28,24},{1,5},{5... | collective-permute-start | bytes 1105928 | tf_op jit(solution)/shard_map/ppermute | solution.py:35
  242.5 9.4 %collective-permute-start.29 = (bf16[4,64,576]{2,1,0:T(8,128)(2,1)S(1)}, bf16[4,64,576]{2,1,0:T(8,128)(2,1)S(1)}, u32[]{:S(2)}, u32[]{:S(2)}) collective-permute-start(bf16[4,64,576]{2,1,0:T(8,128)(2,1)S(1)} %get-tuple-element.395), channel_id=1, source_target_pairs={{0,8},{4,12},{8,0},{12,4},{16,24},{20,28},{24,16},{28,20},{1,9},{5... | collective-permute-start | bytes 884744 | tf_op jit(solution)/shard_map/ppermute | solution.py:35
  259.2 20.5 %collective-permute-start.38 = (bf16[4,80,384]{2,1,0:T(8,128)(2,1)S(1)}, bf16[4,80,384]{2,1,0:T(8,128)(2,1)S(1)}, u32[]{:S(2)}, u32[]{:S(2)}) collective-permute-start(bf16[4,80,384]{2,1,0:T(8,128)(2,1)S(1)} %get-tuple-element.410), channel_id=1, source_target_pairs={{0,4},{4,0},{8,12},{12,8},{16,20},{20,16},{24,28},{28,24},{1,5},{5... | collective-permute-start | bytes 737288 | tf_op jit(solution)/shard_map/ppermute | solution.py:35
  261.0 11.4 %collective-permute-start.34 = (bf16[2,80,576]{2,1,0:T(8,128)(2,1)S(1)}, bf16[2,80,576]{2,1,0:T(8,128)(2,1)S(1)}, u32[]{:S(2)}, u32[]{:S(2)}) collective-permute-start(bf16[2,80,576]{2,1,0:T(8,128)(2,1)S(1)} %get-tuple-element.423), channel_id=1, source_target_pairs={{0,8},{4,12},{8,0},{12,4},{16,24},{20,28},{24,16},{28,20},{1,9},{5... | collective-permute-start | bytes 552968 | tf_op jit(solution)/shard_map/ppermute | solution.py:35
  261.7 20.6 %collective-permute-start.28 = (bf16[1120,256]{1,0:T(8,128)(2,1)S(1)}, bf16[1120,256]{1,0:T(8,128)(2,1)S(1)}, u32[]{:S(2)}, u32[]{:S(2)}) collective-permute-start(bf16[1120,256]{1,0:T(8,128)(2,1)S(1)} %add_convert_fusion.2), channel_id=1, source_target_pairs={{0,2},{1,3},{2,0},{3,1},{4,6},{5,7},{6,4},{7,5},{8,10},{9,11},{10,... | collective-permute-start | bytes 1720328 | tf_op jit(solution)/shard_map/ppermute | solution.py:35
  262.8 7.1 %collective-permute-start.35 = (bf16[2,64,576]{2,1,0:T(8,128)(2,1)S(1)}, bf16[2,64,576]{2,1,0:T(8,128)(2,1)S(1)}, u32[]{:S(2)}, u32[]{:S(2)}) collective-permute-start(bf16[2,64,576]{2,1,0:T(8,128)(2,1)S(1)} %get-tuple-element.424), channel_id=1, source_target_pairs={{0,4},{4,0},{8,12},{12,8},{16,20},{20,16},{24,28},{28,24},{1,5},{5... | collective-permute-start | bytes 442376 | tf_op jit(solution)/shard_map/ppermute | solution.py:35
  263.5 16.2 %collective-permute-start.39 = (bf16[4,64,384]{2,1,0:T(8,128)(2,1)S(1)}, bf16[4,64,384]{2,1,0:T(8,128)(2,1)S(1)}, u32[]{:S(2)}, u32[]{:S(2)}) collective-permute-start(bf16[4,64,384]{2,1,0:T(8,128)(2,1)S(1)} %get-tuple-element.434), channel_id=1, source_target_pairs={{0,8},{4,12},{8,0},{12,4},{16,24},{20,28},{24,16},{28,20},{1,9},{5... | collective-permute-start | bytes 589832 | tf_op jit(solution)/shard_map/ppermute | solution.py:35
  269.9 34.8 %collective-permute-start.40 = (bf16[1,288,1120]{2,1,0:T(8,128)(2,1)S(1)}, bf16[1,288,1120]{2,1,0:T(8,128)(2,1)S(1)}, u32[]{:S(2)}, u32[]{:S(2)}) collective-permute-start(bf16[1,288,1120]{2,1,0:T(8,128)(2,1)S(1)} %get-tuple-element.457), channel_id=1, source_target_pairs={{0,16},{4,20},{8,24},{12,28},{16,0},{20,4},{24,8},{28,12},{1,17},{... | collective-permute-start | bytes 1935368 | tf_op jit(solution)/shard_map/ppermute | solution.py:35
  272.4 9.4 %collective-permute-start.37 = (bf16[4,80,576]{2,1,0:T(8,128)(2,1)S(1)}, bf16[4,80,576]{2,1,0:T(8,128)(2,1)S(1)}, u32[]{:S(2)}, u32[]{:S(2)}) collective-permute-start(bf16[4,80,576]{2,1,0:T(8,128)(2,1)S(1)} %get-tuple-element.433), channel_id=1, source_target_pairs={{0,4},{4,0},{8,12},{12,8},{16,20},{20,16},{24,28},{28,24},{1,5},{5... | collective-permute-start | bytes 1105928 | tf_op jit(solution)/shard_map/ppermute | solution.py:35
  279.7 25.7 %collective-permute-start.32 = (bf16[1120,256]{1,0:T(8,128)(2,1)S(1)}, bf16[1120,256]{1,0:T(8,128)(2,1)S(1)}, u32[]{:S(2)}, u32[]{:S(2)}) collective-permute-start(bf16[1120,256]{1,0:T(8,128)(2,1)S(1)} %get-tuple-element.420), channel_id=1, source_target_pairs={{0,1},{1,0},{2,3},{3,2},{4,5},{5,4},{6,7},{7,6},{8,9},{9,8},{10,11... | collective-permute-start | bytes 1720328 | tf_op jit(solution)/shard_map/ppermute | solution.py:35
  279.7 27.7 %collective-permute-start.33 = (bf16[1120,256]{1,0:T(8,128)(2,1)S(1)}, bf16[1120,256]{1,0:T(8,128)(2,1)S(1)}, u32[]{:S(2)}, u32[]{:S(2)}) collective-permute-start(bf16[1120,256]{1,0:T(8,128)(2,1)S(1)} %get-tuple-element.422), channel_id=1, source_target_pairs={{0,1},{1,0},{2,3},{3,2},{4,5},{5,4},{6,7},{7,6},{8,9},{9,8},{10,11... | collective-permute-start | bytes 1720328 | tf_op jit(solution)/shard_map/ppermute | solution.py:35
  281.8 21.2 %collective-permute-start.36 = (f32[4,12,140]{2,1,0:T(8,128)S(1)}, f32[4,12,140]{2,1,0:T(8,128)S(1)}, u32[]{:S(2)}, u32[]{:S(2)}) collective-permute-start(f32[4,12,140]{2,1,0:T(8,128)S(1)} %get-tuple-element.505), channel_id=1, source_target_pairs={{0,16},{4,20},{8,24},{12,28},{16,0},{20,4},{24,8},{28,12},{1,17},{... | collective-permute-start | bytes 80648 | tf_op jit(solution)/shard_map/ppermute | solution.py:35
  283.0 28.2 %collective-permute-start.44 = (bf16[2,80,576]{2,1,0:T(8,128)(2,1)S(1)}, bf16[2,80,576]{2,1,0:T(8,128)(2,1)S(1)}, u32[]{:S(2)}, u32[]{:S(2)}) collective-permute-start(bf16[2,80,576]{2,1,0:T(8,128)(2,1)S(1)} %get-tuple-element.464), channel_id=1, source_target_pairs={{0,8},{4,12},{8,0},{12,4},{16,24},{20,28},{24,16},{28,20},{1,9},{5... | collective-permute-start | bytes 552968 | tf_op jit(solution)/shard_map/ppermute | solution.py:35
  303.1 8.2 %collective-permute-start.46 = (bf16[2,64,384]{2,1,0:T(8,128)(2,1)S(1)}, bf16[2,64,384]{2,1,0:T(8,128)(2,1)S(1)}, u32[]{:S(2)}, u32[]{:S(2)}) collective-permute-start(bf16[2,64,384]{2,1,0:T(8,128)(2,1)S(1)} %get-tuple-element.466), channel_id=1, source_target_pairs={{0,4},{4,0},{8,12},{12,8},{16,20},{20,16},{24,28},{28,24},{1,5},{5... | collective-permute-start | bytes 294920 | tf_op jit(solution)/shard_map/ppermute | solution.py:35
  305.4 5.8 %collective-permute-start.45 = (bf16[2,80,384]{2,1,0:T(8,128)(2,1)S(1)}, bf16[2,80,384]{2,1,0:T(8,128)(2,1)S(1)}, u32[]{:S(2)}, u32[]{:S(2)}) collective-permute-start(bf16[2,80,384]{2,1,0:T(8,128)(2,1)S(1)} %get-tuple-element.465), channel_id=1, source_target_pairs={{0,8},{4,12},{8,0},{12,4},{16,24},{20,28},{24,16},{28,20},{1,9},{5... | collective-permute-start | bytes 368648 | tf_op jit(solution)/shard_map/ppermute | solution.py:35
  305.4 5.2 %collective-permute-start.42 = (f32[2,12,140]{2,1,0:T(8,128)S(1)}, f32[2,12,140]{2,1,0:T(8,128)S(1)}, u32[]{:S(2)}, u32[]{:S(2)}) collective-permute-start(f32[2,12,140]{2,1,0:T(8,128)S(1)} %get-tuple-element.507), channel_id=1, source_target_pairs={{0,8},{4,12},{8,0},{12,4},{16,24},{20,28},{24,16},{28,20},{1,9},{5... | collective-permute-start | bytes 40328 | tf_op jit(solution)/shard_map/ppermute | solution.py:35
  308.4 16.9 %copy-start.21 = (bf16[2,256,1120]{1,2,0:T(8,128)(2,1)S(1)}, bf16[2,256,1120]{1,2,0:T(8,128)(2,1)}, u32[]{:S(2)}) copy-start(bf16[2,256,1120]{1,2,0:T(8,128)(2,1)} %param.21) | copy-start | bytes 3440644
  308.4 16.9 %copy-start.29 = (f32[1120,512]{1,0:T(8,128)S(1)}, f32[1120,512]{1,0:T(8,128)}, u32[]{:S(2)}) copy-start(f32[1120,512]{1,0:T(8,128)} %copy-done.28) | copy-start | bytes 6881284
  308.4 16.9 %collective-permute-start.41 = (bf16[1120,256]{1,0:T(8,128)(2,1)}, bf16[1120,256]{1,0:T(8,128)(2,1)}, u32[]{:S(2)}, u32[]{:S(2)}) collective-permute-start(bf16[1120,256]{1,0:T(8,128)(2,1)} %add_convert_fusion), channel_id=1, source_target_pairs={{0,2},{1,3},{2,0},{3,1},{4,6},{5,7},{6,4},{7,5},{8,10},{9,11},{10,... | collective-permute-start | bytes 1720328 | tf_op jit(solution)/shard_map/ppermute | solution.py:35
  310.6 3.8 %collective-permute-start.43 = (f32[1,12,140]{2,1,0:T(8,128)S(1)}, f32[1,12,140]{2,1,0:T(8,128)S(1)}, u32[]{:S(2)}, u32[]{:S(2)}) collective-permute-start(f32[1,12,140]{2,1,0:T(8,128)S(1)} %get-tuple-element.509), channel_id=1, source_target_pairs={{0,4},{4,0},{8,12},{12,8},{16,20},{20,16},{24,28},{28,24},{1,5},{5... | collective-permute-start | bytes 20168 | tf_op jit(solution)/shard_map/ppermute | solution.py:35
  314.4 9.8 %collective-permute-start.47 = (f32[1,12,140]{2,1,0:T(8,128)S(1)}, f32[1,12,140]{2,1,0:T(8,128)S(1)}, u32[]{:S(2)}, u32[]{:S(2)}) collective-permute-start(f32[1,12,140]{2,1,0:T(8,128)S(1)} %add.63), channel_id=1, source_target_pairs={{0,1},{1,0},{2,3},{3,2},{4,5},{5,4},{6,7},{7,6},{8,9},{9,8},{10,11... | collective-permute-start | bytes 20168 | tf_op jit(solution)/shard_map/ppermute | solution.py:35
  319.5 17.0 %collective-permute-start.49 = (bf16[1,144,576]{2,1,0:T(8,128)(2,1)}, bf16[1,144,576]{2,1,0:T(8,128)(2,1)S(1)}, u32[]{:S(2)}, u32[]{:S(2)}) collective-permute-start(bf16[1,144,576]{2,1,0:T(8,128)(2,1)} %copy-done.76), channel_id=1, source_target_pairs={{0,16},{4,20},{8,24},{12,28},{16,0},{20,4},{24,8},{28,12},{1,17},{... | collective-permute-start | bytes 497672 | tf_op jit(solution)/shard_map/ppermute | solution.py:35
  321.3 21.3 %collective-permute-start.54 = (bf16[1,80,576]{2,1,0:T(8,128)(2,1)}, bf16[1,80,576]{2,1,0:T(8,128)(2,1)S(1)}, u32[]{:S(2)}, u32[]{:S(2)}) collective-permute-start(bf16[1,80,576]{2,1,0:T(8,128)(2,1)} %copy-done.78), channel_id=1, source_target_pairs={{0,16},{4,20},{8,24},{12,28},{16,0},{20,4},{24,8},{28,12},{1,17},{... | collective-permute-start | bytes 276488 | tf_op jit(solution)/shard_map/ppermute | solution.py:35
  322.5 18.3 %collective-permute-start.50 = (bf16[1,144,384]{2,1,0:T(8,128)(2,1)}, bf16[1,144,384]{2,1,0:T(8,128)(2,1)S(1)}, u32[]{:S(2)}, u32[]{:S(2)}) collective-permute-start(bf16[1,144,384]{2,1,0:T(8,128)(2,1)} %copy-done.77), channel_id=1, source_target_pairs={{0,16},{4,20},{8,24},{12,28},{16,0},{20,4},{24,8},{28,12},{1,17},{... | collective-permute-start | bytes 331784 | tf_op jit(solution)/shard_map/ppermute | solution.py:35
  324.2 17.8 %collective-permute-start.48 = (f32[1,12,140]{2,1,0:T(8,128)S(1)}, f32[1,12,140]{2,1,0:T(8,128)S(1)}, u32[]{:S(2)}, u32[]{:S(2)}) collective-permute-start(f32[1,12,140]{2,1,0:T(8,128)S(1)} %add.64), channel_id=1, source_target_pairs={{0,2},{1,3},{2,0},{3,1},{4,6},{5,7},{6,4},{7,5},{8,10},{9,11},{10,... | collective-permute-start | bytes 20168 | tf_op jit(solution)/shard_map/ppermute | solution.py:35
  341.0 8.8 %collective-permute-start.52 = (bf16[144,960]{1,0:T(8,128)(2,1)S(1)}, bf16[144,960]{1,0:T(8,128)(2,1)S(1)}, u32[]{:S(2)}, u32[]{:S(2)}) collective-permute-start(bf16[144,960]{1,0:T(8,128)(2,1)S(1)} %maximum_maximum_fusion.refs_0_), channel_id=1, source_target_pairs={{0,2},{1,3},{2,0},{3,1},{4,6},{5,7},{6,4},{7,5},{8,10},{9,11},{10,... | collective-permute-start | bytes 829448 | tf_op jit(solution)/shard_map/ppermute | solution.py:35
  342.0 10.2 %collective-permute-start.51 = (bf16[144,960]{1,0:T(8,128)(2,1)S(1)}, bf16[144,960]{1,0:T(8,128)(2,1)S(1)}, u32[]{:S(2)}, u32[]{:S(2)}) collective-permute-start(bf16[144,960]{1,0:T(8,128)(2,1)S(1)} %maximum_maximum_fusion.refs_0_), channel_id=1, source_target_pairs={{0,1},{1,0},{2,3},{3,2},{4,5},{5,4},{6,7},{7,6},{8,9},{9,8},{10,11... | collective-permute-start | bytes 829448 | tf_op jit(solution)/shard_map/ppermute | solution.py:35
  349.8 2.4 collective-permute-start.53
  (79 other events, 412.5 us)

commit v4 on v3

--- a/solution.py
+++ b/solution.py
@@ -1490,24 +1490,24 @@
         final = c == cells_here - 1
         last = attend_group(c, 0, last)
         if final:
+            last = advance(running, last)
+            last = out_part.step(last)
             for earlier in range(c):
                 last = normed_reduction(earlier, last)
-            last = advance(running, last)
-            last = out_part.step(last)
             parts, last = mix_reductions(0, last)
             mix_parts.append(parts)
-            for part in back_normed:
-                last = part.step(last)
         last = attend_group(c, 1, last)
         if c == 0:
             last = advance(running, last)
+    for part in back_normed:
+        last = part.step(last)
     while len(out_part.order) >= len(cell_bits):
         last = out_part.step(last)
     parts, last = mix_reductions(1, last)
     mix_parts.append(parts + [out_part])
     last = advance(mix_parts[0], last)
-    last = normed_reduction(cells_here - 1, last)
     done = [part.got for part in running if part.labels and not part.order]
+    last = normed_reduction(cells_here - 1, (last, done))
     vectors = VectorSum(
         vector_blocks(
             scalars,
@@ -1525,7 +1525,7 @@
     last = advance(mix_parts[1], (last, [part.got for part in back_normed[:-1]]))
     last = vectors.step(last)
     last = advance(mix_parts[0], last)
-    last = back_normed[-1].step((last, done))
+    last = back_normed[-1].step(last)
     last = vectors.step(last)
     last = advance(mix_parts[1], last)
     last = vectors.step(last)

time: 361 us -> 357 us (0.989)
  Pallas kernels: 191 us -> 186 us
    unnamed x177 -> x173, local copies, waits for them, and re-layouts: 45.5 us -> 41.5 us
  transfers between devices with their start and end apart: 55 -> 55, of which waited for: 16 -> 17; matrix products, arithmetic and copies ran while one was open for 3% -> 4% of each run, Pallas kernels for 45% -> 43%
where the time goes in v4:
time: 357 us; the launch traced here: 351 us
  Pallas kernels  186 us (52%)
  waiting for transfers between devices  54.6 us (15%)
  starting transfers between devices  48.2 us (14%)
  local copies, waits for them, and re-layouts  46.7 us (13%)
  other arithmetic  9.05 us (3%)
  between operations  6.19 us (2%)
    pallas_call x17, Pallas kernels, no_grid_call(): pl.pallas_call(body, out_shape=out_shape, in_specs=in_specs, out_specs=ja...  96.8 us
    pallas_call x10, Pallas kernels, grid_call(): pl.pallas_call(body, out_shape=out_shape, grid_spec=pltpu.PrefetchScalarG...  79.6 us
    ppermute x55, waiting for transfers between devices, swap_with(): return lax.ppermute(array, axis, [(i, i ^ bit) for i in range(count)])  54.6 us
    ppermute x55, starting transfers between devices, swap_with(): return lax.ppermute(array, axis, [(i, i ^ bit) for i in range(count)])  48.2 us
    unnamed x173, local copies, waits for them, and re-layouts  41.5 us
    pallas_call x17, Pallas kernels, add_halves(): pl.pallas_call(partial(add_halves_kernel, len(pairs)), out_shape=(shape,...  9.38 us
  transfers between devices with their start and end apart: 55, of which 17 were waited for; matrix products, arithmetic and copies ran while one was open for 4% of the time, Pallas kernels for 43%

profile of v4, /device:TPU:0, one launch (start us, length us, event | category | flops | bytes accessed | tf_op | source)
XLA Modules:
  0.0 350.5 jit_solution(17350689597448652881)
XLA Ops:
  4.0 1.4 widen.2.refs_0_.refs_4_
  5.9 2.5 collective-permute-start.1
  10.5 3.2 copy-done.72
  13.7 3.0 own_weights.1
  17.8 4.2 %copy-done.2 = bf16[4480,1120]{0,1:T(8,128)(2,1)S(1)} copy-done((bf16[4480,1120]{0,1:T(8,128)(2,1)S(1)}, bf16[4480,1120]{0,1:T(8,128)(2,1)}, u32[]{:S(2)}) %copy-start.2) | copy-done | bytes 10035224
  22.0 9.9 %active_back.1.refs_0_ = f32[512,4480]{1,0:T(8,128)S(1)} custom-call(s32[6]{0:T(128)S(1)} %pad_add_fusion.scalars.me, bf16[512,1120]{1,0:T(8,128)(2,1)S(1)} %bitcast.76, bf16[1120,4480]{1,0:T(8,128)(2,1)S(1)} %bitcast.52), custom_call_target="tpu_custom_call" | custom-call | flops 1 | bytes 1 | tf_op jit(solution)/shard_map/active_back/pallas_call | solution.py:729
  32.8 1.5 collective-permute-done.2.refs_3_.refs_7_
  34.3 14.5 %attend_forward.2 = (bf16[9,64,1024]{2,1,0:T(8,128)(2,1)S(1)}, bf16[6,64,1024]{2,1,0:T(8,128)(2,1)S(1)}, f32[5,64,1024]{2,1,0:T(8,128)S(1)}, bf16[1152,1024]{1,0...) custom-call(s32[6]{0:T(128)S(1)} %pad_add_fusion.scalars.me, ...), custom_call_target="tpu_custom_call" | custom-call | flops 14000000000 | bytes 1 | tf_op jit(solution)/shard_map/attend_forward/pallas_call | solution.py:134
  48.9 1.4 copy-done.6
  54.1 1.4 collective-permute-start.5
  55.6 13.7 %attend_forward.3 = (bf16[9,64,1024]{2,1,0:T(8,128)(2,1)S(1)}, bf16[6,64,1024]{2,1,0:T(8,128)(2,1)S(1)}, f32[5,64,1024]{2,1,0:T(8,128)S(1)}, bf16[1152,1024]{1,0...) custom-call(s32[6]{0:T(128)S(1)} %pad_add_fusion.scalars.me, ...), custom_call_target="tpu_custom_call" | custom-call | flops 14000000000 | bytes 1 | tf_op jit(solution)/shard_map/attend_forward/pallas_call | solution.py:134
  71.7 1.5 collective-permute-start.11
  73.7 2.8 second_norm.2
  80.1 2.7 second_norm.3
  82.9 4.5 %copy-done = bf16[1120,4480]{1,0:T(8,128)(2,1)S(1)} copy-done((bf16[1120,4480]{1,0:T(8,128)(2,1)S(1)}, bf16[1120,4480]{1,0:T(8,128)(2,1)}, u32[]{:S(2)}) %copy-start) | copy-done | bytes 10035224
  87.4 15.3 %hidden_layer.1 = (bf16[512,4480]{1,0:T(8,128)(2,1)S(1)}, bf16[512,4480]{1,0:T(8,128)(2,1)S(1)}, f32[1,4480]{1,0:T(1,128)S(1)}) custom-call(s32[6]{0:T(128)S(1)} %pad_add_fusion.scalars.me, f32[512,4480]{1,0:T(8,128)S(1)} %active_back.1.refs_0_, bf16[1120,4480]{1,0:T(8,128)(2,1)S(1)} %copy-done, f32[1,4480]{1,0:T(1,128)S(1)} %reshape.84.refs_2_, ...), custom_call_target="tpu_custom_call" | custom-call | flops 1 | bytes 1 | tf_op jit(solution)/shard_map/hidden_layer/pallas_call | solution.py:729
  102.7 6.9 %down_outer.2 = bf16[2,8,144,1120]{3,2,1,0:T(8,128)(2,1)S(1)} custom-call(s32[6]{0:T(128)S(1)} %pad_add_fusion.scalars.me, bf16[2,1120,256]{2,1,0:T(8,128)(2,1)S(1)} %bitcast.56, bf16[512,4480]{1,0:T(8,128)(2,1)S(1)} %get-tuple-element.314.right.refs_0_), custom_call_target="tpu_custom_call" | custom-call | flops 1 | bytes 1 | tf_op jit(solution)/shard_map/down_outer/pallas_call | solution.py:729
  110.0 5.3 %up_outer.2 = bf16[2,8,144,1120]{3,2,1,0:T(8,128)(2,1)S(1)} custom-call(s32[6]{0:T(128)S(1)} %pad_add_fusion.scalars.me, bf16[512,4480]{1,0:T(8,128)(2,1)S(1)} %get-tuple-element.305.right.back_upper, bf16[1120,256]{1,0:T(8,128)(2,1)S(1)} %copy-done.30, bf16[1120,256]{1,0:T(8,128)(2,1)S(1)} %get-tuple-element.296.refs_1_), custom_call_target="tpu_custom_call" | custom-call | flops 1 | bytes 1 | tf_op jit(solution)/shard_map/up_outer/pallas_call | solution.py:729
  115.4 3.0 collective-permute-done.12.refs_0_
  118.5 9.6 %down_outer.3 = (bf16[1,8,96,1120]{3,2,1,0:T(8,128)(2,1)}, bf16[1,8,96,1120]{3,2,1,0:T(8,128)(2,1)S(1)}, bf16[2,4,96,1120]{3,2,1,0:T(8,128)(2,1)}, bf16[2,4,96,1120]{3,2,1,0:T(8,128)(2,1)S(1)}) custom-call(s32[6]{0:T(128)S(1)} %pad_add_fusion.scalars.me, bf16[2,1120,256]{2,1,0:T(8,128)(2,1)S(1)} %bitcast.57, ...), custom_call_target="tpu_custom_call" | custom-call | flops 1 | bytes 1 | tf_op jit(solution)/shard_map/down_outer/pallas_call | solution.py:729
  128.1 1.3 copy-done.10
  129.6 7.2 %up_outer.3 = (bf16[2,4,96,1120]{3,2,1,0:T(8,128)(2,1)}, bf16[2,4,96,1120]{3,2,1,0:T(8,128)(2,1)S(1)}, bf16[2,4,96,1120]{3,2,1,0:T(8,128)(2,1)}, bf16[2,4,96,1120]{3,2,1,0:T(8,128)(2,1)S(1)}) custom-call(s32[6]{0:T(128)S(1)} %pad_add_fusion.scalars.me, ...), custom_call_target="tpu_custom_call", output_to_operand_aliasing={{2}: (5, {}), {3}: (6, {})} | custom-call | flops 1 | bytes 1 | tf_op jit(solution)/shard_map/up_outer/pallas_call | solution.py:729
  138.1 2.1 collective-permute-start.17
  140.2 1.6 collective-permute-start.18
  141.8 3.8 %copy-done.1 = bf16[1120,4480]{1,0:T(8,128)(2,1)S(1)} copy-done((bf16[1120,4480]{1,0:T(8,128)(2,1)S(1)}, bf16[1120,4480]{1,0:T(8,128)(2,1)}, u32[]{:S(2)}) %copy-start.1) | copy-done | bytes 10035224
  145.7 13.0 %middle_back.1 = (f32[1120,512]{1,0:T(8,128)S(1)}, bf16[1120,512]{1,0:T(8,128)(2,1)S(1)}, f32[8,1120]{1,0:T(8,128)S(1)}, bf16[2,5,64,256]{3,2,1,0:T(8,128)(2,1)S...) custom-call(s32[6]{0:T(128)S(1)} %pad_add_fusion.scalars.me, ...), custom_call_target="tpu_custom_call" | custom-call | flops 1 | bytes 1 | tf_op jit(solution)/shard_map/middle_back/pallas_call | solution.py:729
  158.6 1.5 copy-done.31
  161.3 3.1 out_outer.1
  165.1 10.3 %block_output.1 = bf16[2,1120,256]{2,1,0:T(8,128)(2,1)} custom-call(s32[6]{0:T(128)S(1)} %pad_add_fusion.scalars.me, bf16[512,4480]{1,0:T(8,128)(2,1)S(1)} %get-tuple-element.314.right.refs_0_, bf16[1120,4480]{1,0:T(8,128)(2,1)S(1)} %bitcast.55, f32[1120]{0:T(1024)S(1)} %copy-done.69, f32[1120,256]{1,0:T(8,128)S(1)} %copy-done.21, f32[1120,256]{1,0:T(8,128)S(1)} %copy-done.23), custom_call_target="tpu_custom_call" | custom-call | flops 1 | bytes 1 | tf_op jit(solution)/shard_map/block_output/pallas_call | solution.py:729
  175.5 2.7 add_halves.17
  179.4 1.6 collective-permute-done.18.refs_1_.refs_3_
  181.0 2.6 add_halves.18
  184.1 1.5 collective-permute-start.22
  186.1 1.5 collective-permute-start.20
  187.8 2.1 collective-permute-done.16.refs_5_
  189.9 9.6 %attend_backward.4.refs_2_ = bf16[1024,576]{1,0:T(8,128)(2,1)S(1)} custom-call(s32[6]{0:T(128)S(1)} %pad_add_fusion.scalars.me, bf16[9,64,1024]{2,1,0:T(8,128)(2,1)S(1)} %copy-done.38, f32[5,64,1024]{2,1,0:T(8,128)S(1)} %copy-done.19, bf16[1,2,5,64,256]{4,3,2,1,0:T(8,128)(2,1)S(1)} %bitcast.72, bf16[1,2,5,64,256]{4,3,2,1,0:T(8,128)(2,1)S(1)} %bitcast.64, ...), custom_call_target="tpu_custom_call" | custom-call | flops 1 | bytes 1 | tf_op jit(solution)/shard_map/attend_backward/pallas_call | solution.py:134
  199.5 6.7 %attend_backward.5.refs_3_.refs_2_ = bf16[1024,384]{1,0:T(8,128)(2,1)S(1)} custom-call(s32[6]{0:T(128)S(1)} %pad_add_fusion.scalars.me, bf16[6,64,1024]{2,1,0:T(8,128)(2,1)S(1)} %copy-done.42, f32[5,64,1024]{2,1,0:T(8,128)S(1)} %copy-done.19, bf16[1,2,5,64,256]{4,3,2,1,0:T(8,128)(2,1)S(1)} %bitcast.73, bf16[1,2,5,64,256]{4,3,2,1,0:T(8,128)(2,1)S(1)} %bitcast.65, ...), custom_call_target="tpu_custom_call" | custom-call | flops 1 | bytes 1 | tf_op jit(solution)/shard_map/attend_backward/pallas_call | solution.py:134
  207.2 1.6 collective-permute-start.25
  209.3 1.4 collective-permute-start.23
  210.7 9.4 %attend_backward.6.refs_3_.refs_2_ = bf16[1024,576]{1,0:T(8,128)(2,1)S(1)} custom-call(s32[6]{0:T(128)S(1)} %pad_add_fusion.scalars.me, bf16[9,64,1024]{2,1,0:T(8,128)(2,1)S(1)} %copy-done.36, f32[5,64,1024]{2,1,0:T(8,128)S(1)} %copy-done.17, bf16[1,2,5,64,256]{4,3,2,1,0:T(8,128)(2,1)S(1)} %bitcast.74, bf16[1,2,5,64,256]{4,3,2,1,0:T(8,128)(2,1)S(1)} %bitcast.66, ...), custom_call_target="tpu_custom_call" | custom-call | flops 1 | bytes 1 | tf_op jit(solution)/shard_map/attend_backward/pallas_call | solution.py:134
  223.1 6.2 %normed_back.2 = (bf16[1120,256]{1,0:T(8,128)(2,1)S(1)}, bf16[1120,256]{1,0:T(8,128)(2,1)S(1)}, bf16[1120,256]{1,0:T(8,128)(2,1)S(1)}, bf16[1120,256]{1,0:T(8,128)(2,1)S(1)}, f32[8,1120]{1,0:T(8,128)S(1)}) custom-call(bf16[1120,576]{1,0:T(8,128)(2,1)S(1)} %copy-done.15, bf16[1120,384]{1,0:T(8,128)(2,1)S(1)} %copy-done.28, ...), custom_call_target="tpu_custom_call" | custom-call | flops 1 | bytes 1 | tf_op jit(solution)/shard_map/normed_back/pallas_call | solution.py:134
  229.9 4.6 %mix_outer.2 = (bf16[4,80,576]{2,1,0:T(8,128)(2,1)S(1)}, bf16[4,80,576]{2,1,0:T(8,128)(2,1)S(1)}, bf16[4,64,576]{2,1,0:T(8,128)(2,1)S(1)}, bf16[4,64,576]{2,1,0:T(8,128)(2,1)S(1)}, f32[1,576]{1,0:T(1,128)S(1)}) custom-call(s32[6]{0:T(128)S(1)} %pad_add_fusion.scalars.me, bf16[1152,1024]{1,0:T(8,128)(2,1)S(1)} %copy-done.7, bf16[1152,1024]{1,0:T(8,128)(2,1)S(1)} %copy-done.9, ...), custom_call_target="tpu_custom_call" | custom-call | flops 1 | bytes 1 | tf_op jit(solution)/shard_map/mix_outer/pallas_call | solution.py:134
  235.7 1.6 collective-permute-start.29
  237.3 1.4 collective-permute-start.31
  238.7 6.6 %attend_backward.7.refs_3_ = bf16[1024,384]{1,0:T(8,128)(2,1)S(1)} custom-call(s32[6]{0:T(128)S(1)} %pad_add_fusion.scalars.me, bf16[6,64,1024]{2,1,0:T(8,128)(2,1)S(1)} %copy-done.40, f32[5,64,1024]{2,1,0:T(8,128)S(1)} %copy-done.17, bf16[1,2,5,64,256]{4,3,2,1,0:T(8,128)(2,1)S(1)} %bitcast.75, bf16[1,2,5,64,256]{4,3,2,1,0:T(8,128)(2,1)S(1)} %bitcast.67, ...), custom_call_target="tpu_custom_call" | custom-call | flops 1 | bytes 1 | tf_op jit(solution)/shard_map/attend_backward/pallas_call | solution.py:134
  245.3 2.6 collective-permute-start.32
  250.3 8.2 %collective-permute-done.31.refs_1_.refs_3_ = bf16[8,80,576]{2,1,0:T(8,128)(2,1)S(1)} collective-permute-done((bf16[8,80,576]{2,1,0:T(8,128)(2,1)S(1)}, bf16[8,80,576]{2,1,0:T(8,128)(2,1)S(1)}, u32[]{:S(2)}, u32[]{:S(2)}) %collective-permute-start.31) | collective-permute-done | bytes 737312 | tf_op jit(solution)/shard_map/ppermute | solution.py:35
  259.0 3.2 mix_outer.3
  265.1 11.5 %collective-permute-done.32 = bf16[1,288,1120]{2,1,0:T(8,128)(2,1)S(1)} collective-permute-done((bf16[1,288,1120]{2,1,0:T(8,128)(2,1)S(1)}, bf16[1,288,1120]{2,1,0:T(8,128)(2,1)S(1)}, u32[]{:S(2)}, u32[]{:S(2)}) %collective-permute-start.32) | collective-permute-done | bytes 645152 | tf_op jit(solution)/shard_map/ppermute | solution.py:35
  277.2 4.6 %normed_back.3 = (bf16[1120,256]{1,0:T(8,128)(2,1)S(1)}, bf16[1120,256]{1,0:T(8,128)(2,1)S(1)}, bf16[1120,256]{1,0:T(8,128)(2,1)S(1)}, bf16[1120,256]{1,0:T(8,128)(2,1)S(1)}, f32[8,1120]{1,0:T(8,128)S(1)}) custom-call(bf16[1120,576]{1,0:T(8,128)(2,1)S(1)} %copy-done.15, bf16[1120,384]{1,0:T(8,128)(2,1)S(1)} %copy-done.28, ...), custom_call_target="tpu_custom_call" | custom-call | flops 1 | bytes 1 | tf_op jit(solution)/shard_map/normed_back/pallas_call | solution.py:134
  282.3 2.1 collective-permute-done.40.refs_1_.refs_3_
  285.7 7.1 %collective-permute-done.39.refs_1_.refs_3_ = bf16[4,80,384]{2,1,0:T(8,128)(2,1)S(1)} collective-permute-done((bf16[4,80,384]{2,1,0:T(8,128)(2,1)S(1)}, bf16[4,80,384]{2,1,0:T(8,128)(2,1)S(1)}, u32[]{:S(2)}, u32[]{:S(2)}) %collective-permute-start.39) | collective-permute-done | bytes 245792 | tf_op jit(solution)/shard_map/ppermute | solution.py:35
  293.6 3.5 collective-permute-start.44
  299.4 1.5 collective-permute-start.42
  303.5 1.5 collective-permute-done.42
  315.7 1.4 collective-permute-start.49
  317.1 1.6 collective-permute-start.54
  318.7 1.3 collective-permute-start.50
  320.8 1.3 collective-permute-start.48
  326.0 4.6 %tokens_back.1 = bf16[2,1120,256]{2,1,0:T(8,128)(2,1)} custom-call(bf16[2,1120,256]{2,1,0:T(8,128)(2,1)S(1)} %bitcast.80, f32[1120]{0:T(1024)S(1)} %copy-done.71, f32[1120,512]{1,0:T(8,128)S(1)} %copy-done.32, bf16[1120,256]{1,0:T(8,128)(2,1)S(1)} %copy-done.33, bf16[1120,256]{1,0:T(8,128)(2,1)S(1)} %copy-done.57, bf16[1120,256]{1,0:T(8,128)(2,1)S(1)} %copy-done.34, ...), custom_call_target="tpu_custom_call" | custom-call | flops 1 | bytes 1 | tf_op jit(solution)/shard_map/tokens_back/pallas_call | solution.py:134
  330.8 1.9 collective-permute-done.49
  332.8 4.2 %collective-permute-done.50 = bf16[1,144,384]{2,1,0:T(8,128)(2,1)S(1)} collective-permute-done((bf16[1,144,384]{2,1,0:T(8,128)(2,1)}, bf16[1,144,384]{2,1,0:T(8,128)(2,1)S(1)}, u32[]{:S(2)}, u32[]{:S(2)}) %collective-permute-start.50) | collective-permute-done | bytes 110624 | tf_op jit(solution)/shard_map/ppermute | solution.py:35
  337.2 1.7 collective-permute-start.52
  340.7 5.3 %collective-permute-done.52.refs_2_ = bf16[144,960]{1,0:T(8,128)(2,1)S(1)} collective-permute-done((bf16[144,960]{1,0:T(8,128)(2,1)S(1)}, bf16[144,960]{1,0:T(8,128)(2,1)S(1)}, u32[]{:S(2)}, u32[]{:S(2)}) %collective-permute-start.52) | collective-permute-done | bytes 276512 | tf_op jit(solution)/shard_map/ppermute | solution.py:35
  (305 shorter events, 61.8 us)
Async XLA Ops:
  5.4 27.4 %collective-permute-start = (bf16[1152,256]{1,0:T(8,128)(2,1)}, bf16[1152,256]{1,0:T(8,128)(2,1)}, u32[]{:S(2)}, u32[]{:S(2)}) collective-permute-start(bf16[1152,256]{1,0:T(8,128)(2,1)} %widen.2.refs_0_.refs_4_), channel_id=1, source_target_pairs={{0,1},{1,0},{2,3},{3,2},{4,5},{5,4},{6,7},{7,6},{8,9},{9,8},{10,11... | collective-permute-start | bytes 1769480 | tf_op jit(solution)/shard_map/ppermute | solution.py:35
  5.9 26.0 %collective-permute-start.1 = (bf16[1152,256]{1,0:T(8,128)(2,1)}, bf16[1152,256]{1,0:T(8,128)(2,1)}, u32[]{:S(2)}, u32[]{:S(2)}) collective-permute-start(bf16[1152,256]{1,0:T(8,128)(2,1)} %widen.2.refs_0_.refs_4_), channel_id=1, source_target_pairs={{0,2},{1,3},{2,0},{3,1},{4,6},{5,7},{6,4},{7,5},{8,10},{9,11},{10,... | collective-permute-start | bytes 1769480 | tf_op jit(solution)/shard_map/ppermute | solution.py:35
  31.9 2.4 collective-permute-start.2
  32.5 23.1 %collective-permute-start.6 = (bf16[1152,256]{1,0:T(8,128)(2,1)S(1)}, bf16[1152,256]{1,0:T(8,128)(2,1)S(1)}, u32[]{:S(2)}, u32[]{:S(2)}) collective-permute-start(bf16[1152,256]{1,0:T(8,128)(2,1)S(1)} %copy-done.46), channel_id=1, source_target_pairs={{0,1},{1,0},{2,3},{3,2},{4,5},{5,4},{6,7},{7,6},{8,9},{9,8},{10,11... | collective-permute-start | bytes 1769480 | tf_op jit(solution)/shard_map/ppermute | solution.py:35
  32.6 20.8 %collective-permute-start.7 = (bf16[1152,256]{1,0:T(8,128)(2,1)S(1)}, bf16[1152,256]{1,0:T(8,128)(2,1)S(1)}, u32[]{:S(2)}, u32[]{:S(2)}) collective-permute-start(bf16[1152,256]{1,0:T(8,128)(2,1)S(1)} %copy-done.46), channel_id=1, source_target_pairs={{0,2},{1,3},{2,0},{3,1},{4,6},{5,7},{6,4},{7,5},{8,10},{9,11},{10,... | collective-permute-start | bytes 1769480 | tf_op jit(solution)/shard_map/ppermute | solution.py:35
  53.3 15.9 %copy-start.50 = (bf16[1152,256]{1,0:T(8,128)(2,1)}, bf16[1152,256]{1,0:T(8,128)(2,1)S(1)}, u32[]{:S(2)}) copy-start(bf16[1152,256]{1,0:T(8,128)(2,1)S(1)} %collective-permute-done.7.refs_2_.refs_6_) | copy-start | bytes 1769476
  53.3 2.3 collective-permute-start.8
  53.7 19.5 %collective-permute-start.3 = (bf16[280,256]{1,0:T(8,128)(2,1)S(1)}, bf16[280,256]{1,0:T(8,128)(2,1)S(1)}, u32[]{:S(2)}, u32[]{:S(2)}) collective-permute-start(bf16[280,256]{1,0:T(8,128)(2,1)S(1)} %get-tuple-element.266), channel_id=1, source_target_pairs={{0,1},{1,0},{2,3},{3,2},{4,5},{5,4},{6,7},{7,6},{8,9},{9,8},{10,11... | collective-permute-start | bytes 430088 | tf_op jit(solution)/shard_map/ppermute | solution.py:35
  53.8 19.8 %collective-permute-start.4 = (bf16[280,256]{1,0:T(8,128)(2,1)S(1)}, bf16[280,256]{1,0:T(8,128)(2,1)S(1)}, u32[]{:S(2)}, u32[]{:S(2)}) collective-permute-start(bf16[280,256]{1,0:T(8,128)(2,1)S(1)} %get-tuple-element.267), channel_id=1, source_target_pairs={{0,2},{1,3},{2,0},{3,1},{4,6},{5,7},{6,4},{7,5},{8,10},{9,11},{10,... | collective-permute-start | bytes 430088 | tf_op jit(solution)/shard_map/ppermute | solution.py:35
  54.1 19.4 %copy-start.25 = (bf16[2,256,1120]{1,2,0:T(8,128)(2,1)S(1)}, bf16[2,256,1120]{1,2,0:T(8,128)(2,1)}, u32[]{:S(2)}) copy-start(bf16[2,256,1120]{1,2,0:T(8,128)(2,1)} %param.21) | copy-start | bytes 3440644
  54.1 19.5 %collective-permute-start.5 = (bf16[280,256]{1,0:T(8,128)(2,1)S(1)}, bf16[280,256]{1,0:T(8,128)(2,1)S(1)}, u32[]{:S(2)}, u32[]{:S(2)}) collective-permute-start(bf16[280,256]{1,0:T(8,128)(2,1)S(1)} %get-tuple-element.268), channel_id=1, source_target_pairs={{0,3},{1,2},{2,1},{3,0},{4,7},{5,6},{6,5},{7,4},{8,11},{9,10},{10,... | collective-permute-start | bytes 430088 | tf_op jit(solution)/shard_map/ppermute | solution.py:35
  55.6 18.1 %copy-start.3 = (bf16[1120,1120]{1,0:T(8,128)(2,1)S(1)}, bf16[1120,1120]{1,0:T(8,128)(2,1)}, u32[]{:S(2)}) copy-start(bf16[1120,1120]{1,0:T(8,128)(2,1)} %weight.5) | copy-start | bytes 7526404
  71.3 7.8 %collective-permute-start.10 = (bf16[280,256]{1,0:T(8,128)(2,1)S(1)}, bf16[280,256]{1,0:T(8,128)(2,1)S(1)}, u32[]{:S(2)}, u32[]{:S(2)}) collective-permute-start(bf16[280,256]{1,0:T(8,128)(2,1)S(1)} %get-tuple-element.284), channel_id=1, source_target_pairs={{0,2},{1,3},{2,0},{3,1},{4,6},{5,7},{6,4},{7,5},{8,10},{9,11},{10,... | collective-permute-start | bytes 430088 | tf_op jit(solution)/shard_map/ppermute | solution.py:35
  71.7 8.4 %collective-permute-start.11 = (bf16[280,256]{1,0:T(8,128)(2,1)S(1)}, bf16[280,256]{1,0:T(8,128)(2,1)S(1)}, u32[]{:S(2)}, u32[]{:S(2)}) collective-permute-start(bf16[280,256]{1,0:T(8,128)(2,1)S(1)} %get-tuple-element.285), channel_id=1, source_target_pairs={{0,3},{1,2},{2,1},{3,0},{4,7},{5,6},{6,5},{7,4},{8,11},{9,10},{10,... | collective-permute-start | bytes 430088 | tf_op jit(solution)/shard_map/ppermute | solution.py:35
  73.2 6.9 %collective-permute-start.9 = (bf16[280,256]{1,0:T(8,128)(2,1)S(1)}, bf16[280,256]{1,0:T(8,128)(2,1)S(1)}, u32[]{:S(2)}, u32[]{:S(2)}) collective-permute-start(bf16[280,256]{1,0:T(8,128)(2,1)S(1)} %get-tuple-element.283), channel_id=1, source_target_pairs={{0,1},{1,0},{2,3},{3,2},{4,5},{5,4},{6,7},{7,6},{8,9},{9,8},{10,11... | collective-permute-start | bytes 430088 | tf_op jit(solution)/shard_map/ppermute | solution.py:35
  82.9 19.8 %copy-start.22 = (f32[1120,256]{1,0:T(8,128)}, f32[1120,256]{1,0:T(8,128)S(1)}, u32[]{:S(2)}) copy-start(f32[1120,256]{1,0:T(8,128)S(1)} %get-tuple-element.306.refs_1_.refs_4_) | copy-start | bytes 3440644
  82.9 19.8 %copy-start.60 = (bf16[1120,256]{1,0:T(8,128)(2,1)}, bf16[1120,256]{1,0:T(8,128)(2,1)S(1)}, u32[]{:S(2)}) copy-start(bf16[1120,256]{1,0:T(8,128)(2,1)S(1)} %get-tuple-element.313.refs_1_) | copy-start | bytes 1720324
  109.6 8.8 %collective-permute-start.12 = (bf16[2,8,144,1120]{3,2,1,0:T(8,128)(2,1)S(1)}, bf16[2,8,144,1120]{3,2,1,0:T(8,128)(2,1)S(1)}, u32[]{:S(2)}, u32[]{:S(2)}) collective-permute-start(bf16[2,8,144,1120]{3,2,1,0:T(8,128)(2,1)S(1)} %down_outer.2), channel_id=1, source_target_pairs={{0,1},{1,0},{2,3},{3,2},{4,5},{5,4},{6,7},{7,6},{8,9},{9,8},{10,11... | collective-permute-start | bytes 15482888 | tf_op jit(solution)/shard_map/ppermute | solution.py:35
  115.3 14.2 %collective-permute-start.13 = (bf16[2,8,144,1120]{3,2,1,0:T(8,128)(2,1)S(1)}, bf16[2,8,144,1120]{3,2,1,0:T(8,128)(2,1)S(1)}, u32[]{:S(2)}, u32[]{:S(2)}) collective-permute-start(bf16[2,8,144,1120]{3,2,1,0:T(8,128)(2,1)S(1)} %up_outer.2), channel_id=1, source_target_pairs={{0,1},{1,0},{2,3},{3,2},{4,5},{5,4},{6,7},{7,6},{8,9},{9,8},{10,11... | collective-permute-start | bytes 15482888 | tf_op jit(solution)/shard_map/ppermute | solution.py:35
  129.4 46.1 %collective-permute-start.15 = (bf16[8,96,1120]{2,1,0:T(8,128)(2,1)}, bf16[8,96,1120]{2,1,0:T(8,128)(2,1)}, u32[]{:S(2)}, u32[]{:S(2)}) collective-permute-start(bf16[8,96,1120]{2,1,0:T(8,128)(2,1)} %bitcast.12), channel_id=1, source_target_pairs={{0,2},{1,3},{2,0},{3,1},{4,6},{5,7},{6,4},{7,5},{8,10},{9,11},{10,... | collective-permute-start | bytes 5160968 | tf_op jit(solution)/shard_map/ppermute | solution.py:35
  138.1 41.3 %collective-permute-start.17 = (bf16[8,96,1120]{2,1,0:T(8,128)(2,1)}, bf16[8,96,1120]{2,1,0:T(8,128)(2,1)S(1)}, u32[]{:S(2)}, u32[]{:S(2)}) collective-permute-start(bf16[8,96,1120]{2,1,0:T(8,128)(2,1)} %bitcast.14), channel_id=1, source_target_pairs={{0,8},{4,12},{8,0},{12,4},{16,24},{20,28},{24,16},{28,20},{1,9},{5... | collective-permute-start | bytes 5160968 | tf_op jit(solution)/shard_map/ppermute | solution.py:35
  140.2 40.7 %collective-permute-start.18 = (bf16[8,96,1120]{2,1,0:T(8,128)(2,1)}, bf16[8,96,1120]{2,1,0:T(8,128)(2,1)}, u32[]{:S(2)}, u32[]{:S(2)}) collective-permute-start(bf16[8,96,1120]{2,1,0:T(8,128)(2,1)} %bitcast.15), channel_id=1, source_target_pairs={{0,4},{4,0},{8,12},{12,8},{16,20},{20,16},{24,28},{28,24},{1,5},{5... | collective-permute-start | bytes 5160968 | tf_op jit(solution)/shard_map/ppermute | solution.py:35
  145.7 19.2 %slice-start = ((s8[10035200]{0:T(1024)(128)(4,1)}), s8[4194304]{0:T(1024)(128)(4,1)S(1)}, s32[]{:S(2)}) async-start(s8[10035200]{0:T(1024)(128)(4,1)} %bitcast.53), calls=%async_computation | async-start | bytes 8388608
  145.7 19.2 %slice-start.1 = ((s8[10035200]{0:T(1024)(128)(4,1)}), s8[1646592]{0:T(1024)(128)(4,1)S(1)}, s32[]{:S(2)}) async-start(s8[10035200]{0:T(1024)(128)(4,1)} %bitcast.53), calls=%async_computation.1 | async-start | bytes 3293184
  160.1 27.5 %collective-permute-start.14 = (bf16[2,2,5,64,256]{4,3,2,1,0:T(8,128)(2,1)S(1)}, bf16[2,2,5,64,256]{4,3,2,1,0:T(8,128)(2,1)S(1)}, u32[]{:S(2)}, u32[]{:S(2)}) collective-permute-start(bf16[2,2,5,64,256]{4,3,2,1,0:T(8,128)(2,1)S(1)} %get-tuple-element.310), channel_id=1, source_target_pairs={{0,2},{1,3},{2,0},{3,1},{4,6},{5,7},{6,4},{7,5},{8,10},{9,11},{10,... | collective-permute-start | bytes 1966088 | tf_op jit(solution)/shard_map/ppermute | solution.py:35
  164.7 56.6 %collective-permute-start.19 = (bf16[16,80,576]{2,1,0:T(8,128)(2,1)S(1)}, bf16[16,80,576]{2,1,0:T(8,128)(2,1)S(1)}, u32[]{:S(2)}, u32[]{:S(2)}) collective-permute-start(bf16[16,80,576]{2,1,0:T(8,128)(2,1)S(1)} %bitcast.81), channel_id=1, source_target_pairs={{0,1},{1,0},{2,3},{3,2},{4,5},{5,4},{6,7},{7,6},{8,9},{9,8},{10,11... | collective-permute-start | bytes 4423688 | tf_op jit(solution)/shard_map/ppermute | solution.py:35
  184.1 22.0 %collective-permute-start.22 = (bf16[4,96,1120]{2,1,0:T(8,128)(2,1)S(1)}, bf16[4,96,1120]{2,1,0:T(8,128)(2,1)S(1)}, u32[]{:S(2)}, u32[]{:S(2)}) collective-permute-start(bf16[4,96,1120]{2,1,0:T(8,128)(2,1)S(1)} %get-tuple-element.339), channel_id=1, source_target_pairs={{0,2},{1,3},{2,0},{3,1},{4,6},{5,7},{6,4},{7,5},{8,10},{9,11},{10,... | collective-permute-start | bytes 2580488 | tf_op jit(solution)/shard_map/ppermute | solution.py:35
  185.6 20.6 %collective-permute-start.21 = (bf16[4,96,1120]{2,1,0:T(8,128)(2,1)S(1)}, bf16[4,96,1120]{2,1,0:T(8,128)(2,1)S(1)}, u32[]{:S(2)}, u32[]{:S(2)}) collective-permute-start(bf16[4,96,1120]{2,1,0:T(8,128)(2,1)S(1)} %get-tuple-element.338), channel_id=1, source_target_pairs={{0,8},{4,12},{8,0},{12,4},{16,24},{20,28},{24,16},{28,20},{1,9},{5... | collective-permute-start | bytes 2580488 | tf_op jit(solution)/shard_map/ppermute | solution.py:35
  186.1 20.3 %collective-permute-start.20 = (bf16[4,96,1120]{2,1,0:T(8,128)(2,1)S(1)}, bf16[4,96,1120]{2,1,0:T(8,128)(2,1)S(1)}, u32[]{:S(2)}, u32[]{:S(2)}) collective-permute-start(bf16[4,96,1120]{2,1,0:T(8,128)(2,1)S(1)} %get-tuple-element.337), channel_id=1, source_target_pairs={{0,4},{4,0},{8,12},{12,8},{16,20},{20,16},{24,28},{28,24},{1,5},{5... | collective-permute-start | bytes 2580488 | tf_op jit(solution)/shard_map/ppermute | solution.py:35
  187.7 2.2 collective-permute-start.16
  207.2 13.0 %collective-permute-start.25 = (bf16[2,96,1120]{2,1,0:T(8,128)(2,1)S(1)}, bf16[2,96,1120]{2,1,0:T(8,128)(2,1)S(1)}, u32[]{:S(2)}, u32[]{:S(2)}) collective-permute-start(bf16[2,96,1120]{2,1,0:T(8,128)(2,1)S(1)} %get-tuple-element.358), channel_id=1, source_target_pairs={{0,4},{4,0},{8,12},{12,8},{16,20},{20,16},{24,28},{28,24},{1,5},{5... | collective-permute-start | bytes 1290248 | tf_op jit(solution)/shard_map/ppermute | solution.py:35
  208.9 11.3 %collective-permute-start.24 = (bf16[2,96,1120]{2,1,0:T(8,128)(2,1)S(1)}, bf16[2,96,1120]{2,1,0:T(8,128)(2,1)S(1)}, u32[]{:S(2)}, u32[]{:S(2)}) collective-permute-start(bf16[2,96,1120]{2,1,0:T(8,128)(2,1)S(1)} %get-tuple-element.353), channel_id=1, source_target_pairs={{0,2},{1,3},{2,0},{3,1},{4,6},{5,7},{6,4},{7,5},{8,10},{9,11},{10,... | collective-permute-start | bytes 1290248 | tf_op jit(solution)/shard_map/ppermute | solution.py:35
  209.3 10.9 %collective-permute-start.23 = (bf16[2,96,1120]{2,1,0:T(8,128)(2,1)S(1)}, bf16[2,96,1120]{2,1,0:T(8,128)(2,1)S(1)}, u32[]{:S(2)}, u32[]{:S(2)}) collective-permute-start(bf16[2,96,1120]{2,1,0:T(8,128)(2,1)S(1)} %get-tuple-element.349), channel_id=1, source_target_pairs={{0,8},{4,12},{8,0},{12,4},{16,24},{20,28},{24,16},{28,20},{1,9},{5... | collective-permute-start | bytes 1290248 | tf_op jit(solution)/shard_map/ppermute | solution.py:35
  229.3 18.7 %collective-permute-start.26 = (bf16[1120,256]{1,0:T(8,128)(2,1)S(1)}, bf16[1120,256]{1,0:T(8,128)(2,1)S(1)}, u32[]{:S(2)}, u32[]{:S(2)}) collective-permute-start(bf16[1120,256]{1,0:T(8,128)(2,1)S(1)} %get-tuple-element.381), channel_id=1, source_target_pairs={{0,1},{1,0},{2,3},{3,2},{4,5},{5,4},{6,7},{7,6},{8,9},{9,8},{10,11... | collective-permute-start | bytes 1720328 | tf_op jit(solution)/shard_map/ppermute | solution.py:35
  229.4 18.6 %collective-permute-start.27 = (bf16[1120,256]{1,0:T(8,128)(2,1)S(1)}, bf16[1120,256]{1,0:T(8,128)(2,1)S(1)}, u32[]{:S(2)}, u32[]{:S(2)}) collective-permute-start(bf16[1120,256]{1,0:T(8,128)(2,1)S(1)} %get-tuple-element.383), channel_id=1, source_target_pairs={{0,1},{1,0},{2,3},{3,2},{4,5},{5,4},{6,7},{7,6},{8,9},{9,8},{10,11... | collective-permute-start | bytes 1720328 | tf_op jit(solution)/shard_map/ppermute | solution.py:35
  234.4 13.5 %collective-permute-start.30 = (bf16[4,80,576]{2,1,0:T(8,128)(2,1)S(1)}, bf16[4,80,576]{2,1,0:T(8,128)(2,1)S(1)}, u32[]{:S(2)}, u32[]{:S(2)}) collective-permute-start(bf16[4,80,576]{2,1,0:T(8,128)(2,1)S(1)} %get-tuple-element.390), channel_id=1, source_target_pairs={{0,4},{4,0},{8,12},{12,8},{16,20},{20,16},{24,28},{28,24},{1,5},{5... | collective-permute-start | bytes 1105928 | tf_op jit(solution)/shard_map/ppermute | solution.py:35
  235.7 9.6 %collective-permute-start.29 = (bf16[4,64,576]{2,1,0:T(8,128)(2,1)S(1)}, bf16[4,64,576]{2,1,0:T(8,128)(2,1)S(1)}, u32[]{:S(2)}, u32[]{:S(2)}) collective-permute-start(bf16[4,64,576]{2,1,0:T(8,128)(2,1)S(1)} %get-tuple-element.400), channel_id=1, source_target_pairs={{0,8},{4,12},{8,0},{12,4},{16,24},{20,28},{24,16},{28,20},{1,9},{5... | collective-permute-start | bytes 884744 | tf_op jit(solution)/shard_map/ppermute | solution.py:35
  237.3 21.2 %collective-permute-start.31 = (bf16[8,80,576]{2,1,0:T(8,128)(2,1)S(1)}, bf16[8,80,576]{2,1,0:T(8,128)(2,1)S(1)}, u32[]{:S(2)}, u32[]{:S(2)}) collective-permute-start(bf16[8,80,576]{2,1,0:T(8,128)(2,1)S(1)} %get-tuple-element.404), channel_id=1, source_target_pairs={{0,2},{1,3},{2,0},{3,1},{4,6},{5,7},{6,4},{7,5},{8,10},{9,11},{10,... | collective-permute-start | bytes 2211848 | tf_op jit(solution)/shard_map/ppermute | solution.py:35
  245.3 31.3 %collective-permute-start.32 = (bf16[1,288,1120]{2,1,0:T(8,128)(2,1)S(1)}, bf16[1,288,1120]{2,1,0:T(8,128)(2,1)S(1)}, u32[]{:S(2)}, u32[]{:S(2)}) collective-permute-start(bf16[1,288,1120]{2,1,0:T(8,128)(2,1)S(1)} %get-tuple-element.417), channel_id=1, source_target_pairs={{0,16},{4,20},{8,24},{12,28},{16,0},{20,4},{24,8},{28,12},{1,17},{... | collective-permute-start | bytes 1935368 | tf_op jit(solution)/shard_map/ppermute | solution.py:35
  248.2 44.6 %collective-permute-start.28 = (bf16[1120,256]{1,0:T(8,128)(2,1)S(1)}, bf16[1120,256]{1,0:T(8,128)(2,1)S(1)}, u32[]{:S(2)}, u32[]{:S(2)}) collective-permute-start(bf16[1120,256]{1,0:T(8,128)(2,1)S(1)} %add_convert_fusion.2), channel_id=1, source_target_pairs={{0,2},{1,3},{2,0},{3,1},{4,6},{5,7},{6,4},{7,5},{8,10},{9,11},{10,... | collective-permute-start | bytes 1720328 | tf_op jit(solution)/shard_map/ppermute | solution.py:35
  262.4 19.4 %collective-permute-start.35 = (bf16[2,80,576]{2,1,0:T(8,128)(2,1)S(1)}, bf16[2,80,576]{2,1,0:T(8,128)(2,1)S(1)}, u32[]{:S(2)}, u32[]{:S(2)}) collective-permute-start(bf16[2,80,576]{2,1,0:T(8,128)(2,1)S(1)} %get-tuple-element.424), channel_id=1, source_target_pairs={{0,8},{4,12},{8,0},{12,4},{16,24},{20,28},{24,16},{28,20},{1,9},{5... | collective-permute-start | bytes 552968 | tf_op jit(solution)/shard_map/ppermute | solution.py:35
  263.0 18.7 %collective-permute-start.36 = (bf16[2,64,576]{2,1,0:T(8,128)(2,1)S(1)}, bf16[2,64,576]{2,1,0:T(8,128)(2,1)S(1)}, u32[]{:S(2)}, u32[]{:S(2)}) collective-permute-start(bf16[2,64,576]{2,1,0:T(8,128)(2,1)S(1)} %get-tuple-element.425), channel_id=1, source_target_pairs={{0,4},{4,0},{8,12},{12,8},{16,20},{20,16},{24,28},{28,24},{1,5},{5... | collective-permute-start | bytes 442376 | tf_op jit(solution)/shard_map/ppermute | solution.py:35
  263.9 20.5 %collective-permute-start.40 = (bf16[4,64,384]{2,1,0:T(8,128)(2,1)S(1)}, bf16[4,64,384]{2,1,0:T(8,128)(2,1)S(1)}, u32[]{:S(2)}, u32[]{:S(2)}) collective-permute-start(bf16[4,64,384]{2,1,0:T(8,128)(2,1)S(1)} %get-tuple-element.435), channel_id=1, source_target_pairs={{0,8},{4,12},{8,0},{12,4},{16,24},{20,28},{24,16},{28,20},{1,9},{5... | collective-permute-start | bytes 589832 | tf_op jit(solution)/shard_map/ppermute | solution.py:35
  276.7 16.1 %collective-permute-start.38 = (bf16[4,80,576]{2,1,0:T(8,128)(2,1)S(1)}, bf16[4,80,576]{2,1,0:T(8,128)(2,1)S(1)}, u32[]{:S(2)}, u32[]{:S(2)}) collective-permute-start(bf16[4,80,576]{2,1,0:T(8,128)(2,1)S(1)} %get-tuple-element.434), channel_id=1, source_target_pairs={{0,4},{4,0},{8,12},{12,8},{16,20},{20,16},{24,28},{28,24},{1,5},{5... | collective-permute-start | bytes 1105928 | tf_op jit(solution)/shard_map/ppermute | solution.py:35
  281.8 17.6 %collective-permute-start.33 = (bf16[1120,256]{1,0:T(8,128)(2,1)S(1)}, bf16[1120,256]{1,0:T(8,128)(2,1)S(1)}, u32[]{:S(2)}, u32[]{:S(2)}) collective-permute-start(bf16[1120,256]{1,0:T(8,128)(2,1)S(1)} %get-tuple-element.421), channel_id=1, source_target_pairs={{0,1},{1,0},{2,3},{3,2},{4,5},{5,4},{6,7},{7,6},{8,9},{9,8},{10,11... | collective-permute-start | bytes 1720328 | tf_op jit(solution)/shard_map/ppermute | solution.py:35
  281.8 19.1 %collective-permute-start.34 = (bf16[1120,256]{1,0:T(8,128)(2,1)S(1)}, bf16[1120,256]{1,0:T(8,128)(2,1)S(1)}, u32[]{:S(2)}, u32[]{:S(2)}) collective-permute-start(bf16[1120,256]{1,0:T(8,128)(2,1)S(1)} %get-tuple-element.423), channel_id=1, source_target_pairs={{0,1},{1,0},{2,3},{3,2},{4,5},{5,4},{6,7},{7,6},{8,9},{9,8},{10,11... | collective-permute-start | bytes 1720328 | tf_op jit(solution)/shard_map/ppermute | solution.py:35
  284.5 8.3 %collective-permute-start.39 = (bf16[4,80,384]{2,1,0:T(8,128)(2,1)S(1)}, bf16[4,80,384]{2,1,0:T(8,128)(2,1)S(1)}, u32[]{:S(2)}, u32[]{:S(2)}) collective-permute-start(bf16[4,80,384]{2,1,0:T(8,128)(2,1)S(1)} %get-tuple-element.410), channel_id=1, source_target_pairs={{0,4},{4,0},{8,12},{12,8},{16,20},{20,16},{24,28},{28,24},{1,5},{5... | collective-permute-start | bytes 737288 | tf_op jit(solution)/shard_map/ppermute | solution.py:35
  292.8 5.8 %collective-permute-start.37 = (f32[4,12,140]{2,1,0:T(8,128)S(1)}, f32[4,12,140]{2,1,0:T(8,128)S(1)}, u32[]{:S(2)}, u32[]{:S(2)}) collective-permute-start(f32[4,12,140]{2,1,0:T(8,128)S(1)} %get-tuple-element.505), channel_id=1, source_target_pairs={{0,16},{4,20},{8,24},{12,28},{16,0},{20,4},{24,8},{28,12},{1,17},{... | collective-permute-start | bytes 80648 | tf_op jit(solution)/shard_map/ppermute | solution.py:35
  293.6 12.0 %collective-permute-start.44 = (bf16[2,80,576]{2,1,0:T(8,128)(2,1)S(1)}, bf16[2,80,576]{2,1,0:T(8,128)(2,1)S(1)}, u32[]{:S(2)}, u32[]{:S(2)}) collective-permute-start(bf16[2,80,576]{2,1,0:T(8,128)(2,1)S(1)} %get-tuple-element.464), channel_id=1, source_target_pairs={{0,8},{4,12},{8,0},{12,4},{16,24},{20,28},{24,16},{28,20},{1,9},{5... | collective-permute-start | bytes 552968 | tf_op jit(solution)/shard_map/ppermute | solution.py:35
  297.1 8.4 %collective-permute-start.46 = (bf16[2,64,384]{2,1,0:T(8,128)(2,1)S(1)}, bf16[2,64,384]{2,1,0:T(8,128)(2,1)S(1)}, u32[]{:S(2)}, u32[]{:S(2)}) collective-permute-start(bf16[2,64,384]{2,1,0:T(8,128)(2,1)S(1)} %get-tuple-element.466), channel_id=1, source_target_pairs={{0,4},{4,0},{8,12},{12,8},{16,20},{20,16},{24,28},{28,24},{1,5},{5... | collective-permute-start | bytes 294920 | tf_op jit(solution)/shard_map/ppermute | solution.py:35
  298.6 6.9 %collective-permute-start.45 = (bf16[2,80,384]{2,1,0:T(8,128)(2,1)S(1)}, bf16[2,80,384]{2,1,0:T(8,128)(2,1)S(1)}, u32[]{:S(2)}, u32[]{:S(2)}) collective-permute-start(bf16[2,80,384]{2,1,0:T(8,128)(2,1)S(1)} %get-tuple-element.465), channel_id=1, source_target_pairs={{0,8},{4,12},{8,0},{12,4},{16,24},{20,28},{24,16},{28,20},{1,9},{5... | collective-permute-start | bytes 368648 | tf_op jit(solution)/shard_map/ppermute | solution.py:35
  299.4 5.5 %collective-permute-start.42 = (f32[2,12,140]{2,1,0:T(8,128)S(1)}, f32[2,12,140]{2,1,0:T(8,128)S(1)}, u32[]{:S(2)}, u32[]{:S(2)}) collective-permute-start(f32[2,12,140]{2,1,0:T(8,128)S(1)} %get-tuple-element.507), channel_id=1, source_target_pairs={{0,8},{4,12},{8,0},{12,4},{16,24},{20,28},{24,16},{28,20},{1,9},{5... | collective-permute-start | bytes 40328 | tf_op jit(solution)/shard_map/ppermute | solution.py:35
  301.9 20.2 %copy-start.26 = (bf16[2,256,1120]{1,2,0:T(8,128)(2,1)S(1)}, bf16[2,256,1120]{1,2,0:T(8,128)(2,1)}, u32[]{:S(2)}) copy-start(bf16[2,256,1120]{1,2,0:T(8,128)(2,1)} %param.21) | copy-start | bytes 3440644
  301.9 20.2 %copy-start.32 = (f32[1120,512]{1,0:T(8,128)S(1)}, f32[1120,512]{1,0:T(8,128)}, u32[]{:S(2)}) copy-start(f32[1120,512]{1,0:T(8,128)} %copy-done.31) | copy-start | bytes 6881284
  301.9 20.2 %collective-permute-start.41 = (bf16[1120,256]{1,0:T(8,128)(2,1)}, bf16[1120,256]{1,0:T(8,128)(2,1)}, u32[]{:S(2)}, u32[]{:S(2)}) collective-permute-start(bf16[1120,256]{1,0:T(8,128)(2,1)} %add_convert_fusion), channel_id=1, source_target_pairs={{0,2},{1,3},{2,0},{3,1},{4,6},{5,7},{6,4},{7,5},{8,10},{9,11},{10,... | collective-permute-start | bytes 1720328 | tf_op jit(solution)/shard_map/ppermute | solution.py:35
  304.9 3.8 %collective-permute-start.43 = (f32[1,12,140]{2,1,0:T(8,128)S(1)}, f32[1,12,140]{2,1,0:T(8,128)S(1)}, u32[]{:S(2)}, u32[]{:S(2)}) collective-permute-start(f32[1,12,140]{2,1,0:T(8,128)S(1)} %get-tuple-element.509), channel_id=1, source_target_pairs={{0,4},{4,0},{8,12},{12,8},{16,20},{20,16},{24,28},{28,24},{1,5},{5... | collective-permute-start | bytes 20168 | tf_op jit(solution)/shard_map/ppermute | solution.py:35
  309.3 10.7 %collective-permute-start.47 = (f32[1,12,140]{2,1,0:T(8,128)}, f32[1,12,140]{2,1,0:T(8,128)}, u32[]{:S(2)}, u32[]{:S(2)}) collective-permute-start(f32[1,12,140]{2,1,0:T(8,128)} %add.63), channel_id=1, source_target_pairs={{0,1},{1,0},{2,3},{3,2},{4,5},{5,4},{6,7},{7,6},{8,9},{9,8},{10,11... | collective-permute-start | bytes 20168 | tf_op jit(solution)/shard_map/ppermute | solution.py:35
  315.7 17.0 %collective-permute-start.49 = (bf16[1,144,576]{2,1,0:T(8,128)(2,1)}, bf16[1,144,576]{2,1,0:T(8,128)(2,1)S(1)}, u32[]{:S(2)}, u32[]{:S(2)}) collective-permute-start(bf16[1,144,576]{2,1,0:T(8,128)(2,1)} %copy-done.73), channel_id=1, source_target_pairs={{0,16},{4,20},{8,24},{12,28},{16,0},{20,4},{24,8},{28,12},{1,17},{... | collective-permute-start | bytes 497672 | tf_op jit(solution)/shard_map/ppermute | solution.py:35
  317.1 22.5 %collective-permute-start.54 = (bf16[1,80,576]{2,1,0:T(8,128)(2,1)}, bf16[1,80,576]{2,1,0:T(8,128)(2,1)S(1)}, u32[]{:S(2)}, u32[]{:S(2)}) collective-permute-start(bf16[1,80,576]{2,1,0:T(8,128)(2,1)} %copy-done.75), channel_id=1, source_target_pairs={{0,16},{4,20},{8,24},{12,28},{16,0},{20,4},{24,8},{28,12},{1,17},{... | collective-permute-start | bytes 276488 | tf_op jit(solution)/shard_map/ppermute | solution.py:35
  318.7 18.3 %collective-permute-start.50 = (bf16[1,144,384]{2,1,0:T(8,128)(2,1)}, bf16[1,144,384]{2,1,0:T(8,128)(2,1)S(1)}, u32[]{:S(2)}, u32[]{:S(2)}) collective-permute-start(bf16[1,144,384]{2,1,0:T(8,128)(2,1)} %copy-done.74), channel_id=1, source_target_pairs={{0,16},{4,20},{8,24},{12,28},{16,0},{20,4},{24,8},{28,12},{1,17},{... | collective-permute-start | bytes 331784 | tf_op jit(solution)/shard_map/ppermute | solution.py:35
  320.8 18.2 %collective-permute-start.48 = (f32[1,12,140]{2,1,0:T(8,128)S(1)}, f32[1,12,140]{2,1,0:T(8,128)S(1)}, u32[]{:S(2)}, u32[]{:S(2)}) collective-permute-start(f32[1,12,140]{2,1,0:T(8,128)S(1)} %add.64), channel_id=1, source_target_pairs={{0,2},{1,3},{2,0},{3,1},{4,6},{5,7},{6,4},{7,5},{8,10},{9,11},{10,... | collective-permute-start | bytes 20168 | tf_op jit(solution)/shard_map/ppermute | solution.py:35
  337.2 8.8 %collective-permute-start.52 = (bf16[144,960]{1,0:T(8,128)(2,1)S(1)}, bf16[144,960]{1,0:T(8,128)(2,1)S(1)}, u32[]{:S(2)}, u32[]{:S(2)}) collective-permute-start(bf16[144,960]{1,0:T(8,128)(2,1)S(1)} %maximum_maximum_fusion.refs_0_), channel_id=1, source_target_pairs={{0,2},{1,3},{2,0},{3,1},{4,6},{5,7},{6,4},{7,5},{8,10},{9,11},{10,... | collective-permute-start | bytes 829448 | tf_op jit(solution)/shard_map/ppermute | solution.py:35
  338.9 9.5 %collective-permute-start.51 = (bf16[144,960]{1,0:T(8,128)(2,1)S(1)}, bf16[144,960]{1,0:T(8,128)(2,1)S(1)}, u32[]{:S(2)}, u32[]{:S(2)}) collective-permute-start(bf16[144,960]{1,0:T(8,128)(2,1)S(1)} %maximum_maximum_fusion.refs_0_), channel_id=1, source_target_pairs={{0,1},{1,0},{2,3},{3,2},{4,5},{5,4},{6,7},{7,6},{8,9},{9,8},{10,11... | collective-permute-start | bytes 829448 | tf_op jit(solution)/shard_map/ppermute | solution.py:35
  346.0 2.4 collective-permute-start.53
  (77 other events, 400.0 us)

commit v5 on v4

--- a/solution.py
+++ b/solution.py
@@ -678,13 +678,20 @@
     )
 
 
-def active_back_kernel(cotangent, down, result):
+def active_back_kernel(cotangent, down, result, rows):
+    @pl.when(pl.program_id(0) == 0)
+    def _():
+        cells, _, span = cotangent.shape
+        for c in range(cells):
+            rows[c * span : (c + 1) * span, :] = cotangent[c].T
+
     for first, last in chunks(down.shape[1]):
-        result[:, first:last] = dot(cotangent[...], down[:, first:last])
+        result[:, first:last] = dot(rows[...], down[:, first:last])
 
 
 def active_back(scalars, cotangent, down):
-    rows, width = cotangent.shape
+    cells, width, span = cotangent.shape
+    rows = cells * span
     tile = hidden_tile(down.shape[1])
     shape = jax.ShapeDtypeStruct((rows, down.shape[1]), jnp.float32)
     return grid_call(
@@ -693,7 +700,7 @@
         [whole(cotangent), pl.BlockSpec((width, tile), lambda g, me: (0, g))],
         pl.BlockSpec((rows, tile), lambda g, me: (0, g)),
         shape,
-        [],
+        [pltpu.VMEM((rows, width), jnp.bfloat16)],
         "active_back",
         1,
         (scalars, cotangent, down),
@@ -716,7 +723,7 @@
         square = upper * upper
         bend = jnp.tanh(inner * upper * (1.0 + 0.044715 * square))
         half = 0.5 + 0.5 * bend
-        slope = half + (0.5 * inner) * upper * (1.0 - bend * bend) * (1.0 + 0.134145 * square)
+        slope = half + 2.0 * half * (1.0 - half) * (inner * upper) * (1.0 + 0.134145 * square)
         active[:, first:last] = (upper * half).astype(jnp.bfloat16)
         back = (back * slope).astype(jnp.bfloat16)
         back_upper[:, first:last] = back
@@ -1324,7 +1331,7 @@
     )
     x_bits = [b for b in reversed(bits_of(seq_count)) if b > 1]
     near = [swap_with(block, "seq", 1) for block in wide]
-    back_active = active_back(scalars, order_after(flat(cotangent), weight), down_turned)
+    back_active = active_back(scalars, order_after(cotangent_turned, weight), down_turned)
     held = [{0: wide[c]} for c in range(cells_here)]
     for c in range(cells_here):
         for bit in x_bits:

time: 357 us -> 349 us (0.978)
  local copies, waits for them, and re-layouts: 46.7 us -> 37.3 us
    unnamed x173 -> x190, local copies, waits for them, and re-layouts: 41.5 us -> 30.8 us
  transfers between devices with their start and end apart: 55 -> 55, of which waited for: 17 -> 16; matrix products, arithmetic and copies ran while one was open for 4% -> 4% of each run, Pallas kernels for 43% -> 45%
where the time goes in v5:
time: 349 us; the launch traced here: 344 us
  Pallas kernels  185 us (53%)
  waiting for transfers between devices  56.3 us (16%)
  starting transfers between devices  49.4 us (14%)
  local copies, waits for them, and re-layouts  37.3 us (11%)
  other arithmetic  9.02 us (3%)
  between operations  6.4 us (2%)
    pallas_call x17, Pallas kernels, no_grid_call(): pl.pallas_call(body, out_shape=out_shape, in_specs=in_specs, out_specs=ja...  94.4 us
    pallas_call x10, Pallas kernels, grid_call(): pl.pallas_call(body, out_shape=out_shape, grid_spec=pltpu.PrefetchScalarG...  79.1 us
    ppermute x55, waiting for transfers between devices, swap_with(): return lax.ppermute(array, axis, [(i, i ^ bit) for i in range(count)])  56.3 us
    ppermute x55, starting transfers between devices, swap_with(): return lax.ppermute(array, axis, [(i, i ^ bit) for i in range(count)])  49.4 us
    unnamed x190, local copies, waits for them, and re-layouts  30.8 us
    pallas_call x17, Pallas kernels, add_halves(): pl.pallas_call(partial(add_halves_kernel, len(pairs)), out_shape=(shape,...  11.5 us
  transfers between devices with their start and end apart: 55, of which 16 were waited for; matrix products, arithmetic and copies ran while one was open for 4% of the time, Pallas kernels for 45%

profile of v5, /device:TPU:0, one launch (start us, length us, event | category | flops | bytes accessed | tf_op | source)
XLA Modules:
  0.0 343.7 jit_solution(12031672399822890529)
XLA Ops:
  2.1 1.3 copy-done.21
  5.2 2.6 collective-permute-start.1
  8.4 3.5 %own_weights.1 = (bf16[960,1152]{1,0:T(8,128)(2,1)S(1)}, f32[960,1]{1,0:T(8,128)S(1)}, bf16[1120,576]{1,0:T(8,128)(2,1)S(1)}, bf16[1120,384]{1,0:T(8,128)(2,1)S(1)}) custom-call(s32[6]{0:T(128)S(1)} %pad_add_fusion.scalars.me, bf16[1120,3360]{1,0:T(8,128)(2,1)S(1)} %bitcast.85, f32[1120]{0:T(1024)S(1)} %copy-done.77, f32[1120]{0:T(1024)S(1)} %copy-done.78), custom_call_target="tpu_custom_call" | custom-call | flops 4000000000 | bytes 1 | tf_op jit(solution)/shard_map/own_weights/pallas_call | solution.py:134
  12.2 9.7 %active_back.1.refs_0_ = f32[512,4480]{1,0:T(8,128)S(1)} custom-call(s32[6]{0:T(128)S(1)} %pad_add_fusion.scalars.me, bf16[2,1120,256]{2,1,0:T(8,128)(2,1)S(1)} %bitcast.59, bf16[1120,4480]{1,0:T(8,128)(2,1)S(1)} %bitcast.53), custom_call_target="tpu_custom_call" | custom-call | flops 1 | bytes 1 | tf_op jit(solution)/shard_map/active_back/pallas_call | solution.py:736
  22.0 3.5 %copy-done.2 = f32[512,4480]{1,0:T(8,128)} copy-done((f32[512,4480]{1,0:T(8,128)}, f32[512,4480]{1,0:T(8,128)S(1)}, u32[]{:S(2)}) %copy-start.2) | copy-done | bytes 9175064
  26.0 2.2 collective-permute-start.7
  28.3 13.7 %attend_forward.2 = (bf16[9,64,1024]{2,1,0:T(8,128)(2,1)S(1)}, bf16[6,64,1024]{2,1,0:T(8,128)(2,1)S(1)}, f32[5,64,1024]{2,1,0:T(8,128)S(1)}, bf16[1152,1024]{1,0...) custom-call(s32[6]{0:T(128)S(1)} %pad_add_fusion.scalars.me, ...), custom_call_target="tpu_custom_call" | custom-call | flops 14000000000 | bytes 1 | tf_op jit(solution)/shard_map/attend_forward/pallas_call | solution.py:134
  42.0 1.5 copy-done.6
  47.0 1.5 collective-permute-start.4
  48.6 13.5 %attend_forward.3 = (bf16[9,64,1024]{2,1,0:T(8,128)(2,1)S(1)}, bf16[6,64,1024]{2,1,0:T(8,128)(2,1)S(1)}, f32[5,64,1024]{2,1,0:T(8,128)S(1)}, bf16[1152,1024]{1,0...) custom-call(s32[6]{0:T(128)S(1)} %pad_add_fusion.scalars.me, ...), custom_call_target="tpu_custom_call" | custom-call | flops 14000000000 | bytes 1 | tf_op jit(solution)/shard_map/attend_forward/pallas_call | solution.py:134
  64.0 1.5 collective-permute-start.10
  66.4 2.8 second_norm.2
  71.9 1.3 collective-permute-done.11.refs_3_
  73.2 2.8 second_norm.3
  76.0 4.4 %copy-done = bf16[1120,4480]{1,0:T(8,128)(2,1)S(1)} copy-done((bf16[1120,4480]{1,0:T(8,128)(2,1)S(1)}, bf16[1120,4480]{1,0:T(8,128)(2,1)}, u32[]{:S(2)}) %copy-start) | copy-done | bytes 10035224
  80.4 15.8 %hidden_layer.1 = (bf16[512,4480]{1,0:T(8,128)(2,1)S(1)}, bf16[512,4480]{1,0:T(8,128)(2,1)S(1)}, f32[1,4480]{1,0:T(1,128)S(1)}) custom-call(s32[6]{0:T(128)S(1)} %pad_add_fusion.scalars.me, f32[512,4480]{1,0:T(8,128)S(1)} %bitcast.58, bf16[1120,4480]{1,0:T(8,128)(2,1)S(1)} %copy-done, f32[1,4480]{1,0:T(1,128)S(1)} %reshape.80.refs_2_, ...), custom_call_target="tpu_custom_call" | custom-call | flops 1 | bytes 1 | tf_op jit(solution)/shard_map/hidden_layer/pallas_call | solution.py:736
  96.3 6.7 %down_outer.2 = bf16[2,8,144,1120]{3,2,1,0:T(8,128)(2,1)S(1)} custom-call(s32[6]{0:T(128)S(1)} %pad_add_fusion.scalars.me, bf16[2,1120,256]{2,1,0:T(8,128)(2,1)S(1)} %bitcast.60, bf16[512,4480]{1,0:T(8,128)(2,1)S(1)} %get-tuple-element.314.right.refs_0_), custom_call_target="tpu_custom_call" | custom-call | flops 1 | bytes 1 | tf_op jit(solution)/shard_map/down_outer/pallas_call | solution.py:736
  103.2 5.3 %up_outer.2 = bf16[2,8,144,1120]{3,2,1,0:T(8,128)(2,1)S(1)} custom-call(s32[6]{0:T(128)S(1)} %pad_add_fusion.scalars.me, bf16[512,4480]{1,0:T(8,128)(2,1)S(1)} %get-tuple-element.305.right.back_upper, bf16[1120,256]{1,0:T(8,128)(2,1)S(1)} %copy-done.27, bf16[1120,256]{1,0:T(8,128)(2,1)S(1)} %get-tuple-element.296.refs_1_), custom_call_target="tpu_custom_call" | custom-call | flops 1 | bytes 1 | tf_op jit(solution)/shard_map/up_outer/pallas_call | solution.py:736
  108.7 3.1 collective-permute-done.12.refs_0_
  111.8 9.6 %down_outer.3 = (bf16[1,8,96,1120]{3,2,1,0:T(8,128)(2,1)}, bf16[1,8,96,1120]{3,2,1,0:T(8,128)(2,1)S(1)}, bf16[2,4,96,1120]{3,2,1,0:T(8,128)(2,1)}, bf16[2,4,96,1120]{3,2,1,0:T(8,128)(2,1)S(1)}) custom-call(s32[6]{0:T(128)S(1)} %pad_add_fusion.scalars.me, bf16[2,1120,256]{2,1,0:T(8,128)(2,1)S(1)} %bitcast.61, ...), custom_call_target="tpu_custom_call" | custom-call | flops 1 | bytes 1 | tf_op jit(solution)/shard_map/down_outer/pallas_call | solution.py:736
  121.5 1.5 collective-permute-start.15
  123.0 7.7 %up_outer.3 = (bf16[2,4,96,1120]{3,2,1,0:T(8,128)(2,1)}, bf16[2,4,96,1120]{3,2,1,0:T(8,128)(2,1)S(1)}, bf16[2,4,96,1120]{3,2,1,0:T(8,128)(2,1)}, bf16[2,4,96,1120]{3,2,1,0:T(8,128)(2,1)S(1)}) custom-call(s32[6]{0:T(128)S(1)} %pad_add_fusion.scalars.me, ...), custom_call_target="tpu_custom_call", output_to_operand_aliasing={{2}: (5, {}), {3}: (6, {})} | custom-call | flops 1 | bytes 1 | tf_op jit(solution)/shard_map/up_outer/pallas_call | solution.py:736
  130.6 1.6 collective-permute-start.17
  132.2 1.5 collective-permute-start.18
  133.8 3.8 %copy-done.1 = bf16[1120,4480]{1,0:T(8,128)(2,1)S(1)} copy-done((bf16[1120,4480]{1,0:T(8,128)(2,1)S(1)}, bf16[1120,4480]{1,0:T(8,128)(2,1)}, u32[]{:S(2)}) %copy-start.1) | copy-done | bytes 10035224
  137.6 12.6 %middle_back.1 = (f32[1120,512]{1,0:T(8,128)S(1)}, bf16[1120,512]{1,0:T(8,128)(2,1)S(1)}, f32[8,1120]{1,0:T(8,128)S(1)}, bf16[2,5,64,256]{3,2,1,0:T(8,128)(2,1)S...) custom-call(s32[6]{0:T(128)S(1)} %pad_add_fusion.scalars.me, ...), custom_call_target="tpu_custom_call" | custom-call | flops 1 | bytes 1 | tf_op jit(solution)/shard_map/middle_back/pallas_call | solution.py:736
  150.8 3.1 out_outer.1
  154.0 1.6 fusion.4
  155.6 10.5 %block_output.1 = bf16[2,1120,256]{2,1,0:T(8,128)(2,1)} custom-call(s32[6]{0:T(128)S(1)} %pad_add_fusion.scalars.me, bf16[512,4480]{1,0:T(8,128)(2,1)S(1)} %get-tuple-element.314.right.refs_0_, bf16[1120,4480]{1,0:T(8,128)(2,1)S(1)} %bitcast.56, f32[1120]{0:T(1024)S(1)} %copy-done.71, f32[1120,256]{1,0:T(8,128)S(1)} %copy-done.17, f32[1120,256]{1,0:T(8,128)S(1)} %copy-done.20), custom_call_target="tpu_custom_call" | custom-call | flops 1 | bytes 1 | tf_op jit(solution)/shard_map/block_output/pallas_call | solution.py:736
  166.1 2.6 add_halves.17
  168.7 2.9 collective-permute-done.17.refs_1_.refs_3_
  171.6 1.3 collective-permute-done.18.refs_1_.refs_3_
  172.9 2.6 add_halves.18
  175.6 2.7 add_halves.19
  179.4 1.5 collective-permute-start.20
  181.1 2.1 collective-permute-done.16.refs_5_
  183.2 9.5 %attend_backward.4.refs_2_ = bf16[1024,576]{1,0:T(8,128)(2,1)S(1)} custom-call(s32[6]{0:T(128)S(1)} %pad_add_fusion.scalars.me, bf16[9,64,1024]{2,1,0:T(8,128)(2,1)S(1)} %copy-done.35, f32[5,64,1024]{2,1,0:T(8,128)S(1)} %copy-done.15, bf16[1,2,5,64,256]{4,3,2,1,0:T(8,128)(2,1)S(1)} %bitcast.76, bf16[1,2,5,64,256]{4,3,2,1,0:T(8,128)(2,1)S(1)} %bitcast.68, ...), custom_call_target="tpu_custom_call" | custom-call | flops 1 | bytes 1 | tf_op jit(solution)/shard_map/attend_backward/pallas_call | solution.py:134
  192.7 6.7 %attend_backward.5.refs_3_.refs_2_ = bf16[1024,384]{1,0:T(8,128)(2,1)S(1)} custom-call(s32[6]{0:T(128)S(1)} %pad_add_fusion.scalars.me, bf16[6,64,1024]{2,1,0:T(8,128)(2,1)S(1)} %copy-done.39, f32[5,64,1024]{2,1,0:T(8,128)S(1)} %copy-done.15, bf16[1,2,5,64,256]{4,3,2,1,0:T(8,128)(2,1)S(1)} %bitcast.77, bf16[1,2,5,64,256]{4,3,2,1,0:T(8,128)(2,1)S(1)} %bitcast.69, ...), custom_call_target="tpu_custom_call" | custom-call | flops 1 | bytes 1 | tf_op jit(solution)/shard_map/attend_backward/pallas_call | solution.py:134
  200.4 1.6 collective-permute-start.25
  202.0 1.5 collective-permute-start.24
  203.5 1.4 collective-permute-start.23
  204.9 9.4 %attend_backward.6.refs_3_.refs_2_ = bf16[1024,576]{1,0:T(8,128)(2,1)S(1)} custom-call(s32[6]{0:T(128)S(1)} %pad_add_fusion.scalars.me, bf16[9,64,1024]{2,1,0:T(8,128)(2,1)S(1)} %copy-done.33, f32[5,64,1024]{2,1,0:T(8,128)S(1)} %copy-done.13, bf16[1,2,5,64,256]{4,3,2,1,0:T(8,128)(2,1)S(1)} %bitcast.78, bf16[1,2,5,64,256]{4,3,2,1,0:T(8,128)(2,1)S(1)} %bitcast.70, ...), custom_call_target="tpu_custom_call" | custom-call | flops 1 | bytes 1 | tf_op jit(solution)/shard_map/attend_backward/pallas_call | solution.py:134
  217.8 4.6 %normed_back.2 = (bf16[1120,256]{1,0:T(8,128)(2,1)S(1)}, bf16[1120,256]{1,0:T(8,128)(2,1)S(1)}, bf16[1120,256]{1,0:T(8,128)(2,1)S(1)}, bf16[1120,256]{1,0:T(8,128)(2,1)S(1)}, f32[8,1120]{1,0:T(8,128)S(1)}) custom-call(bf16[1120,576]{1,0:T(8,128)(2,1)S(1)} %copy-done.11, bf16[1120,384]{1,0:T(8,128)(2,1)S(1)} %copy-done.25, ...), custom_call_target="tpu_custom_call" | custom-call | flops 1 | bytes 1 | tf_op jit(solution)/shard_map/normed_back/pallas_call | solution.py:134
  223.0 4.6 %mix_outer.2 = (bf16[4,80,576]{2,1,0:T(8,128)(2,1)S(1)}, bf16[4,80,576]{2,1,0:T(8,128)(2,1)S(1)}, bf16[4,64,576]{2,1,0:T(8,128)(2,1)S(1)}, bf16[4,64,576]{2,1,0:T(8,128)(2,1)S(1)}, f32[1,576]{1,0:T(1,128)S(1)}) custom-call(s32[6]{0:T(128)S(1)} %pad_add_fusion.scalars.me, bf16[1152,1024]{1,0:T(8,128)(2,1)S(1)} %copy-done.7, bf16[1152,1024]{1,0:T(8,128)(2,1)S(1)} %copy-done.9, ...), custom_call_target="tpu_custom_call" | custom-call | flops 1 | bytes 1 | tf_op jit(solution)/shard_map/mix_outer/pallas_call | solution.py:134
  228.7 1.6 collective-permute-start.29
  230.9 6.6 %attend_backward.7.refs_3_ = bf16[1024,384]{1,0:T(8,128)(2,1)S(1)} custom-call(s32[6]{0:T(128)S(1)} %pad_add_fusion.scalars.me, bf16[6,64,1024]{2,1,0:T(8,128)(2,1)S(1)} %copy-done.37, f32[5,64,1024]{2,1,0:T(8,128)S(1)} %copy-done.13, bf16[1,2,5,64,256]{4,3,2,1,0:T(8,128)(2,1)S(1)} %bitcast.79, bf16[1,2,5,64,256]{4,3,2,1,0:T(8,128)(2,1)S(1)} %bitcast.71, ...), custom_call_target="tpu_custom_call" | custom-call | flops 1 | bytes 1 | tf_op jit(solution)/shard_map/attend_backward/pallas_call | solution.py:134
  238.1 2.6 collective-permute-start.32
  242.8 8.7 %collective-permute-done.31.refs_1_.refs_3_ = bf16[8,80,576]{2,1,0:T(8,128)(2,1)S(1)} collective-permute-done((bf16[8,80,576]{2,1,0:T(8,128)(2,1)S(1)}, bf16[8,80,576]{2,1,0:T(8,128)(2,1)S(1)}, u32[]{:S(2)}, u32[]{:S(2)}) %collective-permute-start.31) | collective-permute-done | bytes 737312 | tf_op jit(solution)/shard_map/ppermute | solution.py:35
  252.0 3.2 mix_outer.3
  258.2 10.9 %collective-permute-done.32 = bf16[1,288,1120]{2,1,0:T(8,128)(2,1)S(1)} collective-permute-done((bf16[1,288,1120]{2,1,0:T(8,128)(2,1)S(1)}, bf16[1,288,1120]{2,1,0:T(8,128)(2,1)S(1)}, u32[]{:S(2)}, u32[]{:S(2)}) %collective-permute-start.32) | collective-permute-done | bytes 645152 | tf_op jit(solution)/shard_map/ppermute | solution.py:35
  270.1 4.7 %normed_back.3 = (bf16[1120,256]{1,0:T(8,128)(2,1)S(1)}, bf16[1120,256]{1,0:T(8,128)(2,1)S(1)}, bf16[1120,256]{1,0:T(8,128)(2,1)S(1)}, bf16[1120,256]{1,0:T(8,128)(2,1)S(1)}, f32[8,1120]{1,0:T(8,128)S(1)}) custom-call(bf16[1120,576]{1,0:T(8,128)(2,1)S(1)} %copy-done.11, bf16[1120,384]{1,0:T(8,128)(2,1)S(1)} %copy-done.25, ...), custom_call_target="tpu_custom_call" | custom-call | flops 1 | bytes 1 | tf_op jit(solution)/shard_map/normed_back/pallas_call | solution.py:134
  275.3 1.5 collective-permute-done.40.refs_1_.refs_3_
  278.6 5.9 %collective-permute-done.39.refs_1_.refs_3_ = bf16[4,80,384]{2,1,0:T(8,128)(2,1)S(1)} collective-permute-done((bf16[4,80,384]{2,1,0:T(8,128)(2,1)S(1)}, bf16[4,80,384]{2,1,0:T(8,128)(2,1)S(1)}, u32[]{:S(2)}, u32[]{:S(2)}) %collective-permute-start.39) | collective-permute-done | bytes 245792 | tf_op jit(solution)/shard_map/ppermute | solution.py:35
  286.2 4.3 %collective-permute-start.44 = (bf16[2,80,576]{2,1,0:T(8,128)(2,1)S(1)}, bf16[2,80,576]{2,1,0:T(8,128)(2,1)S(1)}, u32[]{:S(2)}, u32[]{:S(2)}) collective-permute-start(bf16[2,80,576]{2,1,0:T(8,128)(2,1)S(1)} %get-tuple-element.464), channel_id=1, source_target_pairs={{0,8},{4,12},{8,0},{12,4},{16,24},{20,28},{24,16},{28,20},{1,9},{5... | collective-permute-start | bytes 552968 | tf_op jit(solution)/shard_map/ppermute | solution.py:35
  290.9 1.8 collective-permute-start.45
  294.1 1.5 collective-permute-start.41
  296.6 1.6 collective-permute-done.42
  300.0 2.0 collective-permute-done.43
  305.1 1.2 dynamic_slice.20
  310.0 1.9 collective-permute-start.54
  318.2 4.5 %tokens_back.1 = bf16[2,1120,256]{2,1,0:T(8,128)(2,1)} custom-call(bf16[2,1120,256]{2,1,0:T(8,128)(2,1)S(1)} %bitcast.83, f32[1120]{0:T(1024)S(1)} %copy-done.73, f32[1120,512]{1,0:T(8,128)S(1)} %copy-done.29, bf16[1120,256]{1,0:T(8,128)(2,1)S(1)} %copy-done.30, bf16[1120,256]{1,0:T(8,128)(2,1)S(1)} %copy-done.59, bf16[1120,256]{1,0:T(8,128)(2,1)S(1)} %copy-done.31, ...), custom_call_target="tpu_custom_call" | custom-call | flops 1 | bytes 1 | tf_op jit(solution)/shard_map/tokens_back/pallas_call | solution.py:134
  322.9 3.2 collective-permute-done.49
  326.2 4.1 %collective-permute-done.50 = bf16[1,144,384]{2,1,0:T(8,128)(2,1)S(1)} collective-permute-done((bf16[1,144,384]{2,1,0:T(8,128)(2,1)}, bf16[1,144,384]{2,1,0:T(8,128)(2,1)S(1)}, u32[]{:S(2)}, u32[]{:S(2)}) %collective-permute-start.50) | collective-permute-done | bytes 110624 | tf_op jit(solution)/shard_map/ppermute | solution.py:35
  332.4 6.7 %collective-permute-done.52.refs_2_ = bf16[144,960]{1,0:T(8,128)(2,1)S(1)} collective-permute-done((bf16[144,960]{1,0:T(8,128)(2,1)S(1)}, bf16[144,960]{1,0:T(8,128)(2,1)S(1)}, u32[]{:S(2)}, u32[]{:S(2)}) %collective-permute-start.52) | collective-permute-done | bytes 276512 | tf_op jit(solution)/shard_map/ppermute | solution.py:35
  (325 shorter events, 53.5 us)
Async XLA Ops:
  4.6 23.7 %copy-start.50 = (bf16[1152,256]{1,0:T(8,128)(2,1)}, bf16[1152,256]{1,0:T(8,128)(2,1)S(1)}, u32[]{:S(2)}) copy-start(bf16[1152,256]{1,0:T(8,128)(2,1)S(1)} %widen.2.refs_0_.refs_4_) | copy-start | bytes 1769476
  4.6 23.6 %collective-permute-start = (bf16[1152,256]{1,0:T(8,128)(2,1)S(1)}, bf16[1152,256]{1,0:T(8,128)(2,1)S(1)}, u32[]{:S(2)}, u32[]{:S(2)}) collective-permute-start(bf16[1152,256]{1,0:T(8,128)(2,1)S(1)} %widen.2.refs_0_.refs_4_), channel_id=1, source_target_pairs={{0,1},{1,0},{2,3},{3,2},{4,5},{5,4},{6,7},{7,6},{8,9},{9,8},{10,11... | collective-permute-start | bytes 1769480 | tf_op jit(solution)/shard_map/ppermute | solution.py:35
  5.2 20.4 %collective-permute-start.1 = (bf16[1152,256]{1,0:T(8,128)(2,1)S(1)}, bf16[1152,256]{1,0:T(8,128)(2,1)S(1)}, u32[]{:S(2)}, u32[]{:S(2)}) collective-permute-start(bf16[1152,256]{1,0:T(8,128)(2,1)S(1)} %widen.2.refs_0_.refs_4_), channel_id=1, source_target_pairs={{0,2},{1,3},{2,0},{3,1},{4,6},{5,7},{6,4},{7,5},{8,10},{9,11},{10,... | collective-permute-start | bytes 1769480 | tf_op jit(solution)/shard_map/ppermute | solution.py:35
  8.4 40.2 %copy-start.42 = (bf16[1152,256]{1,0:T(8,128)(2,1)}, bf16[1152,256]{1,0:T(8,128)(2,1)S(1)}, u32[]{:S(2)}) copy-start(bf16[1152,256]{1,0:T(8,128)(2,1)S(1)} %widen.3.refs_0_.refs_4_) | copy-start | bytes 1769476
  25.5 2.7 collective-permute-start.2
  25.7 22.8 %collective-permute-start.6 = (bf16[1152,256]{1,0:T(8,128)(2,1)S(1)}, bf16[1152,256]{1,0:T(8,128)(2,1)S(1)}, u32[]{:S(2)}, u32[]{:S(2)}) collective-permute-start(bf16[1152,256]{1,0:T(8,128)(2,1)S(1)} %widen.3.refs_0_.refs_4_), channel_id=1, source_target_pairs={{0,1},{1,0},{2,3},{3,2},{4,5},{5,4},{6,7},{7,6},{8,9},{9,8},{10,11... | collective-permute-start | bytes 1769480 | tf_op jit(solution)/shard_map/ppermute | solution.py:35
  26.0 20.5 %collective-permute-start.7 = (bf16[1152,256]{1,0:T(8,128)(2,1)S(1)}, bf16[1152,256]{1,0:T(8,128)(2,1)S(1)}, u32[]{:S(2)}, u32[]{:S(2)}) collective-permute-start(bf16[1152,256]{1,0:T(8,128)(2,1)S(1)} %widen.3.refs_0_.refs_4_), channel_id=1, source_target_pairs={{0,2},{1,3},{2,0},{3,1},{4,6},{5,7},{6,4},{7,5},{8,10},{9,11},{10,... | collective-permute-start | bytes 1769480 | tf_op jit(solution)/shard_map/ppermute | solution.py:35
  28.3 47.7 %slice-start.6 = ((s8[9175040]{0:T(1024)(128)(4,1)}), s8[4194304]{0:T(1024)(128)(4,1)S(1)}, s32[]{:S(2)}) async-start(s8[9175040]{0:T(1024)(128)(4,1)} %bitcast.57), calls=%async_computation.6 | async-start | bytes 8388608
  28.3 47.7 %slice-start.7 = ((s8[9175040]{0:T(1024)(128)(4,1)}), s8[4194304]{0:T(1024)(128)(4,1)S(1)}, s32[]{:S(2)}) async-start(s8[9175040]{0:T(1024)(128)(4,1)} %bitcast.57), calls=%async_computation.7 | async-start | bytes 8388608
  46.5 2.0 collective-permute-start.8
  46.5 19.6 %collective-permute-start.3 = (bf16[280,256]{1,0:T(8,128)(2,1)S(1)}, bf16[280,256]{1,0:T(8,128)(2,1)S(1)}, u32[]{:S(2)}, u32[]{:S(2)}) collective-permute-start(bf16[280,256]{1,0:T(8,128)(2,1)S(1)} %get-tuple-element.266), channel_id=1, source_target_pairs={{0,1},{1,0},{2,3},{3,2},{4,5},{5,4},{6,7},{7,6},{8,9},{9,8},{10,11... | collective-permute-start | bytes 430088 | tf_op jit(solution)/shard_map/ppermute | solution.py:35
  47.0 19.4 %collective-permute-start.4 = (bf16[280,256]{1,0:T(8,128)(2,1)S(1)}, bf16[280,256]{1,0:T(8,128)(2,1)S(1)}, u32[]{:S(2)}, u32[]{:S(2)}) collective-permute-start(bf16[280,256]{1,0:T(8,128)(2,1)S(1)} %get-tuple-element.267), channel_id=1, source_target_pairs={{0,2},{1,3},{2,0},{3,1},{4,6},{5,7},{6,4},{7,5},{8,10},{9,11},{10,... | collective-permute-start | bytes 430088 | tf_op jit(solution)/shard_map/ppermute | solution.py:35
  48.5 27.5 %slice-start.8 = ((s8[9175040]{0:T(1024)(128)(4,1)}), s8[786432]{0:T(1024)(128)(4,1)S(1)}, s32[]{:S(2)}) async-start(s8[9175040]{0:T(1024)(128)(4,1)} %bitcast.57), calls=%async_computation.8 | async-start | bytes 1572864
  48.5 17.9 %collective-permute-start.5 = (bf16[280,256]{1,0:T(8,128)(2,1)S(1)}, bf16[280,256]{1,0:T(8,128)(2,1)S(1)}, u32[]{:S(2)}, u32[]{:S(2)}) collective-permute-start(bf16[280,256]{1,0:T(8,128)(2,1)S(1)} %get-tuple-element.268), channel_id=1, source_target_pairs={{0,3},{1,2},{2,1},{3,0},{4,7},{5,6},{6,5},{7,4},{8,11},{9,10},{10,... | collective-permute-start | bytes 430088 | tf_op jit(solution)/shard_map/ppermute | solution.py:35
  64.0 7.8 %collective-permute-start.10 = (bf16[280,256]{1,0:T(8,128)(2,1)S(1)}, bf16[280,256]{1,0:T(8,128)(2,1)S(1)}, u32[]{:S(2)}, u32[]{:S(2)}) collective-permute-start(bf16[280,256]{1,0:T(8,128)(2,1)S(1)} %get-tuple-element.284), channel_id=1, source_target_pairs={{0,2},{1,3},{2,0},{3,1},{4,6},{5,7},{6,4},{7,5},{8,10},{9,11},{10,... | collective-permute-start | bytes 430088 | tf_op jit(solution)/shard_map/ppermute | solution.py:35
  65.6 7.6 %collective-permute-start.11 = (bf16[280,256]{1,0:T(8,128)(2,1)S(1)}, bf16[280,256]{1,0:T(8,128)(2,1)S(1)}, u32[]{:S(2)}, u32[]{:S(2)}) collective-permute-start(bf16[280,256]{1,0:T(8,128)(2,1)S(1)} %get-tuple-element.285), channel_id=1, source_target_pairs={{0,3},{1,2},{2,1},{3,0},{4,7},{5,6},{6,5},{7,4},{8,11},{9,10},{10,... | collective-permute-start | bytes 430088 | tf_op jit(solution)/shard_map/ppermute | solution.py:35
  66.1 7.1 %collective-permute-start.9 = (bf16[280,256]{1,0:T(8,128)(2,1)S(1)}, bf16[280,256]{1,0:T(8,128)(2,1)S(1)}, u32[]{:S(2)}, u32[]{:S(2)}) collective-permute-start(bf16[280,256]{1,0:T(8,128)(2,1)S(1)} %get-tuple-element.283), channel_id=1, source_target_pairs={{0,1},{1,0},{2,3},{3,2},{4,5},{5,4},{6,7},{7,6},{8,9},{9,8},{10,11... | collective-permute-start | bytes 430088 | tf_op jit(solution)/shard_map/ppermute | solution.py:35
  75.9 20.3 %copy-start.18 = (f32[1120,256]{1,0:T(8,128)}, f32[1120,256]{1,0:T(8,128)S(1)}, u32[]{:S(2)}) copy-start(f32[1120,256]{1,0:T(8,128)S(1)} %get-tuple-element.306.refs_1_.refs_4_) | copy-start | bytes 3440644
  76.0 20.3 %copy-start.62 = (bf16[1120,256]{1,0:T(8,128)(2,1)}, bf16[1120,256]{1,0:T(8,128)(2,1)S(1)}, u32[]{:S(2)}) copy-start(bf16[1120,256]{1,0:T(8,128)(2,1)S(1)} %get-tuple-element.313.refs_1_) | copy-start | bytes 1720324
  103.0 8.8 %collective-permute-start.12 = (bf16[2,8,144,1120]{3,2,1,0:T(8,128)(2,1)S(1)}, bf16[2,8,144,1120]{3,2,1,0:T(8,128)(2,1)S(1)}, u32[]{:S(2)}, u32[]{:S(2)}) collective-permute-start(bf16[2,8,144,1120]{3,2,1,0:T(8,128)(2,1)S(1)} %down_outer.2), channel_id=1, source_target_pairs={{0,1},{1,0},{2,3},{3,2},{4,5},{5,4},{6,7},{7,6},{8,9},{9,8},{10,11... | collective-permute-start | bytes 15482888 | tf_op jit(solution)/shard_map/ppermute | solution.py:35
  108.6 14.4 %collective-permute-start.13 = (bf16[2,8,144,1120]{3,2,1,0:T(8,128)(2,1)S(1)}, bf16[2,8,144,1120]{3,2,1,0:T(8,128)(2,1)S(1)}, u32[]{:S(2)}, u32[]{:S(2)}) collective-permute-start(bf16[2,8,144,1120]{3,2,1,0:T(8,128)(2,1)S(1)} %up_outer.2), channel_id=1, source_target_pairs={{0,1},{1,0},{2,3},{3,2},{4,5},{5,4},{6,7},{7,6},{8,9},{9,8},{10,11... | collective-permute-start | bytes 15482888 | tf_op jit(solution)/shard_map/ppermute | solution.py:35
  121.5 44.6 %collective-permute-start.15 = (bf16[8,96,1120]{2,1,0:T(8,128)(2,1)}, bf16[8,96,1120]{2,1,0:T(8,128)(2,1)}, u32[]{:S(2)}, u32[]{:S(2)}) collective-permute-start(bf16[8,96,1120]{2,1,0:T(8,128)(2,1)} %bitcast.11), channel_id=1, source_target_pairs={{0,2},{1,3},{2,0},{3,1},{4,6},{5,7},{6,4},{7,5},{8,10},{9,11},{10,... | collective-permute-start | bytes 5160968 | tf_op jit(solution)/shard_map/ppermute | solution.py:35
  130.6 41.0 %collective-permute-start.17 = (bf16[8,96,1120]{2,1,0:T(8,128)(2,1)}, bf16[8,96,1120]{2,1,0:T(8,128)(2,1)}, u32[]{:S(2)}, u32[]{:S(2)}) collective-permute-start(bf16[8,96,1120]{2,1,0:T(8,128)(2,1)} %bitcast.13), channel_id=1, source_target_pairs={{0,8},{4,12},{8,0},{12,4},{16,24},{20,28},{24,16},{28,20},{1,9},{5... | collective-permute-start | bytes 5160968 | tf_op jit(solution)/shard_map/ppermute | solution.py:35
  132.2 40.7 %collective-permute-start.18 = (bf16[8,96,1120]{2,1,0:T(8,128)(2,1)}, bf16[8,96,1120]{2,1,0:T(8,128)(2,1)}, u32[]{:S(2)}, u32[]{:S(2)}) collective-permute-start(bf16[8,96,1120]{2,1,0:T(8,128)(2,1)} %bitcast.14), channel_id=1, source_target_pairs={{0,4},{4,0},{8,12},{12,8},{16,20},{20,16},{24,28},{28,24},{1,5},{5... | collective-permute-start | bytes 5160968 | tf_op jit(solution)/shard_map/ppermute | solution.py:35
  150.2 30.7 %collective-permute-start.14 = (bf16[2,2,5,64,256]{4,3,2,1,0:T(8,128)(2,1)S(1)}, bf16[2,2,5,64,256]{4,3,2,1,0:T(8,128)(2,1)S(1)}, u32[]{:S(2)}, u32[]{:S(2)}) collective-permute-start(bf16[2,2,5,64,256]{4,3,2,1,0:T(8,128)(2,1)S(1)} %get-tuple-element.310), channel_id=1, source_target_pairs={{0,2},{1,3},{2,0},{3,1},{4,6},{5,7},{6,4},{7,5},{8,10},{9,11},{10,... | collective-permute-start | bytes 1966088 | tf_op jit(solution)/shard_map/ppermute | solution.py:35
  155.5 60.0 %collective-permute-start.19 = (bf16[16,80,576]{2,1,0:T(8,128)(2,1)}, bf16[16,80,576]{2,1,0:T(8,128)(2,1)S(1)}, u32[]{:S(2)}, u32[]{:S(2)}) collective-permute-start(bf16[16,80,576]{2,1,0:T(8,128)(2,1)} %bitcast.17), channel_id=1, source_target_pairs={{0,1},{1,0},{2,3},{3,2},{4,5},{5,4},{6,7},{7,6},{8,9},{9,8},{10,11... | collective-permute-start | bytes 4423688 | tf_op jit(solution)/shard_map/ppermute | solution.py:35
  178.3 21.0 %collective-permute-start.22 = (bf16[4,96,1120]{2,1,0:T(8,128)(2,1)S(1)}, bf16[4,96,1120]{2,1,0:T(8,128)(2,1)S(1)}, u32[]{:S(2)}, u32[]{:S(2)}) collective-permute-start(bf16[4,96,1120]{2,1,0:T(8,128)(2,1)S(1)} %get-tuple-element.339), channel_id=1, source_target_pairs={{0,2},{1,3},{2,0},{3,1},{4,6},{5,7},{6,4},{7,5},{8,10},{9,11},{10,... | collective-permute-start | bytes 2580488 | tf_op jit(solution)/shard_map/ppermute | solution.py:35
  178.9 20.4 %collective-permute-start.21 = (bf16[4,96,1120]{2,1,0:T(8,128)(2,1)S(1)}, bf16[4,96,1120]{2,1,0:T(8,128)(2,1)S(1)}, u32[]{:S(2)}, u32[]{:S(2)}) collective-permute-start(bf16[4,96,1120]{2,1,0:T(8,128)(2,1)S(1)} %get-tuple-element.338), channel_id=1, source_target_pairs={{0,8},{4,12},{8,0},{12,4},{16,24},{20,28},{24,16},{28,20},{1,9},{5... | collective-permute-start | bytes 2580488 | tf_op jit(solution)/shard_map/ppermute | solution.py:35
  179.4 20.2 %collective-permute-start.20 = (bf16[4,96,1120]{2,1,0:T(8,128)(2,1)S(1)}, bf16[4,96,1120]{2,1,0:T(8,128)(2,1)S(1)}, u32[]{:S(2)}, u32[]{:S(2)}) collective-permute-start(bf16[4,96,1120]{2,1,0:T(8,128)(2,1)S(1)} %get-tuple-element.337), channel_id=1, source_target_pairs={{0,4},{4,0},{8,12},{12,8},{16,20},{20,16},{24,28},{28,24},{1,5},{5... | collective-permute-start | bytes 2580488 | tf_op jit(solution)/shard_map/ppermute | solution.py:35
  181.0 2.2 collective-permute-start.16
  200.4 14.0 %collective-permute-start.25 = (bf16[2,96,1120]{2,1,0:T(8,128)(2,1)S(1)}, bf16[2,96,1120]{2,1,0:T(8,128)(2,1)S(1)}, u32[]{:S(2)}, u32[]{:S(2)}) collective-permute-start(bf16[2,96,1120]{2,1,0:T(8,128)(2,1)S(1)} %get-tuple-element.358), channel_id=1, source_target_pairs={{0,4},{4,0},{8,12},{12,8},{16,20},{20,16},{24,28},{28,24},{1,5},{5... | collective-permute-start | bytes 1290248 | tf_op jit(solution)/shard_map/ppermute | solution.py:35
  202.0 12.3 %collective-permute-start.24 = (bf16[2,96,1120]{2,1,0:T(8,128)(2,1)S(1)}, bf16[2,96,1120]{2,1,0:T(8,128)(2,1)S(1)}, u32[]{:S(2)}, u32[]{:S(2)}) collective-permute-start(bf16[2,96,1120]{2,1,0:T(8,128)(2,1)S(1)} %get-tuple-element.353), channel_id=1, source_target_pairs={{0,2},{1,3},{2,0},{3,1},{4,6},{5,7},{6,4},{7,5},{8,10},{9,11},{10,... | collective-permute-start | bytes 1290248 | tf_op jit(solution)/shard_map/ppermute | solution.py:35
  203.5 10.9 %collective-permute-start.23 = (bf16[2,96,1120]{2,1,0:T(8,128)(2,1)S(1)}, bf16[2,96,1120]{2,1,0:T(8,128)(2,1)S(1)}, u32[]{:S(2)}, u32[]{:S(2)}) collective-permute-start(bf16[2,96,1120]{2,1,0:T(8,128)(2,1)S(1)} %get-tuple-element.349), channel_id=1, source_target_pairs={{0,8},{4,12},{8,0},{12,4},{16,24},{20,28},{24,16},{28,20},{1,9},{5... | collective-permute-start | bytes 1290248 | tf_op jit(solution)/shard_map/ppermute | solution.py:35
  222.5 18.2 %collective-permute-start.26 = (bf16[1120,256]{1,0:T(8,128)(2,1)S(1)}, bf16[1120,256]{1,0:T(8,128)(2,1)S(1)}, u32[]{:S(2)}, u32[]{:S(2)}) collective-permute-start(bf16[1120,256]{1,0:T(8,128)(2,1)S(1)} %get-tuple-element.381), channel_id=1, source_target_pairs={{0,1},{1,0},{2,3},{3,2},{4,5},{5,4},{6,7},{7,6},{8,9},{9,8},{10,11... | collective-permute-start | bytes 1720328 | tf_op jit(solution)/shard_map/ppermute | solution.py:35
  222.5 18.2 %collective-permute-start.27 = (bf16[1120,256]{1,0:T(8,128)(2,1)S(1)}, bf16[1120,256]{1,0:T(8,128)(2,1)S(1)}, u32[]{:S(2)}, u32[]{:S(2)}) collective-permute-start(bf16[1120,256]{1,0:T(8,128)(2,1)S(1)} %get-tuple-element.383), channel_id=1, source_target_pairs={{0,1},{1,0},{2,3},{3,2},{4,5},{5,4},{6,7},{7,6},{8,9},{9,8},{10,11... | collective-permute-start | bytes 1720328 | tf_op jit(solution)/shard_map/ppermute | solution.py:35
  227.6 13.1 %collective-permute-start.30 = (bf16[4,80,576]{2,1,0:T(8,128)(2,1)S(1)}, bf16[4,80,576]{2,1,0:T(8,128)(2,1)S(1)}, u32[]{:S(2)}, u32[]{:S(2)}) collective-permute-start(bf16[4,80,576]{2,1,0:T(8,128)(2,1)S(1)} %get-tuple-element.390), channel_id=1, source_target_pairs={{0,4},{4,0},{8,12},{12,8},{16,20},{20,16},{24,28},{28,24},{1,5},{5... | collective-permute-start | bytes 1105928 | tf_op jit(solution)/shard_map/ppermute | solution.py:35
  228.7 9.4 %collective-permute-start.29 = (bf16[4,64,576]{2,1,0:T(8,128)(2,1)S(1)}, bf16[4,64,576]{2,1,0:T(8,128)(2,1)S(1)}, u32[]{:S(2)}, u32[]{:S(2)}) collective-permute-start(bf16[4,64,576]{2,1,0:T(8,128)(2,1)S(1)} %get-tuple-element.400), channel_id=1, source_target_pairs={{0,8},{4,12},{8,0},{12,4},{16,24},{20,28},{24,16},{28,20},{1,9},{5... | collective-permute-start | bytes 884744 | tf_op jit(solution)/shard_map/ppermute | solution.py:35
  230.3 21.2 %collective-permute-start.31 = (bf16[8,80,576]{2,1,0:T(8,128)(2,1)S(1)}, bf16[8,80,576]{2,1,0:T(8,128)(2,1)S(1)}, u32[]{:S(2)}, u32[]{:S(2)}) collective-permute-start(bf16[8,80,576]{2,1,0:T(8,128)(2,1)S(1)} %get-tuple-element.404), channel_id=1, source_target_pairs={{0,2},{1,3},{2,0},{3,1},{4,6},{5,7},{6,4},{7,5},{8,10},{9,11},{10,... | collective-permute-start | bytes 2211848 | tf_op jit(solution)/shard_map/ppermute | solution.py:35
  238.1 31.0 %collective-permute-start.32 = (bf16[1,288,1120]{2,1,0:T(8,128)(2,1)S(1)}, bf16[1,288,1120]{2,1,0:T(8,128)(2,1)S(1)}, u32[]{:S(2)}, u32[]{:S(2)}) collective-permute-start(bf16[1,288,1120]{2,1,0:T(8,128)(2,1)S(1)} %get-tuple-element.417), channel_id=1, source_target_pairs={{0,16},{4,20},{8,24},{12,28},{16,0},{20,4},{24,8},{28,12},{1,17},{... | collective-permute-start | bytes 1935368 | tf_op jit(solution)/shard_map/ppermute | solution.py:35
  240.9 44.5 %collective-permute-start.28 = (bf16[1120,256]{1,0:T(8,128)(2,1)S(1)}, bf16[1120,256]{1,0:T(8,128)(2,1)S(1)}, u32[]{:S(2)}, u32[]{:S(2)}) collective-permute-start(bf16[1120,256]{1,0:T(8,128)(2,1)S(1)} %add_convert_fusion.2), channel_id=1, source_target_pairs={{0,2},{1,3},{2,0},{3,1},{4,6},{5,7},{6,4},{7,5},{8,10},{9,11},{10,... | collective-permute-start | bytes 1720328 | tf_op jit(solution)/shard_map/ppermute | solution.py:35
  255.4 19.4 %collective-permute-start.35 = (bf16[2,80,576]{2,1,0:T(8,128)(2,1)S(1)}, bf16[2,80,576]{2,1,0:T(8,128)(2,1)S(1)}, u32[]{:S(2)}, u32[]{:S(2)}) collective-permute-start(bf16[2,80,576]{2,1,0:T(8,128)(2,1)S(1)} %get-tuple-element.424), channel_id=1, source_target_pairs={{0,8},{4,12},{8,0},{12,4},{16,24},{20,28},{24,16},{28,20},{1,9},{5... | collective-permute-start | bytes 552968 | tf_op jit(solution)/shard_map/ppermute | solution.py:35
  256.0 18.7 %collective-permute-start.36 = (bf16[2,64,576]{2,1,0:T(8,128)(2,1)S(1)}, bf16[2,64,576]{2,1,0:T(8,128)(2,1)S(1)}, u32[]{:S(2)}, u32[]{:S(2)}) collective-permute-start(bf16[2,64,576]{2,1,0:T(8,128)(2,1)S(1)} %get-tuple-element.425), channel_id=1, source_target_pairs={{0,4},{4,0},{8,12},{12,8},{16,20},{20,16},{24,28},{28,24},{1,5},{5... | collective-permute-start | bytes 442376 | tf_op jit(solution)/shard_map/ppermute | solution.py:35
  257.0 19.8 %collective-permute-start.40 = (bf16[4,64,384]{2,1,0:T(8,128)(2,1)S(1)}, bf16[4,64,384]{2,1,0:T(8,128)(2,1)S(1)}, u32[]{:S(2)}, u32[]{:S(2)}) collective-permute-start(bf16[4,64,384]{2,1,0:T(8,128)(2,1)S(1)} %get-tuple-element.435), channel_id=1, source_target_pairs={{0,8},{4,12},{8,0},{12,4},{16,24},{20,28},{24,16},{28,20},{1,9},{5... | collective-permute-start | bytes 589832 | tf_op jit(solution)/shard_map/ppermute | solution.py:35
  269.1 16.3 %collective-permute-start.38 = (bf16[4,80,576]{2,1,0:T(8,128)(2,1)S(1)}, bf16[4,80,576]{2,1,0:T(8,128)(2,1)S(1)}, u32[]{:S(2)}, u32[]{:S(2)}) collective-permute-start(bf16[4,80,576]{2,1,0:T(8,128)(2,1)S(1)} %get-tuple-element.434), channel_id=1, source_target_pairs={{0,4},{4,0},{8,12},{12,8},{16,20},{20,16},{24,28},{28,24},{1,5},{5... | collective-permute-start | bytes 1105928 | tf_op jit(solution)/shard_map/ppermute | solution.py:35
  274.8 18.1 %collective-permute-start.33 = (bf16[1120,256]{1,0:T(8,128)(2,1)S(1)}, bf16[1120,256]{1,0:T(8,128)(2,1)S(1)}, u32[]{:S(2)}, u32[]{:S(2)}) collective-permute-start(bf16[1120,256]{1,0:T(8,128)(2,1)S(1)} %get-tuple-element.421), channel_id=1, source_target_pairs={{0,1},{1,0},{2,3},{3,2},{4,5},{5,4},{6,7},{7,6},{8,9},{9,8},{10,11... | collective-permute-start | bytes 1720328 | tf_op jit(solution)/shard_map/ppermute | solution.py:35
  274.8 18.3 %collective-permute-start.34 = (bf16[1120,256]{1,0:T(8,128)(2,1)S(1)}, bf16[1120,256]{1,0:T(8,128)(2,1)S(1)}, u32[]{:S(2)}, u32[]{:S(2)}) collective-permute-start(bf16[1120,256]{1,0:T(8,128)(2,1)S(1)} %get-tuple-element.423), channel_id=1, source_target_pairs={{0,1},{1,0},{2,3},{3,2},{4,5},{5,4},{6,7},{7,6},{8,9},{9,8},{10,11... | collective-permute-start | bytes 1720328 | tf_op jit(solution)/shard_map/ppermute | solution.py:35
  276.8 7.7 %collective-permute-start.39 = (bf16[4,80,384]{2,1,0:T(8,128)(2,1)S(1)}, bf16[4,80,384]{2,1,0:T(8,128)(2,1)S(1)}, u32[]{:S(2)}, u32[]{:S(2)}) collective-permute-start(bf16[4,80,384]{2,1,0:T(8,128)(2,1)S(1)} %get-tuple-element.410), channel_id=1, source_target_pairs={{0,4},{4,0},{8,12},{12,8},{16,20},{20,16},{24,28},{28,24},{1,5},{5... | collective-permute-start | bytes 737288 | tf_op jit(solution)/shard_map/ppermute | solution.py:35
  284.6 6.3 %collective-permute-start.37 = (f32[4,12,140]{2,1,0:T(8,128)S(1)}, f32[4,12,140]{2,1,0:T(8,128)S(1)}, u32[]{:S(2)}, u32[]{:S(2)}) collective-permute-start(f32[4,12,140]{2,1,0:T(8,128)S(1)} %get-tuple-element.505), channel_id=1, source_target_pairs={{0,16},{4,20},{8,24},{12,28},{16,0},{20,4},{24,8},{28,12},{1,17},{... | collective-permute-start | bytes 80648 | tf_op jit(solution)/shard_map/ppermute | solution.py:35
  286.2 12.4 %collective-permute-start.44 = (bf16[2,80,576]{2,1,0:T(8,128)(2,1)S(1)}, bf16[2,80,576]{2,1,0:T(8,128)(2,1)S(1)}, u32[]{:S(2)}, u32[]{:S(2)}) collective-permute-start(bf16[2,80,576]{2,1,0:T(8,128)(2,1)S(1)} %get-tuple-element.464), channel_id=1, source_target_pairs={{0,8},{4,12},{8,0},{12,4},{16,24},{20,28},{24,16},{28,20},{1,9},{5... | collective-permute-start | bytes 552968 | tf_op jit(solution)/shard_map/ppermute | solution.py:35
  290.6 8.1 %collective-permute-start.46 = (bf16[2,64,384]{2,1,0:T(8,128)(2,1)S(1)}, bf16[2,64,384]{2,1,0:T(8,128)(2,1)S(1)}, u32[]{:S(2)}, u32[]{:S(2)}) collective-permute-start(bf16[2,64,384]{2,1,0:T(8,128)(2,1)S(1)} %get-tuple-element.466), channel_id=1, source_target_pairs={{0,4},{4,0},{8,12},{12,8},{16,20},{20,16},{24,28},{28,24},{1,5},{5... | collective-permute-start | bytes 294920 | tf_op jit(solution)/shard_map/ppermute | solution.py:35
  290.9 7.8 %collective-permute-start.45 = (bf16[2,80,384]{2,1,0:T(8,128)(2,1)S(1)}, bf16[2,80,384]{2,1,0:T(8,128)(2,1)S(1)}, u32[]{:S(2)}, u32[]{:S(2)}) collective-permute-start(bf16[2,80,384]{2,1,0:T(8,128)(2,1)S(1)} %get-tuple-element.465), channel_id=1, source_target_pairs={{0,8},{4,12},{8,0},{12,4},{16,24},{20,28},{24,16},{28,20},{1,9},{5... | collective-permute-start | bytes 368648 | tf_op jit(solution)/shard_map/ppermute | solution.py:35
  292.8 5.3 %collective-permute-start.42 = (f32[2,12,140]{2,1,0:T(8,128)S(1)}, f32[2,12,140]{2,1,0:T(8,128)S(1)}, u32[]{:S(2)}, u32[]{:S(2)}) collective-permute-start(f32[2,12,140]{2,1,0:T(8,128)S(1)} %get-tuple-element.507), channel_id=1, source_target_pairs={{0,8},{4,12},{8,0},{12,4},{16,24},{20,28},{24,16},{28,20},{1,9},{5... | collective-permute-start | bytes 40328 | tf_op jit(solution)/shard_map/ppermute | solution.py:35
  294.1 20.2 %copy-start.23 = (bf16[2,256,1120]{1,2,0:T(8,128)(2,1)S(1)}, bf16[2,256,1120]{1,2,0:T(8,128)(2,1)}, u32[]{:S(2)}) copy-start(bf16[2,256,1120]{1,2,0:T(8,128)(2,1)} %param.21) | copy-start | bytes 3440644
  294.1 20.2 %copy-start.29 = (f32[1120,512]{1,0:T(8,128)S(1)}, f32[1120,512]{1,0:T(8,128)}, u32[]{:S(2)}) copy-start(f32[1120,512]{1,0:T(8,128)} %copy-done.28) | copy-start | bytes 6881284
  294.1 20.2 %collective-permute-start.41 = (bf16[1120,256]{1,0:T(8,128)(2,1)}, bf16[1120,256]{1,0:T(8,128)(2,1)}, u32[]{:S(2)}, u32[]{:S(2)}) collective-permute-start(bf16[1120,256]{1,0:T(8,128)(2,1)} %add_convert_fusion), channel_id=1, source_target_pairs={{0,2},{1,3},{2,0},{3,1},{4,6},{5,7},{6,4},{7,5},{8,10},{9,11},{10,... | collective-permute-start | bytes 1720328 | tf_op jit(solution)/shard_map/ppermute | solution.py:35
  298.2 3.8 %collective-permute-start.43 = (f32[1,12,140]{2,1,0:T(8,128)S(1)}, f32[1,12,140]{2,1,0:T(8,128)S(1)}, u32[]{:S(2)}, u32[]{:S(2)}) collective-permute-start(f32[1,12,140]{2,1,0:T(8,128)S(1)} %get-tuple-element.509), channel_id=1, source_target_pairs={{0,4},{4,0},{8,12},{12,8},{16,20},{20,16},{24,28},{28,24},{1,5},{5... | collective-permute-start | bytes 20168 | tf_op jit(solution)/shard_map/ppermute | solution.py:35
  302.6 10.4 %collective-permute-start.47 = (f32[1,12,140]{2,1,0:T(8,128)}, f32[1,12,140]{2,1,0:T(8,128)}, u32[]{:S(2)}, u32[]{:S(2)}) collective-permute-start(f32[1,12,140]{2,1,0:T(8,128)} %add.63), channel_id=1, source_target_pairs={{0,1},{1,0},{2,3},{3,2},{4,5},{5,4},{6,7},{7,6},{8,9},{9,8},{10,11... | collective-permute-start | bytes 20168 | tf_op jit(solution)/shard_map/ppermute | solution.py:35
  309.0 17.1 %collective-permute-start.49 = (bf16[1,144,576]{2,1,0:T(8,128)(2,1)}, bf16[1,144,576]{2,1,0:T(8,128)(2,1)S(1)}, u32[]{:S(2)}, u32[]{:S(2)}) collective-permute-start(bf16[1,144,576]{2,1,0:T(8,128)(2,1)} %copy-done.74), channel_id=1, source_target_pairs={{0,16},{4,20},{8,24},{12,28},{16,0},{20,4},{24,8},{28,12},{1,17},{... | collective-permute-start | bytes 497672 | tf_op jit(solution)/shard_map/ppermute | solution.py:35
  310.0 21.2 %collective-permute-start.54 = (bf16[1,80,576]{2,1,0:T(8,128)(2,1)}, bf16[1,80,576]{2,1,0:T(8,128)(2,1)S(1)}, u32[]{:S(2)}, u32[]{:S(2)}) collective-permute-start(bf16[1,80,576]{2,1,0:T(8,128)(2,1)} %copy-done.76), channel_id=1, source_target_pairs={{0,16},{4,20},{8,24},{12,28},{16,0},{20,4},{24,8},{28,12},{1,17},{... | collective-permute-start | bytes 276488 | tf_op jit(solution)/shard_map/ppermute | solution.py:35
  312.0 18.3 %collective-permute-start.50 = (bf16[1,144,384]{2,1,0:T(8,128)(2,1)}, bf16[1,144,384]{2,1,0:T(8,128)(2,1)S(1)}, u32[]{:S(2)}, u32[]{:S(2)}) collective-permute-start(bf16[1,144,384]{2,1,0:T(8,128)(2,1)} %copy-done.75), channel_id=1, source_target_pairs={{0,16},{4,20},{8,24},{12,28},{16,0},{20,4},{24,8},{28,12},{1,17},{... | collective-permute-start | bytes 331784 | tf_op jit(solution)/shard_map/ppermute | solution.py:35
  313.7 16.9 %collective-permute-start.48 = (f32[1,12,140]{2,1,0:T(8,128)S(1)}, f32[1,12,140]{2,1,0:T(8,128)S(1)}, u32[]{:S(2)}, u32[]{:S(2)}) collective-permute-start(f32[1,12,140]{2,1,0:T(8,128)S(1)} %add.64), channel_id=1, source_target_pairs={{0,2},{1,3},{2,0},{3,1},{4,6},{5,7},{6,4},{7,5},{8,10},{9,11},{10,... | collective-permute-start | bytes 20168 | tf_op jit(solution)/shard_map/ppermute | solution.py:35
  330.5 8.7 %collective-permute-start.52 = (bf16[144,960]{1,0:T(8,128)(2,1)S(1)}, bf16[144,960]{1,0:T(8,128)(2,1)S(1)}, u32[]{:S(2)}, u32[]{:S(2)}) collective-permute-start(bf16[144,960]{1,0:T(8,128)(2,1)S(1)} %maximum_maximum_fusion.refs_0_), channel_id=1, source_target_pairs={{0,2},{1,3},{2,0},{3,1},{4,6},{5,7},{6,4},{7,5},{8,10},{9,11},{10,... | collective-permute-start | bytes 829448 | tf_op jit(solution)/shard_map/ppermute | solution.py:35
  330.6 10.9 %collective-permute-start.51 = (bf16[144,960]{1,0:T(8,128)(2,1)S(1)}, bf16[144,960]{1,0:T(8,128)(2,1)S(1)}, u32[]{:S(2)}, u32[]{:S(2)}) collective-permute-start(bf16[144,960]{1,0:T(8,128)(2,1)S(1)} %maximum_maximum_fusion.refs_0_), channel_id=1, source_target_pairs={{0,1},{1,0},{2,3},{3,2},{4,5},{5,4},{6,7},{7,6},{8,9},{9,8},{10,11... | collective-permute-start | bytes 829448 | tf_op jit(solution)/shard_map/ppermute | solution.py:35
  339.2 2.4 collective-permute-start.53
  (86 other events, 526.7 us)
